TPU v7x, 32 devices: a whole 2x2x4 slice. The times are simulated.
32 devices in a mesh: tile: 8 (over y, x, core), rep: 4 (over z).
Axes of the slice: x: 2, y: 2, z: 4, core: 2. Of those that a mesh axis runs over, the one named last changes fastest.
Arguments:
- inputs: bfloat16 [8192, 1024], P(('rep', 'tile')), parts along dimension 0, may hold values from -6 to 6
- queries: bfloat16 [8192, 1024], P(('rep', 'tile')), parts along dimension 0, may hold values from -180 to 180
- key_vectors: bfloat16 [8192, 1024], P(('rep', 'tile')), parts along dimension 0, may hold values from -6 to 6
- values: bfloat16 [8192, 1024], P(('rep', 'tile')), parts along dimension 0, may hold values from -16 to 16
- out_weight: bfloat16 [1024, 1024], replicated, may hold values from -0.1875 to 0.1875
- norm_gain: float32 [1024], replicated, may hold values from 0.5 to 1.5
- routes: int32 [8192, 2], P(('rep', 'tile')), parts along dimension 0, may hold values from 0 to 7, all different within a row; in each aligned block of 128 rows (0 to 127, 128 to 255, ...) at most 64 rows name the same one
- route_gates: float32 [8192, 2], P(('rep', 'tile')), parts along dimension 0, may hold values from 0.2 to 1
- w_gate: bfloat16 [8, 1024, 1408], P('tile'), may hold values from -0.1875 to 0.1875
- w_up: bfloat16 [8, 1024, 1408], P('tile'), may hold values from -0.1875 to 0.1875
- w_down: bfloat16 [8, 1408, 1024], P('tile'), may hold values from -0.15625 to 0.15625
Outputs:
- layer_out: bfloat16 [8192, 1024], P(('rep', 'tile')), parts along dimension 0
There are 4 independent parts, one for each index of `rep`. A program takes and returns all parts, laid end to end along the dimension named above; an argument that names none is the same for every part. Nothing has to cross between parts.
Inputs may be any that keep to these rules, and one draw needn't show every extreme that they name: `routes`: in each aligned block of 128 tokens no expert is named by more than 64 tokens, and some expert is named by exactly that many; each token names 2 different experts.
All inputs are finite; a program needn't handle non-finite values.
Results may differ from a plain program's by a relative error of at most 0.0061.
Values may be sent and summed in bfloat16 or wider, within the bound.
No kernel may reach another device: no remote copies, remote signals or barrier semaphores. Data moves between devices by JAX's collectives and lax.ppermute only.
A program may use at most 64 MiB of HBM per device.

v0:
```python
import jax
import jax.numpy as jnp
from jax import lax
from jax.sharding import PartitionSpec as P

HEADS = 16
HD = 64
IL_DEV = 4
XL = 8
DP = 8
R_IL = 2
R_XL = 2
R_DP = 2


def with_halo(shard, sides, width):
    for axis, dim in sides:
        count, length = (lax.axis_size(axis), shard.shape[dim])
        up = [(i, (i + 1) % count) for i in range(count - 1)]
        down = [(j, i) for i, j in up]
        last = lax.slice_in_dim(shard, length - width, length, axis=dim)
        initial = lax.slice_in_dim(shard, 0, width, axis=dim)
        before = lax.ppermute(last, axis, up)
        after = lax.ppermute(initial, axis, down)
        shard = jnp.concatenate([before, shard, after], axis=dim)
    return shard


def local_attention(query_block, key_block, value_block, first_inline, total_inlines):
    query_count = query_block.shape[0]
    key_count = key_block.shape[0]
    plane = XL * DP
    query_pos = jnp.arange(query_count, dtype=jnp.int32)
    key_pos = jnp.arange(key_count, dtype=jnp.int32)
    query_il = query_pos // plane
    query_xl = query_pos // DP % XL
    query_dp = query_pos % DP
    key_il = key_pos // plane - R_IL
    key_xl = key_pos // DP % XL
    key_dp = key_pos % DP
    near = jnp.abs(query_il[:, None] - key_il[None, :]) <= R_IL
    near = near & (jnp.abs(query_xl[:, None] - key_xl[None, :]) <= R_XL)
    near = near & (jnp.abs(query_dp[:, None] - key_dp[None, :]) <= R_DP)
    inside = (first_inline + key_il >= 0) & (first_inline + key_il < total_inlines)
    near = near & inside[None, :]
    query_heads = query_block.reshape(query_count, HEADS, HD)
    key_heads = key_block.reshape(key_count, HEADS, HD)
    value_heads = value_block.reshape(key_count, HEADS, HD)
    scores = jnp.einsum(
        "qhd,khd->hqk", query_heads, key_heads, preferred_element_type=jnp.float32
    ) * (1.0 / HD**0.5)
    scores = jnp.where(near[None], scores, jnp.float32(-1e30))
    highest = jnp.max(scores, axis=-1, keepdims=True)
    weights = jnp.exp(scores - highest)
    weights = jnp.where(near[None], weights, jnp.float32(0.0))
    totals = jnp.sum(weights, axis=-1, keepdims=True)
    probs = (weights / totals).astype(jnp.bfloat16)
    attended = jnp.einsum("hqk,khd->qhd", probs, value_heads, preferred_element_type=jnp.float32)
    return attended.astype(jnp.bfloat16).reshape(query_count, HEADS * HD)


def expert_rows(token_rows, gate_mat, up_mat, down_mat):
    gate_part = jnp.dot(token_rows, gate_mat, preferred_element_type=jnp.float32)
    up_part = jnp.dot(token_rows, up_mat, preferred_element_type=jnp.float32)
    hidden = (jax.nn.silu(gate_part) * up_part).astype(jnp.bfloat16)
    return jnp.dot(hidden, down_mat, preferred_element_type=jnp.float32).astype(jnp.bfloat16)


def slot_ranks(routes, experts, block_rows):
    row_count = routes.shape[0]
    expert_ids = jnp.arange(experts, dtype=jnp.int32)
    matches = routes[:, :, None] == expert_ids[None, None, :]
    hits = jnp.sum(matches.astype(jnp.int32), axis=1)
    hits = hits.reshape(row_count // block_rows, block_rows, experts)
    earlier = (jnp.cumsum(hits, axis=1) - hits).reshape(row_count, experts)
    return jnp.sum(jnp.where(matches, earlier[:, None, :], 0), axis=-1)


def local(
    inputs,
    queries,
    key_vectors,
    values,
    out_weight,
    norm_gain,
    routes,
    route_gates,
    w_gate,
    w_up,
    w_down,
):
    row_count = inputs.shape[0]
    model = inputs.shape[1]
    tiles = lax.axis_size("tile")
    first_inline = lax.axis_index("tile") * IL_DEV
    width = R_IL * XL * DP
    key_value = jnp.concatenate([key_vectors, values], axis=1)
    extended = with_halo(key_value, (("tile", 0),), width)
    attended = local_attention(
        queries, extended[:, :model], extended[:, model:], first_inline, IL_DEV * tiles
    )
    residual = (
        inputs.astype(jnp.float32)
        + jnp.dot(attended, out_weight, preferred_element_type=jnp.float32)
    ).astype(jnp.bfloat16)
    resid_float = residual.astype(jnp.float32)
    mean_square = jnp.mean(resid_float * resid_float, axis=-1, keepdims=True)
    normed = (resid_float * lax.rsqrt(mean_square + 1e-06) * norm_gain[None, :]).astype(
        jnp.bfloat16
    )
    route_width = routes.shape[1]
    block_rows = row_count // 2
    capacity = row_count * route_width // tiles
    slot_rank = slot_ranks(routes, tiles, block_rows)
    gate_mat = w_gate[0]
    up_mat = w_up[0]
    down_mat = w_down[0]
    pieces = []
    for piece_index in range(2):
        lower = piece_index * block_rows
        part_routes = routes[lower : lower + block_rows]
        part_rank = slot_rank[lower : lower + block_rows]
        part_normed = normed[lower : lower + block_rows]
        positions = part_routes * capacity + part_rank
        copies = jnp.broadcast_to(
            part_normed[:, None, :], (block_rows, route_width, model)
        ).reshape(-1, model)
        outgoing = (
            jnp.zeros((tiles * capacity, model), jnp.bfloat16).at[positions.reshape(-1)].set(copies)
        )
        outgoing = outgoing.reshape(tiles, capacity, model)
        received = lax.all_to_all(outgoing, "tile", split_axis=0, concat_axis=0, tiled=True)
        produced = expert_rows(received.reshape(-1, model), gate_mat, up_mat, down_mat).reshape(
            received.shape
        )
        returned = lax.all_to_all(produced, "tile", split_axis=0, concat_axis=0, tiled=True)
        pieces.append(returned.reshape(-1, model)[positions])
    picked = jnp.concatenate(pieces, axis=0)
    combined = jnp.sum(route_gates[:, :, None] * picked.astype(jnp.float32), axis=1)
    return (resid_float + combined).astype(jnp.bfloat16)


def solution(mesh):
    return jax.shard_map(
        local,
        mesh=mesh,
        in_specs=(
            P(("rep", "tile"), None),
            P(("rep", "tile"), None),
            P(("rep", "tile"), None),
            P(("rep", "tile"), None),
            P(),
            P(),
            P(("rep", "tile"), None),
            P(("rep", "tile"), None),
            P("tile", None, None),
            P("tile", None, None),
            P("tile", None, None),
        ),
        out_specs=P(("rep", "tile"), None),
        check_vma=False,
    )
```

profile of v0, /device:TPU:0, one launch (start us, length us, event | category | flops | bytes accessed | tf_op | source)
XLA Modules:
  0.0 141.6 jit_solution(16365286529693400286)
XLA Ops:
  4.3 3.1 %collective-permute-start = (bf16[128,2048]{1,0:T(8,128)(2,1)}, bf16[128,2048]{1,0:T(8,128)(2,1)}, u32[]{:S(2)}, u32[]{:S(2)}) collective-permute-start(bf16[128,2048]{1,0:T(8,128)(2,1)} %get-tuple-element.11), channel_id=1, source_target_pairs={{0,4},{4,8},{8,12},{12,16},{16,20},{20,24},{24,28},{1,5},{5,9},{9,... | collective-permute-start | bytes 1572872 | tf_op jit(solution)/shard_map/ppermute | solution.py:23
  17.1 2.4 %copy.29 = bf16[512,1024]{0,1:T(8,128)(2,1)} copy(bf16[512,1024]{1,0:T(8,128)(2,1)} %get-tuple-element.9) | data formatting | bytes 2097152 | tf_op jit(solution)/shard_map/slice | solution.py:100
  19.5 2.3 %copy.28 = bf16[512,1024]{0,1:T(8,128)(2,1)} copy(bf16[512,1024]{1,0:T(8,128)(2,1)} %get-tuple-element.10) | data formatting | bytes 2097152 | tf_op jit(solution)/shard_map/slice | solution.py:100
  21.8 7.8 %fusion.61 = (f32[16,256]{1,0:T(8,128)S(1)}, f32[16,256,512]{1,2,0:T(8,128)}) fusion(pred[256,512]{0,1:T(8,128)(4,1)S(1)} %fusion.42, bf16[512,16,64]{0,2,1:T(8,128)(2,1)} %bitcast.67, bf16[256,16,64]{0,2,1:T(8,128)(2,1)S(1)} %bitcast.69), kind=kOutput, calls=%fused_computation.107 | convolution fusion | flops 278921728 | bytes 10108928 | tf_op jit(solution)/shard_map/sub | solution.py:54
  29.5 4.7 %fusion.24 = bf16[16,64,256]{2,1,0:T(8,128)(2,1)S(1)} fusion(bf16[512,16,64]{0,2,1:T(8,128)(2,1)} %bitcast.68, f32[16,256,512]{1,2,0:T(8,128)} %get-tuple-element.18, f32[16,256]{1,0:T(8,128)S(1)} %get-tuple-element.17), kind=kOutput, calls=%fused_computation.35 | convolution fusion | flops 272891904 | bytes 9977856 | tf_op jit(solution)/shard_map/hqk,khd->qhd/dot_general | solution.py:58
  37.2 2.0 %reshape.365 = bf16[256,1024]{1,0:T(8,128)(2,1)} reshape(bf16[128,2,1024]{2,1,0:T(2,128)(2,1)} %broadcast_in_dim.43) | data formatting | bytes 1048576 | tf_op jit(solution)/shard_map/reshape | solution.py:127
  39.2 3.1 %scatter_custom_fusion = bf16[512,1024]{1,0:T(8,128)(2,1)} fusion(s32[256]{0:T(256)} %bitcast.73, bf16[256,1024]{1,0:T(8,128)(2,1)} %reshape.365, bf16[]{:T(256)} %constant.125.clone.1), kind=kCustom, calls=%fused_computation.44 | custom fusion | bytes 1049088 | tf_op jit(solution)/shard_map/scatter | solution.py:129
  42.3 11.4 %all-to-all-start = ((bf16[8,64,1024]{2,1,0:T(8,128)(2,1)}), bf16[8,64,1024]{2,1,0:T(8,128)(2,1)}, u32[]{:S(2)}, u32[]{:S(2)}) async-start(bf16[8,64,1024]{2,1,0:T(8,128)(2,1)} %bitcast.63), calls=%async_computation | async-start | bytes 2097152 | tf_op jit(solution)/shard_map/all_to_all | solution.py:132
  58.1 3.2 %scatter_custom_fusion.1 = bf16[512,1024]{1,0:T(8,128)(2,1)} fusion(s32[256]{0:T(256)S(1)} %bitcast.74, bf16[256,1024]{1,0:T(8,128)(2,1)} %reshape.373, bf16[]{:T(256)} %constant.125.clone.1), kind=kCustom, calls=%fused_computation.42 | custom fusion | bytes 1049088 | tf_op jit(solution)/shard_map/scatter | solution.py:129
  61.3 8.0 %all-to-all-done = bf16[8,64,1024]{2,1,0:T(8,128)(2,1)} async-done(((bf16[8,64,1024]{2,1,0:T(8,128)(2,1)}), bf16[8,64,1024]{2,1,0:T(8,128)(2,1)}, u32[]{:S(2)}, u32[]{:S(2)}) %all-to-all-start) | async-done | bytes 1048608 | tf_op jit(solution)/shard_map/all_to_all | solution.py:132
  69.3 4.4 %all-to-all-start.2 = ((bf16[8,64,1024]{2,1,0:T(8,128)(2,1)}), bf16[8,64,1024]{2,1,0:T(8,128)(2,1)}, u32[]{:S(2)}, u32[]{:S(2)}) async-start(bf16[8,64,1024]{2,1,0:T(8,128)(2,1)} %bitcast.64), calls=%async_computation.2 | async-start | bytes 2097152 | tf_op jit(solution)/shard_map/all_to_all | solution.py:132
  73.7 4.6 %fusion.16 = f32[512,1408]{1,0:T(8,128)} fusion(bf16[512,1024]{1,0:T(8,128)(2,1)} %bitcast.10, bf16[1,1024,1408]{2,1,0:T(8,128)(2,1)S(1)} %copy-done), kind=kOutput, calls=%fused_computation.25 | convolution fusion | flops 1476395008 | bytes 6815744 | tf_op jit(solution)/shard_map/dot_general | solution.py:63
  78.3 8.3 %fusion.18 = bf16[512,1024]{1,0:T(8,128)(2,1)} fusion(bf16[1,1408,1024]{2,1,0:T(8,128)(2,1)} %param.21, bf16[512,1024]{1,0:T(8,128)(2,1)} %bitcast.10, bf16[1,1024,1408]{2,1,0:T(8,128)(2,1)} %param.20, f32[512,1408]{1,0:T(8,128)} %fusion.16), kind=kOutput, calls=%fused_computation.32 | convolution fusion | flops 2957639680 | bytes 10747904 | tf_op jit(solution)/shard_map/dot_general | solution.py:66
  86.6 2.4 %all-to-all-done.2 = bf16[8,64,1024]{2,1,0:T(8,128)(2,1)} async-done(((bf16[8,64,1024]{2,1,0:T(8,128)(2,1)}), bf16[8,64,1024]{2,1,0:T(8,128)(2,1)}, u32[]{:S(2)}, u32[]{:S(2)}) %all-to-all-start.2) | async-done | bytes 1048608 | tf_op jit(solution)/shard_map/all_to_all | solution.py:132
  89.0 4.2 %all-to-all-start.1 = ((bf16[8,64,1024]{2,1,0:T(8,128)(2,1)}), bf16[8,64,1024]{2,1,0:T(8,128)(2,1)}, u32[]{:S(2)}, u32[]{:S(2)}) async-start(bf16[8,64,1024]{2,1,0:T(8,128)(2,1)} %bitcast.66), calls=%async_computation.1 | async-start | bytes 2097152 | tf_op jit(solution)/shard_map/all_to_all | solution.py:136
  93.2 4.6 %fusion.14 = f32[512,1408]{1,0:T(8,128)} fusion(bf16[512,1024]{1,0:T(8,128)(2,1)} %bitcast.18, bf16[1,1024,1408]{2,1,0:T(8,128)(2,1)S(1)} %copy-done), kind=kOutput, calls=%fused_computation.23 | convolution fusion | flops 1476395008 | bytes 6815744 | tf_op jit(solution)/shard_map/dot_general | solution.py:63
  97.8 8.3 %fusion.21 = bf16[512,1024]{1,0:T(8,128)(2,1)} fusion(bf16[1,1408,1024]{2,1,0:T(8,128)(2,1)} %param.21, bf16[512,1024]{1,0:T(8,128)(2,1)} %bitcast.18, bf16[1,1024,1408]{2,1,0:T(8,128)(2,1)} %param.20, f32[512,1408]{1,0:T(8,128)} %fusion.14), kind=kOutput, calls=%fused_computation.33 | convolution fusion | flops 2957639680 | bytes 10747904 | tf_op jit(solution)/shard_map/dot_general | solution.py:66
  106.1 2.5 %all-to-all-done.1 = bf16[8,64,1024]{2,1,0:T(8,128)(2,1)} async-done(((bf16[8,64,1024]{2,1,0:T(8,128)(2,1)}), bf16[8,64,1024]{2,1,0:T(8,128)(2,1)}, u32[]{:S(2)}, u32[]{:S(2)}) %all-to-all-start.1) | async-done | bytes 1048608 | tf_op jit(solution)/shard_map/all_to_all | solution.py:136
  108.6 4.5 %all-to-all-start.3 = ((bf16[8,64,1024]{2,1,0:T(8,128)(2,1)}), bf16[8,64,1024]{2,1,0:T(8,128)(2,1)}, u32[]{:S(2)}, u32[]{:S(2)}) async-start(bf16[8,64,1024]{2,1,0:T(8,128)(2,1)} %bitcast.65), calls=%async_computation.3 | async-start | bytes 2097152 | tf_op jit(solution)/shard_map/all_to_all | solution.py:136
  114.5 3.7 %gather_fusion = bf16[256,1024]{1,0:T(8,128)(2,1)} fusion(bf16[512,1024]{1,0:T(8,128)(2,1)} %bitcast.15, s32[1024]{0:T(1024)S(1)} %pad_clamp_fusion.1), kind=kCustom, calls=%fused_computation | custom fusion | bytes 1049600 | tf_op jit(solution)/shard_map/gather | solution.py:137
  118.2 2.0 %reshape.346 = bf16[128,2,1024]{2,1,0:T(2,128)(2,1)} reshape(bf16[256,1024]{1,0:T(8,128)(2,1)} %gather_fusion) | data formatting | bytes 1048576 | tf_op jit(solution)/shard_map/gather | solution.py:137
  120.3 8.1 %all-to-all-done.3 = bf16[8,64,1024]{2,1,0:T(8,128)(2,1)} async-done(((bf16[8,64,1024]{2,1,0:T(8,128)(2,1)}), bf16[8,64,1024]{2,1,0:T(8,128)(2,1)}, u32[]{:S(2)}, u32[]{:S(2)}) %all-to-all-start.3) | async-done | bytes 1048608 | tf_op jit(solution)/shard_map/all_to_all | solution.py:136
  128.3 3.7 %gather_fusion.1 = bf16[256,1024]{1,0:T(8,128)(2,1)} fusion(bf16[512,1024]{1,0:T(8,128)(2,1)} %bitcast.20, s32[1024]{0:T(1024)S(1)} %pad_clamp_fusion), kind=kCustom, calls=%fused_computation.1 | custom fusion | bytes 1049600 | tf_op jit(solution)/shard_map/gather | solution.py:137
  134.1 6.5 %multiply_reduce_fusion = f32[256,1024]{1,0:T(8,128)S(1)} fusion(bf16[128,2,1024]{2,1,0:T(2,128)(2,1)} %reshape.354, bf16[128,2,1024]{2,1,0:T(2,128)(2,1)} %reshape.346, f32[256,2]{1,0:T(8,128)S(1)} %copy.32), kind=kLoop, calls=%fused_computation.28 | loop fusion | flops 1835008 | bytes 2099200 | tf_op jit(solution)/shard_map/reduce_sum | solution.py:139
  (66 shorter events, 25.4 us)
Async XLA Ops:
  0.0 73.7 %copy-start = (bf16[1,1024,1408]{2,1,0:T(8,128)(2,1)S(1)}, bf16[1,1024,1408]{2,1,0:T(8,128)(2,1)}, u32[]{:S(2)}) copy-start(bf16[1,1024,1408]{2,1,0:T(8,128)(2,1)} %param.19) | copy-start | bytes 8650756
  0.0 9.9 %copy-start.3 = (bf16[256,1024]{1,0:T(8,128)(2,1)S(1)}, bf16[256,1024]{1,0:T(8,128)(2,1)}, u32[]{:S(2)}) copy-start(bf16[256,1024]{1,0:T(8,128)(2,1)} %param.12) | copy-start | bytes 1572868
  0.0 10.9 %copy-start.6 = (s32[256,2]{0,1:T(2,128)S(1)}, s32[256,2]{0,1:T(2,128)}, u32[]{:S(2)}) copy-start(s32[256,2]{0,1:T(2,128)} %param.17) | copy-start | bytes 6148
  2.3 1.0 copy-start.1
  4.3 9.6 %collective-permute-start = (bf16[128,2048]{1,0:T(8,128)(2,1)}, bf16[128,2048]{1,0:T(8,128)(2,1)}, u32[]{:S(2)}, u32[]{:S(2)}) collective-permute-start(bf16[128,2048]{1,0:T(8,128)(2,1)} %get-tuple-element.11), channel_id=1, source_target_pairs={{0,4},{4,8},{8,12},{12,16},{16,20},{20,24},{24,28},{1,5},{5,9},{9,... | collective-permute-start | bytes 1572872 | tf_op jit(solution)/shard_map/ppermute | solution.py:23
  7.5 6.4 %collective-permute-start.1 = (bf16[128,2048]{1,0:T(8,128)(2,1)}, bf16[128,2048]{1,0:T(8,128)(2,1)}, u32[]{:S(2)}, u32[]{:S(2)}) collective-permute-start(bf16[128,2048]{1,0:T(8,128)(2,1)} %get-tuple-element.12), channel_id=1, source_target_pairs={{4,0},{8,4},{12,8},{16,12},{20,16},{24,20},{28,24},{5,1},{9,5},{13... | collective-permute-start | bytes 1572872 | tf_op jit(solution)/shard_map/ppermute | solution.py:24
  17.1 4.6 %copy-start.4 = (bf16[256,1024]{0,1:T(8,128)(2,1)S(1)}, bf16[256,1024]{0,1:T(8,128)(2,1)}, u32[]{:S(2)}) copy-start(bf16[256,1024]{0,1:T(8,128)(2,1)} %copy.30) | copy-start | bytes 1572868
  29.5 4.7 %copy-start.2 = (bf16[1024,1024]{1,0:T(8,128)(2,1)S(1)}, bf16[1024,1024]{1,0:T(8,128)(2,1)}, u32[]{:S(2)}) copy-start(bf16[1024,1024]{1,0:T(8,128)(2,1)} %param.15) | copy-start | bytes 6291460
  29.5 4.7 %copy-start.5 = (bf16[256,1024]{1,0:T(8,128)(2,1)S(1)}, bf16[256,1024]{1,0:T(8,128)(2,1)}, u32[]{:S(2)}) copy-start(bf16[256,1024]{1,0:T(8,128)(2,1)} %param.11) | copy-start | bytes 1572868
  34.2 0.9 copy-start.7
  35.3 18.4 %copy-start.10 = (s32[128,2]{0,1:T(2,128)S(1)}, s32[128,2]{0,1:T(2,128)}, u32[]{:S(2)}) copy-start(s32[128,2]{0,1:T(2,128)} %get-tuple-element.16) | copy-start | bytes 3076
  42.3 26.9 %all-to-all-start = ((bf16[8,64,1024]{2,1,0:T(8,128)(2,1)}), bf16[8,64,1024]{2,1,0:T(8,128)(2,1)}, u32[]{:S(2)}, u32[]{:S(2)}) async-start(bf16[8,64,1024]{2,1,0:T(8,128)(2,1)} %bitcast.63), calls=%async_computation | async-start | bytes 2097152 | tf_op jit(solution)/shard_map/all_to_all | solution.py:132
  69.3 19.7 %all-to-all-start.2 = ((bf16[8,64,1024]{2,1,0:T(8,128)(2,1)}), bf16[8,64,1024]{2,1,0:T(8,128)(2,1)}, u32[]{:S(2)}, u32[]{:S(2)}) async-start(bf16[8,64,1024]{2,1,0:T(8,128)(2,1)} %bitcast.64), calls=%async_computation.2 | async-start | bytes 2097152 | tf_op jit(solution)/shard_map/all_to_all | solution.py:132
  89.0 19.7 %all-to-all-start.1 = ((bf16[8,64,1024]{2,1,0:T(8,128)(2,1)}), bf16[8,64,1024]{2,1,0:T(8,128)(2,1)}, u32[]{:S(2)}, u32[]{:S(2)}) async-start(bf16[8,64,1024]{2,1,0:T(8,128)(2,1)} %bitcast.66), calls=%async_computation.1 | async-start | bytes 2097152 | tf_op jit(solution)/shard_map/all_to_all | solution.py:136
  97.8 15.3 %copy-start.9 = (s32[128,2]{0,1:T(2,128)S(1)}, s32[128,2]{0,1:T(2,128)}, u32[]{:S(2)}) copy-start(s32[128,2]{0,1:T(2,128)} %get-tuple-element.5) | copy-start | bytes 3076
  97.8 15.6 %copy-start.8 = (s32[128,2]{0,1:T(2,128)S(1)}, s32[128,2]{0,1:T(2,128)}, u32[]{:S(2)}) copy-start(s32[128,2]{0,1:T(2,128)} %get-tuple-element.15) | copy-start | bytes 3076
  108.6 19.7 %all-to-all-start.3 = ((bf16[8,64,1024]{2,1,0:T(8,128)(2,1)}), bf16[8,64,1024]{2,1,0:T(8,128)(2,1)}, u32[]{:S(2)}, u32[]{:S(2)}) async-start(bf16[8,64,1024]{2,1,0:T(8,128)(2,1)} %bitcast.65), calls=%async_computation.3 | async-start | bytes 2097152 | tf_op jit(solution)/shard_map/all_to_all | solution.py:136
where the time goes:
time: 143 us; the launch traced here: 142 us
  local copies, waits for them, and re-layouts  39.2 us (27%)
  matrix products  39 us (27%)
  starting transfers between devices  29 us (20%)
  waiting for transfers between devices  21 us (15%)
  other arithmetic  13 us (9%)
    dot_general x2, matrix products, expert_rows(): jnp.dot(hidden, down_mat, preferred_element_type=jnp.float32)  16.5 us
    all_to_all x2, starting transfers between devices, local(): lax.all_to_all(outgoing, 'tile', split_axis=0, concat_axis=0, tiled=True)  15.9 us
    gather x4, local copies, waits for them, and re-layouts, local(): pieces.append(returned.reshape(-1, model)[positions])  11.5 us
    all_to_all x2, waiting for transfers between devices, local(): lax.all_to_all(produced, 'tile', split_axis=0, concat_axis=0, tiled=True)  10.6 us
    all_to_all x2, waiting for transfers between devices, local(): lax.all_to_all(outgoing, 'tile', split_axis=0, concat_axis=0, tiled=True)  10.4 us
    dot_general x2, matrix products, expert_rows(): jnp.dot(token_rows, gate_mat, preferred_element_type=jnp.float32)  9.18 us
    all_to_all x2, starting transfers between devices, local(): lax.all_to_all(produced, 'tile', split_axis=0, concat_axis=0, tiled=True)  8.73 us
    sub x1, matrix products, local_attention(): weights = jnp.exp(scores - highest)  7.78 us
  transfers between devices with their start and end apart: 6, of which 4 were waited for; matrix products, arithmetic and copies ran while one was open for 32% of the time, Pallas kernels for 0%

commit v1 on v0

v1 whole, which is shorter than its diff:
```python
import functools

import jax
import jax.numpy as jnp
from jax import lax
from jax.experimental import pallas as pl
from jax.experimental.pallas import tpu as pltpu
from jax.sharding import PartitionSpec as P

HEADS = 16
HD = 64
IL_DEV = 4
XL = 8
DP = 8
R_IL = 2
R_XL = 2
R_DP = 2
PLANE = XL * DP
META = 16
MIB = 1024 * 1024
F32 = jnp.float32
BF16 = jnp.bfloat16
VMEM = pl.BlockSpec(memory_space=pltpu.VMEM)
SMEM = pl.BlockSpec(memory_space=pltpu.SMEM)


def cost(flops, transcendentals, args, outs):
    moved = sum(a.size * a.dtype.itemsize for a in args)
    moved += sum(o.size * o.dtype.itemsize for o in outs)
    return pl.CostEstimate(flops=flops, transcendentals=transcendentals, bytes_accessed=moved)


def window_bias(queries, first_query, keys, first_key, live):
    q = lax.broadcasted_iota(jnp.int32, (queries, keys), 0) + first_query
    k = lax.broadcasted_iota(jnp.int32, (queries, keys), 1) + (first_key + PLANE * R_IL)
    near = jnp.abs(q // PLANE + R_IL - k // PLANE) <= R_IL
    near = near & (jnp.abs(q // DP % XL - k // DP % XL) <= R_XL)
    near = near & (jnp.abs(q % DP - k % DP) <= R_DP)
    if live is not None:
        near = near & (live > 0)
    return jnp.where(near, F32(0.0), F32(-1e30))


def attention_kernel(half, live, q, k, v, halo, x, w, gain, meta, resid, payload, att):
    rows = q.shape[0]
    own = k.shape[0]
    wide = halo.shape[0] // 2
    start = half * rows
    bias_own = window_bias(rows, start, own, 0, None)
    first = -wide if half == 0 else own
    bias_halo = window_bias(rows, start, wide, first, live[half])
    lane = lax.broadcasted_iota(jnp.int32, (rows, 2 * HD), 1)
    nt = (((1,), (1,)), ((), ()))
    for pair in range(HEADS // 2):
        cols = slice(pair * 2 * HD, (pair + 1) * 2 * HD)
        query = q[:, cols] * BF16(1.0 / HD**0.5)
        key_own, key_halo = k[:, cols], halo[:wide, cols]
        val_own, val_halo = v[:, cols], halo[wide:, cols]
        outs = []
        for side in range(2):
            mine = (lane < HD) if side == 0 else (lane >= HD)
            qh = jnp.where(mine, query, BF16(0.0))
            s_own = lax.dot_general(qh, key_own, nt, preferred_element_type=F32) + bias_own
            s_halo = lax.dot_general(qh, key_halo, nt, preferred_element_type=F32) + bias_halo
            top = jnp.maximum(
                jnp.max(s_own, axis=1, keepdims=True), jnp.max(s_halo, axis=1, keepdims=True)
            )
            p_own = jnp.exp(s_own - top)
            p_halo = jnp.exp(s_halo - top)
            total = jnp.sum(p_own, axis=1, keepdims=True) + jnp.sum(p_halo, axis=1, keepdims=True)
            o = jnp.dot(p_own.astype(BF16), val_own, preferred_element_type=F32)
            o = o + jnp.dot(p_halo.astype(BF16), val_halo, preferred_element_type=F32)
            outs.append(o / total)
        att[:, cols] = jnp.where(lane < HD, outs[0], outs[1]).astype(BF16)
    res = x[...].astype(F32) + jnp.dot(att[...], w[...], preferred_element_type=F32)
    res = res.astype(BF16)
    resid[...] = res
    res = res.astype(F32)
    square = jnp.mean(res * res, axis=1, keepdims=True)
    normed = (res * lax.rsqrt(square + 1e-06) * gain[...]).astype(BF16)
    payload[:rows, :] = normed
    if meta is not None:
        payload[rows:, :] = jnp.broadcast_to(meta[...], (META, meta.shape[1]))


def attend(half, live, q, k, v, halo, x, w, gain, meta):
    rows, model = q.shape[0] // 2, q.shape[1]
    whole = lambda a: pl.BlockSpec(a.shape, lambda i: (0,) * a.ndim)
    part = pl.BlockSpec((rows, model), lambda i: (half, 0))
    args = [live, q, k, v, halo, x, w, gain]
    specs = [SMEM, part, whole(k), whole(v), whole(halo), part, whole(w), whole(gain)]
    extra = 0
    if meta is not None:
        args.append(meta)
        specs.append(whole(meta))
        extra = META
        body = functools.partial(attention_kernel, half)
    else:

        def body(live, q, k, v, halo, x, w, gain, resid, payload, att):
            attention_kernel(half, live, q, k, v, halo, x, w, gain, None, resid, payload, att)

    outs = [
        jax.ShapeDtypeStruct((rows, model), BF16),
        jax.ShapeDtypeStruct((rows + extra, model), BF16),
    ]
    keys = k.shape[0] + halo.shape[0] // 2
    return pl.pallas_call(
        body,
        grid=(1,),
        in_specs=specs,
        out_specs=[pl.BlockSpec(o.shape, lambda i: (0, 0)) for o in outs],
        out_shape=outs,
        scratch_shapes=[pltpu.VMEM((rows, model), BF16)],
        compiler_params=pltpu.CompilerParams(vmem_limit_bytes=24 * MIB),
        cost_estimate=cost(
            4 * rows * keys * model + 2 * rows * model * model, HEADS * rows * keys, args, outs
        ),
        name=f"attention_half{half}",
    )(*args)


def pick_matrices(payload, block, rows, capacity, expert):
    base = block * (rows + META) + rows
    meta = payload[base : base + META, :].astype(F32)
    item = [meta[:, i * rows : (i + 1) * rows] for i in range(8)]
    hit0, hit1 = item[0] == expert, item[1] == expert
    hits = jnp.where(hit0 | hit1, F32(1.0), F32(0.0))
    upper = lax.broadcasted_iota(jnp.int32, (rows, rows), 0) < lax.broadcasted_iota(
        jnp.int32, (rows, rows), 1
    )
    upper = jnp.where(upper, F32(1.0), F32(0.0)).astype(BF16)
    rank = jnp.dot(hits.astype(BF16), upper, preferred_element_type=F32)
    rank = jnp.where(hits > 0, rank, F32(-1.0))
    gate = jnp.where(hit0, item[2] + item[3] + item[4], F32(0.0))
    gate = gate + jnp.where(hit1, item[5] + item[6] + item[7], F32(0.0))
    slot = lax.broadcasted_iota(jnp.int32, (capacity, rows), 0).astype(F32)
    return slot == rank[:1, :], gate[:1, :]


def experts_kernel(blocks, rows, capacity, me, *refs):
    count = len(refs) - 7
    payloads, (w_gate, w_up, w_down, out_mine, out_sib, x, hidden) = refs[:count], refs[count:]
    expert = me[0].astype(F32)
    place = 0
    for payload in payloads:
        for block in range(blocks):
            hot, _ = pick_matrices(payload, block, rows, capacity, expert)
            hot = jnp.where(hot, F32(1.0), F32(0.0)).astype(BF16)
            base = block * (rows + META)
            picked = jnp.dot(hot, payload[base : base + rows, :], preferred_element_type=F32)
            x[place : place + capacity, :] = picked.astype(BF16)
            place += capacity
    width = w_gate.shape[1]
    for at in range(0, width, 256):
        cols = slice(at, min(at + 256, width))
        g = jnp.dot(x[...], w_gate[:, cols], preferred_element_type=F32)
        u = jnp.dot(x[...], w_up[:, cols], preferred_element_type=F32)
        hidden[:, cols] = (g / (1.0 + jnp.exp(-g)) * u).astype(BF16)
    half = place // 2
    for at in range(0, w_down.shape[1], 256):
        cols = slice(at, at + 256)
        o = jnp.dot(hidden[...], w_down[:, cols], preferred_element_type=F32).astype(BF16)
        out_mine[:, cols] = o[:half]
        out_sib[:, cols] = o[half:]


def experts(me, mine, sib, w_gate, w_up, w_down, blocks, rows, capacity):
    model, width = w_gate.shape
    slots = (len(mine) + len(sib)) * blocks * capacity
    outs = [jax.ShapeDtypeStruct((slots // 2, model), BF16)] * 2
    args = [me, *mine, *sib, w_gate, w_up, w_down]
    return pl.pallas_call(
        functools.partial(experts_kernel, blocks, rows, capacity),
        in_specs=[SMEM] + [VMEM] * (len(args) - 1),
        out_specs=[VMEM] * 2,
        out_shape=outs,
        scratch_shapes=[pltpu.VMEM((slots, model), BF16), pltpu.VMEM((slots, width), BF16)],
        compiler_params=pltpu.CompilerParams(vmem_limit_bytes=32 * MIB),
        cost_estimate=cost(6 * slots * model * width, slots * width, args, outs),
        name=f"experts_{slots}",
    )(*args)


def spread(payload, block, rows, capacity, experts_two, outs_two):
    weights, values = [], []
    for expert, out in zip(experts_two, outs_two):
        hot, gate = pick_matrices(payload, block, rows, capacity, expert)
        full = jnp.where(hot, gate, F32(0.0))
        high = full.astype(BF16)
        weights += [high, (full - high.astype(F32)).astype(BF16)]
        values += [out, out]
    return lax.dot_general(
        jnp.concatenate(weights, axis=0),
        jnp.concatenate(values, axis=0),
        (((0,), (0,)), ((), ())),
        preferred_element_type=F32,
    )


def combine_kernel(blocks, rows, capacity, groups, added, me, *refs):
    payloads = refs[:groups]
    outs_me, outs_sib = refs[groups], refs[groups + 1]
    carry = refs[groups + 2] if added else None
    results = refs[groups + 2 + (1 if added else 0) :]
    both = (me[0].astype(F32), me[1].astype(F32))
    core = me[2]
    for group in range(groups):
        for block in range(blocks):
            slot = (group * blocks + block) * capacity
            span = slice(slot, slot + capacity)
            total = spread(
                payloads[group], block, rows, capacity, both, (outs_me[span, :], outs_sib[span, :])
            )
            at = slice(block * rows, (block + 1) * rows)
            if added:
                extra = carry[at, :].astype(F32)
                total = total + jnp.where(core == group, extra, F32(0.0))
            results[group][at, :] = total.astype(BF16)


def combine(me, payloads, outs_me, outs_sib, carry, blocks, rows, capacity):
    model = payloads[0].shape[1]
    groups = len(payloads)
    args = [me, *payloads, outs_me, outs_sib] + ([] if carry is None else [carry])
    outs = [jax.ShapeDtypeStruct((blocks * rows, model), BF16)] * groups
    return pl.pallas_call(
        functools.partial(combine_kernel, blocks, rows, capacity, groups, carry is not None),
        in_specs=[SMEM] + [VMEM] * (len(args) - 1),
        out_specs=[VMEM] * groups,
        out_shape=outs,
        compiler_params=pltpu.CompilerParams(vmem_limit_bytes=24 * MIB),
        cost_estimate=cost(8 * groups * blocks * rows * capacity * model, 0, args, outs),
        name=f"combine_{groups}",
    )(*args)


def finish_kernel(blocks, rows, capacity, me, *refs):
    out = refs[-1]
    both = (me[0].astype(F32), me[1].astype(F32))
    for block in range(blocks):
        payload, resid, mine, sib, from_x, from_y = refs[block * 6 : block * 6 + 6]
        total = spread(payload, 0, rows, capacity, both, (mine[:capacity, :], sib[:capacity, :]))
        total = total + from_x[...].astype(F32) + from_y[...].astype(F32)
        total = total + resid[...].astype(F32)
        out[block * rows : (block + 1) * rows, :] = total.astype(BF16)


def finish(me, parts, rows, capacity):
    model = parts[0][0].shape[1]
    args = [me] + [a for part in parts for a in part]
    outs = [jax.ShapeDtypeStruct((len(parts) * rows, model), BF16)]
    return pl.pallas_call(
        functools.partial(finish_kernel, len(parts), rows, capacity),
        in_specs=[SMEM] + [VMEM] * (len(args) - 1),
        out_specs=VMEM,
        out_shape=outs[0],
        compiler_params=pltpu.CompilerParams(vmem_limit_bytes=24 * MIB),
        cost_estimate=cost(8 * len(parts) * rows * capacity * model, 0, args, outs),
        name="finish",
    )(*args)


def expert_rows(token_rows, gate_mat, up_mat, down_mat):
    gate_part = jnp.dot(token_rows, gate_mat, preferred_element_type=F32)
    up_part = jnp.dot(token_rows, up_mat, preferred_element_type=F32)
    hidden = (jax.nn.silu(gate_part) * up_part).astype(BF16)
    return jnp.dot(hidden, down_mat, preferred_element_type=F32).astype(BF16)


def slot_ranks(routes, experts_count, block_rows):
    row_count = routes.shape[0]
    expert_ids = jnp.arange(experts_count, dtype=jnp.int32)
    matches = routes[:, :, None] == expert_ids[None, None, :]
    hits = jnp.sum(matches.astype(jnp.int32), axis=1)
    hits = hits.reshape(row_count // block_rows, block_rows, experts_count)
    earlier = (jnp.cumsum(hits, axis=1) - hits).reshape(row_count, experts_count)
    return jnp.sum(jnp.where(matches, earlier[:, None, :], 0), axis=-1)


def routed_all_to_all(normed_parts, resid_parts, routes, route_gates, w_gate, w_up, w_down):
    tiles = lax.axis_size("tile")
    row_count, route_width = routes.shape
    block_rows, model = normed_parts[0].shape
    capacity = row_count * route_width // tiles
    slot_rank = slot_ranks(routes, tiles, block_rows)
    pieces = []
    for index, part_normed in enumerate(normed_parts):
        rows = slice(index * block_rows, (index + 1) * block_rows)
        positions = routes[rows] * capacity + slot_rank[rows]
        copies = jnp.broadcast_to(
            part_normed[:, None, :], (block_rows, route_width, model)
        ).reshape(-1, model)
        outgoing = jnp.zeros((tiles * capacity, model), BF16).at[positions.reshape(-1)].set(copies)
        outgoing = outgoing.reshape(tiles, capacity, model)
        received = lax.all_to_all(outgoing, "tile", split_axis=0, concat_axis=0, tiled=True)
        produced = expert_rows(received.reshape(-1, model), w_gate, w_up, w_down)
        produced = produced.reshape(received.shape)
        returned = lax.all_to_all(produced, "tile", split_axis=0, concat_axis=0, tiled=True)
        picked = returned.reshape(-1, model)[positions].astype(F32)
        combined = jnp.sum(route_gates[rows][:, :, None] * picked, axis=1)
        pieces.append((resid_parts[index].astype(F32) + combined).astype(BF16))
    return jnp.concatenate(pieces, axis=0)


def swap(array, bit):
    return lax.ppermute(array, "tile", [(i, i ^ bit) for i in range(8)])


def swap_turned(array):
    return lax.ppermute(array, "tile", [(i, i ^ (2 if i % 2 else 4)) for i in range(8)])


def routed_gather(payloads, resids, w_gate, w_up, w_down, rows, capacity):
    tile = lax.axis_index("tile")
    core = tile % 2
    me = jnp.stack([tile, tile ^ 1, core]).astype(jnp.int32)
    run = functools.partial(
        experts, w_gate=w_gate, w_up=w_up, w_down=w_down, blocks=1, rows=rows, capacity=capacity
    )
    sizes = dict(blocks=1, rows=rows, capacity=capacity)
    moved = []
    for own in payloads:
        from_x, from_y = swap(own, 2), swap(own, 4)
        moved.append((own, from_x, from_y, swap_turned(jnp.where(core == 0, from_x, from_y))))
    parts = []
    for index, (own, from_x, from_y, diag) in enumerate(moved):
        near = (own, from_x, from_y)
        near_mine, near_sib = run(me, near, [swap(a, 1) for a in near])
        diag_mine, diag_sib = run(me, [diag], [swap(diag, 1)])
        back_diag = swap(diag_sib, 1)
        back_near = swap(near_sib, 1)
        (sum_diag,) = combine(me, [diag], diag_mine, back_diag, None, **sizes)
        carry = swap_turned(sum_diag)
        sum_x, sum_y = combine(
            me, [from_x, from_y], near_mine[capacity:], back_near[capacity:], carry, **sizes
        )
        parts.append((own, resids[index], near_mine, back_near, swap(sum_x, 2), swap(sum_y, 4)))
    return finish(me, parts, rows, capacity)


def local(
    inputs,
    queries,
    key_vectors,
    values,
    out_weight,
    norm_gain,
    routes,
    route_gates,
    w_gate,
    w_up,
    w_down,
):
    row_count = inputs.shape[0]
    tiles = lax.axis_size("tile")
    tile = lax.axis_index("tile")
    width = R_IL * PLANE
    rows = row_count // 2
    capacity = row_count * routes.shape[1] // tiles
    up = [(i, i + 1) for i in range(tiles - 1)]
    down = [(j, i) for i, j in up]
    before = lax.ppermute(
        jnp.concatenate([key_vectors[-width:], values[-width:]], axis=0), "tile", up
    )
    after = lax.ppermute(
        jnp.concatenate([key_vectors[:width], values[:width]], axis=0), "tile", down
    )
    live = jnp.stack([tile > 0, tile < tiles - 1]).astype(jnp.int32)
    fast = tiles == 8
    metas = [None, None]
    if fast:
        items = [routes[:, 0].astype(F32), routes[:, 1].astype(F32)]
        for k in range(2):
            gate = route_gates[:, k]
            high = lax.reduce_precision(gate, 8, 7)
            mid = lax.reduce_precision(gate - high, 8, 7)
            items += [high, mid, gate - high - mid]
        metas = [
            jnp.concatenate([a[h * rows : (h + 1) * rows] for a in items]).astype(BF16)[None]
            for h in range(2)
        ]
    resids, payloads = [], []
    for half, halo in enumerate((before, after)):
        resid, payload = attend(
            half, live, queries, key_vectors, values, halo, inputs, out_weight,
            norm_gain[None, :], metas[half],
        )
        resids.append(resid)
        payloads.append(payload)
    if fast:
        return routed_gather(payloads, resids, w_gate[0], w_up[0], w_down[0], rows, capacity)
    return routed_all_to_all(
        payloads, resids, routes, route_gates, w_gate[0], w_up[0], w_down[0]
    )


def solution(mesh):
    return jax.shard_map(
        local,
        mesh=mesh,
        in_specs=(
            P(("rep", "tile"), None),
            P(("rep", "tile"), None),
            P(("rep", "tile"), None),
            P(("rep", "tile"), None),
            P(),
            P(),
            P(("rep", "tile"), None),
            P(("rep", "tile"), None),
            P("tile", None, None),
            P("tile", None, None),
            P("tile", None, None),
        ),
        out_specs=P(("rep", "tile"), None),
        check_vma=False,
    )
```

time: 143 us -> 99.9 us (0.70)
  matrix products: 39 us -> 0 us
  Pallas kernels: 0 us -> 37.5 us
  local copies, waits for them, and re-layouts: 39.2 us -> 13.5 us
  other arithmetic: 13 us -> 2.89 us
  waiting for transfers between devices: 21 us -> 16.3 us
    pallas_call x0 -> x11, Pallas kernels: none -> 37.5 us  [the longest x4 17.1 us: experts(): pl.pallas_call(functools.partial(experts_kernel, blocks, rows, capacity),...]
    dot_general x6 -> x0, matrix products: 31.3 us -> none  [the longest x2 16.5 us: expert_rows(): jnp.dot(hidden, down_mat, preferred_element_type=jnp.float32)]
    all_to_all x4 -> x0, starting transfers between devices: 24.6 us -> none  [the longest x2 15.9 us: local(): lax.all_to_all(outgoing, 'tile', split_axis=0, concat_axis=0, tiled=True)]
    ppermute x2 -> x26, starting transfers between devices: 4.42 us -> 28.8 us  [the longest x20 20.1 us: swap(): return lax.ppermute(array, 'tile', [(i, i ^ bit) for i in range(8)])]
    all_to_all x4 -> x0, waiting for transfers between devices: 21 us -> none  [the longest x2 10.6 us: local(): lax.all_to_all(produced, 'tile', split_axis=0, concat_axis=0, tiled=True)]
    ppermute x2 -> x26, waiting for transfers between devices: 0.01 us -> 16.3 us  [the longest x20 13 us: swap(): return lax.ppermute(array, 'tile', [(i, i ^ bit) for i in range(8)])]
    gather x4 -> x0, local copies, waits for them, and re-layouts: 11.5 us -> none  [local(): pieces.append(returned.reshape(-1, model)[positions])]
    unnamed x25 -> x45, local copies, waits for them, and re-layouts: 4.03 us -> 12 us
  transfers between devices with their start and end apart: 6 -> 26, of which waited for: 4 -> 7; matrix products, arithmetic and copies ran while one was open for 32% -> 2% of each run, Pallas kernels for 0% -> 35%
where the time goes in v1:
time: 99.9 us; the launch traced here: 99.3 us
  Pallas kernels  37.5 us (38%)
  starting transfers between devices  28.8 us (29%)
  waiting for transfers between devices  16.3 us (16%)
  local copies, waits for them, and re-layouts  13.5 us (14%)
  other arithmetic  2.89 us (3%)
    ppermute x20, starting transfers between devices, swap(): return lax.ppermute(array, 'tile', [(i, i ^ bit) for i in range(8)])  20.1 us
    pallas_call x4, Pallas kernels, experts(): pl.pallas_call(functools.partial(experts_kernel, blocks, rows, capacity),...  17.1 us
    pallas_call x2, Pallas kernels, attend(): pl.pallas_call(body, grid=(1,), in_specs=specs, out_specs=[pl.BlockSpec(o...  13.1 us
    ppermute x20, waiting for transfers between devices, swap(): return lax.ppermute(array, 'tile', [(i, i ^ bit) for i in range(8)])  13 us
    unnamed x45, local copies, waits for them, and re-layouts  12 us
    pallas_call x4, Pallas kernels, combine(): pl.pallas_call(functools.partial(combine_kernel, blocks, rows, capacity,...  4.75 us
    ppermute x4, starting transfers between devices, swap_turned(): lax.ppermute(array, 'tile', [(i, i ^ (2 if i % 2 else 4)) for i in range(...  4.25 us
    ppermute x4, waiting for transfers between devices, swap_turned(): lax.ppermute(array, 'tile', [(i, i ^ (2 if i % 2 else 4)) for i in range(...  3.23 us
  transfers between devices with their start and end apart: 26, of which 7 were waited for; matrix products, arithmetic and copies ran while one was open for 2% of the time, Pallas kernels for 35%

profile of v1, /device:TPU:0, one launch (start us, length us, event | category | flops | bytes accessed | tf_op | source)
XLA Modules:
  0.0 99.3 jit_solution(15439459223985811949)
XLA Ops:
  0.0 1.4 %fusion.2 = (bf16[128,1024]{1,0:T(8,128)(2,1)S(1)}, bf16[128,1024]{1,0:T(8,128)(2,1)S(1)}, bf16[128,1024]{1,0:T(8,128)(2,1)S(1)}, bf16[128,1024]{1,0:T(8,128)(2,1)S(1)}) fusion(bf16[256,1024]{1,0:T(8,128)(2,1)} %k.3, bf16[256,1024]{1,0:T(8,128)(2,1)} %v.3), kind=kLoop, calls=%fused_computation.38 | loop fusion | bytes 2097152 | tf_op jit(solution)/shard_map/slice | solution.py:367
  2.3 3.2 %collective-permute-start = (bf16[256,1024]{1,0:T(8,128)(2,1)}, bf16[256,1024]{1,0:T(8,128)(2,1)}, u32[]{:S(2)}, u32[]{:S(2)}) collective-permute-start(bf16[256,1024]{1,0:T(8,128)(2,1)} %pad_maximum_fusion), channel_id=1, source_target_pairs={{0,4},{4,8},{8,12},{12,16},{16,20},{20,24},{24,28},{1,5},{5,9},{9,... | collective-permute-start | bytes 1572872 | tf_op jit(solution)/shard_map/ppermute | solution.py:363
  10.0 6.5 %attention_half0.1 = (bf16[128,1024]{1,0:T(8,128)(2,1)S(1)}, bf16[144,1024]{1,0:T(8,128)(2,1)}) custom-call(s32[2]{0:T(128)S(1)} %add_convert_fusion.live, bf16[256,1024]{1,0:T(8,128)(2,1)S(1)} %copy-done.8, bf16[256,1024]{1,0:T(8,128)(2,1)S(1)} %copy-done.5, bf16[256,1024]{1,0:T(8,128)(2,1)S(1)} %copy-done.6, bf16[256,1024]{1,0:T(8,128)(2,1)} %collective-permute-done.halo, ...), custom_call_target="tpu_custom_call" | custom-call | flops 469762048 | bytes 5281800 | tf_op jit(solution)/shard_map/attention_half0/pallas_call | solution.py:108
  17.1 11.0 %collective-permute-start.2 = (bf16[144,1024]{1,0:T(8,128)(2,1)}, bf16[144,1024]{1,0:T(8,128)(2,1)}, u32[]{:S(2)}, u32[]{:S(2)}) collective-permute-start(bf16[144,1024]{1,0:T(8,128)(2,1)} %get-tuple-element.21.refs_0_), channel_id=1, source_target_pairs={{0,16},{4,20},{8,24},{12,28},{16,0},{20,4},{24,8},{28,12},{1,17},{... | collective-permute-start | bytes 884744 | tf_op jit(solution)/shard_map/ppermute | solution.py:307
  28.2 1.6 %copy-done.4 = bf16[1024,1024]{1,0:T(8,128)(2,1)S(1)} copy-done((bf16[1024,1024]{1,0:T(8,128)(2,1)S(1)}, bf16[1024,1024]{1,0:T(8,128)(2,1)}, u32[]{:S(2)}) %copy-start.4) | copy-done | bytes 2097176
  32.9 6.7 %attention_half1.1 = (bf16[128,1024]{1,0:T(8,128)(2,1)S(1)}, bf16[144,1024]{1,0:T(8,128)(2,1)}) custom-call(s32[2]{0:T(128)S(1)} %add_convert_fusion.live, bf16[256,1024]{1,0:T(8,128)(2,1)S(1)} %copy-done.9, bf16[256,1024]{1,0:T(8,128)(2,1)S(1)} %copy-done.5, bf16[256,1024]{1,0:T(8,128)(2,1)S(1)} %copy-done.7, ...), custom_call_target="tpu_custom_call" | custom-call | flops 469762048 | bytes 5281800 | tf_op jit(solution)/shard_map/attention_half1/pallas_call | solution.py:108
  40.3 2.0 %collective-permute-start.14 = (bf16[144,1024]{1,0:T(8,128)(2,1)}, bf16[144,1024]{1,0:T(8,128)(2,1)S(1)}, u32[]{:S(2)}, u32[]{:S(2)}) collective-permute-start(bf16[144,1024]{1,0:T(8,128)(2,1)} %get-tuple-element.29.refs_0_.refs_6_), channel_id=1, source_target_pairs={{0,8},{4,12},{8,0},{12,4},{16,24},{20,28},{24,16},{28,20},{1,9},{5... | collective-permute-start | bytes 884744 | tf_op jit(solution)/shard_map/ppermute | solution.py:307
  44.0 3.3 %collective-permute-done.15.refs_2_.refs_1_ = bf16[144,1024]{1,0:T(8,128)(2,1)S(1)} collective-permute-done((bf16[144,1024]{1,0:T(8,128)(2,1)}, bf16[144,1024]{1,0:T(8,128)(2,1)S(1)}, u32[]{:S(2)}, u32[]{:S(2)}) %collective-permute-start.15) | collective-permute-done | bytes 294944 | tf_op jit(solution)/shard_map/ppermute | solution.py:307
  47.3 1.5 %collective-permute-done.14.refs_1_.refs_0_ = bf16[144,1024]{1,0:T(8,128)(2,1)S(1)} collective-permute-done((bf16[144,1024]{1,0:T(8,128)(2,1)}, bf16[144,1024]{1,0:T(8,128)(2,1)S(1)}, u32[]{:S(2)}, u32[]{:S(2)}) %collective-permute-start.14) | collective-permute-done | bytes 294944 | tf_op jit(solution)/shard_map/ppermute | solution.py:307
  49.3 1.6 %collective-permute-start.20 = (bf16[144,1024]{1,0:T(8,128)(2,1)S(1)}, bf16[144,1024]{1,0:T(8,128)(2,1)S(1)}, u32[]{:S(2)}, u32[]{:S(2)}) collective-permute-start(bf16[144,1024]{1,0:T(8,128)(2,1)S(1)} %broadcast_select_fusion), channel_id=1, source_target_pairs={{0,16},{4,12},{8,24},{12,4},{16,0},{20,28},{24,8},{28,20},{1,17},{... | collective-permute-start | bytes 884744 | tf_op jit(solution)/shard_map/ppermute | solution.py:311
  51.5 1.8 %copy-done.1 = bf16[1,1024,1408]{2,1,0:T(8,128)(2,1)S(1)} copy-done((bf16[1,1024,1408]{2,1,0:T(8,128)(2,1)S(1)}, bf16[1,1024,1408]{2,1,0:T(8,128)(2,1)}, u32[]{:S(2)}) %copy-start.1) | copy-done | bytes 2883608
  53.3 1.8 %copy-done.2 = bf16[1,1408,1024]{2,1,0:T(8,128)(2,1)S(1)} copy-done((bf16[1,1408,1024]{2,1,0:T(8,128)(2,1)S(1)}, bf16[1,1408,1024]{2,1,0:T(8,128)(2,1)}, u32[]{:S(2)}) %copy-start.2) | copy-done | bytes 2883608
  55.1 6.1 %experts_384.2 = (bf16[192,1024]{1,0:T(8,128)(2,1)S(1)}, bf16[192,1024]{1,0:T(8,128)(2,1)S(1)}) custom-call(s32[3]{0:T(128)S(1)} %pad_add_fusion.me, bf16[144,1024]{1,0:T(8,128)(2,1)} %get-tuple-element.21.refs_0_, bf16[144,1024]{1,0:T(8,128)(2,1)} %collective-permute-done.1.refs_1_.refs_0_, bf16[144,1024]{1,0:T(8,128)(2,1)} %collective-permute-done.2.refs_2_.refs_1_, ...), custom_call_target="tpu_custom_call" | custom-call | flops 3321888768 | bytes 11206668 | tf_op jit(solution)/shard_map/experts_384/pallas_call | solution.py:173
  61.9 6.1 %experts_384.3 = (bf16[192,1024]{1,0:T(8,128)(2,1)S(1)}, bf16[192,1024]{1,0:T(8,128)(2,1)S(1)}) custom-call(s32[3]{0:T(128)S(1)} %pad_add_fusion.me, bf16[144,1024]{1,0:T(8,128)(2,1)} %get-tuple-element.29.refs_0_.refs_6_, bf16[144,1024]{1,0:T(8,128)(2,1)S(1)} %collective-permute-done.14.refs_1_.refs_0_, ...), custom_call_target="tpu_custom_call" | custom-call | flops 3321888768 | bytes 11206668 | tf_op jit(solution)/shard_map/experts_384/pallas_call | solution.py:173
  68.5 2.4 %experts_128.2 = (bf16[64,1024]{1,0:T(8,128)(2,1)S(1)}, bf16[64,1024]{1,0:T(8,128)(2,1)S(1)}) custom-call(s32[3]{0:T(128)S(1)} %pad_add_fusion.me, bf16[144,1024]{1,0:T(8,128)(2,1)S(1)} %collective-permute-done.7.refs_0_, bf16[144,1024]{1,0:T(8,128)(2,1)S(1)} %collective-permute-done.8.refs_1_, bf16[1024,1408]{1,0:T(8,128)(2,1)S(1)} %bitcast.53, ...), custom_call_target="tpu_custom_call" | custom-call | flops 1107296256 | bytes 9502732 | tf_op jit(solution)/shard_map/experts_128/pallas_call | solution.py:173
  71.1 2.4 %experts_128.3 = (bf16[64,1024]{1,0:T(8,128)(2,1)S(1)}, bf16[64,1024]{1,0:T(8,128)(2,1)S(1)}) custom-call(s32[3]{0:T(128)S(1)} %pad_add_fusion.me, bf16[144,1024]{1,0:T(8,128)(2,1)S(1)} %collective-permute-done.20.refs_0_, bf16[144,1024]{1,0:T(8,128)(2,1)S(1)} %collective-permute-done.21.refs_1_, bf16[1024,1408]{1,0:T(8,128)(2,1)S(1)} %bitcast.54, ...), custom_call_target="tpu_custom_call" | custom-call | flops 1107296256 | bytes 9502732 | tf_op jit(solution)/shard_map/experts_128/pallas_call | solution.py:173
  76.5 1.6 %collective-permute-start.23 = (bf16[128,1024]{1,0:T(8,128)(2,1)S(1)}, bf16[128,1024]{1,0:T(8,128)(2,1)S(1)}, u32[]{:S(2)}, u32[]{:S(2)}) collective-permute-start(bf16[128,1024]{1,0:T(8,128)(2,1)S(1)} %combine_1.3), channel_id=1, source_target_pairs={{0,16},{4,12},{8,24},{12,4},{16,0},{20,28},{24,8},{28,20},{1,17},{... | collective-permute-start | bytes 786440 | tf_op jit(solution)/shard_map/ppermute | solution.py:311
  78.2 3.2 %collective-permute-done.10.refs_4_ = bf16[128,1024]{1,0:T(8,128)(2,1)S(1)} collective-permute-done((bf16[128,1024]{1,0:T(8,128)(2,1)S(1)}, bf16[128,1024]{1,0:T(8,128)(2,1)S(1)}, u32[]{:S(2)}, u32[]{:S(2)}) %collective-permute-start.10) | collective-permute-done | bytes 262176 | tf_op jit(solution)/shard_map/ppermute | solution.py:311
  81.4 1.7 %combine_2.2 = (bf16[128,1024]{1,0:T(8,128)(2,1)S(1)}, bf16[128,1024]{1,0:T(8,128)(2,1)S(1)}) custom-call(s32[3]{0:T(128)S(1)} %pad_add_fusion.me, bf16[144,1024]{1,0:T(8,128)(2,1)} %collective-permute-done.1.refs_1_.refs_0_, bf16[144,1024]{1,0:T(8,128)(2,1)} %collective-permute-done.2.refs_2_.refs_1_, bf16[128,1024]{1,0:T(8,128)(2,1)S(1)} %slice.118.refs_2_, ...), custom_call_target="tpu_custom_call" | custom-call | flops 134217728 | bytes 1900556 | tf_op jit(solution)/shard_map/combine_2/pallas_call | solution.py:227
  83.7 1.9 %collective-permute-start.12 = (bf16[128,1024]{1,0:T(8,128)(2,1)S(1)}, bf16[128,1024]{1,0:T(8,128)(2,1)S(1)}, u32[]{:S(2)}, u32[]{:S(2)}) collective-permute-start(bf16[128,1024]{1,0:T(8,128)(2,1)S(1)} %get-tuple-element.28), channel_id=1, source_target_pairs={{0,16},{4,20},{8,24},{12,28},{16,0},{20,4},{24,8},{28,12},{1,17},{... | collective-permute-start | bytes 786440 | tf_op jit(solution)/shard_map/ppermute | solution.py:307
  87.0 1.5 %collective-permute-start.25 = (bf16[128,1024]{1,0:T(8,128)(2,1)S(1)}, bf16[128,1024]{1,0:T(8,128)(2,1)S(1)}, u32[]{:S(2)}, u32[]{:S(2)}) collective-permute-start(bf16[128,1024]{1,0:T(8,128)(2,1)S(1)} %get-tuple-element.36), channel_id=1, source_target_pairs={{0,16},{4,20},{8,24},{12,28},{16,0},{20,4},{24,8},{28,12},{1,17},{... | collective-permute-start | bytes 786440 | tf_op jit(solution)/shard_map/ppermute | solution.py:307
  88.5 3.9 %collective-permute-done.11.refs_4_ = bf16[128,1024]{1,0:T(8,128)(2,1)S(1)} collective-permute-done((bf16[128,1024]{1,0:T(8,128)(2,1)S(1)}, bf16[128,1024]{1,0:T(8,128)(2,1)S(1)}, u32[]{:S(2)}, u32[]{:S(2)}) %collective-permute-start.11) | collective-permute-done | bytes 262176 | tf_op jit(solution)/shard_map/ppermute | solution.py:307
  93.0 3.3 %collective-permute-done.24.refs_10_ = bf16[128,1024]{1,0:T(8,128)(2,1)S(1)} collective-permute-done((bf16[128,1024]{1,0:T(8,128)(2,1)S(1)}, bf16[128,1024]{1,0:T(8,128)(2,1)S(1)}, u32[]{:S(2)}, u32[]{:S(2)}) %collective-permute-start.24) | collective-permute-done | bytes 262176 | tf_op jit(solution)/shard_map/ppermute | solution.py:307
  96.7 2.6 %finish.1 = bf16[256,1024]{1,0:T(8,128)(2,1)} custom-call(s32[3]{0:T(128)S(1)} %pad_add_fusion.me, bf16[144,1024]{1,0:T(8,128)(2,1)} %get-tuple-element.21.refs_0_, bf16[128,1024]{1,0:T(8,128)(2,1)S(1)} %copy-done.13, bf16[192,1024]{1,0:T(8,128)(2,1)S(1)} %get-tuple-element.23.refs_2_, bf16[192,1024]{1,0:T(8,128)(2,1)S(1)} %collective-permute-done.6.refs_3_, ...), custom_call_target="tpu_custom_call" | custom-call | flops 134217728 | bytes 4259852 | tf_op jit(solution)/shard_map/finish/pallas_call | solution.py:253
  (100 shorter events, 19.8 us)
Async XLA Ops:
  2.3 5.6 %collective-permute-start = (bf16[256,1024]{1,0:T(8,128)(2,1)}, bf16[256,1024]{1,0:T(8,128)(2,1)}, u32[]{:S(2)}, u32[]{:S(2)}) collective-permute-start(bf16[256,1024]{1,0:T(8,128)(2,1)} %pad_maximum_fusion), channel_id=1, source_target_pairs={{0,4},{4,8},{8,12},{12,16},{16,20},{20,24},{24,28},{1,5},{5,9},{9,... | collective-permute-start | bytes 1572872 | tf_op jit(solution)/shard_map/ppermute | solution.py:363
  6.3 21.9 %collective-permute-start.13 = (bf16[256,1024]{1,0:T(8,128)(2,1)}, bf16[256,1024]{1,0:T(8,128)(2,1)}, u32[]{:S(2)}, u32[]{:S(2)}) collective-permute-start(bf16[256,1024]{1,0:T(8,128)(2,1)} %pad_maximum_fusion.1), channel_id=1, source_target_pairs={{4,0},{8,4},{12,8},{16,12},{20,16},{24,20},{28,24},{5,1},{9,5},{13... | collective-permute-start | bytes 1572872 | tf_op jit(solution)/shard_map/ppermute | solution.py:366
  17.1 25.3 %collective-permute-start.2 = (bf16[144,1024]{1,0:T(8,128)(2,1)}, bf16[144,1024]{1,0:T(8,128)(2,1)}, u32[]{:S(2)}, u32[]{:S(2)}) collective-permute-start(bf16[144,1024]{1,0:T(8,128)(2,1)} %get-tuple-element.21.refs_0_), channel_id=1, source_target_pairs={{0,16},{4,20},{8,24},{12,28},{16,0},{20,4},{24,8},{28,12},{1,17},{... | collective-permute-start | bytes 884744 | tf_op jit(solution)/shard_map/ppermute | solution.py:307
  28.2 14.7 %collective-permute-start.1 = (bf16[144,1024]{1,0:T(8,128)(2,1)}, bf16[144,1024]{1,0:T(8,128)(2,1)}, u32[]{:S(2)}, u32[]{:S(2)}) collective-permute-start(bf16[144,1024]{1,0:T(8,128)(2,1)} %get-tuple-element.21.refs_0_), channel_id=1, source_target_pairs={{0,8},{4,12},{8,0},{12,4},{16,24},{20,28},{24,16},{28,20},{1,9},{5... | collective-permute-start | bytes 884744 | tf_op jit(solution)/shard_map/ppermute | solution.py:307
  40.3 7.0 %collective-permute-start.15 = (bf16[144,1024]{1,0:T(8,128)(2,1)}, bf16[144,1024]{1,0:T(8,128)(2,1)S(1)}, u32[]{:S(2)}, u32[]{:S(2)}) collective-permute-start(bf16[144,1024]{1,0:T(8,128)(2,1)} %get-tuple-element.29.refs_0_.refs_6_), channel_id=1, source_target_pairs={{0,16},{4,20},{8,24},{12,28},{16,0},{20,4},{24,8},{28,12},{1,17},{... | collective-permute-start | bytes 884744 | tf_op jit(solution)/shard_map/ppermute | solution.py:307
  40.3 8.5 %collective-permute-start.14 = (bf16[144,1024]{1,0:T(8,128)(2,1)}, bf16[144,1024]{1,0:T(8,128)(2,1)S(1)}, u32[]{:S(2)}, u32[]{:S(2)}) collective-permute-start(bf16[144,1024]{1,0:T(8,128)(2,1)} %get-tuple-element.29.refs_0_.refs_6_), channel_id=1, source_target_pairs={{0,8},{4,12},{8,0},{12,4},{16,24},{20,28},{24,16},{28,20},{1,9},{5... | collective-permute-start | bytes 884744 | tf_op jit(solution)/shard_map/ppermute | solution.py:307
  42.4 6.9 %collective-permute-start.3 = (bf16[144,1024]{1,0:T(8,128)(2,1)}, bf16[144,1024]{1,0:T(8,128)(2,1)S(1)}, u32[]{:S(2)}, u32[]{:S(2)}) collective-permute-start(bf16[144,1024]{1,0:T(8,128)(2,1)} %get-tuple-element.21.refs_0_), channel_id=1, source_target_pairs={{0,4},{4,0},{8,12},{12,8},{16,20},{20,16},{24,28},{28,24},{1,5},{5... | collective-permute-start | bytes 884744 | tf_op jit(solution)/shard_map/ppermute | solution.py:307
  42.4 8.5 %collective-permute-start.5 = (bf16[144,1024]{1,0:T(8,128)(2,1)}, bf16[144,1024]{1,0:T(8,128)(2,1)S(1)}, u32[]{:S(2)}, u32[]{:S(2)}) collective-permute-start(bf16[144,1024]{1,0:T(8,128)(2,1)} %collective-permute-done.2.refs_2_.refs_1_), channel_id=1, source_target_pairs={{0,4},{4,0},{8,12},{12,8},{16,20},{20,16},{24,28},{28,24},{1,5},{5... | collective-permute-start | bytes 884744 | tf_op jit(solution)/shard_map/ppermute | solution.py:307
  42.9 8.0 %collective-permute-start.4 = (bf16[144,1024]{1,0:T(8,128)(2,1)}, bf16[144,1024]{1,0:T(8,128)(2,1)S(1)}, u32[]{:S(2)}, u32[]{:S(2)}) collective-permute-start(bf16[144,1024]{1,0:T(8,128)(2,1)} %collective-permute-done.1.refs_1_.refs_0_), channel_id=1, source_target_pairs={{0,4},{4,0},{8,12},{12,8},{16,20},{20,16},{24,28},{28,24},{1,5},{5... | collective-permute-start | bytes 884744 | tf_op jit(solution)/shard_map/ppermute | solution.py:307
  47.3 13.9 %collective-permute-start.16 = (bf16[144,1024]{1,0:T(8,128)(2,1)}, bf16[144,1024]{1,0:T(8,128)(2,1)S(1)}, u32[]{:S(2)}, u32[]{:S(2)}) collective-permute-start(bf16[144,1024]{1,0:T(8,128)(2,1)} %get-tuple-element.29.refs_0_.refs_6_), channel_id=1, source_target_pairs={{0,4},{4,0},{8,12},{12,8},{16,20},{20,16},{24,28},{28,24},{1,5},{5... | collective-permute-start | bytes 884744 | tf_op jit(solution)/shard_map/ppermute | solution.py:307
  48.8 12.5 %collective-permute-start.7 = (bf16[144,1024]{1,0:T(8,128)(2,1)S(1)}, bf16[144,1024]{1,0:T(8,128)(2,1)S(1)}, u32[]{:S(2)}, u32[]{:S(2)}) collective-permute-start(bf16[144,1024]{1,0:T(8,128)(2,1)S(1)} %broadcast_select_fusion.1), channel_id=1, source_target_pairs={{0,16},{4,12},{8,24},{12,4},{16,0},{20,28},{24,8},{28,20},{1,17},{... | collective-permute-start | bytes 884744 | tf_op jit(solution)/shard_map/ppermute | solution.py:311
  49.3 12.4 %collective-permute-start.20 = (bf16[144,1024]{1,0:T(8,128)(2,1)S(1)}, bf16[144,1024]{1,0:T(8,128)(2,1)S(1)}, u32[]{:S(2)}, u32[]{:S(2)}) collective-permute-start(bf16[144,1024]{1,0:T(8,128)(2,1)S(1)} %broadcast_select_fusion), channel_id=1, source_target_pairs={{0,16},{4,12},{8,24},{12,4},{16,0},{20,28},{24,8},{28,20},{1,17},{... | collective-permute-start | bytes 884744 | tf_op jit(solution)/shard_map/ppermute | solution.py:311
  50.9 10.9 %collective-permute-start.18 = (bf16[144,1024]{1,0:T(8,128)(2,1)S(1)}, bf16[144,1024]{1,0:T(8,128)(2,1)S(1)}, u32[]{:S(2)}, u32[]{:S(2)}) collective-permute-start(bf16[144,1024]{1,0:T(8,128)(2,1)S(1)} %collective-permute-done.15.refs_2_.refs_1_), channel_id=1, source_target_pairs={{0,4},{4,0},{8,12},{12,8},{16,20},{20,16},{24,28},{28,24},{1,5},{5... | collective-permute-start | bytes 884744 | tf_op jit(solution)/shard_map/ppermute | solution.py:307
  50.9 10.9 %collective-permute-start.17 = (bf16[144,1024]{1,0:T(8,128)(2,1)S(1)}, bf16[144,1024]{1,0:T(8,128)(2,1)S(1)}, u32[]{:S(2)}, u32[]{:S(2)}) collective-permute-start(bf16[144,1024]{1,0:T(8,128)(2,1)S(1)} %collective-permute-done.14.refs_1_.refs_0_), channel_id=1, source_target_pairs={{0,4},{4,0},{8,12},{12,8},{16,20},{20,16},{24,28},{28,24},{1,5},{5... | collective-permute-start | bytes 884744 | tf_op jit(solution)/shard_map/ppermute | solution.py:307
  61.2 16.9 %collective-permute-start.6 = (bf16[192,1024]{1,0:T(8,128)(2,1)S(1)}, bf16[192,1024]{1,0:T(8,128)(2,1)S(1)}, u32[]{:S(2)}, u32[]{:S(2)}) collective-permute-start(bf16[192,1024]{1,0:T(8,128)(2,1)S(1)} %get-tuple-element.24), channel_id=1, source_target_pairs={{0,4},{4,0},{8,12},{12,8},{16,20},{20,16},{24,28},{28,24},{1,5},{5... | collective-permute-start | bytes 1179656 | tf_op jit(solution)/shard_map/ppermute | solution.py:307
  61.3 7.1 %collective-permute-start.8 = (bf16[144,1024]{1,0:T(8,128)(2,1)S(1)}, bf16[144,1024]{1,0:T(8,128)(2,1)S(1)}, u32[]{:S(2)}, u32[]{:S(2)}) collective-permute-start(bf16[144,1024]{1,0:T(8,128)(2,1)S(1)} %collective-permute-done.7.refs_0_), channel_id=1, source_target_pairs={{0,4},{4,0},{8,12},{12,8},{16,20},{20,16},{24,28},{28,24},{1,5},{5... | collective-permute-start | bytes 884744 | tf_op jit(solution)/shard_map/ppermute | solution.py:307
  61.8 9.3 %collective-permute-start.21 = (bf16[144,1024]{1,0:T(8,128)(2,1)S(1)}, bf16[144,1024]{1,0:T(8,128)(2,1)S(1)}, u32[]{:S(2)}, u32[]{:S(2)}) collective-permute-start(bf16[144,1024]{1,0:T(8,128)(2,1)S(1)} %collective-permute-done.20.refs_0_), channel_id=1, source_target_pairs={{0,4},{4,0},{8,12},{12,8},{16,20},{20,16},{24,28},{28,24},{1,5},{5... | collective-permute-start | bytes 884744 | tf_op jit(solution)/shard_map/ppermute | solution.py:307
  68.0 10.2 %collective-permute-start.19 = (bf16[192,1024]{1,0:T(8,128)(2,1)S(1)}, bf16[192,1024]{1,0:T(8,128)(2,1)S(1)}, u32[]{:S(2)}, u32[]{:S(2)}) collective-permute-start(bf16[192,1024]{1,0:T(8,128)(2,1)S(1)} %get-tuple-element.32), channel_id=1, source_target_pairs={{0,4},{4,0},{8,12},{12,8},{16,20},{20,16},{24,28},{28,24},{1,5},{5... | collective-permute-start | bytes 1179656 | tf_op jit(solution)/shard_map/ppermute | solution.py:307
  75.0 6.4 %collective-permute-start.10 = (bf16[128,1024]{1,0:T(8,128)(2,1)S(1)}, bf16[128,1024]{1,0:T(8,128)(2,1)S(1)}, u32[]{:S(2)}, u32[]{:S(2)}) collective-permute-start(bf16[128,1024]{1,0:T(8,128)(2,1)S(1)} %combine_1.2), channel_id=1, source_target_pairs={{0,16},{4,12},{8,24},{12,4},{16,0},{20,28},{24,8},{28,20},{1,17},{... | collective-permute-start | bytes 786440 | tf_op jit(solution)/shard_map/ppermute | solution.py:311
  76.5 9.2 %collective-permute-start.23 = (bf16[128,1024]{1,0:T(8,128)(2,1)S(1)}, bf16[128,1024]{1,0:T(8,128)(2,1)S(1)}, u32[]{:S(2)}, u32[]{:S(2)}) collective-permute-start(bf16[128,1024]{1,0:T(8,128)(2,1)S(1)} %combine_1.3), channel_id=1, source_target_pairs={{0,16},{4,12},{8,24},{12,4},{16,0},{20,28},{24,8},{28,20},{1,17},{... | collective-permute-start | bytes 786440 | tf_op jit(solution)/shard_map/ppermute | solution.py:311
  83.1 9.3 %collective-permute-start.11 = (bf16[128,1024]{1,0:T(8,128)(2,1)S(1)}, bf16[128,1024]{1,0:T(8,128)(2,1)S(1)}, u32[]{:S(2)}, u32[]{:S(2)}) collective-permute-start(bf16[128,1024]{1,0:T(8,128)(2,1)S(1)} %get-tuple-element.27), channel_id=1, source_target_pairs={{0,8},{4,12},{8,0},{12,4},{16,24},{20,28},{24,16},{28,20},{1,9},{5... | collective-permute-start | bytes 786440 | tf_op jit(solution)/shard_map/ppermute | solution.py:307
  83.7 9.2 %collective-permute-start.12 = (bf16[128,1024]{1,0:T(8,128)(2,1)S(1)}, bf16[128,1024]{1,0:T(8,128)(2,1)S(1)}, u32[]{:S(2)}, u32[]{:S(2)}) collective-permute-start(bf16[128,1024]{1,0:T(8,128)(2,1)S(1)} %get-tuple-element.28), channel_id=1, source_target_pairs={{0,16},{4,20},{8,24},{12,28},{16,0},{20,4},{24,8},{28,12},{1,17},{... | collective-permute-start | bytes 786440 | tf_op jit(solution)/shard_map/ppermute | solution.py:307
  86.9 9.4 %collective-permute-start.24 = (bf16[128,1024]{1,0:T(8,128)(2,1)S(1)}, bf16[128,1024]{1,0:T(8,128)(2,1)S(1)}, u32[]{:S(2)}, u32[]{:S(2)}) collective-permute-start(bf16[128,1024]{1,0:T(8,128)(2,1)S(1)} %get-tuple-element.35), channel_id=1, source_target_pairs={{0,8},{4,12},{8,0},{12,4},{16,24},{20,28},{24,16},{28,20},{1,9},{5... | collective-permute-start | bytes 786440 | tf_op jit(solution)/shard_map/ppermute | solution.py:307
  87.0 9.7 %collective-permute-start.25 = (bf16[128,1024]{1,0:T(8,128)(2,1)S(1)}, bf16[128,1024]{1,0:T(8,128)(2,1)S(1)}, u32[]{:S(2)}, u32[]{:S(2)}) collective-permute-start(bf16[128,1024]{1,0:T(8,128)(2,1)S(1)} %get-tuple-element.36), channel_id=1, source_target_pairs={{0,16},{4,20},{8,24},{12,28},{16,0},{20,4},{24,8},{28,12},{1,17},{... | collective-permute-start | bytes 786440 | tf_op jit(solution)/shard_map/ppermute | solution.py:307
  (21 other events, 125.7 us)

commit v2 on v1

--- a/solution.py
+++ b/solution.py
@@ -22,6 +22,7 @@
 BF16 = jnp.bfloat16
 VMEM = pl.BlockSpec(memory_space=pltpu.VMEM)
 SMEM = pl.BlockSpec(memory_space=pltpu.SMEM)
+ANY = pl.BlockSpec(memory_space=pl.ANY)
 
 
 def cost(flops, transcendentals, args, outs):
@@ -30,49 +31,126 @@
     return pl.CostEstimate(flops=flops, transcendentals=transcendentals, bytes_accessed=moved)
 
 
-def window_bias(queries, first_query, keys, first_key, live):
-    q = lax.broadcasted_iota(jnp.int32, (queries, keys), 0) + first_query
-    k = lax.broadcasted_iota(jnp.int32, (queries, keys), 1) + (first_key + PLANE * R_IL)
+NT = (((1,), (1,)), ((), ()))
+TN = (((0,), (0,)), ((), ()))
+
+
+def window_bias(keys, first_key, queries, first_query, live):
+    k = lax.broadcasted_iota(jnp.int32, (keys, queries), 0) + (first_key + PLANE * R_IL)
+    q = lax.broadcasted_iota(jnp.int32, (keys, queries), 1) + first_query
     near = jnp.abs(q // PLANE + R_IL - k // PLANE) <= R_IL
     near = near & (jnp.abs(q // DP % XL - k // DP % XL) <= R_XL)
     near = near & (jnp.abs(q % DP - k % DP) <= R_DP)
     if live is not None:
         near = near & (live > 0)
-    return jnp.where(near, F32(0.0), F32(-1e30))
-
-
-def attention_kernel(half, live, q, k, v, halo, x, w, gain, meta, resid, payload, att):
+    bias = jnp.where(near, F32(0.0), F32(-1e30))
+    return jnp.concatenate([bias, bias], axis=1)
+
+
+def two_heads(query):
+    lane = lax.broadcasted_iota(jnp.int32, query.shape, 1)
+    query = query * BF16(1.0 / HD**0.5)
+    zero = BF16(0.0)
+    return jnp.concatenate(
+        [jnp.where(lane < HD, query, zero), jnp.where(lane >= HD, query, zero)], axis=0
+    )
+
+
+def interior_kernel(count, *refs):
+    q, k, v = refs[:3]
+    sources = refs[3 : 3 + count]
+    acc, tops, sums = refs[3 + count : 6 + count]
+    kept = refs[6 + count : 6 + 2 * count]
+    tail = refs[6 + 2 * count : -2]
+    bias, sems = refs[-2:]
+    copies = [(a, b) for a, b in zip(sources, kept)]
+    if tail:
+        wide = tail[0].shape[1] // 2
+        start = sources[1].shape[1] - wide
+        for i in range(2):
+            copies.append(
+                (sources[1 + i].at[:, pl.ds(start, wide)], tail[0].at[:, pl.ds(i * wide, wide)])
+            )
+    copies = [pltpu.make_async_copy(a, b, sems.at[i]) for i, (a, b) in enumerate(copies)]
+    for copy in copies:
+        copy.start()
     rows = q.shape[0]
-    own = k.shape[0]
-    wide = halo.shape[0] // 2
-    start = half * rows
-    bias_own = window_bias(rows, start, own, 0, None)
-    first = -wide if half == 0 else own
-    bias_halo = window_bias(rows, start, wide, first, live[half])
-    lane = lax.broadcasted_iota(jnp.int32, (rows, 2 * HD), 1)
-    nt = (((1,), (1,)), ((), ()))
+    bias[...] = window_bias(rows, 0, rows, 0, None)
     for pair in range(HEADS // 2):
         cols = slice(pair * 2 * HD, (pair + 1) * 2 * HD)
-        query = q[:, cols] * BF16(1.0 / HD**0.5)
-        key_own, key_halo = k[:, cols], halo[:wide, cols]
-        val_own, val_halo = v[:, cols], halo[wide:, cols]
-        outs = []
+        s = lax.dot_general(k[:, cols], two_heads(q[:, cols]), NT, preferred_element_type=F32)
+        s = s + bias[...]
+        top = jnp.max(s, axis=0, keepdims=True)
+        p = jnp.exp(s - top)
+        total = jnp.sum(p, axis=0, keepdims=True)
+        o = lax.dot_general(v[:, cols], p.astype(BF16), TN, preferred_element_type=F32)
+        base = pair * 2 * HD
+        acc[base : base + HD, :] = o[:HD, :rows]
+        acc[base + HD : base + 2 * HD, :] = o[HD:, rows:]
         for side in range(2):
-            mine = (lane < HD) if side == 0 else (lane >= HD)
-            qh = jnp.where(mine, query, BF16(0.0))
-            s_own = lax.dot_general(qh, key_own, nt, preferred_element_type=F32) + bias_own
-            s_halo = lax.dot_general(qh, key_halo, nt, preferred_element_type=F32) + bias_halo
-            top = jnp.maximum(
-                jnp.max(s_own, axis=1, keepdims=True), jnp.max(s_halo, axis=1, keepdims=True)
-            )
-            p_own = jnp.exp(s_own - top)
-            p_halo = jnp.exp(s_halo - top)
-            total = jnp.sum(p_own, axis=1, keepdims=True) + jnp.sum(p_halo, axis=1, keepdims=True)
-            o = jnp.dot(p_own.astype(BF16), val_own, preferred_element_type=F32)
-            o = o + jnp.dot(p_halo.astype(BF16), val_halo, preferred_element_type=F32)
-            outs.append(o / total)
-        att[:, cols] = jnp.where(lane < HD, outs[0], outs[1]).astype(BF16)
-    res = x[...].astype(F32) + jnp.dot(att[...], w[...], preferred_element_type=F32)
+            span = slice(side * rows, (side + 1) * rows)
+            tops[2 * pair + side : 2 * pair + side + 1, :] = top[:, span]
+            sums[2 * pair + side : 2 * pair + side + 1, :] = total[:, span]
+    for copy in copies:
+        copy.wait()
+
+
+def interior(q, k, v, weights, tail):
+    rows, model = q.shape
+    outs = [
+        pltpu.VMEM((model, rows), F32),
+        pltpu.VMEM((HEADS, rows), F32),
+        pltpu.VMEM((HEADS, rows), F32),
+    ]
+    outs += [pltpu.VMEM(w.shape, w.dtype) for w in weights]
+    if tail:
+        outs.append(pltpu.VMEM((weights[1].shape[0], 2 * tail), weights[1].dtype))
+    copies = len(weights) + (2 if tail else 0)
+    args = [q, k, v, *weights]
+    flat = [jax.ShapeDtypeStruct(w.shape, w.dtype) for w in weights]
+    return pl.pallas_call(
+        functools.partial(interior_kernel, len(weights)),
+        in_specs=[VMEM] * 3 + [ANY] * len(weights),
+        out_specs=[VMEM] * len(outs),
+        out_shape=outs,
+        scratch_shapes=[pltpu.VMEM((rows, 2 * rows), F32), pltpu.SemaphoreType.DMA((copies,))],
+        compiler_params=pltpu.CompilerParams(vmem_limit_bytes=24 * MIB),
+        cost_estimate=cost(4 * rows * rows * model, HEADS * rows * rows, args, flat),
+        name="interior",
+    )(*args)
+
+
+def edge_kernel(half, live, q, halo, acc, tops, sums, x, w, gain, *rest):
+    meta = rest[0] if len(rest) == 5 else None
+    resid, payload, bias, att = rest[-4:]
+    rows = q.shape[0]
+    wide = halo.shape[0] // 2
+    first = -wide if half == 0 else 2 * rows
+    bias[...] = window_bias(wide, first, rows, half * rows, live[half])
+    span = slice(half * rows, (half + 1) * rows)
+    for pair in range(HEADS // 2):
+        cols = slice(pair * 2 * HD, (pair + 1) * 2 * HD)
+        s = lax.dot_general(
+            halo[:wide, cols], two_heads(q[:, cols]), NT, preferred_element_type=F32
+        )
+        s = s + bias[...]
+        both = [slice(2 * pair + side, 2 * pair + side + 1) for side in range(2)]
+        before = jnp.concatenate([tops[b, span] for b in both], axis=1)
+        top = jnp.maximum(before, jnp.max(s, axis=0, keepdims=True))
+        shrink = jnp.exp(before - top)
+        p = jnp.exp(s - top)
+        total = jnp.concatenate([sums[b, span] for b in both], axis=1) * shrink
+        total = total + jnp.sum(p, axis=0, keepdims=True)
+        o = lax.dot_general(halo[wide:, cols], p.astype(BF16), TN, preferred_element_type=F32)
+        inverse = 1.0 / total
+        for side in range(2):
+            base = pair * 2 * HD + side * HD
+            at = slice(side * rows, (side + 1) * rows)
+            value = acc[base : base + HD, span] * shrink[:, at]
+            value = value + o[side * HD : (side + 1) * HD, at]
+            att[base : base + HD, :] = (value * inverse[:, at]).astype(BF16)
+    res = x[...].astype(F32)
+    res = res + lax.dot_general(att[...], w[...], TN, preferred_element_type=F32)
     res = res.astype(BF16)
     resid[...] = res
     res = res.astype(F32)
@@ -83,100 +161,123 @@
         payload[rows:, :] = jnp.broadcast_to(meta[...], (META, meta.shape[1]))
 
 
-def attend(half, live, q, k, v, halo, x, w, gain, meta):
+def edge(half, live, q, halo, acc, tops, sums, x, w, gain, meta):
     rows, model = q.shape[0] // 2, q.shape[1]
+    wide = halo.shape[0] // 2
     whole = lambda a: pl.BlockSpec(a.shape, lambda i: (0,) * a.ndim)
     part = pl.BlockSpec((rows, model), lambda i: (half, 0))
-    args = [live, q, k, v, halo, x, w, gain]
-    specs = [SMEM, part, whole(k), whole(v), whole(halo), part, whole(w), whole(gain)]
-    extra = 0
-    if meta is not None:
-        args.append(meta)
-        specs.append(whole(meta))
-        extra = META
-        body = functools.partial(attention_kernel, half)
-    else:
-
-        def body(live, q, k, v, halo, x, w, gain, resid, payload, att):
-            attention_kernel(half, live, q, k, v, halo, x, w, gain, None, resid, payload, att)
-
-    outs = [
+    args = [live, q, halo, acc, tops, sums, x, w, gain] + ([] if meta is None else [meta])
+    specs = [SMEM, part, whole(halo), VMEM, VMEM, VMEM, part, VMEM, whole(gain)]
+    specs += [] if meta is None else [whole(meta)]
+    extra = 0 if meta is None else META
+    flat = [
         jax.ShapeDtypeStruct((rows, model), BF16),
         jax.ShapeDtypeStruct((rows + extra, model), BF16),
     ]
-    keys = k.shape[0] + halo.shape[0] // 2
     return pl.pallas_call(
-        body,
+        functools.partial(edge_kernel, half),
         grid=(1,),
         in_specs=specs,
-        out_specs=[pl.BlockSpec(o.shape, lambda i: (0, 0)) for o in outs],
-        out_shape=outs,
-        scratch_shapes=[pltpu.VMEM((rows, model), BF16)],
+        out_specs=[pl.BlockSpec(o.shape, lambda i: (0, 0)) for o in flat],
+        out_shape=flat,
+        scratch_shapes=[pltpu.VMEM((wide, 2 * rows), F32), pltpu.VMEM((model, rows), BF16)],
         compiler_params=pltpu.CompilerParams(vmem_limit_bytes=24 * MIB),
         cost_estimate=cost(
-            4 * rows * keys * model + 2 * rows * model * model, HEADS * rows * keys, args, outs
+            4 * rows * wide * model + 2 * rows * model * model, HEADS * rows * wide, args, flat
         ),
-        name=f"attention_half{half}",
+        name=f"edge_half{half}",
     )(*args)
 
 
-def pick_matrices(payload, block, rows, capacity, expert):
+def meta_items(payload, block, rows):
     base = block * (rows + META) + rows
     meta = payload[base : base + META, :].astype(F32)
-    item = [meta[:, i * rows : (i + 1) * rows] for i in range(8)]
-    hit0, hit1 = item[0] == expert, item[1] == expert
-    hits = jnp.where(hit0 | hit1, F32(1.0), F32(0.0))
+    return [meta[:, i * rows : (i + 1) * rows] for i in range(8)]
+
+
+def slot_rows(hits):
+    rows = hits.shape[1]
     upper = lax.broadcasted_iota(jnp.int32, (rows, rows), 0) < lax.broadcasted_iota(
         jnp.int32, (rows, rows), 1
     )
     upper = jnp.where(upper, F32(1.0), F32(0.0)).astype(BF16)
     rank = jnp.dot(hits.astype(BF16), upper, preferred_element_type=F32)
-    rank = jnp.where(hits > 0, rank, F32(-1.0))
-    gate = jnp.where(hit0, item[2] + item[3] + item[4], F32(0.0))
-    gate = gate + jnp.where(hit1, item[5] + item[6] + item[7], F32(0.0))
+    return jnp.where(hits > 0, rank, F32(-1.0))
+
+
+def pick_matrices(payload, block, rows, capacity, wanted):
+    item = meta_items(payload, block, rows)
+    named = [(item[0] == e, item[1] == e) for e in wanted]
+    ranks = slot_rows(
+        jnp.concatenate([jnp.where(a | b, F32(1.0), F32(0.0)) for a, b in named], axis=0)
+    )
     slot = lax.broadcasted_iota(jnp.int32, (capacity, rows), 0).astype(F32)
-    return slot == rank[:1, :], gate[:1, :]
-
-
-def experts_kernel(blocks, rows, capacity, me, *refs):
-    count = len(refs) - 7
-    payloads, (w_gate, w_up, w_down, out_mine, out_sib, x, hidden) = refs[:count], refs[count:]
+    result = []
+    for i, (a, b) in enumerate(named):
+        gate = jnp.where(a, item[2] + item[3] + item[4], F32(0.0))
+        gate = gate + jnp.where(b, item[5] + item[6] + item[7], F32(0.0))
+        result.append((slot == ranks[i * META : i * META + 1, :], gate[:1, :]))
+    return result
+
+
+def experts_kernel(rows, capacity, tailed, me, *refs):
+    ends = 8 if tailed else 7
+    count = len(refs) - ends
+    payloads = refs[:count]
+    w_gate, w_up, w_down = refs[count : count + 3]
+    tail = refs[count + 3] if tailed else None
+    out_mine, out_sib, x, hidden = refs[-4:]
     expert = me[0].astype(F32)
-    place = 0
-    for payload in payloads:
-        for block in range(blocks):
-            hot, _ = pick_matrices(payload, block, rows, capacity, expert)
-            hot = jnp.where(hot, F32(1.0), F32(0.0)).astype(BF16)
-            base = block * (rows + META)
-            picked = jnp.dot(hot, payload[base : base + rows, :], preferred_element_type=F32)
-            x[place : place + capacity, :] = picked.astype(BF16)
-            place += capacity
+    groups = count // 2
+    order = [payloads[side * groups + g] for g in range(groups) for side in range(2)]
+    hits = []
+    for payload in order:
+        item = meta_items(payload, 0, rows)
+        hits.append(jnp.where((item[0] == expert) | (item[1] == expert), F32(1.0), F32(0.0)))
+    ranks = slot_rows(jnp.concatenate(hits, axis=0))
+    slot = lax.broadcasted_iota(jnp.int32, (2 * capacity, rows), 0).astype(F32)
+    for g in range(groups):
+        first = ranks[2 * g * META : 2 * g * META + 1, :]
+        second = ranks[(2 * g + 1) * META : (2 * g + 1) * META + 1, :]
+        second = jnp.where(second >= 0, second + capacity, F32(-1.0))
+        hot = jnp.concatenate([slot == first, slot == second], axis=1)
+        hot = jnp.where(hot, F32(1.0), F32(0.0)).astype(BF16)
+        tokens = jnp.concatenate([order[2 * g][:rows, :], order[2 * g + 1][:rows, :]], axis=0)
+        picked = jnp.dot(hot, tokens, preferred_element_type=F32)
+        x[2 * g * capacity : (2 * g + 2) * capacity, :] = picked.astype(BF16)
     width = w_gate.shape[1]
-    for at in range(0, width, 256):
-        cols = slice(at, min(at + 256, width))
-        g = jnp.dot(x[...], w_gate[:, cols], preferred_element_type=F32)
-        u = jnp.dot(x[...], w_up[:, cols], preferred_element_type=F32)
+    step = 256
+    for at in range(0, width, step):
+        wide = min(step, width - at)
+        cols = slice(at, at + wide)
+        if tail is not None and wide < step:
+            both = jnp.dot(x[...], tail[...], preferred_element_type=F32)
+            g, u = both[:, :wide], both[:, wide:]
+        else:
+            g = jnp.dot(x[...], w_gate[:, cols], preferred_element_type=F32)
+            u = jnp.dot(x[...], w_up[:, cols], preferred_element_type=F32)
         hidden[:, cols] = (g / (1.0 + jnp.exp(-g)) * u).astype(BF16)
-    half = place // 2
-    for at in range(0, w_down.shape[1], 256):
-        cols = slice(at, at + 256)
+    for at in range(0, w_down.shape[1], step):
+        cols = slice(at, at + step)
         o = jnp.dot(hidden[...], w_down[:, cols], preferred_element_type=F32).astype(BF16)
-        out_mine[:, cols] = o[:half]
-        out_sib[:, cols] = o[half:]
-
-
-def experts(me, mine, sib, w_gate, w_up, w_down, blocks, rows, capacity):
-    model, width = w_gate.shape
-    slots = (len(mine) + len(sib)) * blocks * capacity
+        for g in range(groups):
+            span = slice(g * capacity, (g + 1) * capacity)
+            out_mine[span, cols] = o[2 * g * capacity : (2 * g + 1) * capacity]
+            out_sib[span, cols] = o[(2 * g + 1) * capacity : (2 * g + 2) * capacity]
+
+
+def experts(me, mine, sib, weights, rows, capacity):
+    model, width = weights[0].shape
+    slots = (len(mine) + len(sib)) * capacity
     outs = [jax.ShapeDtypeStruct((slots // 2, model), BF16)] * 2
-    args = [me, *mine, *sib, w_gate, w_up, w_down]
+    args = [me, *mine, *sib, *weights]
     return pl.pallas_call(
-        functools.partial(experts_kernel, blocks, rows, capacity),
+        functools.partial(experts_kernel, rows, capacity, len(weights) == 4),
         in_specs=[SMEM] + [VMEM] * (len(args) - 1),
         out_specs=[VMEM] * 2,
         out_shape=outs,
         scratch_shapes=[pltpu.VMEM((slots, model), BF16), pltpu.VMEM((slots, width), BF16)],
-        compiler_params=pltpu.CompilerParams(vmem_limit_bytes=32 * MIB),
+        compiler_params=pltpu.CompilerParams(vmem_limit_bytes=24 * MIB),
         cost_estimate=cost(6 * slots * model * width, slots * width, args, outs),
         name=f"experts_{slots}",
     )(*args)
@@ -184,8 +285,8 @@
 
 def spread(payload, block, rows, capacity, experts_two, outs_two):
     weights, values = [], []
-    for expert, out in zip(experts_two, outs_two):
-        hot, gate = pick_matrices(payload, block, rows, capacity, expert)
+    picks = pick_matrices(payload, block, rows, capacity, experts_two)
+    for (hot, gate), out in zip(picks, outs_two):
         full = jnp.where(hot, gate, F32(0.0))
         high = full.astype(BF16)
         weights += [high, (full - high.astype(F32)).astype(BF16)]
@@ -311,13 +412,11 @@
     return lax.ppermute(array, "tile", [(i, i ^ (2 if i % 2 else 4)) for i in range(8)])
 
 
-def routed_gather(payloads, resids, w_gate, w_up, w_down, rows, capacity):
+def routed_gather(payloads, resids, weights, rows, capacity):
     tile = lax.axis_index("tile")
     core = tile % 2
     me = jnp.stack([tile, tile ^ 1, core]).astype(jnp.int32)
-    run = functools.partial(
-        experts, w_gate=w_gate, w_up=w_up, w_down=w_down, blocks=1, rows=rows, capacity=capacity
-    )
+    run = functools.partial(experts, weights=weights, rows=rows, capacity=capacity)
     sizes = dict(blocks=1, rows=rows, capacity=capacity)
     moved = []
     for own in payloads:
@@ -360,16 +459,14 @@
     capacity = row_count * routes.shape[1] // tiles
     up = [(i, i + 1) for i in range(tiles - 1)]
     down = [(j, i) for i, j in up]
-    before = lax.ppermute(
-        jnp.concatenate([key_vectors[-width:], values[-width:]], axis=0), "tile", up
-    )
-    after = lax.ppermute(
-        jnp.concatenate([key_vectors[:width], values[:width]], axis=0), "tile", down
-    )
+    last = jnp.concatenate([key_vectors[-width:], values[-width:]], axis=0)
+    before = lax.ppermute(last, "tile", up)
     live = jnp.stack([tile > 0, tile < tiles - 1]).astype(jnp.int32)
     fast = tiles == 8
-    metas = [None, None]
+    weights, metas, tail = [out_weight], [None, None], 0
     if fast:
+        weights += [w_gate[0], w_up[0], w_down[0]]
+        tail = 128 if w_gate.shape[2] % 256 == 128 else 0
         items = [routes[:, 0].astype(F32), routes[:, 1].astype(F32)]
         for k in range(2):
             gate = route_gates[:, k]
@@ -380,16 +477,20 @@
             jnp.concatenate([a[h * rows : (h + 1) * rows] for a in items]).astype(BF16)[None]
             for h in range(2)
         ]
+    acc, tops, sums, *kept = interior(queries, key_vectors, values, weights, tail)
+    first = jnp.concatenate([key_vectors[:width], values[:width]], axis=0)
+    first, acc = lax.optimization_barrier((first, acc))
+    after = lax.ppermute(first, "tile", down)
     resids, payloads = [], []
     for half, halo in enumerate((before, after)):
-        resid, payload = attend(
-            half, live, queries, key_vectors, values, halo, inputs, out_weight,
+        resid, payload = edge(
+            half, live, queries, halo, acc, tops, sums, inputs, kept[0],
             norm_gain[None, :], metas[half],
         )
         resids.append(resid)
         payloads.append(payload)
     if fast:
-        return routed_gather(payloads, resids, w_gate[0], w_up[0], w_down[0], rows, capacity)
+        return routed_gather(payloads, resids, kept[1:], rows, capacity)
     return routed_all_to_all(
         payloads, resids, routes, route_gates, w_gate[0], w_up[0], w_down[0]
     )

time: 99.9 us -> 104 us (1.041)
  local copies, waits for them, and re-layouts: 13.5 us -> 28 us
  starting transfers between devices: 28.8 us -> 23.2 us
  Pallas kernels: 37.5 us -> 32 us
    unnamed x45 -> x63, local copies, waits for them, and re-layouts: 12 us -> 26.5 us
    ppermute x20, starting transfers between devices: 20.1 us -> 14.3 us  [swap(): return lax.ppermute(array, 'tile', [(i, i ^ bit) for i in range(8)])]
    pallas_call x6 -> x7, Pallas kernels: 30.2 us -> 24.6 us  [the longest x4 14.3 us: experts(): pl.pallas_call(functools.partial(experts_kernel, rows, capacity, len(weig...]
  transfers between devices with their start and end apart: 26 -> 26, of which waited for: 7 -> 7; matrix products, arithmetic and copies ran while one was open for 2% -> 2% of each run, Pallas kernels for 35% -> 28%
where the time goes in v2:
time: 104 us; the launch traced here: 103 us
  Pallas kernels  32 us (31%)
  local copies, waits for them, and re-layouts  28 us (27%)
  starting transfers between devices  23.2 us (22%)
  waiting for transfers between devices  16.8 us (16%)
  other arithmetic  2.87 us (3%)
    unnamed x63, local copies, waits for them, and re-layouts  26.5 us
    pallas_call x4, Pallas kernels, experts(): pl.pallas_call(functools.partial(experts_kernel, rows, capacity, len(weig...  14.3 us
    ppermute x20, starting transfers between devices, swap(): return lax.ppermute(array, 'tile', [(i, i ^ bit) for i in range(8)])  14.3 us
    ppermute x20, waiting for transfers between devices, swap(): return lax.ppermute(array, 'tile', [(i, i ^ bit) for i in range(8)])  13.6 us
    pallas_call x2, Pallas kernels, edge(): pl.pallas_call(functools.partial(edge_kernel, half), grid=(1,), in_specs=...  6.37 us
    pallas_call x4, Pallas kernels, combine(): pl.pallas_call(functools.partial(combine_kernel, blocks, rows, capacity,...  4.8 us
    ppermute x4, starting transfers between devices, swap_turned(): lax.ppermute(array, 'tile', [(i, i ^ (2 if i % 2 else 4)) for i in range(...  4.25 us
    pallas_call x1, Pallas kernels, interior(): pl.pallas_call(functools.partial(interior_kernel, len(weights)), in_specs...  3.87 us
  transfers between devices with their start and end apart: 26, of which 7 were waited for; matrix products, arithmetic and copies ran while one was open for 2% of the time, Pallas kernels for 28%

profile of v2, /device:TPU:0, one launch (start us, length us, event | category | flops | bytes accessed | tf_op | source)
XLA Modules:
  0.0 103.1 jit_solution(5872884851275462023)
XLA Ops:
  2.2 3.2 %collective-permute-start = (bf16[256,1024]{1,0:T(8,128)(2,1)}, bf16[256,1024]{1,0:T(8,128)(2,1)}, u32[]{:S(2)}, u32[]{:S(2)}) collective-permute-start(bf16[256,1024]{1,0:T(8,128)(2,1)} %pad_maximum_fusion), channel_id=1, source_target_pairs={{0,4},{4,8},{8,12},{12,16},{16,20},{20,24},{24,28},{1,5},{5,9},{9,... | collective-permute-start | bytes 1572872 | tf_op jit(solution)/shard_map/ppermute | solution.py:463
  6.3 1.8 %copy-done.12 = bf16[1,1024,1408]{2,1,0:T(8,128)(2,1)S(1)} copy-done((bf16[1,1024,1408]{2,1,0:T(8,128)(2,1)S(1)}, bf16[1,1024,1408]{2,1,0:T(8,128)(2,1)}, u32[]{:S(2)}) %copy-start.12) | copy-done | bytes 2883608
  8.1 1.8 %copy-done.13 = bf16[1,1408,1024]{2,1,0:T(8,128)(2,1)S(1)} copy-done((bf16[1,1408,1024]{2,1,0:T(8,128)(2,1)S(1)}, bf16[1,1408,1024]{2,1,0:T(8,128)(2,1)}, u32[]{:S(2)}) %copy-start.13) | copy-done | bytes 2883608
  10.9 1.6 %copy-done.20 = bf16[1024,1024]{1,0:T(8,128)(2,1)S(1)} copy-done((bf16[1024,1024]{1,0:T(8,128)(2,1)S(1)}, bf16[1024,1024]{1,0:T(8,128)(2,1)}, u32[]{:S(2)}) %copy-start.20) | copy-done | bytes 2097176
  12.5 3.9 %interior.1 = (f32[1024,256]{1,0:T(8,128)S(1)}, f32[16,256]{1,0:T(8,128)S(1)}, f32[16,256]{1,0:T(8,128)S(1)}, bf16[1024,1024]{1,0:T(8,128)(2,1)S(1)}, bf16[1024,...) custom-call(bf16[256,1024]{1,0:T(8,128)(2,1)S(1)} %copy-done.7, ...), custom_call_target="tpu_custom_call" | custom-call | flops 268435456 | bytes 23068672 | tf_op jit(solution)/shard_map/interior/pallas_call | solution.py:111
  18.0 1.6 %copy-done.2 = bf16[1408,1024]{1,0:T(8,128)(2,1)} copy-done((bf16[1408,1024]{1,0:T(8,128)(2,1)}, bf16[1408,1024]{1,0:T(8,128)(2,1)S(1)}, u32[]{:S(2)}) %copy-start.2) | copy-done | bytes 2883608
  24.5 1.6 %copy-done.5 = bf16[1024,1024]{1,0:T(8,128)(2,1)S(1)} copy-done((bf16[1024,1024]{1,0:T(8,128)(2,1)S(1)}, bf16[1024,1024]{1,0:T(8,128)(2,1)}, u32[]{:S(2)}) %copy-start.5) | copy-done | bytes 2097176
  28.4 3.2 %edge_half0.1 = (bf16[128,1024]{1,0:T(8,128)(2,1)S(1)}, bf16[144,1024]{1,0:T(8,128)(2,1)}) custom-call(s32[2]{0:T(128)S(1)} %add_convert_fusion.live, bf16[256,1024]{1,0:T(8,128)(2,1)S(1)} %copy-done.7, bf16[256,1024]{1,0:T(8,128)(2,1)} %collective-permute-done.halo, f32[1024,256]{1,0:T(8,128)S(1)} %copy-done.9, f32[16,256]{1,0:T(8,128)S(1)} %get-tuple-element.33.tops, ...), custom_call_target="tpu_custom_call" | custom-call | flops 335544320 | bytes 5314568 | tf_op jit(solution)/shard_map/edge_half0/pallas_call | solution.py:177
  32.3 5.0 %collective-permute-start.2 = (bf16[144,1024]{1,0:T(8,128)(2,1)}, bf16[144,1024]{1,0:T(8,128)(2,1)}, u32[]{:S(2)}, u32[]{:S(2)}) collective-permute-start(bf16[144,1024]{1,0:T(8,128)(2,1)} %get-tuple-element.36.refs_0_), channel_id=1, source_target_pairs={{0,16},{4,20},{8,24},{12,28},{16,0},{20,4},{24,8},{28,12},{1,17},{... | collective-permute-start | bytes 884744 | tf_op jit(solution)/shard_map/ppermute | solution.py:408
  37.8 1.6 %copy-done.6 = bf16[1024,1024]{1,0:T(8,128)(2,1)S(1)} copy-done((bf16[1024,1024]{1,0:T(8,128)(2,1)S(1)}, bf16[1024,1024]{1,0:T(8,128)(2,1)}, u32[]{:S(2)}) %copy-start.6) | copy-done | bytes 2097176
  41.7 3.2 %edge_half1.1 = (bf16[128,1024]{1,0:T(8,128)(2,1)S(1)}, bf16[144,1024]{1,0:T(8,128)(2,1)}) custom-call(s32[2]{0:T(128)S(1)} %add_convert_fusion.live, bf16[256,1024]{1,0:T(8,128)(2,1)S(1)} %copy-done.7, bf16[256,1024]{1,0:T(8,128)(2,1)} %collective-permute-done.13.halo, f32[1024,256]{1,0:T(8,128)S(1)} %copy-done.10, f32[16,256]{1,0:T(8,128)S(1)} %get-tuple-element.33.tops, ...), custom_call_target="tpu_custom_call" | custom-call | flops 335544320 | bytes 5314568 | tf_op jit(solution)/shard_map/edge_half1/pallas_call | solution.py:177
  48.7 4.8 %collective-permute-done.15.refs_2_.refs_1_ = bf16[144,1024]{1,0:T(8,128)(2,1)S(1)} collective-permute-done((bf16[144,1024]{1,0:T(8,128)(2,1)}, bf16[144,1024]{1,0:T(8,128)(2,1)S(1)}, u32[]{:S(2)}, u32[]{:S(2)}) %collective-permute-start.15) | collective-permute-done | bytes 294944 | tf_op jit(solution)/shard_map/ppermute | solution.py:408
  56.9 1.8 %copy-done.1 = bf16[1024,1408]{1,0:T(8,128)(2,1)S(1)} copy-done((bf16[1024,1408]{1,0:T(8,128)(2,1)S(1)}, bf16[1024,1408]{1,0:T(8,128)(2,1)}, u32[]{:S(2)}) %copy-start.1) | copy-done | bytes 2883608
  58.7 1.8 %copy-done.3 = bf16[1408,1024]{1,0:T(8,128)(2,1)S(1)} copy-done((bf16[1408,1024]{1,0:T(8,128)(2,1)S(1)}, bf16[1408,1024]{1,0:T(8,128)(2,1)}, u32[]{:S(2)}) %copy-start.3) | copy-done | bytes 2883608
  61.6 5.1 %experts_384.2 = (bf16[192,1024]{1,0:T(8,128)(2,1)S(1)}, bf16[192,1024]{1,0:T(8,128)(2,1)S(1)}) custom-call(s32[3]{0:T(128)S(1)} %pad_add_fusion.me, bf16[144,1024]{1,0:T(8,128)(2,1)} %get-tuple-element.36.refs_0_, bf16[144,1024]{1,0:T(8,128)(2,1)} %collective-permute-done.1.refs_1_.refs_0_, bf16[144,1024]{1,0:T(8,128)(2,1)} %collective-permute-done.2.refs_2_.refs_1_, ...), custom_call_target="tpu_custom_call" | custom-call | flops 3321888768 | bytes 11730956 | tf_op jit(solution)/shard_map/experts_384/pallas_call | solution.py:274
  67.4 4.9 %experts_384.3 = (bf16[192,1024]{1,0:T(8,128)(2,1)S(1)}, bf16[192,1024]{1,0:T(8,128)(2,1)S(1)}) custom-call(s32[3]{0:T(128)S(1)} %pad_add_fusion.me, bf16[144,1024]{1,0:T(8,128)(2,1)} %get-tuple-element.49.refs_0_.refs_6_, bf16[144,1024]{1,0:T(8,128)(2,1)S(1)} %collective-permute-done.14.refs_1_.refs_0_, ...), custom_call_target="tpu_custom_call" | custom-call | flops 3321888768 | bytes 11730956 | tf_op jit(solution)/shard_map/experts_384/pallas_call | solution.py:274
  72.8 2.2 %experts_128.2 = (bf16[64,1024]{1,0:T(8,128)(2,1)S(1)}, bf16[64,1024]{1,0:T(8,128)(2,1)S(1)}) custom-call(s32[3]{0:T(128)S(1)} %pad_add_fusion.me, bf16[144,1024]{1,0:T(8,128)(2,1)S(1)} %collective-permute-done.7.refs_0_, bf16[144,1024]{1,0:T(8,128)(2,1)S(1)} %collective-permute-done.8.refs_1_, bf16[1024,1408]{1,0:T(8,128)(2,1)S(1)} %get-tuple-element.38.refs_6_.refs_2_, ...), custom_call_target="tpu_custom_call" | custom-call | flops 1107296256 | bytes 10027020 | tf_op jit(solution)/shard_map/experts_128/pallas_call | solution.py:274
  75.3 2.2 %experts_128.3 = (bf16[64,1024]{1,0:T(8,128)(2,1)S(1)}, bf16[64,1024]{1,0:T(8,128)(2,1)S(1)}) custom-call(s32[3]{0:T(128)S(1)} %pad_add_fusion.me, bf16[144,1024]{1,0:T(8,128)(2,1)S(1)} %collective-permute-done.20.refs_0_, bf16[144,1024]{1,0:T(8,128)(2,1)S(1)} %collective-permute-done.21.refs_1_, bf16[1024,1408]{1,0:T(8,128)(2,1)S(1)} %get-tuple-element.38.refs_6_.refs_2_, ...), custom_call_target="tpu_custom_call" | custom-call | flops 1107296256 | bytes 10027020 | tf_op jit(solution)/shard_map/experts_128/pallas_call | solution.py:274
  82.2 3.2 %collective-permute-done.10.refs_4_ = bf16[128,1024]{1,0:T(8,128)(2,1)S(1)} collective-permute-done((bf16[128,1024]{1,0:T(8,128)(2,1)S(1)}, bf16[128,1024]{1,0:T(8,128)(2,1)S(1)}, u32[]{:S(2)}, u32[]{:S(2)}) %collective-permute-start.10) | collective-permute-done | bytes 262176 | tf_op jit(solution)/shard_map/ppermute | solution.py:412
  85.4 1.7 %combine_2.2 = (bf16[128,1024]{1,0:T(8,128)(2,1)S(1)}, bf16[128,1024]{1,0:T(8,128)(2,1)S(1)}) custom-call(s32[3]{0:T(128)S(1)} %pad_add_fusion.me, bf16[144,1024]{1,0:T(8,128)(2,1)} %collective-permute-done.1.refs_1_.refs_0_, bf16[144,1024]{1,0:T(8,128)(2,1)} %collective-permute-done.2.refs_2_.refs_1_, bf16[128,1024]{1,0:T(8,128)(2,1)S(1)} %slice.120.refs_2_, ...), custom_call_target="tpu_custom_call" | custom-call | flops 134217728 | bytes 1900556 | tf_op jit(solution)/shard_map/combine_2/pallas_call | solution.py:328
  87.7 1.6 %collective-permute-start.12 = (bf16[128,1024]{1,0:T(8,128)(2,1)S(1)}, bf16[128,1024]{1,0:T(8,128)(2,1)S(1)}, u32[]{:S(2)}, u32[]{:S(2)}) collective-permute-start(bf16[128,1024]{1,0:T(8,128)(2,1)S(1)} %get-tuple-element.47), channel_id=1, source_target_pairs={{0,16},{4,20},{8,24},{12,28},{16,0},{20,4},{24,8},{28,12},{1,17},{... | collective-permute-start | bytes 786440 | tf_op jit(solution)/shard_map/ppermute | solution.py:408
  92.5 3.9 %collective-permute-done.11.refs_4_ = bf16[128,1024]{1,0:T(8,128)(2,1)S(1)} collective-permute-done((bf16[128,1024]{1,0:T(8,128)(2,1)S(1)}, bf16[128,1024]{1,0:T(8,128)(2,1)S(1)}, u32[]{:S(2)}, u32[]{:S(2)}) %collective-permute-start.11) | collective-permute-done | bytes 262176 | tf_op jit(solution)/shard_map/ppermute | solution.py:408
  96.9 3.3 %collective-permute-done.24.refs_10_ = bf16[128,1024]{1,0:T(8,128)(2,1)S(1)} collective-permute-done((bf16[128,1024]{1,0:T(8,128)(2,1)S(1)}, bf16[128,1024]{1,0:T(8,128)(2,1)S(1)}, u32[]{:S(2)}, u32[]{:S(2)}) %collective-permute-start.24) | collective-permute-done | bytes 262176 | tf_op jit(solution)/shard_map/ppermute | solution.py:408
  100.5 2.6 %finish.1 = bf16[256,1024]{1,0:T(8,128)(2,1)} custom-call(s32[3]{0:T(128)S(1)} %pad_add_fusion.me, bf16[144,1024]{1,0:T(8,128)(2,1)} %get-tuple-element.36.refs_0_, bf16[128,1024]{1,0:T(8,128)(2,1)S(1)} %copy-done.22, bf16[192,1024]{1,0:T(8,128)(2,1)S(1)} %get-tuple-element.42.refs_2_, bf16[192,1024]{1,0:T(8,128)(2,1)S(1)} %collective-permute-done.6.refs_3_, ...), custom_call_target="tpu_custom_call" | custom-call | flops 134217728 | bytes 4259852 | tf_op jit(solution)/shard_map/finish/pallas_call | solution.py:354
  (119 shorter events, 35.3 us)
Async XLA Ops:
  2.2 22.3 %collective-permute-start = (bf16[256,1024]{1,0:T(8,128)(2,1)}, bf16[256,1024]{1,0:T(8,128)(2,1)}, u32[]{:S(2)}, u32[]{:S(2)}) collective-permute-start(bf16[256,1024]{1,0:T(8,128)(2,1)} %pad_maximum_fusion), channel_id=1, source_target_pairs={{0,4},{4,8},{8,12},{12,16},{16,20},{20,24},{24,28},{1,5},{5,9},{9,... | collective-permute-start | bytes 1572872 | tf_op jit(solution)/shard_map/ppermute | solution.py:463
  22.8 15.1 %collective-permute-start.13 = (bf16[256,1024]{1,0:T(8,128)(2,1)}, bf16[256,1024]{1,0:T(8,128)(2,1)}, u32[]{:S(2)}, u32[]{:S(2)}) collective-permute-start(bf16[256,1024]{1,0:T(8,128)(2,1)} %pad_maximum_fusion.1), channel_id=1, source_target_pairs={{4,0},{8,4},{12,8},{16,12},{20,16},{24,20},{28,24},{5,1},{9,5},{13... | collective-permute-start | bytes 1572872 | tf_op jit(solution)/shard_map/ppermute | solution.py:483
  32.3 14.9 %collective-permute-start.2 = (bf16[144,1024]{1,0:T(8,128)(2,1)}, bf16[144,1024]{1,0:T(8,128)(2,1)}, u32[]{:S(2)}, u32[]{:S(2)}) collective-permute-start(bf16[144,1024]{1,0:T(8,128)(2,1)} %get-tuple-element.36.refs_0_), channel_id=1, source_target_pairs={{0,16},{4,20},{8,24},{12,28},{16,0},{20,4},{24,8},{28,12},{1,17},{... | collective-permute-start | bytes 884744 | tf_op jit(solution)/shard_map/ppermute | solution.py:408
  37.2 10.4 %collective-permute-start.1 = (bf16[144,1024]{1,0:T(8,128)(2,1)}, bf16[144,1024]{1,0:T(8,128)(2,1)}, u32[]{:S(2)}, u32[]{:S(2)}) collective-permute-start(bf16[144,1024]{1,0:T(8,128)(2,1)} %get-tuple-element.36.refs_0_), channel_id=1, source_target_pairs={{0,8},{4,12},{8,0},{12,4},{16,24},{20,28},{24,16},{28,20},{1,9},{5... | collective-permute-start | bytes 884744 | tf_op jit(solution)/shard_map/ppermute | solution.py:408
  45.6 7.9 %collective-permute-start.15 = (bf16[144,1024]{1,0:T(8,128)(2,1)}, bf16[144,1024]{1,0:T(8,128)(2,1)S(1)}, u32[]{:S(2)}, u32[]{:S(2)}) collective-permute-start(bf16[144,1024]{1,0:T(8,128)(2,1)} %get-tuple-element.49.refs_0_.refs_6_), channel_id=1, source_target_pairs={{0,16},{4,20},{8,24},{12,28},{16,0},{20,4},{24,8},{28,12},{1,17},{... | collective-permute-start | bytes 884744 | tf_op jit(solution)/shard_map/ppermute | solution.py:408
  46.1 8.2 %collective-permute-start.14 = (bf16[144,1024]{1,0:T(8,128)(2,1)}, bf16[144,1024]{1,0:T(8,128)(2,1)S(1)}, u32[]{:S(2)}, u32[]{:S(2)}) collective-permute-start(bf16[144,1024]{1,0:T(8,128)(2,1)} %get-tuple-element.49.refs_0_.refs_6_), channel_id=1, source_target_pairs={{0,8},{4,12},{8,0},{12,4},{16,24},{20,28},{24,16},{28,20},{1,9},{5... | collective-permute-start | bytes 884744 | tf_op jit(solution)/shard_map/ppermute | solution.py:408
  47.1 8.2 %collective-permute-start.3 = (bf16[144,1024]{1,0:T(8,128)(2,1)}, bf16[144,1024]{1,0:T(8,128)(2,1)S(1)}, u32[]{:S(2)}, u32[]{:S(2)}) collective-permute-start(bf16[144,1024]{1,0:T(8,128)(2,1)} %get-tuple-element.36.refs_0_), channel_id=1, source_target_pairs={{0,4},{4,0},{8,12},{12,8},{16,20},{20,16},{24,28},{28,24},{1,5},{5... | collective-permute-start | bytes 884744 | tf_op jit(solution)/shard_map/ppermute | solution.py:408
  47.1 9.3 %collective-permute-start.5 = (bf16[144,1024]{1,0:T(8,128)(2,1)}, bf16[144,1024]{1,0:T(8,128)(2,1)S(1)}, u32[]{:S(2)}, u32[]{:S(2)}) collective-permute-start(bf16[144,1024]{1,0:T(8,128)(2,1)} %collective-permute-done.2.refs_2_.refs_1_), channel_id=1, source_target_pairs={{0,4},{4,0},{8,12},{12,8},{16,20},{20,16},{24,28},{28,24},{1,5},{5... | collective-permute-start | bytes 884744 | tf_op jit(solution)/shard_map/ppermute | solution.py:408
  47.6 8.8 %collective-permute-start.4 = (bf16[144,1024]{1,0:T(8,128)(2,1)}, bf16[144,1024]{1,0:T(8,128)(2,1)S(1)}, u32[]{:S(2)}, u32[]{:S(2)}) collective-permute-start(bf16[144,1024]{1,0:T(8,128)(2,1)} %collective-permute-done.1.refs_1_.refs_0_), channel_id=1, source_target_pairs={{0,4},{4,0},{8,12},{12,8},{16,20},{20,16},{24,28},{28,24},{1,5},{5... | collective-permute-start | bytes 884744 | tf_op jit(solution)/shard_map/ppermute | solution.py:408
  53.5 13.2 %collective-permute-start.16 = (bf16[144,1024]{1,0:T(8,128)(2,1)}, bf16[144,1024]{1,0:T(8,128)(2,1)S(1)}, u32[]{:S(2)}, u32[]{:S(2)}) collective-permute-start(bf16[144,1024]{1,0:T(8,128)(2,1)} %get-tuple-element.49.refs_0_.refs_6_), channel_id=1, source_target_pairs={{0,4},{4,0},{8,12},{12,8},{16,20},{20,16},{24,28},{28,24},{1,5},{5... | collective-permute-start | bytes 884744 | tf_op jit(solution)/shard_map/ppermute | solution.py:408
  54.3 12.6 %collective-permute-start.7 = (bf16[144,1024]{1,0:T(8,128)(2,1)S(1)}, bf16[144,1024]{1,0:T(8,128)(2,1)S(1)}, u32[]{:S(2)}, u32[]{:S(2)}) collective-permute-start(bf16[144,1024]{1,0:T(8,128)(2,1)S(1)} %broadcast_select_fusion.1), channel_id=1, source_target_pairs={{0,16},{4,12},{8,24},{12,4},{16,0},{20,28},{24,8},{28,20},{1,17},{... | collective-permute-start | bytes 884744 | tf_op jit(solution)/shard_map/ppermute | solution.py:412
  55.3 12.0 %collective-permute-start.20 = (bf16[144,1024]{1,0:T(8,128)(2,1)S(1)}, bf16[144,1024]{1,0:T(8,128)(2,1)S(1)}, u32[]{:S(2)}, u32[]{:S(2)}) collective-permute-start(bf16[144,1024]{1,0:T(8,128)(2,1)S(1)} %broadcast_select_fusion), channel_id=1, source_target_pairs={{0,16},{4,12},{8,24},{12,4},{16,0},{20,28},{24,8},{28,20},{1,17},{... | collective-permute-start | bytes 884744 | tf_op jit(solution)/shard_map/ppermute | solution.py:412
  56.4 11.0 %collective-permute-start.18 = (bf16[144,1024]{1,0:T(8,128)(2,1)S(1)}, bf16[144,1024]{1,0:T(8,128)(2,1)S(1)}, u32[]{:S(2)}, u32[]{:S(2)}) collective-permute-start(bf16[144,1024]{1,0:T(8,128)(2,1)S(1)} %collective-permute-done.15.refs_2_.refs_1_), channel_id=1, source_target_pairs={{0,4},{4,0},{8,12},{12,8},{16,20},{20,16},{24,28},{28,24},{1,5},{5... | collective-permute-start | bytes 884744 | tf_op jit(solution)/shard_map/ppermute | solution.py:408
  56.4 11.0 %collective-permute-start.17 = (bf16[144,1024]{1,0:T(8,128)(2,1)S(1)}, bf16[144,1024]{1,0:T(8,128)(2,1)S(1)}, u32[]{:S(2)}, u32[]{:S(2)}) collective-permute-start(bf16[144,1024]{1,0:T(8,128)(2,1)S(1)} %collective-permute-done.14.refs_1_.refs_0_), channel_id=1, source_target_pairs={{0,4},{4,0},{8,12},{12,8},{16,20},{20,16},{24,28},{28,24},{1,5},{5... | collective-permute-start | bytes 884744 | tf_op jit(solution)/shard_map/ppermute | solution.py:408
  66.7 15.4 %collective-permute-start.6 = (bf16[192,1024]{1,0:T(8,128)(2,1)S(1)}, bf16[192,1024]{1,0:T(8,128)(2,1)S(1)}, u32[]{:S(2)}, u32[]{:S(2)}) collective-permute-start(bf16[192,1024]{1,0:T(8,128)(2,1)S(1)} %get-tuple-element.43), channel_id=1, source_target_pairs={{0,4},{4,0},{8,12},{12,8},{16,20},{20,16},{24,28},{28,24},{1,5},{5... | collective-permute-start | bytes 1179656 | tf_op jit(solution)/shard_map/ppermute | solution.py:408
  66.8 6.0 %collective-permute-start.8 = (bf16[144,1024]{1,0:T(8,128)(2,1)S(1)}, bf16[144,1024]{1,0:T(8,128)(2,1)S(1)}, u32[]{:S(2)}, u32[]{:S(2)}) collective-permute-start(bf16[144,1024]{1,0:T(8,128)(2,1)S(1)} %collective-permute-done.7.refs_0_), channel_id=1, source_target_pairs={{0,4},{4,0},{8,12},{12,8},{16,20},{20,16},{24,28},{28,24},{1,5},{5... | collective-permute-start | bytes 884744 | tf_op jit(solution)/shard_map/ppermute | solution.py:408
  67.3 8.0 %collective-permute-start.21 = (bf16[144,1024]{1,0:T(8,128)(2,1)S(1)}, bf16[144,1024]{1,0:T(8,128)(2,1)S(1)}, u32[]{:S(2)}, u32[]{:S(2)}) collective-permute-start(bf16[144,1024]{1,0:T(8,128)(2,1)S(1)} %collective-permute-done.20.refs_0_), channel_id=1, source_target_pairs={{0,4},{4,0},{8,12},{12,8},{16,20},{20,16},{24,28},{28,24},{1,5},{5... | collective-permute-start | bytes 884744 | tf_op jit(solution)/shard_map/ppermute | solution.py:408
  72.3 9.8 %collective-permute-start.19 = (bf16[192,1024]{1,0:T(8,128)(2,1)S(1)}, bf16[192,1024]{1,0:T(8,128)(2,1)S(1)}, u32[]{:S(2)}, u32[]{:S(2)}) collective-permute-start(bf16[192,1024]{1,0:T(8,128)(2,1)S(1)} %get-tuple-element.52), channel_id=1, source_target_pairs={{0,4},{4,0},{8,12},{12,8},{16,20},{20,16},{24,28},{28,24},{1,5},{5... | collective-permute-start | bytes 1179656 | tf_op jit(solution)/shard_map/ppermute | solution.py:408
  78.9 6.4 %collective-permute-start.10 = (bf16[128,1024]{1,0:T(8,128)(2,1)S(1)}, bf16[128,1024]{1,0:T(8,128)(2,1)S(1)}, u32[]{:S(2)}, u32[]{:S(2)}) collective-permute-start(bf16[128,1024]{1,0:T(8,128)(2,1)S(1)} %combine_1.2), channel_id=1, source_target_pairs={{0,16},{4,12},{8,24},{12,4},{16,0},{20,28},{24,8},{28,20},{1,17},{... | collective-permute-start | bytes 786440 | tf_op jit(solution)/shard_map/ppermute | solution.py:412
  81.0 8.3 %collective-permute-start.23 = (bf16[128,1024]{1,0:T(8,128)(2,1)S(1)}, bf16[128,1024]{1,0:T(8,128)(2,1)S(1)}, u32[]{:S(2)}, u32[]{:S(2)}) collective-permute-start(bf16[128,1024]{1,0:T(8,128)(2,1)S(1)} %combine_1.3), channel_id=1, source_target_pairs={{0,16},{4,12},{8,24},{12,4},{16,0},{20,28},{24,8},{28,20},{1,17},{... | collective-permute-start | bytes 786440 | tf_op jit(solution)/shard_map/ppermute | solution.py:412
  87.1 9.3 %collective-permute-start.11 = (bf16[128,1024]{1,0:T(8,128)(2,1)S(1)}, bf16[128,1024]{1,0:T(8,128)(2,1)S(1)}, u32[]{:S(2)}, u32[]{:S(2)}) collective-permute-start(bf16[128,1024]{1,0:T(8,128)(2,1)S(1)} %get-tuple-element.46), channel_id=1, source_target_pairs={{0,8},{4,12},{8,0},{12,4},{16,24},{20,28},{24,16},{28,20},{1,9},{5... | collective-permute-start | bytes 786440 | tf_op jit(solution)/shard_map/ppermute | solution.py:408
  87.7 9.2 %collective-permute-start.12 = (bf16[128,1024]{1,0:T(8,128)(2,1)S(1)}, bf16[128,1024]{1,0:T(8,128)(2,1)S(1)}, u32[]{:S(2)}, u32[]{:S(2)}) collective-permute-start(bf16[128,1024]{1,0:T(8,128)(2,1)S(1)} %get-tuple-element.47), channel_id=1, source_target_pairs={{0,16},{4,20},{8,24},{12,28},{16,0},{20,4},{24,8},{28,12},{1,17},{... | collective-permute-start | bytes 786440 | tf_op jit(solution)/shard_map/ppermute | solution.py:408
  90.5 9.7 %collective-permute-start.24 = (bf16[128,1024]{1,0:T(8,128)(2,1)S(1)}, bf16[128,1024]{1,0:T(8,128)(2,1)S(1)}, u32[]{:S(2)}, u32[]{:S(2)}) collective-permute-start(bf16[128,1024]{1,0:T(8,128)(2,1)S(1)} %get-tuple-element.55), channel_id=1, source_target_pairs={{0,8},{4,12},{8,0},{12,4},{16,24},{20,28},{24,16},{28,20},{1,9},{5... | collective-permute-start | bytes 786440 | tf_op jit(solution)/shard_map/ppermute | solution.py:408
  91.5 9.0 %collective-permute-start.25 = (bf16[128,1024]{1,0:T(8,128)(2,1)S(1)}, bf16[128,1024]{1,0:T(8,128)(2,1)S(1)}, u32[]{:S(2)}, u32[]{:S(2)}) collective-permute-start(bf16[128,1024]{1,0:T(8,128)(2,1)S(1)} %get-tuple-element.56), channel_id=1, source_target_pairs={{0,16},{4,20},{8,24},{12,28},{16,0},{20,4},{24,8},{28,12},{1,17},{... | collective-permute-start | bytes 786440 | tf_op jit(solution)/shard_map/ppermute | solution.py:408
  (30 other events, 129.3 us)

commit v3 on v2

v3 whole, which is shorter than its diff:
```python
import functools

import jax
import jax.numpy as jnp
from jax import lax
from jax.experimental import pallas as pl
from jax.experimental.pallas import tpu as pltpu
from jax.sharding import PartitionSpec as P

HEADS = 16
HD = 64
IL_DEV = 4
XL = 8
DP = 8
R_IL = 2
R_XL = 2
R_DP = 2
PLANE = XL * DP
META = 16
MIB = 1024 * 1024
LONG = 30
F32 = jnp.float32
BF16 = jnp.bfloat16
VMEM = pl.BlockSpec(memory_space=pltpu.VMEM)
SMEM = pl.BlockSpec(memory_space=pltpu.SMEM)
ANY = pl.BlockSpec(memory_space=pl.ANY)


def far(array):
    return pltpu.with_memory_space_constraint(array, pltpu.HBM)


def cost(flops, transcendentals, args, outs):
    moved = sum(a.size * a.dtype.itemsize for a in args)
    moved += sum(o.size * o.dtype.itemsize for o in outs)
    return pl.CostEstimate(flops=flops, transcendentals=transcendentals, bytes_accessed=moved)


NT = (((1,), (1,)), ((), ()))
TN = (((0,), (0,)), ((), ()))


def window_bias(keys, first_key, queries, first_query, live):
    k = lax.broadcasted_iota(jnp.int32, (keys, queries), 0) + (first_key + PLANE * R_IL)
    q = lax.broadcasted_iota(jnp.int32, (keys, queries), 1) + first_query
    near = jnp.abs(q // PLANE + R_IL - k // PLANE) <= R_IL
    near = near & (jnp.abs(q // DP % XL - k // DP % XL) <= R_XL)
    near = near & (jnp.abs(q % DP - k % DP) <= R_DP)
    if live is not None:
        near = near & (live > 0)
    bias = jnp.where(near, F32(0.0), F32(-1e30))
    return jnp.concatenate([bias, bias], axis=1)


def two_heads(query):
    lane = lax.broadcasted_iota(jnp.int32, query.shape, 1)
    query = query * BF16(1.0 / HD**0.5)
    zero = BF16(0.0)
    return jnp.concatenate(
        [jnp.where(lane < HD, query, zero), jnp.where(lane >= HD, query, zero)], axis=0
    )


def pack_kernel(width, k, v, last, first, sems):
    end = k.shape[0] - width
    copies = [
        (k.at[pl.ds(end, width)], last.at[pl.ds(0, width)]),
        (v.at[pl.ds(end, width)], last.at[pl.ds(width, width)]),
        (k.at[pl.ds(0, width)], first.at[pl.ds(0, width)]),
        (v.at[pl.ds(0, width)], first.at[pl.ds(width, width)]),
    ]
    copies = [pltpu.make_async_copy(a, b, sems.at[i]) for i, (a, b) in enumerate(copies)]
    for copy in copies:
        copy.start()
    for copy in copies:
        copy.wait()


def pack(k, v, width):
    flat = [jax.ShapeDtypeStruct((2 * width, k.shape[1]), k.dtype)] * 2
    return pl.pallas_call(
        functools.partial(pack_kernel, width),
        in_specs=[ANY] * 2,
        out_specs=[VMEM] * 2,
        out_shape=flat,
        scratch_shapes=[pltpu.SemaphoreType.DMA((4,))],
        compiler_params=pltpu.CompilerParams(vmem_limit_bytes=12 * MIB),
        cost_estimate=cost(0, 0, flat, flat),
        name="pack",
    )(*[far(a) for a in (k, v)])


def interior_kernel(q, k, v, acc, tops, sums, bias):
    rows = q.shape[0]
    bias[...] = window_bias(rows, 0, rows, 0, None)
    for pair in range(HEADS // 2):
        cols = slice(pair * 2 * HD, (pair + 1) * 2 * HD)
        s = lax.dot_general(k[:, cols], two_heads(q[:, cols]), NT, preferred_element_type=F32)
        s = s + bias[...]
        top = jnp.max(s, axis=0, keepdims=True)
        p = jnp.exp(s - top)
        total = jnp.sum(p, axis=0, keepdims=True)
        o = lax.dot_general(v[:, cols], p.astype(BF16), TN, preferred_element_type=F32)
        base = pair * 2 * HD
        acc[base : base + HD, :] = o[:HD, :rows]
        acc[base + HD : base + 2 * HD, :] = o[HD:, rows:]
        for side in range(2):
            span = slice(side * rows, (side + 1) * rows)
            tops[2 * pair + side : 2 * pair + side + 1, :] = top[:, span]
            sums[2 * pair + side : 2 * pair + side + 1, :] = total[:, span]


def interior(q, k, v):
    rows, model = q.shape
    flat = [jax.ShapeDtypeStruct(shape, F32) for shape in ((model, rows), (HEADS, rows), (HEADS, rows))]
    args = [far(a) for a in (q, k, v)]
    return pl.pallas_call(
        interior_kernel,
        in_specs=[VMEM] * 3,
        out_specs=[VMEM] * 3,
        out_shape=[pltpu.HBM(o.shape, o.dtype) for o in flat],
        scratch_shapes=[pltpu.VMEM((rows, 2 * rows), F32)],
        compiler_params=pltpu.CompilerParams(vmem_limit_bytes=12 * MIB),
        cost_estimate=cost(LONG * 4 * rows * rows * model, HEADS * rows * rows, args, flat),
        name="interior",
    )(*args)


def edge_kernel(live, q, before, behind, tops, sums, gain, acc_far, x_far, w_far, *rest):
    meta = rest[0] if len(rest) == 9 else None
    resid, payload = rest[-8:-6]
    bias, att, acc, x, w, sems = rest[-6:]
    step = 2 * HD
    pairs = HEADS // 2
    fetches = []
    for pair in range(pairs):
        span = pl.ds(pair * step, step)
        fetches.append((acc_far.at[span], acc.at[span]))
    fetches += [(x_far, x), (w_far, w)]
    fetches = [pltpu.make_async_copy(a, b, sems.at[i]) for i, (a, b) in enumerate(fetches)]
    for fetch in fetches:
        fetch.start()
    rows = q.shape[0] // 2
    wide = before.shape[0] // 2
    halos = (before, behind)
    for half in range(2):
        first = -wide if half == 0 else 2 * rows
        bias[half] = window_bias(wide, first, rows, half * rows, live[half])
    for pair in range(pairs):
        cols = slice(pair * step, (pair + 1) * step)
        fetches[pair].wait()
        for half, halo in enumerate(halos):
            span = slice(half * rows, (half + 1) * rows)
            queries = two_heads(q[span, cols])
            s = lax.dot_general(halo[:wide, cols], queries, NT, preferred_element_type=F32)
            s = s + bias[half]
            both = [slice(2 * pair + side, 2 * pair + side + 1) for side in range(2)]
            old = jnp.concatenate([tops[b, span] for b in both], axis=1)
            top = jnp.maximum(old, jnp.max(s, axis=0, keepdims=True))
            shrink = jnp.exp(old - top)
            p = jnp.exp(s - top)
            total = jnp.concatenate([sums[b, span] for b in both], axis=1) * shrink
            total = total + jnp.sum(p, axis=0, keepdims=True)
            o = lax.dot_general(halo[wide:, cols], p.astype(BF16), TN, preferred_element_type=F32)
            inverse = 1.0 / total
            for side in range(2):
                at = slice(side * rows, (side + 1) * rows)
                base = pair * step + side * HD
                value = acc[base : base + HD, span] * shrink[:, at]
                value = value + o[side * HD : (side + 1) * HD, at]
                att[base : base + HD, span] = (value * inverse[:, at]).astype(BF16)
    fetches[pairs].wait()
    fetches[pairs + 1].wait()
    for half in range(2):
        span = slice(half * rows, (half + 1) * rows)
        res = x[span, :].astype(F32)
        res = res + lax.dot_general(att[:, span], w[...], TN, preferred_element_type=F32)
        res = res.astype(BF16)
        resid[span, :] = res
        res = res.astype(F32)
        square = jnp.mean(res * res, axis=1, keepdims=True)
        normed = (res * lax.rsqrt(square + 1e-06) * gain[...]).astype(BF16)
        start = half * payload.shape[0] // 2
        payload[start : start + rows, :] = normed
        if meta is not None:
            payload[start + rows : start + rows + META, :] = jnp.broadcast_to(
                meta[half : half + 1, :], (META, meta.shape[1])
            )


def edge(live, q, before, behind, acc, tops, sums, x, w, gain, meta):
    rows, model = q.shape[0] // 2, q.shape[1]
    wide = before.shape[0] // 2
    before, behind, acc, tops, sums = [far(a) for a in (before, behind, acc, tops, sums)]
    args = [live, q, before, behind, tops, sums, gain, acc, x, w]
    args += [] if meta is None else [meta]
    specs = [SMEM] + [VMEM] * 6 + [ANY] * 3 + ([] if meta is None else [VMEM])
    extra = 0 if meta is None else META
    flat = [
        jax.ShapeDtypeStruct((2 * rows, model), BF16),
        jax.ShapeDtypeStruct((2 * (rows + extra), model), BF16),
    ]
    return pl.pallas_call(
        edge_kernel,
        in_specs=specs,
        out_specs=[VMEM] * 2,
        out_shape=[pltpu.HBM(o.shape, o.dtype) for o in flat],
        scratch_shapes=[
            pltpu.VMEM((2, wide, 2 * rows), F32),
            pltpu.VMEM((model, 2 * rows), BF16),
            pltpu.VMEM(acc.shape, acc.dtype),
            pltpu.VMEM(x.shape, x.dtype),
            pltpu.VMEM(w.shape, w.dtype),
            pltpu.SemaphoreType.DMA((HEADS // 2 + 2,)),
        ],
        compiler_params=pltpu.CompilerParams(vmem_limit_bytes=12 * MIB),
        cost_estimate=cost(
            LONG * (8 * rows * wide * model + 4 * rows * model * model), 2 * HEADS * rows * wide, args, flat
        ),
        name="edge",
    )(*args)


def meta_items(payload, block, rows):
    base = block * (rows + META) + rows
    meta = payload[base : base + META, :].astype(F32)
    return [meta[:, i * rows : (i + 1) * rows] for i in range(8)]


def slot_rows(hits):
    rows = hits.shape[1]
    upper = lax.broadcasted_iota(jnp.int32, (rows, rows), 0) < lax.broadcasted_iota(
        jnp.int32, (rows, rows), 1
    )
    upper = jnp.where(upper, F32(1.0), F32(0.0)).astype(BF16)
    rank = jnp.dot(hits.astype(BF16), upper, preferred_element_type=F32)
    return jnp.where(hits > 0, rank, F32(-1.0))


def pick_matrices(payload, block, rows, capacity, wanted):
    item = meta_items(payload, block, rows)
    named = [(item[0] == e, item[1] == e) for e in wanted]
    ranks = slot_rows(
        jnp.concatenate([jnp.where(a | b, F32(1.0), F32(0.0)) for a, b in named], axis=0)
    )
    slot = lax.broadcasted_iota(jnp.int32, (capacity, rows), 0).astype(F32)
    result = []
    for i, (a, b) in enumerate(named):
        gate = jnp.where(a, item[2] + item[3] + item[4], F32(0.0))
        gate = gate + jnp.where(b, item[5] + item[6] + item[7], F32(0.0))
        result.append((slot == ranks[i * META : i * META + 1, :], gate[:1, :]))
    return result


def experts_kernel(order, rows, capacity, me, *refs):
    payloads = refs[:-8]
    w_gate, w_up, w_down, out_mine, out_sib, x, hidden, tail = refs[-8:]
    width, model, step = w_gate.shape[1], w_down.shape[1], 256
    expert = me[0].astype(F32)
    groups = len(order) // 2
    hits = []
    for array, block in order:
        item = meta_items(payloads[array], block, rows)
        hits.append(jnp.where((item[0] == expert) | (item[1] == expert), F32(1.0), F32(0.0)))
    ranks = slot_rows(jnp.concatenate(hits, axis=0))
    slot = lax.broadcasted_iota(jnp.int32, (2 * capacity, rows), 0).astype(F32)
    for g in range(groups):
        first = ranks[2 * g * META : 2 * g * META + 1, :]
        second = ranks[(2 * g + 1) * META : (2 * g + 1) * META + 1, :]
        second = jnp.where(second >= 0, second + capacity, F32(-1.0))
        hot = jnp.concatenate([slot == first, slot == second], axis=1)
        hot = jnp.where(hot, F32(1.0), F32(0.0)).astype(BF16)
        tokens = []
        for array, block in order[2 * g : 2 * g + 2]:
            base = block * (rows + META)
            tokens.append(payloads[array][base : base + rows, :])
        picked = jnp.dot(hot, jnp.concatenate(tokens, axis=0), preferred_element_type=F32)
        x[2 * g * capacity : (2 * g + 2) * capacity, :] = picked.astype(BF16)
    for at in range(0, width, step):
        wide = min(step, width - at)
        cols = slice(at, at + wide)
        if wide < step:
            tail[:, :wide] = w_gate[:, cols]
            tail[:, wide : 2 * wide] = w_up[:, cols]
            both = jnp.dot(x[...], tail[...], preferred_element_type=F32)
            g, u = both[:, :wide], both[:, wide:]
        else:
            g = jnp.dot(x[...], w_gate[:, cols], preferred_element_type=F32)
            u = jnp.dot(x[...], w_up[:, cols], preferred_element_type=F32)
        hidden[:, cols] = (g / (1.0 + jnp.exp(-g)) * u).astype(BF16)
    for at in range(0, model, step):
        cols = slice(at, at + step)
        o = jnp.dot(hidden[...], w_down[:, cols], preferred_element_type=F32).astype(BF16)
        for g in range(groups):
            span = slice(g * capacity, (g + 1) * capacity)
            out_mine[span, cols] = o[2 * g * capacity : (2 * g + 1) * capacity]
            out_sib[span, cols] = o[(2 * g + 1) * capacity : (2 * g + 2) * capacity]


def experts(me, payloads, order, weights, rows, capacity):
    model, width = weights[0].shape
    slots = len(order) * capacity
    left = width % 256
    outs = [jax.ShapeDtypeStruct((slots // 2, model), BF16)] * 2
    args = [me, *payloads, *weights]
    return pl.pallas_call(
        functools.partial(experts_kernel, order, rows, capacity),
        in_specs=[SMEM] + [VMEM] * (len(args) - 1),
        out_specs=[VMEM] * 2,
        out_shape=outs,
        scratch_shapes=[
            pltpu.VMEM((slots, model), BF16),
            pltpu.VMEM((slots, width), BF16),
            pltpu.VMEM((model, max(2 * left, 256)), BF16),
        ],
        compiler_params=pltpu.CompilerParams(vmem_limit_bytes=12 * MIB),
        cost_estimate=cost(6 * slots * model * width, slots * width, args, outs),
        name=f"experts_{slots}",
    )(*args)


def spread(payload, block, rows, capacity, experts_two, outs_two):
    weights, values = [], []
    picks = pick_matrices(payload, block, rows, capacity, experts_two)
    for (hot, gate), out in zip(picks, outs_two):
        full = jnp.where(hot, gate, F32(0.0))
        high = full.astype(BF16)
        weights += [high, (full - high.astype(F32)).astype(BF16)]
        values += [out, out]
    return lax.dot_general(
        jnp.concatenate(weights, axis=0),
        jnp.concatenate(values, axis=0),
        (((0,), (0,)), ((), ())),
        preferred_element_type=F32,
    )


def combine_kernel(rows, capacity, me, payload, outs_me, outs_sib, *refs):
    result = refs[-1]
    both = (me[0].astype(F32), me[1].astype(F32))
    for block in range(payload.shape[0] // (rows + META)):
        span = slice(block * capacity, (block + 1) * capacity)
        total = spread(payload, block, rows, capacity, both, (outs_me[span, :], outs_sib[span, :]))
        at = slice(block * rows, (block + 1) * rows)
        if len(refs) == 2:
            total = total + refs[0][at, :].astype(F32)
        result[at, :] = total.astype(BF16)


def combine(me, payload, outs_me, outs_sib, carry, rows, capacity):
    blocks, model = payload.shape[0] // (rows + META), payload.shape[1]
    args = [me, payload, outs_me, outs_sib] + ([] if carry is None else [carry])
    outs = [jax.ShapeDtypeStruct((blocks * rows, model), BF16)]
    return pl.pallas_call(
        functools.partial(combine_kernel, rows, capacity),
        in_specs=[SMEM] + [VMEM] * (len(args) - 1),
        out_specs=VMEM,
        out_shape=outs[0],
        compiler_params=pltpu.CompilerParams(vmem_limit_bytes=12 * MIB),
        cost_estimate=cost(8 * blocks * rows * capacity * model, 0, args, outs),
        name="combine",
    )(*args)


def base_kernel(rows, capacity, me, payload, resid, outs_me, outs_sib, result):
    both = (me[0].astype(F32), me[1].astype(F32))
    for block in range(payload.shape[0] // (rows + META)):
        span = slice(block * capacity, (block + 1) * capacity)
        total = spread(payload, block, rows, capacity, both, (outs_me[span, :], outs_sib[span, :]))
        at = slice(block * rows, (block + 1) * rows)
        result[at, :] = total + resid[at, :].astype(F32)


def base(me, payload, resid, outs_me, outs_sib, rows, capacity):
    args = [me, payload, resid, outs_me, outs_sib]
    out = jax.ShapeDtypeStruct(resid.shape, F32)
    return pl.pallas_call(
        functools.partial(base_kernel, rows, capacity),
        in_specs=[SMEM] + [VMEM] * 4,
        out_specs=VMEM,
        out_shape=out,
        compiler_params=pltpu.CompilerParams(vmem_limit_bytes=12 * MIB),
        cost_estimate=cost(8 * resid.size * capacity, 0, args, [out]),
        name="base",
    )(*args)


def finish_kernel(total, first, second, out):
    out[...] = (total[...] + first[...].astype(F32) + second[...].astype(F32)).astype(BF16)


def finish(total, first, second):
    args = [total, first, second]
    return pl.pallas_call(
        finish_kernel,
        in_specs=[VMEM] * 3,
        out_specs=VMEM,
        out_shape=jax.ShapeDtypeStruct(first.shape, first.dtype),
        compiler_params=pltpu.CompilerParams(vmem_limit_bytes=12 * MIB),
        cost_estimate=cost(3 * total.size, 0, args, args[1:2]),
        name="finish",
    )(*args)


def expert_rows(token_rows, gate_mat, up_mat, down_mat):
    gate_part = jnp.dot(token_rows, gate_mat, preferred_element_type=F32)
    up_part = jnp.dot(token_rows, up_mat, preferred_element_type=F32)
    hidden = (jax.nn.silu(gate_part) * up_part).astype(BF16)
    return jnp.dot(hidden, down_mat, preferred_element_type=F32).astype(BF16)


def slot_ranks(routes, experts_count, block_rows):
    row_count = routes.shape[0]
    expert_ids = jnp.arange(experts_count, dtype=jnp.int32)
    matches = routes[:, :, None] == expert_ids[None, None, :]
    hits = jnp.sum(matches.astype(jnp.int32), axis=1)
    hits = hits.reshape(row_count // block_rows, block_rows, experts_count)
    earlier = (jnp.cumsum(hits, axis=1) - hits).reshape(row_count, experts_count)
    return jnp.sum(jnp.where(matches, earlier[:, None, :], 0), axis=-1)


def routed_all_to_all(normed, resid, routes, route_gates, w_gate, w_up, w_down):
    tiles = lax.axis_size("tile")
    row_count, route_width = routes.shape
    block_rows, model = row_count // 2, normed.shape[1]
    capacity = row_count * route_width // tiles
    slot_rank = slot_ranks(routes, tiles, block_rows)
    pieces = []
    for index in range(2):
        rows = slice(index * block_rows, (index + 1) * block_rows)
        part_normed = normed[rows]
        positions = routes[rows] * capacity + slot_rank[rows]
        copies = jnp.broadcast_to(
            part_normed[:, None, :], (block_rows, route_width, model)
        ).reshape(-1, model)
        outgoing = jnp.zeros((tiles * capacity, model), BF16).at[positions.reshape(-1)].set(copies)
        outgoing = outgoing.reshape(tiles, capacity, model)
        received = lax.all_to_all(outgoing, "tile", split_axis=0, concat_axis=0, tiled=True)
        produced = expert_rows(received.reshape(-1, model), w_gate, w_up, w_down)
        produced = produced.reshape(received.shape)
        returned = lax.all_to_all(produced, "tile", split_axis=0, concat_axis=0, tiled=True)
        picked = returned.reshape(-1, model)[positions].astype(F32)
        combined = jnp.sum(route_gates[rows][:, :, None] * picked, axis=1)
        pieces.append((resid[rows].astype(F32) + combined).astype(BF16))
    return jnp.concatenate(pieces, axis=0)


def swap(array, bit):
    return lax.ppermute(array, "tile", [(i, i ^ bit) for i in range(8)])


def swap_by_core(array, bits):
    return lax.ppermute(array, "tile", [(i, i ^ bits[i % 2]) for i in range(8)])


def after(first, *later):
    return lax.optimization_barrier((first, *later))[1:]


def routed_gather(payload, resid, weights, rows, capacity):
    tile = lax.axis_index("tile")
    me = jnp.stack([tile, tile ^ 1]).astype(jnp.int32)
    sizes = dict(rows=rows, capacity=capacity)

    def evaluate(mine, theirs):
        order = [(0, 0), (1, 0), (0, 1), (1, 1)]
        kept, sent = experts(me, (mine, theirs), order, weights, **sizes)
        return kept, swap(sent, 1)

    sib = swap(payload, 1)
    first = swap_by_core(payload, (2, 4))
    out_own = evaluate(payload, sib)
    (first,) = after(out_own[0], first)
    diag = swap_by_core(first, (4, 2))
    out_first = evaluate(first, swap(first, 1))
    (diag,) = after(out_first[0], diag)
    second = swap_by_core(*after(diag, payload), (4, 2))
    out_diag = evaluate(diag, swap(diag, 1))
    sum_diag = combine(me, diag, *out_diag, None, **sizes)
    carry = swap_by_core(sum_diag, (4, 2))
    (second,) = after(sum_diag, second)
    out_second = evaluate(second, swap(second, 1))
    sum_second = combine(me, second, *out_second, None, **sizes)
    back_second = swap_by_core(sum_second, (4, 2))
    sum_first = combine(me, first, *out_first, *after(sum_second, carry), **sizes)
    back_first = swap_by_core(sum_first, (2, 4))
    total = base(me, payload, resid, *after(sum_first, *out_own), **sizes)
    return finish(total, back_first, back_second)


def local(
    inputs,
    queries,
    key_vectors,
    values,
    out_weight,
    norm_gain,
    routes,
    route_gates,
    w_gate,
    w_up,
    w_down,
):
    row_count = inputs.shape[0]
    tiles = lax.axis_size("tile")
    tile = lax.axis_index("tile")
    width = R_IL * PLANE
    rows = row_count // 2
    capacity = row_count * routes.shape[1] // tiles
    up = [(i, i + 1) for i in range(tiles - 1)]
    down = [(j, i) for i, j in up]
    last, first = pack(key_vectors, values, width)
    before = lax.ppermute(last, "tile", up)
    behind = lax.ppermute(first, "tile", down)
    live = jnp.stack([tile > 0, tile < tiles - 1]).astype(jnp.int32)
    fast = tiles == 8
    meta = None
    if fast:
        items = [routes[:, 0].astype(F32), routes[:, 1].astype(F32)]
        for k in range(2):
            gate = route_gates[:, k]
            high = lax.reduce_precision(gate, 8, 7)
            mid = lax.reduce_precision(gate - high, 8, 7)
            items += [high, mid, gate - high - mid]
        meta = jnp.stack(items).reshape(len(items), 2, rows).swapaxes(0, 1)
        meta = meta.reshape(2, len(items) * rows).astype(BF16)
    acc, tops, sums = interior(queries, key_vectors, values)
    resid, payload = edge(
        live, queries, before, behind, acc, tops, sums, inputs, out_weight,
        norm_gain[None, :], meta,
    )
    if fast:
        weights = (w_gate[0], w_up[0], w_down[0])
        return routed_gather(payload, resid, weights, rows, capacity)
    return routed_all_to_all(payload, resid, routes, route_gates, w_gate[0], w_up[0], w_down[0])


def solution(mesh):
    return jax.shard_map(
        local,
        mesh=mesh,
        in_specs=(
            P(("rep", "tile"), None),
            P(("rep", "tile"), None),
            P(("rep", "tile"), None),
            P(("rep", "tile"), None),
            P(),
            P(),
            P(("rep", "tile"), None),
            P(("rep", "tile"), None),
            P("tile", None, None),
            P("tile", None, None),
            P("tile", None, None),
        ),
        out_specs=P(("rep", "tile"), None),
        check_vma=False,
    )
```

time: 104 us -> 84.4 us (0.81)
  local copies, waits for them, and re-layouts: 28 us -> 6.45 us
  waiting for transfers between devices: 16.8 us -> 26.4 us
  starting transfers between devices: 23.2 us -> 15.3 us
  Pallas kernels: 32 us -> 34.7 us
  other arithmetic: 2.87 us -> 1 us
    unnamed x63 -> x28, local copies, waits for them, and re-layouts: 26.5 us -> 5.69 us
    ppermute x5 -> x7, waiting for transfers between devices: 3.22 us -> 16.4 us  [the longest x6 16.4 us: swap_by_core(): return lax.ppermute(array, 'tile', [(i, i ^ bits[i % 2]) for i in range(8)])]
    ppermute x20 -> x8, starting transfers between devices: 14.3 us -> 8.59 us  [swap(): return lax.ppermute(array, 'tile', [(i, i ^ bit) for i in range(8)])]
    ppermute x20 -> x8, waiting for transfers between devices: 13.6 us -> 9.97 us  [swap(): return lax.ppermute(array, 'tile', [(i, i ^ bit) for i in range(8)])]
    pallas_call x12, Pallas kernels: 32 us -> 34.7 us  [the longest x4 14.5 us: experts(): pl.pallas_call(functools.partial(experts_kernel, order, rows, capacity),...]
    concatenate x2 -> x0, other arithmetic: 1.66 us -> none  [the longest x1 0.84 us: local(): first = jnp.concatenate([key_vectors[:width], values[:width]], axis=0)]
    slice x5 -> x0, local copies, waits for them, and re-layouts: 1.48 us -> none  [the longest x1 1.41 us: local(): first = jnp.concatenate([key_vectors[:width], values[:width]], axis=0)]
    ppermute x5 -> x7, starting transfers between devices: 5.71 us -> 4.35 us  [the longest x6 3.06 us: swap_by_core(): return lax.ppermute(array, 'tile', [(i, i ^ bits[i % 2]) for i in range(8)])]
  transfers between devices with their start and end apart: 26 -> 16, of which waited for: 7 -> 11; matrix products, arithmetic and copies ran while one was open for 2% -> 2% of each run, Pallas kernels for 28% -> 28%
where the time goes in v3:
time: 84.4 us; the launch traced here: 84 us
  Pallas kernels  34.7 us (41%)
  waiting for transfers between devices  26.4 us (31%)
  starting transfers between devices  15.3 us (18%)
  local copies, waits for them, and re-layouts  6.45 us (8%)
  other arithmetic  1 us (1%)
    ppermute x6, waiting for transfers between devices, swap_by_core(): return lax.ppermute(array, 'tile', [(i, i ^ bits[i % 2]) for i in range(8)])  16.4 us
    pallas_call x4, Pallas kernels, experts(): pl.pallas_call(functools.partial(experts_kernel, order, rows, capacity),...  14.5 us
    ppermute x8, waiting for transfers between devices, swap(): return lax.ppermute(array, 'tile', [(i, i ^ bit) for i in range(8)])  9.97 us
    ppermute x8, starting transfers between devices, swap(): return lax.ppermute(array, 'tile', [(i, i ^ bit) for i in range(8)])  8.59 us
    pallas_call x1, Pallas kernels, edge(): pl.pallas_call(edge_kernel, in_specs=specs, out_specs=[VMEM] * 2, out_sha...  7.7 us
    unnamed x28, local copies, waits for them, and re-layouts  5.69 us
    pallas_call x1, Pallas kernels, interior(): pl.pallas_call(interior_kernel, in_specs=[VMEM] * 3, out_specs=[VMEM] * 3...  5.46 us
    pallas_call x3, Pallas kernels, combine(): pl.pallas_call(functools.partial(combine_kernel, rows, capacity), in_spec...  3.61 us
  transfers between devices with their start and end apart: 16, of which 11 were waited for; matrix products, arithmetic and copies ran while one was open for 2% of the time, Pallas kernels for 28%

profile of v3, /device:TPU:0, one launch (start us, length us, event | category | flops | bytes accessed | tf_op | source)
XLA Modules:
  0.0 84.0 jit_solution(14482068331993322313)
XLA Ops:
  0.0 1.2 %pack.1 = (bf16[256,1024]{1,0:T(8,128)(2,1)S(1)}, bf16[256,1024]{1,0:T(8,128)(2,1)S(1)}) custom-call(bf16[256,1024]{1,0:T(8,128)(2,1)} %k.3, bf16[256,1024]{1,0:T(8,128)(2,1)} %v.3), custom_call_target="tpu_custom_call" | custom-call | bytes 2097152 | tf_op jit(solution)/shard_map/pack/pallas_call | solution.py:81
  1.2 2.4 %collective-permute-start = (bf16[256,1024]{1,0:T(8,128)(2,1)S(1)}, bf16[256,1024]{1,0:T(8,128)(2,1)S(1)}, u32[]{:S(2)}, u32[]{:S(2)}) collective-permute-start(bf16[256,1024]{1,0:T(8,128)(2,1)S(1)} %get-tuple-element.27), channel_id=1, source_target_pairs={{0,4},{4,8},{8,12},{12,16},{16,20},{20,24},{24,28},{1,5},{5,9},{9,... | collective-permute-start | bytes 1572872 | tf_op jit(solution)/shard_map/ppermute | solution.py:513
  3.6 1.3 %collective-permute-start.1 = (bf16[256,1024]{1,0:T(8,128)(2,1)S(1)}, bf16[256,1024]{1,0:T(8,128)(2,1)S(1)}, u32[]{:S(2)}, u32[]{:S(2)}) collective-permute-start(bf16[256,1024]{1,0:T(8,128)(2,1)S(1)} %get-tuple-element.28), channel_id=1, source_target_pairs={{4,0},{8,4},{12,8},{16,12},{20,16},{24,20},{28,24},{5,1},{9,5},{13... | collective-permute-start | bytes 1572872 | tf_op jit(solution)/shard_map/ppermute | solution.py:514
  6.7 5.5 %interior.1 = (f32[1024,256]{1,0:T(8,128)}, f32[16,256]{1,0:T(8,128)}, f32[16,256]{1,0:T(8,128)}) custom-call(bf16[256,1024]{1,0:T(8,128)(2,1)} %q.3, bf16[256,1024]{1,0:T(8,128)(2,1)} %k.3, bf16[256,1024]{1,0:T(8,128)(2,1)} %v.3), custom_call_target="tpu_custom_call" | custom-call | flops 8053063680 | bytes 2654208 | tf_op jit(solution)/shard_map/interior/pallas_call | solution.py:117
  13.1 7.7 %edge.1 = (bf16[256,1024]{1,0:T(8,128)(2,1)}, bf16[288,1024]{1,0:T(8,128)(2,1)}) custom-call(s32[2]{0:T(128)S(1)} %add_convert_fusion.live, bf16[256,1024]{1,0:T(8,128)(2,1)S(1)} %copy-done.8, bf16[256,1024]{1,0:T(8,128)(2,1)} %copy-done.11, bf16[256,1024]{1,0:T(8,128)(2,1)} %copy-done.12, f32[16,256]{1,0:T(8,128)} %get-tuple-element.29.tops, ...), custom_call_target="tpu_custom_call" | custom-call | flops 20132659200 | bytes 6397960 | tf_op jit(solution)/shard_map/edge/pallas_call | solution.py:203
  20.8 7.4 %collective-permute-start.2 = (bf16[288,1024]{1,0:T(8,128)(2,1)}, bf16[288,1024]{1,0:T(8,128)(2,1)}, u32[]{:S(2)}, u32[]{:S(2)}) collective-permute-start(bf16[288,1024]{1,0:T(8,128)(2,1)} %get-tuple-element.41.refs_0_.payload), channel_id=1, source_target_pairs={{0,4},{4,0},{8,12},{12,8},{16,20},{20,16},{24,28},{28,24},{1,5},{5... | collective-permute-start | bytes 1769480 | tf_op jit(solution)/shard_map/ppermute | solution.py:449
  28.2 1.5 %collective-permute-start.3 = (bf16[288,1024]{1,0:T(8,128)(2,1)}, bf16[288,1024]{1,0:T(8,128)(2,1)S(1)}, u32[]{:S(2)}, u32[]{:S(2)}) collective-permute-start(bf16[288,1024]{1,0:T(8,128)(2,1)} %get-tuple-element.41.refs_0_.payload), channel_id=1, source_target_pairs={{0,8},{4,20},{8,0},{12,28},{16,24},{20,4},{24,16},{28,12},{1,9},{5... | collective-permute-start | bytes 1769480 | tf_op jit(solution)/shard_map/ppermute | solution.py:453
  30.2 1.8 %copy-done.1 = bf16[1,1024,1408]{2,1,0:T(8,128)(2,1)S(1)} copy-done((bf16[1,1024,1408]{2,1,0:T(8,128)(2,1)S(1)}, bf16[1,1024,1408]{2,1,0:T(8,128)(2,1)}, u32[]{:S(2)}) %copy-start.1) | copy-done | bytes 2883608
  32.0 1.8 %copy-done.3 = bf16[1,1408,1024]{2,1,0:T(8,128)(2,1)S(1)} copy-done((bf16[1,1408,1024]{2,1,0:T(8,128)(2,1)S(1)}, bf16[1,1408,1024]{2,1,0:T(8,128)(2,1)}, u32[]{:S(2)}) %copy-start.3) | copy-done | bytes 2883608
  34.9 4.0 %experts_256.4 = (bf16[128,1024]{1,0:T(8,128)(2,1)S(1)}, bf16[128,1024]{1,0:T(8,128)(2,1)S(1)}) custom-call(s32[2]{0:T(128)S(1)} %pad_add_fusion.me, bf16[288,1024]{1,0:T(8,128)(2,1)S(1)} %copy-done.4, bf16[288,1024]{1,0:T(8,128)(2,1)} %collective-permute-done.2.refs_1_, bf16[1024,1408]{1,0:T(8,128)(2,1)S(1)} %bitcast.17, bf16[1024,1408]{1,0:T(8,128)(2,1)S(1)} %bitcast.21, ...), custom_call_target="tpu_custom_call" | custom-call | flops 2214592512 | bytes 10354696 | tf_op jit(solution)/shard_map/experts_256/pallas_call | solution.py:306
  39.3 1.6 %collective-permute-done.4.refs_1_ = bf16[288,1024]{1,0:T(8,128)(2,1)S(1)} collective-permute-done((bf16[288,1024]{1,0:T(8,128)(2,1)S(1)}, bf16[288,1024]{1,0:T(8,128)(2,1)S(1)}, u32[]{:S(2)}, u32[]{:S(2)}) %collective-permute-start.4) | collective-permute-done | bytes 589856 | tf_op jit(solution)/shard_map/ppermute | solution.py:449
  40.9 3.4 %experts_256.5 = (bf16[128,1024]{1,0:T(8,128)(2,1)S(1)}, bf16[128,1024]{1,0:T(8,128)(2,1)S(1)}) custom-call(s32[2]{0:T(128)S(1)} %pad_add_fusion.me, bf16[288,1024]{1,0:T(8,128)(2,1)S(1)} %collective-permute-done.3.refs_0_.payload, bf16[288,1024]{1,0:T(8,128)(2,1)S(1)} %collective-permute-done.4.refs_1_, bf16[1024,1408]{1,0:T(8,128)(2,1)S(1)} %bitcast.18, ...), custom_call_target="tpu_custom_call" | custom-call | flops 2214592512 | bytes 10354696 | tf_op jit(solution)/shard_map/experts_256/pallas_call | solution.py:306
  44.4 4.8 %collective-permute-done.6.refs_0_.payload = bf16[288,1024]{1,0:T(8,128)(2,1)S(1)} collective-permute-done((bf16[288,1024]{1,0:T(8,128)(2,1)S(1)}, bf16[288,1024]{1,0:T(8,128)(2,1)S(1)}, u32[]{:S(2)}, u32[]{:S(2)}) %collective-permute-start.6) | collective-permute-done | bytes 589856 | tf_op jit(solution)/shard_map/ppermute | solution.py:453
  49.2 2.0 %collective-permute-done.7.refs_1_ = bf16[288,1024]{1,0:T(8,128)(2,1)S(1)} collective-permute-done((bf16[288,1024]{1,0:T(8,128)(2,1)S(1)}, bf16[288,1024]{1,0:T(8,128)(2,1)S(1)}, u32[]{:S(2)}, u32[]{:S(2)}) %collective-permute-start.7) | collective-permute-done | bytes 589856 | tf_op jit(solution)/shard_map/ppermute | solution.py:449
  51.2 3.4 %experts_256.6 = (bf16[128,1024]{1,0:T(8,128)(2,1)S(1)}, bf16[128,1024]{1,0:T(8,128)(2,1)S(1)}) custom-call(s32[2]{0:T(128)S(1)} %pad_add_fusion.me, bf16[288,1024]{1,0:T(8,128)(2,1)S(1)} %collective-permute-done.6.refs_0_.payload, bf16[288,1024]{1,0:T(8,128)(2,1)S(1)} %collective-permute-done.7.refs_1_, bf16[1024,1408]{1,0:T(8,128)(2,1)S(1)} %bitcast.19, ...), custom_call_target="tpu_custom_call" | custom-call | flops 2214592512 | bytes 10354696 | tf_op jit(solution)/shard_map/experts_256/pallas_call | solution.py:306
  54.8 1.4 %collective-permute-done.8.outs_sib = bf16[128,1024]{1,0:T(8,128)(2,1)S(1)} collective-permute-done((bf16[128,1024]{1,0:T(8,128)(2,1)S(1)}, bf16[128,1024]{1,0:T(8,128)(2,1)S(1)}, u32[]{:S(2)}, u32[]{:S(2)}) %collective-permute-start.8) | collective-permute-done | bytes 262176 | tf_op jit(solution)/shard_map/ppermute | solution.py:449
  57.4 1.6 %collective-permute-done.9.refs_0_.payload = bf16[288,1024]{1,0:T(8,128)(2,1)S(1)} collective-permute-done((bf16[288,1024]{1,0:T(8,128)(2,1)S(1)}, bf16[288,1024]{1,0:T(8,128)(2,1)S(1)}, u32[]{:S(2)}, u32[]{:S(2)}) %collective-permute-start.9) | collective-permute-done | bytes 589856 | tf_op jit(solution)/shard_map/ppermute | solution.py:453
  59.1 2.0 %collective-permute-done.10.refs_1_ = bf16[288,1024]{1,0:T(8,128)(2,1)S(1)} collective-permute-done((bf16[288,1024]{1,0:T(8,128)(2,1)S(1)}, bf16[288,1024]{1,0:T(8,128)(2,1)S(1)}, u32[]{:S(2)}, u32[]{:S(2)}) %collective-permute-start.10) | collective-permute-done | bytes 589856 | tf_op jit(solution)/shard_map/ppermute | solution.py:449
  61.1 3.7 %experts_256.7 = (bf16[128,1024]{1,0:T(8,128)(2,1)S(1)}, bf16[128,1024]{1,0:T(8,128)(2,1)S(1)}) custom-call(s32[2]{0:T(128)S(1)} %pad_add_fusion.me, bf16[288,1024]{1,0:T(8,128)(2,1)S(1)} %collective-permute-done.9.refs_0_.payload, bf16[288,1024]{1,0:T(8,128)(2,1)S(1)} %collective-permute-done.10.refs_1_, bf16[1024,1408]{1,0:T(8,128)(2,1)S(1)} %bitcast.20, ...), custom_call_target="tpu_custom_call" | custom-call | flops 2214592512 | bytes 10354696 | tf_op jit(solution)/shard_map/experts_256/pallas_call | solution.py:306
  66.4 1.2 %combine.4 = bf16[256,1024]{1,0:T(8,128)(2,1)S(1)} custom-call(s32[2]{0:T(128)S(1)} %pad_add_fusion.me, bf16[288,1024]{1,0:T(8,128)(2,1)S(1)} %collective-permute-done.9.refs_0_.payload, bf16[128,1024]{1,0:T(8,128)(2,1)S(1)} %get-tuple-element.43.outs_me, bf16[128,1024]{1,0:T(8,128)(2,1)S(1)} %collective-permute-done.11.outs_sib), custom_call_target="tpu_custom_call" | custom-call | flops 134217728 | bytes 1638408 | tf_op jit(solution)/shard_map/combine/pallas_call | solution.py:354
  68.3 1.2 %combine.5 = bf16[256,1024]{1,0:T(8,128)(2,1)S(1)} custom-call(s32[2]{0:T(128)S(1)} %pad_add_fusion.me, bf16[288,1024]{1,0:T(8,128)(2,1)S(1)} %collective-permute-done.3.refs_0_.payload, bf16[128,1024]{1,0:T(8,128)(2,1)S(1)} %get-tuple-element.36.outs_me, bf16[128,1024]{1,0:T(8,128)(2,1)S(1)} %collective-permute-done.5.outs_sib, ...), custom_call_target="tpu_custom_call" | custom-call | flops 134217728 | bytes 2162696 | tf_op jit(solution)/shard_map/combine/pallas_call | solution.py:354
  69.5 1.6 %collective-permute-start.14 = (bf16[256,1024]{1,0:T(8,128)(2,1)S(1)}, bf16[256,1024]{1,0:T(8,128)(2,1)S(1)}, u32[]{:S(2)}, u32[]{:S(2)}) collective-permute-start(bf16[256,1024]{1,0:T(8,128)(2,1)S(1)} %combine.5), channel_id=1, source_target_pairs={{0,8},{4,20},{8,0},{12,28},{16,24},{20,4},{24,16},{28,12},{1,9},{5... | collective-permute-start | bytes 1572872 | tf_op jit(solution)/shard_map/ppermute | solution.py:453
  71.0 1.5 %collective-permute-done.13.outs_sib = bf16[128,1024]{1,0:T(8,128)(2,1)S(1)} collective-permute-done((bf16[128,1024]{1,0:T(8,128)(2,1)S(1)}, bf16[128,1024]{1,0:T(8,128)(2,1)S(1)}, u32[]{:S(2)}, u32[]{:S(2)}) %collective-permute-start.13) | collective-permute-done | bytes 262176 | tf_op jit(solution)/shard_map/ppermute | solution.py:449
  73.8 9.3 %collective-permute-done.14.first = bf16[256,1024]{1,0:T(8,128)(2,1)S(1)} collective-permute-done((bf16[256,1024]{1,0:T(8,128)(2,1)S(1)}, bf16[256,1024]{1,0:T(8,128)(2,1)S(1)}, u32[]{:S(2)}, u32[]{:S(2)}) %collective-permute-start.14) | collective-permute-done | bytes 524320 | tf_op jit(solution)/shard_map/ppermute | solution.py:453
  (58 shorter events, 10.5 us)
Async XLA Ops:
  1.2 10.9 %collective-permute-start = (bf16[256,1024]{1,0:T(8,128)(2,1)S(1)}, bf16[256,1024]{1,0:T(8,128)(2,1)S(1)}, u32[]{:S(2)}, u32[]{:S(2)}) collective-permute-start(bf16[256,1024]{1,0:T(8,128)(2,1)S(1)} %get-tuple-element.27), channel_id=1, source_target_pairs={{0,4},{4,8},{8,12},{12,16},{16,20},{20,24},{24,28},{1,5},{5,9},{9,... | collective-permute-start | bytes 1572872 | tf_op jit(solution)/shard_map/ppermute | solution.py:513
  3.6 8.5 %collective-permute-start.1 = (bf16[256,1024]{1,0:T(8,128)(2,1)S(1)}, bf16[256,1024]{1,0:T(8,128)(2,1)S(1)}, u32[]{:S(2)}, u32[]{:S(2)}) collective-permute-start(bf16[256,1024]{1,0:T(8,128)(2,1)S(1)} %get-tuple-element.28), channel_id=1, source_target_pairs={{4,0},{8,4},{12,8},{16,12},{20,16},{24,20},{28,24},{5,1},{9,5},{13... | collective-permute-start | bytes 1572872 | tf_op jit(solution)/shard_map/ppermute | solution.py:514
  6.6 6.4 %copy-start.7 = (bf16[1024,1024]{1,0:T(8,128)(2,1)S(1)}, bf16[1024,1024]{1,0:T(8,128)(2,1)}, u32[]{:S(2)}) copy-start(bf16[1024,1024]{1,0:T(8,128)(2,1)} %w_far.1) | copy-start | bytes 6291460
  6.6 6.4 %copy-start.8 = (bf16[256,1024]{1,0:T(8,128)(2,1)S(1)}, bf16[256,1024]{1,0:T(8,128)(2,1)}, u32[]{:S(2)}) copy-start(bf16[256,1024]{1,0:T(8,128)(2,1)} %q.3) | copy-start | bytes 1572868
  6.6 6.4 %copy-start.9 = (bf16[256,1024]{1,0:T(8,128)(2,1)S(1)}, bf16[256,1024]{1,0:T(8,128)(2,1)}, u32[]{:S(2)}) copy-start(bf16[256,1024]{1,0:T(8,128)(2,1)} %x_far.1) | copy-start | bytes 1572868
  6.6 6.4 %copy-start.10 = (f32[1024]{0:T(1024)S(1)}, f32[1024]{0:T(1024)}, u32[]{:S(2)}) copy-start(f32[1024]{0:T(1024)} %param.16) | copy-start | bytes 12292
  13.1 17.1 %copy-start = (bf16[1,1024,1408]{2,1,0:T(8,128)(2,1)S(1)}, bf16[1,1024,1408]{2,1,0:T(8,128)(2,1)}, u32[]{:S(2)}) copy-start(bf16[1,1024,1408]{2,1,0:T(8,128)(2,1)} %param.19) | copy-start | bytes 8650756
  20.8 9.3 %collective-permute-start.2 = (bf16[288,1024]{1,0:T(8,128)(2,1)}, bf16[288,1024]{1,0:T(8,128)(2,1)}, u32[]{:S(2)}, u32[]{:S(2)}) collective-permute-start(bf16[288,1024]{1,0:T(8,128)(2,1)} %get-tuple-element.41.refs_0_.payload), channel_id=1, source_target_pairs={{0,4},{4,0},{8,12},{12,8},{16,20},{20,16},{24,28},{28,24},{1,5},{5... | collective-permute-start | bytes 1769480 | tf_op jit(solution)/shard_map/ppermute | solution.py:449
  28.2 10.6 %collective-permute-start.3 = (bf16[288,1024]{1,0:T(8,128)(2,1)}, bf16[288,1024]{1,0:T(8,128)(2,1)S(1)}, u32[]{:S(2)}, u32[]{:S(2)}) collective-permute-start(bf16[288,1024]{1,0:T(8,128)(2,1)} %get-tuple-element.41.refs_0_.payload), channel_id=1, source_target_pairs={{0,8},{4,20},{8,0},{12,28},{16,24},{20,4},{24,16},{28,12},{1,9},{5... | collective-permute-start | bytes 1769480 | tf_op jit(solution)/shard_map/ppermute | solution.py:453
  38.8 10.3 %copy-start.5 = (bf16[288,1024]{1,0:T(8,128)(2,1)S(1)}, bf16[288,1024]{1,0:T(8,128)(2,1)}, u32[]{:S(2)}) copy-start(bf16[288,1024]{1,0:T(8,128)(2,1)} %get-tuple-element.41.refs_0_.payload) | copy-start | bytes 1769476
  38.9 2.1 %collective-permute-start.4 = (bf16[288,1024]{1,0:T(8,128)(2,1)S(1)}, bf16[288,1024]{1,0:T(8,128)(2,1)S(1)}, u32[]{:S(2)}, u32[]{:S(2)}) collective-permute-start(bf16[288,1024]{1,0:T(8,128)(2,1)S(1)} %collective-permute-done.3.refs_0_.payload), channel_id=1, source_target_pairs={{0,4},{4,0},{8,12},{12,8},{16,20},{20,16},{24,28},{28,24},{1,5},{5... | collective-permute-start | bytes 1769480 | tf_op jit(solution)/shard_map/ppermute | solution.py:449
  39.3 9.9 %collective-permute-start.6 = (bf16[288,1024]{1,0:T(8,128)(2,1)S(1)}, bf16[288,1024]{1,0:T(8,128)(2,1)S(1)}, u32[]{:S(2)}, u32[]{:S(2)}) collective-permute-start(bf16[288,1024]{1,0:T(8,128)(2,1)S(1)} %collective-permute-done.3.refs_0_.payload), channel_id=1, source_target_pairs={{0,16},{4,12},{8,24},{12,4},{16,0},{20,28},{24,8},{28,20},{1,17},{... | collective-permute-start | bytes 1769480 | tf_op jit(solution)/shard_map/ppermute | solution.py:453
  49.2 2.0 %collective-permute-start.7 = (bf16[288,1024]{1,0:T(8,128)(2,1)S(1)}, bf16[288,1024]{1,0:T(8,128)(2,1)S(1)}, u32[]{:S(2)}, u32[]{:S(2)}) collective-permute-start(bf16[288,1024]{1,0:T(8,128)(2,1)S(1)} %collective-permute-done.6.refs_0_.payload), channel_id=1, source_target_pairs={{0,4},{4,0},{8,12},{12,8},{16,20},{20,16},{24,28},{28,24},{1,5},{5... | collective-permute-start | bytes 1769480 | tf_op jit(solution)/shard_map/ppermute | solution.py:449
  49.2 9.9 %collective-permute-start.9 = (bf16[288,1024]{1,0:T(8,128)(2,1)S(1)}, bf16[288,1024]{1,0:T(8,128)(2,1)S(1)}, u32[]{:S(2)}, u32[]{:S(2)}) collective-permute-start(bf16[288,1024]{1,0:T(8,128)(2,1)S(1)} %copy-done.5), channel_id=1, source_target_pairs={{0,16},{4,12},{8,24},{12,4},{16,0},{20,28},{24,8},{28,20},{1,17},{... | collective-permute-start | bytes 1769480 | tf_op jit(solution)/shard_map/ppermute | solution.py:453
  51.2 9.9 %copy-start.2 = (bf16[1,1024,1408]{2,1,0:T(8,128)(2,1)S(1)}, bf16[1,1024,1408]{2,1,0:T(8,128)(2,1)}, u32[]{:S(2)}) copy-start(bf16[1,1024,1408]{2,1,0:T(8,128)(2,1)} %param.20) | copy-start | bytes 8650756
  54.6 1.6 %collective-permute-start.8 = (bf16[128,1024]{1,0:T(8,128)(2,1)S(1)}, bf16[128,1024]{1,0:T(8,128)(2,1)S(1)}, u32[]{:S(2)}, u32[]{:S(2)}) collective-permute-start(bf16[128,1024]{1,0:T(8,128)(2,1)S(1)} %get-tuple-element.40), channel_id=1, source_target_pairs={{0,4},{4,0},{8,12},{12,8},{16,20},{20,16},{24,28},{28,24},{1,5},{5... | collective-permute-start | bytes 786440 | tf_op jit(solution)/shard_map/ppermute | solution.py:449
  59.1 2.0 %collective-permute-start.10 = (bf16[288,1024]{1,0:T(8,128)(2,1)S(1)}, bf16[288,1024]{1,0:T(8,128)(2,1)S(1)}, u32[]{:S(2)}, u32[]{:S(2)}) collective-permute-start(bf16[288,1024]{1,0:T(8,128)(2,1)S(1)} %collective-permute-done.9.refs_0_.payload), channel_id=1, source_target_pairs={{0,4},{4,0},{8,12},{12,8},{16,20},{20,16},{24,28},{28,24},{1,5},{5... | collective-permute-start | bytes 1769480 | tf_op jit(solution)/shard_map/ppermute | solution.py:449
  59.1 9.2 %collective-permute-start.12 = (bf16[256,1024]{1,0:T(8,128)(2,1)S(1)}, bf16[256,1024]{1,0:T(8,128)(2,1)S(1)}, u32[]{:S(2)}, u32[]{:S(2)}) collective-permute-start(bf16[256,1024]{1,0:T(8,128)(2,1)S(1)} %combine.3), channel_id=1, source_target_pairs={{0,16},{4,12},{8,24},{12,4},{16,0},{20,28},{24,8},{28,20},{1,17},{... | collective-permute-start | bytes 1572872 | tf_op jit(solution)/shard_map/ppermute | solution.py:453
  64.8 7.8 %copy-start.6 = (bf16[256,1024]{1,0:T(8,128)(2,1)S(1)}, bf16[256,1024]{1,0:T(8,128)(2,1)}, u32[]{:S(2)}) copy-start(bf16[256,1024]{1,0:T(8,128)(2,1)} %get-tuple-element.33.resid) | copy-start | bytes 1572868
  64.8 1.6 %collective-permute-start.11 = (bf16[128,1024]{1,0:T(8,128)(2,1)S(1)}, bf16[128,1024]{1,0:T(8,128)(2,1)S(1)}, u32[]{:S(2)}, u32[]{:S(2)}) collective-permute-start(bf16[128,1024]{1,0:T(8,128)(2,1)S(1)} %get-tuple-element.44), channel_id=1, source_target_pairs={{0,4},{4,0},{8,12},{12,8},{16,20},{20,16},{24,28},{28,24},{1,5},{5... | collective-permute-start | bytes 786440 | tf_op jit(solution)/shard_map/ppermute | solution.py:449
  65.0 3.3 %collective-permute-start.5 = (bf16[128,1024]{1,0:T(8,128)(2,1)S(1)}, bf16[128,1024]{1,0:T(8,128)(2,1)S(1)}, u32[]{:S(2)}, u32[]{:S(2)}) collective-permute-start(bf16[128,1024]{1,0:T(8,128)(2,1)S(1)} %get-tuple-element.37), channel_id=1, source_target_pairs={{0,4},{4,0},{8,12},{12,8},{16,20},{20,16},{24,28},{28,24},{1,5},{5... | collective-permute-start | bytes 786440 | tf_op jit(solution)/shard_map/ppermute | solution.py:449
  69.5 13.6 %collective-permute-start.14 = (bf16[256,1024]{1,0:T(8,128)(2,1)S(1)}, bf16[256,1024]{1,0:T(8,128)(2,1)S(1)}, u32[]{:S(2)}, u32[]{:S(2)}) collective-permute-start(bf16[256,1024]{1,0:T(8,128)(2,1)S(1)} %combine.5), channel_id=1, source_target_pairs={{0,8},{4,20},{8,0},{12,28},{16,24},{20,4},{24,16},{28,12},{1,9},{5... | collective-permute-start | bytes 1572872 | tf_op jit(solution)/shard_map/ppermute | solution.py:453
  71.0 12.1 %collective-permute-start.15 = (bf16[256,1024]{1,0:T(8,128)(2,1)S(1)}, bf16[256,1024]{1,0:T(8,128)(2,1)S(1)}, u32[]{:S(2)}, u32[]{:S(2)}) collective-permute-start(bf16[256,1024]{1,0:T(8,128)(2,1)S(1)} %combine.4), channel_id=1, source_target_pairs={{0,16},{4,12},{8,24},{12,4},{16,0},{20,28},{24,8},{28,20},{1,17},{... | collective-permute-start | bytes 1572872 | tf_op jit(solution)/shard_map/ppermute | solution.py:453
  71.0 1.5 %collective-permute-start.13 = (bf16[128,1024]{1,0:T(8,128)(2,1)S(1)}, bf16[128,1024]{1,0:T(8,128)(2,1)S(1)}, u32[]{:S(2)}, u32[]{:S(2)}) collective-permute-start(bf16[128,1024]{1,0:T(8,128)(2,1)S(1)} %get-tuple-element.46), channel_id=1, source_target_pairs={{0,4},{4,0},{8,12},{12,8},{16,20},{20,16},{24,28},{28,24},{1,5},{5... | collective-permute-start | bytes 786440 | tf_op jit(solution)/shard_map/ppermute | solution.py:449
  (5 other events, 6.5 us)

commit v4 on v3

--- a/solution.py
+++ b/solution.py
@@ -118,7 +118,7 @@
         interior_kernel,
         in_specs=[VMEM] * 3,
         out_specs=[VMEM] * 3,
-        out_shape=[pltpu.HBM(o.shape, o.dtype) for o in flat],
+        out_shape=flat,
         scratch_shapes=[pltpu.VMEM((rows, 2 * rows), F32)],
         compiler_params=pltpu.CompilerParams(vmem_limit_bytes=12 * MIB),
         cost_estimate=cost(LONG * 4 * rows * rows * model, HEADS * rows * rows, args, flat),
@@ -146,29 +146,36 @@
     for half in range(2):
         first = -wide if half == 0 else 2 * rows
         bias[half] = window_bias(wide, first, rows, half * rows, live[half])
+    cells = [(pair, half) for pair in range(pairs) for half in range(2)]
+    scores = []
+    for pair, half in cells:
+        cols = slice(pair * step, (pair + 1) * step)
+        queries = two_heads(q[half * rows : (half + 1) * rows, cols])
+        s = lax.dot_general(halos[half][:wide, cols], queries, NT, preferred_element_type=F32)
+        scores.append(s + bias[half])
+    weights = []
+    for (pair, half), s in zip(cells, scores):
+        span = slice(half * rows, (half + 1) * rows)
+        both = [slice(2 * pair + side, 2 * pair + side + 1) for side in range(2)]
+        old = jnp.concatenate([tops[b, span] for b in both], axis=1)
+        top = jnp.maximum(old, jnp.max(s, axis=0, keepdims=True))
+        shrink = jnp.exp(old - top)
+        p = jnp.exp(s - top)
+        total = jnp.concatenate([sums[b, span] for b in both], axis=1) * shrink
+        total = total + jnp.sum(p, axis=0, keepdims=True)
+        weights.append((p.astype(BF16), shrink, 1.0 / total))
     for pair in range(pairs):
+        fetches[pair].wait()
+    for (pair, half), (p, shrink, inverse) in zip(cells, weights):
+        span = slice(half * rows, (half + 1) * rows)
         cols = slice(pair * step, (pair + 1) * step)
-        fetches[pair].wait()
-        for half, halo in enumerate(halos):
-            span = slice(half * rows, (half + 1) * rows)
-            queries = two_heads(q[span, cols])
-            s = lax.dot_general(halo[:wide, cols], queries, NT, preferred_element_type=F32)
-            s = s + bias[half]
-            both = [slice(2 * pair + side, 2 * pair + side + 1) for side in range(2)]
-            old = jnp.concatenate([tops[b, span] for b in both], axis=1)
-            top = jnp.maximum(old, jnp.max(s, axis=0, keepdims=True))
-            shrink = jnp.exp(old - top)
-            p = jnp.exp(s - top)
-            total = jnp.concatenate([sums[b, span] for b in both], axis=1) * shrink
-            total = total + jnp.sum(p, axis=0, keepdims=True)
-            o = lax.dot_general(halo[wide:, cols], p.astype(BF16), TN, preferred_element_type=F32)
-            inverse = 1.0 / total
-            for side in range(2):
-                at = slice(side * rows, (side + 1) * rows)
-                base = pair * step + side * HD
-                value = acc[base : base + HD, span] * shrink[:, at]
-                value = value + o[side * HD : (side + 1) * HD, at]
-                att[base : base + HD, span] = (value * inverse[:, at]).astype(BF16)
+        o = lax.dot_general(halos[half][wide:, cols], p, TN, preferred_element_type=F32)
+        for side in range(2):
+            at = slice(side * rows, (side + 1) * rows)
+            base = pair * step + side * HD
+            value = acc[base : base + HD, span] * shrink[:, at]
+            value = value + o[side * HD : (side + 1) * HD, at]
+            att[base : base + HD, span] = (value * inverse[:, at]).astype(BF16)
     fetches[pairs].wait()
     fetches[pairs + 1].wait()
     for half in range(2):
@@ -191,7 +198,6 @@
 def edge(live, q, before, behind, acc, tops, sums, x, w, gain, meta):
     rows, model = q.shape[0] // 2, q.shape[1]
     wide = before.shape[0] // 2
-    before, behind, acc, tops, sums = [far(a) for a in (before, behind, acc, tops, sums)]
     args = [live, q, before, behind, tops, sums, gain, acc, x, w]
     args += [] if meta is None else [meta]
     specs = [SMEM] + [VMEM] * 6 + [ANY] * 3 + ([] if meta is None else [VMEM])
@@ -457,9 +463,7 @@
     return lax.optimization_barrier((first, *later))[1:]
 
 
-def routed_gather(payload, resid, weights, rows, capacity):
-    tile = lax.axis_index("tile")
-    me = jnp.stack([tile, tile ^ 1]).astype(jnp.int32)
+def routed_gather(me, payload, resid, weights, rows, capacity):
     sizes = dict(rows=rows, capacity=capacity)
 
     def evaluate(mine, theirs):
@@ -509,10 +513,12 @@
     capacity = row_count * routes.shape[1] // tiles
     up = [(i, i + 1) for i in range(tiles - 1)]
     down = [(j, i) for i, j in up]
+    live = jnp.stack([tile > 0, tile < tiles - 1]).astype(jnp.int32)
+    me = jnp.stack([tile, tile ^ 1]).astype(jnp.int32)
+    live, me, key_vectors = lax.optimization_barrier((live, me, key_vectors))
     last, first = pack(key_vectors, values, width)
     before = lax.ppermute(last, "tile", up)
     behind = lax.ppermute(first, "tile", down)
-    live = jnp.stack([tile > 0, tile < tiles - 1]).astype(jnp.int32)
     fast = tiles == 8
     meta = None
     if fast:
@@ -531,7 +537,7 @@
     )
     if fast:
         weights = (w_gate[0], w_up[0], w_down[0])
-        return routed_gather(payload, resid, weights, rows, capacity)
+        return routed_gather(me, payload, resid, weights, rows, capacity)
     return routed_all_to_all(payload, resid, routes, route_gates, w_gate[0], w_up[0], w_down[0])
 
 

time: 84.4 us -> 80.7 us (0.956)
  local copies, waits for them, and re-layouts: 6.45 us -> 1.89 us
  waiting for transfers between devices: 26.4 us -> 30 us
  Pallas kernels: 34.7 us -> 31.3 us
    unnamed x28 -> x22, local copies, waits for them, and re-layouts: 5.69 us -> 1.13 us
    ppermute x6, waiting for transfers between devices: 16.4 us -> 19.7 us  [swap_by_core(): return lax.ppermute(array, 'tile', [(i, i ^ bits[i % 2]) for i in range(8)])]
    pallas_call x1, Pallas kernels: 7.7 us -> 5.66 us  [edge(): pl.pallas_call(edge_kernel, in_specs=specs, out_specs=[VMEM] * 2, out_sha...]
    pallas_call x1, Pallas kernels: 5.46 us -> 4.51 us  [interior(): pl.pallas_call(interior_kernel, in_specs=[VMEM] * 3, out_specs=[VMEM] * 3...]
  transfers between devices with their start and end apart: 16 -> 16, of which waited for: 11 -> 12; matrix products, arithmetic and copies ran while one was open for 2% -> 2% of each run, Pallas kernels for 28% -> 28%
where the time goes in v4:
time: 80.7 us; the launch traced here: 80.4 us
  Pallas kernels  31.3 us (39%)
  waiting for transfers between devices  30 us (37%)
  starting transfers between devices  16 us (20%)
  local copies, waits for them, and re-layouts  1.89 us (2%)
  other arithmetic  0.99 us (1%)
    ppermute x6, waiting for transfers between devices, swap_by_core(): return lax.ppermute(array, 'tile', [(i, i ^ bits[i % 2]) for i in range(8)])  19.7 us
    pallas_call x4, Pallas kernels, experts(): pl.pallas_call(functools.partial(experts_kernel, order, rows, capacity),...  14.1 us
    ppermute x8, waiting for transfers between devices, swap(): return lax.ppermute(array, 'tile', [(i, i ^ bit) for i in range(8)])  10.3 us
    ppermute x8, starting transfers between devices, swap(): return lax.ppermute(array, 'tile', [(i, i ^ bit) for i in range(8)])  9.26 us
    pallas_call x1, Pallas kernels, edge(): pl.pallas_call(edge_kernel, in_specs=specs, out_specs=[VMEM] * 2, out_sha...  5.66 us
    pallas_call x1, Pallas kernels, interior(): pl.pallas_call(interior_kernel, in_specs=[VMEM] * 3, out_specs=[VMEM] * 3...  4.51 us
    pallas_call x3, Pallas kernels, combine(): pl.pallas_call(functools.partial(combine_kernel, rows, capacity), in_spec...  3.61 us
    ppermute x6, starting transfers between devices, swap_by_core(): return lax.ppermute(array, 'tile', [(i, i ^ bits[i % 2]) for i in range(8)])  3.05 us
  transfers between devices with their start and end apart: 16, of which 12 were waited for; matrix products, arithmetic and copies ran while one was open for 2% of the time, Pallas kernels for 28%

profile of v4, /device:TPU:0, one launch (start us, length us, event | category | flops | bytes accessed | tf_op | source)
XLA Modules:
  0.0 80.4 jit_solution(15400176041313619910)
XLA Ops:
  0.2 1.2 %pack.1 = (bf16[256,1024]{1,0:T(8,128)(2,1)S(1)}, bf16[256,1024]{1,0:T(8,128)(2,1)S(1)}) custom-call(bf16[256,1024]{1,0:T(8,128)(2,1)} %k.1, bf16[256,1024]{1,0:T(8,128)(2,1)} %v.3), custom_call_target="tpu_custom_call" | custom-call | bytes 2097152 | tf_op jit(solution)/shard_map/pack/pallas_call | solution.py:81
  1.4 2.4 %collective-permute-start = (bf16[256,1024]{1,0:T(8,128)(2,1)S(1)}, bf16[256,1024]{1,0:T(8,128)(2,1)S(1)}, u32[]{:S(2)}, u32[]{:S(2)}) collective-permute-start(bf16[256,1024]{1,0:T(8,128)(2,1)S(1)} %get-tuple-element.33), channel_id=1, source_target_pairs={{0,4},{4,8},{8,12},{12,16},{16,20},{20,24},{24,28},{1,5},{5,9},{9,... | collective-permute-start | bytes 1572872 | tf_op jit(solution)/shard_map/ppermute | solution.py:520
  3.8 1.3 %collective-permute-start.1 = (bf16[256,1024]{1,0:T(8,128)(2,1)S(1)}, bf16[256,1024]{1,0:T(8,128)(2,1)S(1)}, u32[]{:S(2)}, u32[]{:S(2)}) collective-permute-start(bf16[256,1024]{1,0:T(8,128)(2,1)S(1)} %get-tuple-element.34), channel_id=1, source_target_pairs={{4,0},{8,4},{12,8},{16,12},{20,16},{24,20},{28,24},{5,1},{9,5},{13... | collective-permute-start | bytes 1572872 | tf_op jit(solution)/shard_map/ppermute | solution.py:521
  6.8 4.5 %interior.1 = (f32[1024,256]{1,0:T(8,128)S(1)}, f32[16,256]{1,0:T(8,128)S(1)}, f32[16,256]{1,0:T(8,128)S(1)}) custom-call(bf16[256,1024]{1,0:T(8,128)(2,1)} %q.3, bf16[256,1024]{1,0:T(8,128)(2,1)} %k.1, bf16[256,1024]{1,0:T(8,128)(2,1)} %v.3), custom_call_target="tpu_custom_call" | custom-call | flops 8053063680 | bytes 2654208 | tf_op jit(solution)/shard_map/interior/pallas_call | solution.py:117
  11.4 5.7 %edge.1 = (bf16[256,1024]{1,0:T(8,128)(2,1)}, bf16[288,1024]{1,0:T(8,128)(2,1)}) custom-call(s32[2]{0:T(128)S(1)} %add_convert_fusion.live, bf16[256,1024]{1,0:T(8,128)(2,1)S(1)} %copy-done.7, bf16[256,1024]{1,0:T(8,128)(2,1)S(1)} %collective-permute-done.before, bf16[256,1024]{1,0:T(8,128)(2,1)S(1)} %collective-permute-done.1.behind, ...), custom_call_target="tpu_custom_call" | custom-call | flops 20132659200 | bytes 6397960 | tf_op jit(solution)/shard_map/edge/pallas_call | solution.py:209
  17.0 8.5 %collective-permute-start.2 = (bf16[288,1024]{1,0:T(8,128)(2,1)}, bf16[288,1024]{1,0:T(8,128)(2,1)S(1)}, u32[]{:S(2)}, u32[]{:S(2)}) collective-permute-start(bf16[288,1024]{1,0:T(8,128)(2,1)} %get-tuple-element.47.refs_0_.payload), channel_id=1, source_target_pairs={{0,4},{4,0},{8,12},{12,8},{16,20},{20,16},{24,28},{28,24},{1,5},{5... | collective-permute-start | bytes 1769480 | tf_op jit(solution)/shard_map/ppermute | solution.py:455
  25.5 1.5 %collective-permute-start.3 = (bf16[288,1024]{1,0:T(8,128)(2,1)}, bf16[288,1024]{1,0:T(8,128)(2,1)S(1)}, u32[]{:S(2)}, u32[]{:S(2)}) collective-permute-start(bf16[288,1024]{1,0:T(8,128)(2,1)} %get-tuple-element.47.refs_0_.payload), channel_id=1, source_target_pairs={{0,8},{4,20},{8,0},{12,28},{16,24},{20,4},{24,16},{28,12},{1,9},{5... | collective-permute-start | bytes 1769480 | tf_op jit(solution)/shard_map/ppermute | solution.py:459
  28.4 3.5 %experts_256.4 = (bf16[128,1024]{1,0:T(8,128)(2,1)S(1)}, bf16[128,1024]{1,0:T(8,128)(2,1)S(1)}) custom-call(s32[2]{0:T(128)S(1)} %pad_add_fusion.me, bf16[288,1024]{1,0:T(8,128)(2,1)S(1)} %copy-done.3, bf16[288,1024]{1,0:T(8,128)(2,1)S(1)} %collective-permute-done.2.refs_1_, bf16[1024,1408]{1,0:T(8,128)(2,1)S(1)} %bitcast.17, ...), custom_call_target="tpu_custom_call" | custom-call | flops 2214592512 | bytes 10354696 | tf_op jit(solution)/shard_map/experts_256/pallas_call | solution.py:312
  31.9 3.7 %collective-permute-done.3.refs_0_.payload = bf16[288,1024]{1,0:T(8,128)(2,1)S(1)} collective-permute-done((bf16[288,1024]{1,0:T(8,128)(2,1)}, bf16[288,1024]{1,0:T(8,128)(2,1)S(1)}, u32[]{:S(2)}, u32[]{:S(2)}) %collective-permute-start.3) | collective-permute-done | bytes 589856 | tf_op jit(solution)/shard_map/ppermute | solution.py:459
  35.6 2.0 %collective-permute-done.4.refs_1_ = bf16[288,1024]{1,0:T(8,128)(2,1)S(1)} collective-permute-done((bf16[288,1024]{1,0:T(8,128)(2,1)S(1)}, bf16[288,1024]{1,0:T(8,128)(2,1)S(1)}, u32[]{:S(2)}, u32[]{:S(2)}) %collective-permute-start.4) | collective-permute-done | bytes 589856 | tf_op jit(solution)/shard_map/ppermute | solution.py:455
  37.6 3.5 %experts_256.5 = (bf16[128,1024]{1,0:T(8,128)(2,1)S(1)}, bf16[128,1024]{1,0:T(8,128)(2,1)S(1)}) custom-call(s32[2]{0:T(128)S(1)} %pad_add_fusion.me, bf16[288,1024]{1,0:T(8,128)(2,1)S(1)} %collective-permute-done.3.refs_0_.payload, bf16[288,1024]{1,0:T(8,128)(2,1)S(1)} %collective-permute-done.4.refs_1_, bf16[1024,1408]{1,0:T(8,128)(2,1)S(1)} %bitcast.18, ...), custom_call_target="tpu_custom_call" | custom-call | flops 2214592512 | bytes 10354696 | tf_op jit(solution)/shard_map/experts_256/pallas_call | solution.py:312
  41.1 4.4 %collective-permute-done.6.refs_0_.payload = bf16[288,1024]{1,0:T(8,128)(2,1)S(1)} collective-permute-done((bf16[288,1024]{1,0:T(8,128)(2,1)S(1)}, bf16[288,1024]{1,0:T(8,128)(2,1)S(1)}, u32[]{:S(2)}, u32[]{:S(2)}) %collective-permute-start.6) | collective-permute-done | bytes 589856 | tf_op jit(solution)/shard_map/ppermute | solution.py:459
  45.5 2.0 %collective-permute-done.7.refs_1_ = bf16[288,1024]{1,0:T(8,128)(2,1)S(1)} collective-permute-done((bf16[288,1024]{1,0:T(8,128)(2,1)S(1)}, bf16[288,1024]{1,0:T(8,128)(2,1)S(1)}, u32[]{:S(2)}, u32[]{:S(2)}) %collective-permute-start.7) | collective-permute-done | bytes 589856 | tf_op jit(solution)/shard_map/ppermute | solution.py:455
  47.5 3.5 %experts_256.6 = (bf16[128,1024]{1,0:T(8,128)(2,1)S(1)}, bf16[128,1024]{1,0:T(8,128)(2,1)S(1)}) custom-call(s32[2]{0:T(128)S(1)} %pad_add_fusion.me, bf16[288,1024]{1,0:T(8,128)(2,1)S(1)} %collective-permute-done.6.refs_0_.payload, bf16[288,1024]{1,0:T(8,128)(2,1)S(1)} %collective-permute-done.7.refs_1_, bf16[1024,1408]{1,0:T(8,128)(2,1)S(1)} %bitcast.19, ...), custom_call_target="tpu_custom_call" | custom-call | flops 2214592512 | bytes 10354696 | tf_op jit(solution)/shard_map/experts_256/pallas_call | solution.py:312
  51.2 1.4 %collective-permute-done.8.outs_sib = bf16[128,1024]{1,0:T(8,128)(2,1)S(1)} collective-permute-done((bf16[128,1024]{1,0:T(8,128)(2,1)S(1)}, bf16[128,1024]{1,0:T(8,128)(2,1)S(1)}, u32[]{:S(2)}, u32[]{:S(2)}) %collective-permute-start.8) | collective-permute-done | bytes 262176 | tf_op jit(solution)/shard_map/ppermute | solution.py:455
  52.6 1.2 %combine.3 = bf16[256,1024]{1,0:T(8,128)(2,1)S(1)} custom-call(s32[2]{0:T(128)S(1)} %pad_add_fusion.me, bf16[288,1024]{1,0:T(8,128)(2,1)S(1)} %collective-permute-done.6.refs_0_.payload, bf16[128,1024]{1,0:T(8,128)(2,1)S(1)} %get-tuple-element.45.outs_me, bf16[128,1024]{1,0:T(8,128)(2,1)S(1)} %collective-permute-done.8.outs_sib), custom_call_target="tpu_custom_call" | custom-call | flops 134217728 | bytes 1638408 | tf_op jit(solution)/shard_map/combine/pallas_call | solution.py:360
  53.8 1.6 %collective-permute-done.9.refs_0_.payload = bf16[288,1024]{1,0:T(8,128)(2,1)S(1)} collective-permute-done((bf16[288,1024]{1,0:T(8,128)(2,1)S(1)}, bf16[288,1024]{1,0:T(8,128)(2,1)S(1)}, u32[]{:S(2)}, u32[]{:S(2)}) %collective-permute-start.9) | collective-permute-done | bytes 589856 | tf_op jit(solution)/shard_map/ppermute | solution.py:459
  55.4 2.0 %collective-permute-done.10.refs_1_ = bf16[288,1024]{1,0:T(8,128)(2,1)S(1)} collective-permute-done((bf16[288,1024]{1,0:T(8,128)(2,1)S(1)}, bf16[288,1024]{1,0:T(8,128)(2,1)S(1)}, u32[]{:S(2)}, u32[]{:S(2)}) %collective-permute-start.10) | collective-permute-done | bytes 589856 | tf_op jit(solution)/shard_map/ppermute | solution.py:455
  57.4 3.7 %experts_256.7 = (bf16[128,1024]{1,0:T(8,128)(2,1)S(1)}, bf16[128,1024]{1,0:T(8,128)(2,1)S(1)}) custom-call(s32[2]{0:T(128)S(1)} %pad_add_fusion.me, bf16[288,1024]{1,0:T(8,128)(2,1)S(1)} %collective-permute-done.9.refs_0_.payload, bf16[288,1024]{1,0:T(8,128)(2,1)S(1)} %collective-permute-done.10.refs_1_, bf16[1024,1408]{1,0:T(8,128)(2,1)S(1)} %bitcast.20, ...), custom_call_target="tpu_custom_call" | custom-call | flops 2214592512 | bytes 10354696 | tf_op jit(solution)/shard_map/experts_256/pallas_call | solution.py:312
  62.7 1.2 %combine.4 = bf16[256,1024]{1,0:T(8,128)(2,1)S(1)} custom-call(s32[2]{0:T(128)S(1)} %pad_add_fusion.me, bf16[288,1024]{1,0:T(8,128)(2,1)S(1)} %collective-permute-done.9.refs_0_.payload, bf16[128,1024]{1,0:T(8,128)(2,1)S(1)} %get-tuple-element.49.outs_me, bf16[128,1024]{1,0:T(8,128)(2,1)S(1)} %collective-permute-done.11.outs_sib), custom_call_target="tpu_custom_call" | custom-call | flops 134217728 | bytes 1638408 | tf_op jit(solution)/shard_map/combine/pallas_call | solution.py:360
  64.6 1.2 %combine.5 = bf16[256,1024]{1,0:T(8,128)(2,1)S(1)} custom-call(s32[2]{0:T(128)S(1)} %pad_add_fusion.me, bf16[288,1024]{1,0:T(8,128)(2,1)S(1)} %collective-permute-done.3.refs_0_.payload, bf16[128,1024]{1,0:T(8,128)(2,1)S(1)} %get-tuple-element.42.outs_me, bf16[128,1024]{1,0:T(8,128)(2,1)S(1)} %collective-permute-done.5.outs_sib, ...), custom_call_target="tpu_custom_call" | custom-call | flops 134217728 | bytes 2162696 | tf_op jit(solution)/shard_map/combine/pallas_call | solution.py:360
  65.8 1.6 %collective-permute-start.14 = (bf16[256,1024]{1,0:T(8,128)(2,1)S(1)}, bf16[256,1024]{1,0:T(8,128)(2,1)S(1)}, u32[]{:S(2)}, u32[]{:S(2)}) collective-permute-start(bf16[256,1024]{1,0:T(8,128)(2,1)S(1)} %combine.5), channel_id=1, source_target_pairs={{0,8},{4,20},{8,0},{12,28},{16,24},{20,4},{24,16},{28,12},{1,9},{5... | collective-permute-start | bytes 1572872 | tf_op jit(solution)/shard_map/ppermute | solution.py:459
  67.3 1.5 %collective-permute-done.13.outs_sib = bf16[128,1024]{1,0:T(8,128)(2,1)S(1)} collective-permute-done((bf16[128,1024]{1,0:T(8,128)(2,1)S(1)}, bf16[128,1024]{1,0:T(8,128)(2,1)S(1)}, u32[]{:S(2)}, u32[]{:S(2)}) %collective-permute-start.13) | collective-permute-done | bytes 262176 | tf_op jit(solution)/shard_map/ppermute | solution.py:455
  70.1 9.3 %collective-permute-done.14.first = bf16[256,1024]{1,0:T(8,128)(2,1)S(1)} collective-permute-done((bf16[256,1024]{1,0:T(8,128)(2,1)S(1)}, bf16[256,1024]{1,0:T(8,128)(2,1)S(1)}, u32[]{:S(2)}, u32[]{:S(2)}) %collective-permute-start.14) | collective-permute-done | bytes 524320 | tf_op jit(solution)/shard_map/ppermute | solution.py:459
  (52 shorter events, 7.9 us)
Async XLA Ops:
  1.4 9.9 %collective-permute-start = (bf16[256,1024]{1,0:T(8,128)(2,1)S(1)}, bf16[256,1024]{1,0:T(8,128)(2,1)S(1)}, u32[]{:S(2)}, u32[]{:S(2)}) collective-permute-start(bf16[256,1024]{1,0:T(8,128)(2,1)S(1)} %get-tuple-element.33), channel_id=1, source_target_pairs={{0,4},{4,8},{8,12},{12,16},{16,20},{20,24},{24,28},{1,5},{5,9},{9,... | collective-permute-start | bytes 1572872 | tf_op jit(solution)/shard_map/ppermute | solution.py:520
  3.8 7.5 %collective-permute-start.1 = (bf16[256,1024]{1,0:T(8,128)(2,1)S(1)}, bf16[256,1024]{1,0:T(8,128)(2,1)S(1)}, u32[]{:S(2)}, u32[]{:S(2)}) collective-permute-start(bf16[256,1024]{1,0:T(8,128)(2,1)S(1)} %get-tuple-element.34), channel_id=1, source_target_pairs={{4,0},{8,4},{12,8},{16,12},{20,16},{24,20},{28,24},{5,1},{9,5},{13... | collective-permute-start | bytes 1572872 | tf_op jit(solution)/shard_map/ppermute | solution.py:521
  6.7 4.6 %copy-start.6 = (bf16[1024,1024]{1,0:T(8,128)(2,1)S(1)}, bf16[1024,1024]{1,0:T(8,128)(2,1)}, u32[]{:S(2)}) copy-start(bf16[1024,1024]{1,0:T(8,128)(2,1)} %w_far.1) | copy-start | bytes 6291460
  6.7 4.6 %copy-start.7 = (bf16[256,1024]{1,0:T(8,128)(2,1)S(1)}, bf16[256,1024]{1,0:T(8,128)(2,1)}, u32[]{:S(2)}) copy-start(bf16[256,1024]{1,0:T(8,128)(2,1)} %q.3) | copy-start | bytes 1572868
  6.7 4.6 %copy-start.8 = (bf16[256,1024]{1,0:T(8,128)(2,1)S(1)}, bf16[256,1024]{1,0:T(8,128)(2,1)}, u32[]{:S(2)}) copy-start(bf16[256,1024]{1,0:T(8,128)(2,1)} %x_far.1) | copy-start | bytes 1572868
  11.3 16.0 %copy-start = (bf16[1,1024,1408]{2,1,0:T(8,128)(2,1)S(1)}, bf16[1,1024,1408]{2,1,0:T(8,128)(2,1)}, u32[]{:S(2)}) copy-start(bf16[1,1024,1408]{2,1,0:T(8,128)(2,1)} %param.19) | copy-start | bytes 8650756
  11.3 16.0 %copy-start.1 = (bf16[1,1024,1408]{2,1,0:T(8,128)(2,1)S(1)}, bf16[1,1024,1408]{2,1,0:T(8,128)(2,1)}, u32[]{:S(2)}) copy-start(bf16[1,1024,1408]{2,1,0:T(8,128)(2,1)} %param.20) | copy-start | bytes 8650756
  11.4 16.0 %copy-start.2 = (bf16[1,1408,1024]{2,1,0:T(8,128)(2,1)S(1)}, bf16[1,1408,1024]{2,1,0:T(8,128)(2,1)}, u32[]{:S(2)}) copy-start(bf16[1,1408,1024]{2,1,0:T(8,128)(2,1)} %param.21) | copy-start | bytes 8650756
  17.0 10.3 %collective-permute-start.2 = (bf16[288,1024]{1,0:T(8,128)(2,1)}, bf16[288,1024]{1,0:T(8,128)(2,1)S(1)}, u32[]{:S(2)}, u32[]{:S(2)}) collective-permute-start(bf16[288,1024]{1,0:T(8,128)(2,1)} %get-tuple-element.47.refs_0_.payload), channel_id=1, source_target_pairs={{0,4},{4,0},{8,12},{12,8},{16,20},{20,16},{24,28},{28,24},{1,5},{5... | collective-permute-start | bytes 1769480 | tf_op jit(solution)/shard_map/ppermute | solution.py:455
  25.5 10.1 %collective-permute-start.3 = (bf16[288,1024]{1,0:T(8,128)(2,1)}, bf16[288,1024]{1,0:T(8,128)(2,1)S(1)}, u32[]{:S(2)}, u32[]{:S(2)}) collective-permute-start(bf16[288,1024]{1,0:T(8,128)(2,1)} %get-tuple-element.47.refs_0_.payload), channel_id=1, source_target_pairs={{0,8},{4,20},{8,0},{12,28},{16,24},{20,4},{24,16},{28,12},{1,9},{5... | collective-permute-start | bytes 1769480 | tf_op jit(solution)/shard_map/ppermute | solution.py:459
  35.6 9.9 %copy-start.4 = (bf16[288,1024]{1,0:T(8,128)(2,1)S(1)}, bf16[288,1024]{1,0:T(8,128)(2,1)}, u32[]{:S(2)}) copy-start(bf16[288,1024]{1,0:T(8,128)(2,1)} %get-tuple-element.47.refs_0_.payload) | copy-start | bytes 1769476
  35.6 2.0 %collective-permute-start.4 = (bf16[288,1024]{1,0:T(8,128)(2,1)S(1)}, bf16[288,1024]{1,0:T(8,128)(2,1)S(1)}, u32[]{:S(2)}, u32[]{:S(2)}) collective-permute-start(bf16[288,1024]{1,0:T(8,128)(2,1)S(1)} %collective-permute-done.3.refs_0_.payload), channel_id=1, source_target_pairs={{0,4},{4,0},{8,12},{12,8},{16,20},{20,16},{24,28},{28,24},{1,5},{5... | collective-permute-start | bytes 1769480 | tf_op jit(solution)/shard_map/ppermute | solution.py:455
  35.6 9.9 %collective-permute-start.6 = (bf16[288,1024]{1,0:T(8,128)(2,1)S(1)}, bf16[288,1024]{1,0:T(8,128)(2,1)S(1)}, u32[]{:S(2)}, u32[]{:S(2)}) collective-permute-start(bf16[288,1024]{1,0:T(8,128)(2,1)S(1)} %collective-permute-done.3.refs_0_.payload), channel_id=1, source_target_pairs={{0,16},{4,12},{8,24},{12,4},{16,0},{20,28},{24,8},{28,20},{1,17},{... | collective-permute-start | bytes 1769480 | tf_op jit(solution)/shard_map/ppermute | solution.py:459
  45.5 2.0 %collective-permute-start.7 = (bf16[288,1024]{1,0:T(8,128)(2,1)S(1)}, bf16[288,1024]{1,0:T(8,128)(2,1)S(1)}, u32[]{:S(2)}, u32[]{:S(2)}) collective-permute-start(bf16[288,1024]{1,0:T(8,128)(2,1)S(1)} %collective-permute-done.6.refs_0_.payload), channel_id=1, source_target_pairs={{0,4},{4,0},{8,12},{12,8},{16,20},{20,16},{24,28},{28,24},{1,5},{5... | collective-permute-start | bytes 1769480 | tf_op jit(solution)/shard_map/ppermute | solution.py:455
  45.5 9.9 %collective-permute-start.9 = (bf16[288,1024]{1,0:T(8,128)(2,1)S(1)}, bf16[288,1024]{1,0:T(8,128)(2,1)S(1)}, u32[]{:S(2)}, u32[]{:S(2)}) collective-permute-start(bf16[288,1024]{1,0:T(8,128)(2,1)S(1)} %copy-done.4), channel_id=1, source_target_pairs={{0,16},{4,12},{8,24},{12,4},{16,0},{20,28},{24,8},{28,20},{1,17},{... | collective-permute-start | bytes 1769480 | tf_op jit(solution)/shard_map/ppermute | solution.py:459
  51.0 1.6 %collective-permute-start.8 = (bf16[128,1024]{1,0:T(8,128)(2,1)S(1)}, bf16[128,1024]{1,0:T(8,128)(2,1)S(1)}, u32[]{:S(2)}, u32[]{:S(2)}) collective-permute-start(bf16[128,1024]{1,0:T(8,128)(2,1)S(1)} %get-tuple-element.46), channel_id=1, source_target_pairs={{0,4},{4,0},{8,12},{12,8},{16,20},{20,16},{24,28},{28,24},{1,5},{5... | collective-permute-start | bytes 786440 | tf_op jit(solution)/shard_map/ppermute | solution.py:455
  55.4 2.0 %collective-permute-start.10 = (bf16[288,1024]{1,0:T(8,128)(2,1)S(1)}, bf16[288,1024]{1,0:T(8,128)(2,1)S(1)}, u32[]{:S(2)}, u32[]{:S(2)}) collective-permute-start(bf16[288,1024]{1,0:T(8,128)(2,1)S(1)} %collective-permute-done.9.refs_0_.payload), channel_id=1, source_target_pairs={{0,4},{4,0},{8,12},{12,8},{16,20},{20,16},{24,28},{28,24},{1,5},{5... | collective-permute-start | bytes 1769480 | tf_op jit(solution)/shard_map/ppermute | solution.py:455
  55.4 9.2 %collective-permute-start.12 = (bf16[256,1024]{1,0:T(8,128)(2,1)S(1)}, bf16[256,1024]{1,0:T(8,128)(2,1)S(1)}, u32[]{:S(2)}, u32[]{:S(2)}) collective-permute-start(bf16[256,1024]{1,0:T(8,128)(2,1)S(1)} %combine.3), channel_id=1, source_target_pairs={{0,16},{4,12},{8,24},{12,4},{16,0},{20,28},{24,8},{28,20},{1,17},{... | collective-permute-start | bytes 1572872 | tf_op jit(solution)/shard_map/ppermute | solution.py:459
  61.1 7.8 %copy-start.5 = (bf16[256,1024]{1,0:T(8,128)(2,1)S(1)}, bf16[256,1024]{1,0:T(8,128)(2,1)}, u32[]{:S(2)}) copy-start(bf16[256,1024]{1,0:T(8,128)(2,1)} %get-tuple-element.39.resid) | copy-start | bytes 1572868
  61.1 1.6 %collective-permute-start.11 = (bf16[128,1024]{1,0:T(8,128)(2,1)S(1)}, bf16[128,1024]{1,0:T(8,128)(2,1)S(1)}, u32[]{:S(2)}, u32[]{:S(2)}) collective-permute-start(bf16[128,1024]{1,0:T(8,128)(2,1)S(1)} %get-tuple-element.50), channel_id=1, source_target_pairs={{0,4},{4,0},{8,12},{12,8},{16,20},{20,16},{24,28},{28,24},{1,5},{5... | collective-permute-start | bytes 786440 | tf_op jit(solution)/shard_map/ppermute | solution.py:455
  61.3 3.3 %collective-permute-start.5 = (bf16[128,1024]{1,0:T(8,128)(2,1)S(1)}, bf16[128,1024]{1,0:T(8,128)(2,1)S(1)}, u32[]{:S(2)}, u32[]{:S(2)}) collective-permute-start(bf16[128,1024]{1,0:T(8,128)(2,1)S(1)} %get-tuple-element.43), channel_id=1, source_target_pairs={{0,4},{4,0},{8,12},{12,8},{16,20},{20,16},{24,28},{28,24},{1,5},{5... | collective-permute-start | bytes 786440 | tf_op jit(solution)/shard_map/ppermute | solution.py:455
  65.8 13.6 %collective-permute-start.14 = (bf16[256,1024]{1,0:T(8,128)(2,1)S(1)}, bf16[256,1024]{1,0:T(8,128)(2,1)S(1)}, u32[]{:S(2)}, u32[]{:S(2)}) collective-permute-start(bf16[256,1024]{1,0:T(8,128)(2,1)S(1)} %combine.5), channel_id=1, source_target_pairs={{0,8},{4,20},{8,0},{12,28},{16,24},{20,4},{24,16},{28,12},{1,9},{5... | collective-permute-start | bytes 1572872 | tf_op jit(solution)/shard_map/ppermute | solution.py:459
  67.3 12.1 %collective-permute-start.15 = (bf16[256,1024]{1,0:T(8,128)(2,1)S(1)}, bf16[256,1024]{1,0:T(8,128)(2,1)S(1)}, u32[]{:S(2)}, u32[]{:S(2)}) collective-permute-start(bf16[256,1024]{1,0:T(8,128)(2,1)S(1)} %combine.4), channel_id=1, source_target_pairs={{0,16},{4,12},{8,24},{12,4},{16,0},{20,28},{24,8},{28,20},{1,17},{... | collective-permute-start | bytes 1572872 | tf_op jit(solution)/shard_map/ppermute | solution.py:459
  67.3 1.5 %collective-permute-start.13 = (bf16[128,1024]{1,0:T(8,128)(2,1)S(1)}, bf16[128,1024]{1,0:T(8,128)(2,1)S(1)}, u32[]{:S(2)}, u32[]{:S(2)}) collective-permute-start(bf16[128,1024]{1,0:T(8,128)(2,1)S(1)} %get-tuple-element.52), channel_id=1, source_target_pairs={{0,4},{4,0},{8,12},{12,8},{16,20},{20,16},{24,28},{28,24},{1,5},{5... | collective-permute-start | bytes 786440 | tf_op jit(solution)/shard_map/ppermute | solution.py:455
  (2 other events, 5.6 us)

commit v5 on v4

--- a/solution.py
+++ b/solution.py
@@ -126,20 +126,12 @@
     )(*args)
 
 
-def edge_kernel(live, q, before, behind, tops, sums, gain, acc_far, x_far, w_far, *rest):
-    meta = rest[0] if len(rest) == 9 else None
-    resid, payload = rest[-8:-6]
-    bias, att, acc, x, w, sems = rest[-6:]
+def edge_kernel(live, q, before, behind, tops, sums, gain, acc, x, w, *rest):
+    meta = rest[0] if len(rest) == 5 else None
+    resid, payload = rest[-4:-2]
+    bias, att = rest[-2:]
     step = 2 * HD
     pairs = HEADS // 2
-    fetches = []
-    for pair in range(pairs):
-        span = pl.ds(pair * step, step)
-        fetches.append((acc_far.at[span], acc.at[span]))
-    fetches += [(x_far, x), (w_far, w)]
-    fetches = [pltpu.make_async_copy(a, b, sems.at[i]) for i, (a, b) in enumerate(fetches)]
-    for fetch in fetches:
-        fetch.start()
     rows = q.shape[0] // 2
     wide = before.shape[0] // 2
     halos = (before, behind)
@@ -164,8 +156,6 @@
         total = jnp.concatenate([sums[b, span] for b in both], axis=1) * shrink
         total = total + jnp.sum(p, axis=0, keepdims=True)
         weights.append((p.astype(BF16), shrink, 1.0 / total))
-    for pair in range(pairs):
-        fetches[pair].wait()
     for (pair, half), (p, shrink, inverse) in zip(cells, weights):
         span = slice(half * rows, (half + 1) * rows)
         cols = slice(pair * step, (pair + 1) * step)
@@ -176,8 +166,6 @@
             value = acc[base : base + HD, span] * shrink[:, at]
             value = value + o[side * HD : (side + 1) * HD, at]
             att[base : base + HD, span] = (value * inverse[:, at]).astype(BF16)
-    fetches[pairs].wait()
-    fetches[pairs + 1].wait()
     for half in range(2):
         span = slice(half * rows, (half + 1) * rows)
         res = x[span, :].astype(F32)
@@ -187,12 +175,13 @@
         res = res.astype(F32)
         square = jnp.mean(res * res, axis=1, keepdims=True)
         normed = (res * lax.rsqrt(square + 1e-06) * gain[...]).astype(BF16)
-        start = half * payload.shape[0] // 2
-        payload[start : start + rows, :] = normed
-        if meta is not None:
-            payload[start + rows : start + rows + META, :] = jnp.broadcast_to(
-                meta[half : half + 1, :], (META, meta.shape[1])
-            )
+        payload[span, :] = normed
+    if meta is not None:
+        copies = [
+            jnp.broadcast_to(meta[half : half + 1, :], (META // 2, meta.shape[1]))
+            for half in range(2)
+        ]
+        payload[2 * rows :, :] = jnp.concatenate(copies, axis=0)
 
 
 def edge(live, q, before, behind, acc, tops, sums, x, w, gain, meta):
@@ -200,24 +189,20 @@
     wide = before.shape[0] // 2
     args = [live, q, before, behind, tops, sums, gain, acc, x, w]
     args += [] if meta is None else [meta]
-    specs = [SMEM] + [VMEM] * 6 + [ANY] * 3 + ([] if meta is None else [VMEM])
+    specs = [SMEM] + [VMEM] * 9 + ([] if meta is None else [VMEM])
     extra = 0 if meta is None else META
     flat = [
         jax.ShapeDtypeStruct((2 * rows, model), BF16),
-        jax.ShapeDtypeStruct((2 * (rows + extra), model), BF16),
+        jax.ShapeDtypeStruct((2 * rows + extra, model), BF16),
     ]
     return pl.pallas_call(
         edge_kernel,
         in_specs=specs,
         out_specs=[VMEM] * 2,
-        out_shape=[pltpu.HBM(o.shape, o.dtype) for o in flat],
+        out_shape=flat,
         scratch_shapes=[
             pltpu.VMEM((2, wide, 2 * rows), F32),
             pltpu.VMEM((model, 2 * rows), BF16),
-            pltpu.VMEM(acc.shape, acc.dtype),
-            pltpu.VMEM(x.shape, x.dtype),
-            pltpu.VMEM(w.shape, w.dtype),
-            pltpu.SemaphoreType.DMA((HEADS // 2 + 2,)),
         ],
         compiler_params=pltpu.CompilerParams(vmem_limit_bytes=12 * MIB),
         cost_estimate=cost(
@@ -228,8 +213,8 @@
 
 
 def meta_items(payload, block, rows):
-    base = block * (rows + META) + rows
-    meta = payload[base : base + META, :].astype(F32)
+    meta = payload[2 * rows :, :].astype(F32)
+    meta = meta[block * META // 2 : (block + 1) * META // 2, :]
     return [meta[:, i * rows : (i + 1) * rows] for i in range(8)]
 
 
@@ -254,7 +239,7 @@
     for i, (a, b) in enumerate(named):
         gate = jnp.where(a, item[2] + item[3] + item[4], F32(0.0))
         gate = gate + jnp.where(b, item[5] + item[6] + item[7], F32(0.0))
-        result.append((slot == ranks[i * META : i * META + 1, :], gate[:1, :]))
+        result.append((slot == ranks[i * META // 2 : i * META // 2 + 1, :], gate[:1, :]))
     return result
 
 
@@ -271,15 +256,14 @@
     ranks = slot_rows(jnp.concatenate(hits, axis=0))
     slot = lax.broadcasted_iota(jnp.int32, (2 * capacity, rows), 0).astype(F32)
     for g in range(groups):
-        first = ranks[2 * g * META : 2 * g * META + 1, :]
-        second = ranks[(2 * g + 1) * META : (2 * g + 1) * META + 1, :]
+        first = ranks[g * META : g * META + 1, :]
+        second = ranks[g * META + META // 2 : g * META + META // 2 + 1, :]
         second = jnp.where(second >= 0, second + capacity, F32(-1.0))
         hot = jnp.concatenate([slot == first, slot == second], axis=1)
         hot = jnp.where(hot, F32(1.0), F32(0.0)).astype(BF16)
         tokens = []
         for array, block in order[2 * g : 2 * g + 2]:
-            base = block * (rows + META)
-            tokens.append(payloads[array][base : base + rows, :])
+            tokens.append(payloads[array][block * rows : (block + 1) * rows, :])
         picked = jnp.dot(hot, jnp.concatenate(tokens, axis=0), preferred_element_type=F32)
         x[2 * g * capacity : (2 * g + 2) * capacity, :] = picked.astype(BF16)
     for at in range(0, width, step):
@@ -344,68 +328,45 @@
 def combine_kernel(rows, capacity, me, payload, outs_me, outs_sib, *refs):
     result = refs[-1]
     both = (me[0].astype(F32), me[1].astype(F32))
-    for block in range(payload.shape[0] // (rows + META)):
+    for block in range(2):
         span = slice(block * capacity, (block + 1) * capacity)
         total = spread(payload, block, rows, capacity, both, (outs_me[span, :], outs_sib[span, :]))
         at = slice(block * rows, (block + 1) * rows)
         if len(refs) == 2:
             total = total + refs[0][at, :].astype(F32)
-        result[at, :] = total.astype(BF16)
-
-
-def combine(me, payload, outs_me, outs_sib, carry, rows, capacity):
-    blocks, model = payload.shape[0] // (rows + META), payload.shape[1]
-    args = [me, payload, outs_me, outs_sib] + ([] if carry is None else [carry])
-    outs = [jax.ShapeDtypeStruct((blocks * rows, model), BF16)]
+        result[at, :] = total.astype(result.dtype)
+
+
+def combine(me, payload, outs_me, outs_sib, rows, capacity, start=None, dtype=BF16):
+    model = payload.shape[1]
+    args = [me, payload, outs_me, outs_sib] + ([] if start is None else [start])
+    out = jax.ShapeDtypeStruct((2 * rows, model), dtype)
     return pl.pallas_call(
         functools.partial(combine_kernel, rows, capacity),
         in_specs=[SMEM] + [VMEM] * (len(args) - 1),
         out_specs=VMEM,
-        out_shape=outs[0],
+        out_shape=out,
         compiler_params=pltpu.CompilerParams(vmem_limit_bytes=12 * MIB),
-        cost_estimate=cost(8 * blocks * rows * capacity * model, 0, args, outs),
+        cost_estimate=cost(8 * out.size * capacity, 0, args, [out]),
         name="combine",
     )(*args)
 
 
-def base_kernel(rows, capacity, me, payload, resid, outs_me, outs_sib, result):
-    both = (me[0].astype(F32), me[1].astype(F32))
-    for block in range(payload.shape[0] // (rows + META)):
-        span = slice(block * capacity, (block + 1) * capacity)
-        total = spread(payload, block, rows, capacity, both, (outs_me[span, :], outs_sib[span, :]))
-        at = slice(block * rows, (block + 1) * rows)
-        result[at, :] = total + resid[at, :].astype(F32)
-
-
-def base(me, payload, resid, outs_me, outs_sib, rows, capacity):
-    args = [me, payload, resid, outs_me, outs_sib]
-    out = jax.ShapeDtypeStruct(resid.shape, F32)
+def add_kernel(a, b, result):
+    result[...] = (a[...].astype(F32) + b[...].astype(F32)).astype(result.dtype)
+
+
+def add(a, b, dtype):
+    out = jax.ShapeDtypeStruct(a.shape, dtype)
     return pl.pallas_call(
-        functools.partial(base_kernel, rows, capacity),
-        in_specs=[SMEM] + [VMEM] * 4,
+        add_kernel,
+        in_specs=[VMEM] * 2,
         out_specs=VMEM,
         out_shape=out,
         compiler_params=pltpu.CompilerParams(vmem_limit_bytes=12 * MIB),
-        cost_estimate=cost(8 * resid.size * capacity, 0, args, [out]),
-        name="base",
-    )(*args)
-
-
-def finish_kernel(total, first, second, out):
-    out[...] = (total[...] + first[...].astype(F32) + second[...].astype(F32)).astype(BF16)
-
-
-def finish(total, first, second):
-    args = [total, first, second]
-    return pl.pallas_call(
-        finish_kernel,
-        in_specs=[VMEM] * 3,
-        out_specs=VMEM,
-        out_shape=jax.ShapeDtypeStruct(first.shape, first.dtype),
-        compiler_params=pltpu.CompilerParams(vmem_limit_bytes=12 * MIB),
-        cost_estimate=cost(3 * total.size, 0, args, args[1:2]),
-        name="finish",
-    )(*args)
+        cost_estimate=cost(out.size, 0, (a, b), [out]),
+        name="add",
+    )(a, b)
 
 
 def expert_rows(token_rows, gate_mat, up_mat, down_mat):
@@ -474,22 +435,25 @@
     sib = swap(payload, 1)
     first = swap_by_core(payload, (2, 4))
     out_own = evaluate(payload, sib)
-    (first,) = after(out_own[0], first)
+    total = combine(me, payload, *out_own, start=resid, dtype=F32, **sizes)
+    (first,) = after(total, first)
     diag = swap_by_core(first, (4, 2))
     out_first = evaluate(first, swap(first, 1))
     (diag,) = after(out_first[0], diag)
     second = swap_by_core(*after(diag, payload), (4, 2))
+    (diag,) = after(out_first[0], diag)
     out_diag = evaluate(diag, swap(diag, 1))
-    sum_diag = combine(me, diag, *out_diag, None, **sizes)
+    sum_diag = combine(me, diag, *out_diag, **sizes)
     carry = swap_by_core(sum_diag, (4, 2))
     (second,) = after(sum_diag, second)
     out_second = evaluate(second, swap(second, 1))
-    sum_second = combine(me, second, *out_second, None, **sizes)
+    sum_first = combine(
+        me, first, *out_first[:1], *after(out_second[0], *out_first[1:]), dtype=F32, **sizes
+    )
+    sum_second = combine(me, second, out_second[0], *after(sum_first, out_second[1]), **sizes)
     back_second = swap_by_core(sum_second, (4, 2))
-    sum_first = combine(me, first, *out_first, *after(sum_second, carry), **sizes)
-    back_first = swap_by_core(sum_first, (2, 4))
-    total = base(me, payload, resid, *after(sum_first, *out_own), **sizes)
-    return finish(total, back_first, back_second)
+    back_first = swap_by_core(add(sum_first, *after(sum_second, carry), BF16), (2, 4))
+    return add(add(total, back_second, F32), back_first, BF16)
 
 
 def local(

time: 80.7 us -> 75.1 us (0.931)
  waiting for transfers between devices: 30 us -> 26.2 us
  Pallas kernels: 31.3 us -> 28.5 us
  starting transfers between devices: 16 us -> 18.1 us
  local copies, waits for them, and re-layouts: 1.89 us -> 0.82 us
    ppermute x8, waiting for transfers between devices: 10.3 us -> 6.98 us  [swap(): return lax.ppermute(array, 'tile', [(i, i ^ bit) for i in range(8)])]
    pallas_call x1, Pallas kernels: 5.66 us -> 2.8 us  [edge(): pl.pallas_call(edge_kernel, in_specs=specs, out_specs=[VMEM] * 2, out_sha...]
    ppermute x8, starting transfers between devices: 9.26 us -> 11 us  [swap(): return lax.ppermute(array, 'tile', [(i, i ^ bit) for i in range(8)])]
    pallas_call x3 -> x4, Pallas kernels: 3.61 us -> 4.81 us  [combine(): pl.pallas_call(functools.partial(combine_kernel, rows, capacity), in_spec...]
    pallas_call x2 -> x3, Pallas kernels: 2.2 us -> 1.06 us  [add(): pl.pallas_call(add_kernel, in_specs=[VMEM] * 2, out_specs=VMEM, out_shape...]
    unnamed x22 -> x16, local copies, waits for them, and re-layouts: 1.13 us -> 0.05 us
  transfers between devices with their start and end apart: 16 -> 16, of which waited for: 12 -> 12; matrix products, arithmetic and copies ran while one was open for 2% -> 2% of each run, Pallas kernels for 28% -> 32%
where the time goes in v5:
time: 75.1 us; the launch traced here: 74.8 us
  Pallas kernels  28.5 us (38%)
  waiting for transfers between devices  26.2 us (35%)
  starting transfers between devices  18.1 us (24%)
  other arithmetic  1 us (1%)
  local copies, waits for them, and re-layouts  0.82 us (1%)
    ppermute x6, waiting for transfers between devices, swap_by_core(): return lax.ppermute(array, 'tile', [(i, i ^ bits[i % 2]) for i in range(8)])  19.2 us
    pallas_call x4, Pallas kernels, experts(): pl.pallas_call(functools.partial(experts_kernel, order, rows, capacity),...  14.1 us
    ppermute x8, starting transfers between devices, swap(): return lax.ppermute(array, 'tile', [(i, i ^ bit) for i in range(8)])  11 us
    ppermute x8, waiting for transfers between devices, swap(): return lax.ppermute(array, 'tile', [(i, i ^ bit) for i in range(8)])  6.98 us
    pallas_call x4, Pallas kernels, combine(): pl.pallas_call(functools.partial(combine_kernel, rows, capacity), in_spec...  4.81 us
    pallas_call x1, Pallas kernels, interior(): pl.pallas_call(interior_kernel, in_specs=[VMEM] * 3, out_specs=[VMEM] * 3...  4.51 us
    ppermute x6, starting transfers between devices, swap_by_core(): return lax.ppermute(array, 'tile', [(i, i ^ bits[i % 2]) for i in range(8)])  3.39 us
    pallas_call x1, Pallas kernels, edge(): pl.pallas_call(edge_kernel, in_specs=specs, out_specs=[VMEM] * 2, out_sha...  2.8 us
  transfers between devices with their start and end apart: 16, of which 12 were waited for; matrix products, arithmetic and copies ran while one was open for 2% of the time, Pallas kernels for 32%

profile of v5, /device:TPU:0, one launch (start us, length us, event | category | flops | bytes accessed | tf_op | source)
XLA Modules:
  0.0 74.8 jit_solution(18045188855554435400)
XLA Ops:
  0.2 1.2 %pack.1 = (bf16[256,1024]{1,0:T(8,128)(2,1)S(1)}, bf16[256,1024]{1,0:T(8,128)(2,1)S(1)}) custom-call(bf16[256,1024]{1,0:T(8,128)(2,1)} %k.1, bf16[256,1024]{1,0:T(8,128)(2,1)} %v.3), custom_call_target="tpu_custom_call" | custom-call | bytes 2097152 | tf_op jit(solution)/shard_map/pack/pallas_call | solution.py:81
  1.4 2.4 %collective-permute-start = (bf16[256,1024]{1,0:T(8,128)(2,1)S(1)}, bf16[256,1024]{1,0:T(8,128)(2,1)S(1)}, u32[]{:S(2)}, u32[]{:S(2)}) collective-permute-start(bf16[256,1024]{1,0:T(8,128)(2,1)S(1)} %get-tuple-element.34), channel_id=1, source_target_pairs={{0,4},{4,8},{8,12},{12,16},{16,20},{20,24},{24,28},{1,5},{5,9},{9,... | collective-permute-start | bytes 1572872 | tf_op jit(solution)/shard_map/ppermute | solution.py:484
  3.8 1.3 %collective-permute-start.1 = (bf16[256,1024]{1,0:T(8,128)(2,1)S(1)}, bf16[256,1024]{1,0:T(8,128)(2,1)S(1)}, u32[]{:S(2)}, u32[]{:S(2)}) collective-permute-start(bf16[256,1024]{1,0:T(8,128)(2,1)S(1)} %get-tuple-element.35), channel_id=1, source_target_pairs={{4,0},{8,4},{12,8},{16,12},{20,16},{24,20},{28,24},{5,1},{9,5},{13... | collective-permute-start | bytes 1572872 | tf_op jit(solution)/shard_map/ppermute | solution.py:485
  6.8 4.5 %interior.1 = (f32[1024,256]{1,0:T(8,128)S(1)}, f32[16,256]{1,0:T(8,128)S(1)}, f32[16,256]{1,0:T(8,128)S(1)}) custom-call(bf16[256,1024]{1,0:T(8,128)(2,1)} %q.3, bf16[256,1024]{1,0:T(8,128)(2,1)} %k.1, bf16[256,1024]{1,0:T(8,128)(2,1)} %v.3), custom_call_target="tpu_custom_call" | custom-call | flops 8053063680 | bytes 2654208 | tf_op jit(solution)/shard_map/interior/pallas_call | solution.py:117
  11.4 2.8 %edge.1 = (bf16[256,1024]{1,0:T(8,128)(2,1)S(1)}, bf16[272,1024]{1,0:T(8,128)(2,1)S(1)}) custom-call(s32[2]{0:T(128)S(1)} %add_convert_fusion.live, bf16[256,1024]{1,0:T(8,128)(2,1)S(1)} %copy-done.4, bf16[256,1024]{1,0:T(8,128)(2,1)S(1)} %collective-permute-done.before, bf16[256,1024]{1,0:T(8,128)(2,1)S(1)} %collective-permute-done.1.behind, ...), custom_call_target="tpu_custom_call" | custom-call | flops 20132659200 | bytes 6365192 | tf_op jit(solution)/shard_map/edge/pallas_call | solution.py:198
  14.2 8.5 %collective-permute-start.2 = (bf16[272,1024]{1,0:T(8,128)(2,1)S(1)}, bf16[272,1024]{1,0:T(8,128)(2,1)S(1)}, u32[]{:S(2)}, u32[]{:S(2)}) collective-permute-start(bf16[272,1024]{1,0:T(8,128)(2,1)S(1)} %get-tuple-element.49.refs_0_.payload), channel_id=1, source_target_pairs={{0,4},{4,0},{8,12},{12,8},{16,20},{20,16},{24,28},{28,24},{1,5},{5... | collective-permute-start | bytes 1671176 | tf_op jit(solution)/shard_map/ppermute | solution.py:416
  22.6 1.5 %collective-permute-start.4 = (bf16[272,1024]{1,0:T(8,128)(2,1)S(1)}, bf16[272,1024]{1,0:T(8,128)(2,1)S(1)}, u32[]{:S(2)}, u32[]{:S(2)}) collective-permute-start(bf16[272,1024]{1,0:T(8,128)(2,1)S(1)} %get-tuple-element.49.refs_0_.payload), channel_id=1, source_target_pairs={{0,8},{4,20},{8,0},{12,28},{16,24},{20,4},{24,16},{28,12},{1,9},{5... | collective-permute-start | bytes 1671176 | tf_op jit(solution)/shard_map/ppermute | solution.py:420
  24.2 3.5 %experts_256.4 = (bf16[128,1024]{1,0:T(8,128)(2,1)S(1)}, bf16[128,1024]{1,0:T(8,128)(2,1)S(1)}) custom-call(s32[2]{0:T(128)S(1)} %pad_add_fusion.me, bf16[272,1024]{1,0:T(8,128)(2,1)S(1)} %get-tuple-element.49.refs_0_.payload, bf16[272,1024]{1,0:T(8,128)(2,1)S(1)} %collective-permute-done.2.refs_1_, bf16[1024,1408]{1,0:T(8,128)(2,1)S(1)} %bitcast.17, ...), custom_call_target="tpu_custom_call" | custom-call | flops 2214592512 | bytes 10289160 | tf_op jit(solution)/shard_map/experts_256/pallas_call | solution.py:296
  28.2 1.2 %collective-permute-done.3.outs_sib = bf16[128,1024]{1,0:T(8,128)(2,1)S(1)} collective-permute-done((bf16[128,1024]{1,0:T(8,128)(2,1)S(1)}, bf16[128,1024]{1,0:T(8,128)(2,1)S(1)}, u32[]{:S(2)}, u32[]{:S(2)}) %collective-permute-start.3) | collective-permute-done | bytes 262176 | tf_op jit(solution)/shard_map/ppermute | solution.py:416
  29.3 1.2 %combine.4.a = f32[256,1024]{1,0:T(8,128)S(1)} custom-call(s32[2]{0:T(128)S(1)} %pad_add_fusion.me, bf16[272,1024]{1,0:T(8,128)(2,1)S(1)} %get-tuple-element.49.refs_0_.payload, bf16[128,1024]{1,0:T(8,128)(2,1)S(1)} %get-tuple-element.40.outs_me, bf16[128,1024]{1,0:T(8,128)(2,1)S(1)} %collective-permute-done.3.outs_sib, ...), custom_call_target="tpu_custom_call" | custom-call | flops 134217728 | bytes 2654216 | tf_op jit(solution)/shard_map/combine/pallas_call | solution.py:344
  30.5 1.6 %collective-permute-done.4.refs_0_.payload = bf16[272,1024]{1,0:T(8,128)(2,1)S(1)} collective-permute-done((bf16[272,1024]{1,0:T(8,128)(2,1)S(1)}, bf16[272,1024]{1,0:T(8,128)(2,1)S(1)}, u32[]{:S(2)}, u32[]{:S(2)}) %collective-permute-start.4) | collective-permute-done | bytes 557088 | tf_op jit(solution)/shard_map/ppermute | solution.py:420
  32.2 2.0 %collective-permute-done.5.refs_1_ = bf16[272,1024]{1,0:T(8,128)(2,1)S(1)} collective-permute-done((bf16[272,1024]{1,0:T(8,128)(2,1)S(1)}, bf16[272,1024]{1,0:T(8,128)(2,1)S(1)}, u32[]{:S(2)}, u32[]{:S(2)}) %collective-permute-start.5) | collective-permute-done | bytes 557088 | tf_op jit(solution)/shard_map/ppermute | solution.py:416
  34.1 3.5 %experts_256.5 = (bf16[128,1024]{1,0:T(8,128)(2,1)S(1)}, bf16[128,1024]{1,0:T(8,128)(2,1)S(1)}) custom-call(s32[2]{0:T(128)S(1)} %pad_add_fusion.me, bf16[272,1024]{1,0:T(8,128)(2,1)S(1)} %collective-permute-done.4.refs_0_.payload, bf16[272,1024]{1,0:T(8,128)(2,1)S(1)} %collective-permute-done.5.refs_1_, bf16[1024,1408]{1,0:T(8,128)(2,1)S(1)} %bitcast.18, ...), custom_call_target="tpu_custom_call" | custom-call | flops 2214592512 | bytes 10289160 | tf_op jit(solution)/shard_map/experts_256/pallas_call | solution.py:296
  37.6 4.1 %collective-permute-done.6.refs_0_.payload = bf16[272,1024]{1,0:T(8,128)(2,1)S(1)} collective-permute-done((bf16[272,1024]{1,0:T(8,128)(2,1)S(1)}, bf16[272,1024]{1,0:T(8,128)(2,1)S(1)}, u32[]{:S(2)}, u32[]{:S(2)}) %collective-permute-start.6) | collective-permute-done | bytes 557088 | tf_op jit(solution)/shard_map/ppermute | solution.py:420
  41.7 1.9 %collective-permute-done.7.refs_1_ = bf16[272,1024]{1,0:T(8,128)(2,1)S(1)} collective-permute-done((bf16[272,1024]{1,0:T(8,128)(2,1)S(1)}, bf16[272,1024]{1,0:T(8,128)(2,1)S(1)}, u32[]{:S(2)}, u32[]{:S(2)}) %collective-permute-start.7) | collective-permute-done | bytes 557088 | tf_op jit(solution)/shard_map/ppermute | solution.py:416
  43.7 3.7 %experts_256.6 = (bf16[128,1024]{1,0:T(8,128)(2,1)S(1)}, bf16[128,1024]{1,0:T(8,128)(2,1)S(1)}) custom-call(s32[2]{0:T(128)S(1)} %pad_add_fusion.me, bf16[272,1024]{1,0:T(8,128)(2,1)S(1)} %collective-permute-done.6.refs_0_.payload, bf16[272,1024]{1,0:T(8,128)(2,1)S(1)} %collective-permute-done.7.refs_1_, bf16[1024,1408]{1,0:T(8,128)(2,1)S(1)} %bitcast.19, ...), custom_call_target="tpu_custom_call" | custom-call | flops 2214592512 | bytes 10289160 | tf_op jit(solution)/shard_map/experts_256/pallas_call | solution.py:296
  47.5 1.4 %collective-permute-done.8.outs_sib = bf16[128,1024]{1,0:T(8,128)(2,1)S(1)} collective-permute-done((bf16[128,1024]{1,0:T(8,128)(2,1)S(1)}, bf16[128,1024]{1,0:T(8,128)(2,1)S(1)}, u32[]{:S(2)}, u32[]{:S(2)}) %collective-permute-start.8) | collective-permute-done | bytes 262176 | tf_op jit(solution)/shard_map/ppermute | solution.py:416
  48.9 1.2 %combine.5 = bf16[256,1024]{1,0:T(8,128)(2,1)S(1)} custom-call(s32[2]{0:T(128)S(1)} %pad_add_fusion.me, bf16[272,1024]{1,0:T(8,128)(2,1)S(1)} %collective-permute-done.6.refs_0_.payload, bf16[128,1024]{1,0:T(8,128)(2,1)S(1)} %get-tuple-element.47.outs_me, bf16[128,1024]{1,0:T(8,128)(2,1)S(1)} %collective-permute-done.8.outs_sib), custom_call_target="tpu_custom_call" | custom-call | flops 134217728 | bytes 1605640 | tf_op jit(solution)/shard_map/combine/pallas_call | solution.py:344
  51.3 1.7 %collective-permute-start.11 = (bf16[128,1024]{1,0:T(8,128)(2,1)S(1)}, bf16[128,1024]{1,0:T(8,128)(2,1)S(1)}, u32[]{:S(2)}, u32[]{:S(2)}) collective-permute-start(bf16[128,1024]{1,0:T(8,128)(2,1)S(1)} %get-tuple-element.52), channel_id=1, source_target_pairs={{0,4},{4,0},{8,12},{12,8},{16,20},{20,16},{24,28},{28,24},{1,5},{5... | collective-permute-start | bytes 786440 | tf_op jit(solution)/shard_map/ppermute | solution.py:416
  53.2 3.5 %experts_256.7 = (bf16[128,1024]{1,0:T(8,128)(2,1)S(1)}, bf16[128,1024]{1,0:T(8,128)(2,1)S(1)}) custom-call(s32[2]{0:T(128)S(1)} %pad_add_fusion.me, bf16[272,1024]{1,0:T(8,128)(2,1)S(1)} %collective-permute-done.9.refs_0_.payload, bf16[272,1024]{1,0:T(8,128)(2,1)S(1)} %collective-permute-done.10.refs_1_, bf16[1024,1408]{1,0:T(8,128)(2,1)S(1)} %bitcast.20, ...), custom_call_target="tpu_custom_call" | custom-call | flops 2214592512 | bytes 10289160 | tf_op jit(solution)/shard_map/experts_256/pallas_call | solution.py:296
  56.9 1.2 %combine.6.a = f32[256,1024]{1,0:T(8,128)S(1)} custom-call(s32[2]{0:T(128)S(1)} %pad_add_fusion.me, bf16[272,1024]{1,0:T(8,128)(2,1)S(1)} %collective-permute-done.4.refs_0_.payload, bf16[128,1024]{1,0:T(8,128)(2,1)S(1)} %get-tuple-element.44.outs_me, bf16[128,1024]{1,0:T(8,128)(2,1)S(1)} %collective-permute-done.11.outs_sib), custom_call_target="tpu_custom_call" | custom-call | flops 134217728 | bytes 2129928 | tf_op jit(solution)/shard_map/combine/pallas_call | solution.py:344
  58.3 1.2 %combine.7 = bf16[256,1024]{1,0:T(8,128)(2,1)S(1)} custom-call(s32[2]{0:T(128)S(1)} %pad_add_fusion.me, bf16[272,1024]{1,0:T(8,128)(2,1)S(1)} %collective-permute-done.9.refs_0_.payload, bf16[128,1024]{1,0:T(8,128)(2,1)S(1)} %get-tuple-element.51.outs_me, bf16[128,1024]{1,0:T(8,128)(2,1)S(1)} %collective-permute-done.12.outs_sib), custom_call_target="tpu_custom_call" | custom-call | flops 134217728 | bytes 1605640 | tf_op jit(solution)/shard_map/combine/pallas_call | solution.py:344
  60.5 1.6 %collective-permute-start.15 = (bf16[256,1024]{1,0:T(8,128)(2,1)S(1)}, bf16[256,1024]{1,0:T(8,128)(2,1)S(1)}, u32[]{:S(2)}, u32[]{:S(2)}) collective-permute-start(bf16[256,1024]{1,0:T(8,128)(2,1)S(1)} %add.10), channel_id=1, source_target_pairs={{0,8},{4,20},{8,0},{12,28},{16,24},{20,4},{24,16},{28,12},{1,9},{5... | collective-permute-start | bytes 1572872 | tf_op jit(solution)/shard_map/ppermute | solution.py:420
  62.1 11.7 %collective-permute-done.13.b = bf16[256,1024]{1,0:T(8,128)(2,1)S(1)} collective-permute-done((bf16[256,1024]{1,0:T(8,128)(2,1)S(1)}, bf16[256,1024]{1,0:T(8,128)(2,1)S(1)}, u32[]{:S(2)}, u32[]{:S(2)}) %collective-permute-start.13) | collective-permute-done | bytes 524320 | tf_op jit(solution)/shard_map/ppermute | solution.py:420
  (48 shorter events, 6.3 us)
Async XLA Ops:
  1.4 9.9 %collective-permute-start = (bf16[256,1024]{1,0:T(8,128)(2,1)S(1)}, bf16[256,1024]{1,0:T(8,128)(2,1)S(1)}, u32[]{:S(2)}, u32[]{:S(2)}) collective-permute-start(bf16[256,1024]{1,0:T(8,128)(2,1)S(1)} %get-tuple-element.34), channel_id=1, source_target_pairs={{0,4},{4,8},{8,12},{12,16},{16,20},{20,24},{24,28},{1,5},{5,9},{9,... | collective-permute-start | bytes 1572872 | tf_op jit(solution)/shard_map/ppermute | solution.py:484
  3.8 7.5 %collective-permute-start.1 = (bf16[256,1024]{1,0:T(8,128)(2,1)S(1)}, bf16[256,1024]{1,0:T(8,128)(2,1)S(1)}, u32[]{:S(2)}, u32[]{:S(2)}) collective-permute-start(bf16[256,1024]{1,0:T(8,128)(2,1)S(1)} %get-tuple-element.35), channel_id=1, source_target_pairs={{4,0},{8,4},{12,8},{16,12},{20,16},{24,20},{28,24},{5,1},{9,5},{13... | collective-permute-start | bytes 1572872 | tf_op jit(solution)/shard_map/ppermute | solution.py:485
  6.7 4.6 %copy-start.3 = (bf16[1024,1024]{1,0:T(8,128)(2,1)S(1)}, bf16[1024,1024]{1,0:T(8,128)(2,1)}, u32[]{:S(2)}) copy-start(bf16[1024,1024]{1,0:T(8,128)(2,1)} %w.1) | copy-start | bytes 6291460
  6.7 4.6 %copy-start.4 = (bf16[256,1024]{1,0:T(8,128)(2,1)S(1)}, bf16[256,1024]{1,0:T(8,128)(2,1)}, u32[]{:S(2)}) copy-start(bf16[256,1024]{1,0:T(8,128)(2,1)} %q.3) | copy-start | bytes 1572868
  6.7 4.6 %copy-start.5 = (bf16[256,1024]{1,0:T(8,128)(2,1)S(1)}, bf16[256,1024]{1,0:T(8,128)(2,1)}, u32[]{:S(2)}) copy-start(bf16[256,1024]{1,0:T(8,128)(2,1)} %x.1) | copy-start | bytes 1572868
  6.7 4.6 %copy-start.6 = (f32[1024]{0:T(1024)S(1)}, f32[1024]{0:T(1024)}, u32[]{:S(2)}) copy-start(f32[1024]{0:T(1024)} %param.16) | copy-start | bytes 12292
  11.3 12.9 %copy-start = (bf16[1,1024,1408]{2,1,0:T(8,128)(2,1)S(1)}, bf16[1,1024,1408]{2,1,0:T(8,128)(2,1)}, u32[]{:S(2)}) copy-start(bf16[1,1024,1408]{2,1,0:T(8,128)(2,1)} %param.19) | copy-start | bytes 8650756
  11.3 12.9 %copy-start.1 = (bf16[1,1024,1408]{2,1,0:T(8,128)(2,1)S(1)}, bf16[1,1024,1408]{2,1,0:T(8,128)(2,1)}, u32[]{:S(2)}) copy-start(bf16[1,1024,1408]{2,1,0:T(8,128)(2,1)} %param.20) | copy-start | bytes 8650756
  11.4 12.9 %copy-start.2 = (bf16[1,1408,1024]{2,1,0:T(8,128)(2,1)S(1)}, bf16[1,1408,1024]{2,1,0:T(8,128)(2,1)}, u32[]{:S(2)}) copy-start(bf16[1,1408,1024]{2,1,0:T(8,128)(2,1)} %param.21) | copy-start | bytes 8650756
  14.2 10.1 %collective-permute-start.2 = (bf16[272,1024]{1,0:T(8,128)(2,1)S(1)}, bf16[272,1024]{1,0:T(8,128)(2,1)S(1)}, u32[]{:S(2)}, u32[]{:S(2)}) collective-permute-start(bf16[272,1024]{1,0:T(8,128)(2,1)S(1)} %get-tuple-element.49.refs_0_.payload), channel_id=1, source_target_pairs={{0,4},{4,0},{8,12},{12,8},{16,20},{20,16},{24,28},{28,24},{1,5},{5... | collective-permute-start | bytes 1671176 | tf_op jit(solution)/shard_map/ppermute | solution.py:416
  22.6 9.5 %collective-permute-start.4 = (bf16[272,1024]{1,0:T(8,128)(2,1)S(1)}, bf16[272,1024]{1,0:T(8,128)(2,1)S(1)}, u32[]{:S(2)}, u32[]{:S(2)}) collective-permute-start(bf16[272,1024]{1,0:T(8,128)(2,1)S(1)} %get-tuple-element.49.refs_0_.payload), channel_id=1, source_target_pairs={{0,8},{4,20},{8,0},{12,28},{16,24},{20,4},{24,16},{28,12},{1,9},{5... | collective-permute-start | bytes 1671176 | tf_op jit(solution)/shard_map/ppermute | solution.py:420
  27.7 1.6 %collective-permute-start.3 = (bf16[128,1024]{1,0:T(8,128)(2,1)S(1)}, bf16[128,1024]{1,0:T(8,128)(2,1)S(1)}, u32[]{:S(2)}, u32[]{:S(2)}) collective-permute-start(bf16[128,1024]{1,0:T(8,128)(2,1)S(1)} %get-tuple-element.41), channel_id=1, source_target_pairs={{0,4},{4,0},{8,12},{12,8},{16,20},{20,16},{24,28},{28,24},{1,5},{5... | collective-permute-start | bytes 786440 | tf_op jit(solution)/shard_map/ppermute | solution.py:416
  32.2 2.0 %collective-permute-start.5 = (bf16[272,1024]{1,0:T(8,128)(2,1)S(1)}, bf16[272,1024]{1,0:T(8,128)(2,1)S(1)}, u32[]{:S(2)}, u32[]{:S(2)}) collective-permute-start(bf16[272,1024]{1,0:T(8,128)(2,1)S(1)} %collective-permute-done.4.refs_0_.payload), channel_id=1, source_target_pairs={{0,4},{4,0},{8,12},{12,8},{16,20},{20,16},{24,28},{28,24},{1,5},{5... | collective-permute-start | bytes 1671176 | tf_op jit(solution)/shard_map/ppermute | solution.py:416
  32.2 9.5 %collective-permute-start.6 = (bf16[272,1024]{1,0:T(8,128)(2,1)S(1)}, bf16[272,1024]{1,0:T(8,128)(2,1)S(1)}, u32[]{:S(2)}, u32[]{:S(2)}) collective-permute-start(bf16[272,1024]{1,0:T(8,128)(2,1)S(1)} %collective-permute-done.4.refs_0_.payload), channel_id=1, source_target_pairs={{0,16},{4,12},{8,24},{12,4},{16,0},{20,28},{24,8},{28,20},{1,17},{... | collective-permute-start | bytes 1671176 | tf_op jit(solution)/shard_map/ppermute | solution.py:420
  41.7 2.0 %collective-permute-start.7 = (bf16[272,1024]{1,0:T(8,128)(2,1)S(1)}, bf16[272,1024]{1,0:T(8,128)(2,1)S(1)}, u32[]{:S(2)}, u32[]{:S(2)}) collective-permute-start(bf16[272,1024]{1,0:T(8,128)(2,1)S(1)} %collective-permute-done.6.refs_0_.payload), channel_id=1, source_target_pairs={{0,4},{4,0},{8,12},{12,8},{16,20},{20,16},{24,28},{28,24},{1,5},{5... | collective-permute-start | bytes 1671176 | tf_op jit(solution)/shard_map/ppermute | solution.py:416
  41.7 9.5 %collective-permute-start.9 = (bf16[272,1024]{1,0:T(8,128)(2,1)S(1)}, bf16[272,1024]{1,0:T(8,128)(2,1)S(1)}, u32[]{:S(2)}, u32[]{:S(2)}) collective-permute-start(bf16[272,1024]{1,0:T(8,128)(2,1)S(1)} %get-tuple-element.49.refs_0_.payload), channel_id=1, source_target_pairs={{0,16},{4,12},{8,24},{12,4},{16,0},{20,28},{24,8},{28,20},{1,17},{... | collective-permute-start | bytes 1671176 | tf_op jit(solution)/shard_map/ppermute | solution.py:420
  47.3 1.6 %collective-permute-start.8 = (bf16[128,1024]{1,0:T(8,128)(2,1)S(1)}, bf16[128,1024]{1,0:T(8,128)(2,1)S(1)}, u32[]{:S(2)}, u32[]{:S(2)}) collective-permute-start(bf16[128,1024]{1,0:T(8,128)(2,1)S(1)} %get-tuple-element.48), channel_id=1, source_target_pairs={{0,4},{4,0},{8,12},{12,8},{16,20},{20,16},{24,28},{28,24},{1,5},{5... | collective-permute-start | bytes 786440 | tf_op jit(solution)/shard_map/ppermute | solution.py:416
  51.3 2.0 %collective-permute-start.10 = (bf16[272,1024]{1,0:T(8,128)(2,1)S(1)}, bf16[272,1024]{1,0:T(8,128)(2,1)S(1)}, u32[]{:S(2)}, u32[]{:S(2)}) collective-permute-start(bf16[272,1024]{1,0:T(8,128)(2,1)S(1)} %collective-permute-done.9.refs_0_.payload), channel_id=1, source_target_pairs={{0,4},{4,0},{8,12},{12,8},{16,20},{20,16},{24,28},{28,24},{1,5},{5... | collective-permute-start | bytes 1671176 | tf_op jit(solution)/shard_map/ppermute | solution.py:416
  51.3 9.2 %collective-permute-start.14 = (bf16[256,1024]{1,0:T(8,128)(2,1)S(1)}, bf16[256,1024]{1,0:T(8,128)(2,1)S(1)}, u32[]{:S(2)}, u32[]{:S(2)}) collective-permute-start(bf16[256,1024]{1,0:T(8,128)(2,1)S(1)} %combine.5), channel_id=1, source_target_pairs={{0,16},{4,12},{8,24},{12,4},{16,0},{20,28},{24,8},{28,20},{1,17},{... | collective-permute-start | bytes 1572872 | tf_op jit(solution)/shard_map/ppermute | solution.py:420
  51.3 5.6 %collective-permute-start.11 = (bf16[128,1024]{1,0:T(8,128)(2,1)S(1)}, bf16[128,1024]{1,0:T(8,128)(2,1)S(1)}, u32[]{:S(2)}, u32[]{:S(2)}) collective-permute-start(bf16[128,1024]{1,0:T(8,128)(2,1)S(1)} %get-tuple-element.52), channel_id=1, source_target_pairs={{0,4},{4,0},{8,12},{12,8},{16,20},{20,16},{24,28},{28,24},{1,5},{5... | collective-permute-start | bytes 786440 | tf_op jit(solution)/shard_map/ppermute | solution.py:416
  56.7 1.6 %collective-permute-start.12 = (bf16[128,1024]{1,0:T(8,128)(2,1)S(1)}, bf16[128,1024]{1,0:T(8,128)(2,1)S(1)}, u32[]{:S(2)}, u32[]{:S(2)}) collective-permute-start(bf16[128,1024]{1,0:T(8,128)(2,1)S(1)} %get-tuple-element.54), channel_id=1, source_target_pairs={{0,4},{4,0},{8,12},{12,8},{16,20},{20,16},{24,28},{28,24},{1,5},{5... | collective-permute-start | bytes 786440 | tf_op jit(solution)/shard_map/ppermute | solution.py:416
  59.5 14.3 %collective-permute-start.13 = (bf16[256,1024]{1,0:T(8,128)(2,1)S(1)}, bf16[256,1024]{1,0:T(8,128)(2,1)S(1)}, u32[]{:S(2)}, u32[]{:S(2)}) collective-permute-start(bf16[256,1024]{1,0:T(8,128)(2,1)S(1)} %combine.7), channel_id=1, source_target_pairs={{0,16},{4,12},{8,24},{12,4},{16,0},{20,28},{24,8},{28,20},{1,17},{... | collective-permute-start | bytes 1572872 | tf_op jit(solution)/shard_map/ppermute | solution.py:420
  60.5 13.4 %collective-permute-start.15 = (bf16[256,1024]{1,0:T(8,128)(2,1)S(1)}, bf16[256,1024]{1,0:T(8,128)(2,1)S(1)}, u32[]{:S(2)}, u32[]{:S(2)}) collective-permute-start(bf16[256,1024]{1,0:T(8,128)(2,1)S(1)} %add.10), channel_id=1, source_target_pairs={{0,8},{4,20},{8,0},{12,28},{16,24},{20,4},{24,16},{28,12},{1,9},{5... | collective-permute-start | bytes 1572872 | tf_op jit(solution)/shard_map/ppermute | solution.py:420

commit v6 on v5

--- a/solution.py
+++ b/solution.py
@@ -127,8 +127,8 @@
 
 
 def edge_kernel(live, q, before, behind, tops, sums, gain, acc, x, w, *rest):
-    meta = rest[0] if len(rest) == 5 else None
-    resid, payload = rest[-4:-2]
+    meta = rest[0] if len(rest) == 7 else None
+    resid, payload0, payload1, whole = rest[-6:-2]
     bias, att = rest[-2:]
     step = 2 * HD
     pairs = HEADS // 2
@@ -175,13 +175,15 @@
         res = res.astype(F32)
         square = jnp.mean(res * res, axis=1, keepdims=True)
         normed = (res * lax.rsqrt(square + 1e-06) * gain[...]).astype(BF16)
-        payload[span, :] = normed
+        (payload0, payload1)[half][:rows, :] = normed
+        whole[span, :] = normed
     if meta is not None:
         copies = [
             jnp.broadcast_to(meta[half : half + 1, :], (META // 2, meta.shape[1]))
             for half in range(2)
         ]
-        payload[2 * rows :, :] = jnp.concatenate(copies, axis=0)
+        payload0[rows:, :] = jnp.concatenate(copies, axis=0)
+        whole[2 * rows :, :] = jnp.concatenate(copies, axis=0)
 
 
 def edge(live, q, before, behind, acc, tops, sums, x, w, gain, meta):
@@ -193,12 +195,14 @@
     extra = 0 if meta is None else META
     flat = [
         jax.ShapeDtypeStruct((2 * rows, model), BF16),
+        jax.ShapeDtypeStruct((rows + extra, model), BF16),
+        jax.ShapeDtypeStruct((rows, model), BF16),
         jax.ShapeDtypeStruct((2 * rows + extra, model), BF16),
     ]
     return pl.pallas_call(
         edge_kernel,
         in_specs=specs,
-        out_specs=[VMEM] * 2,
+        out_specs=[VMEM] * 4,
         out_shape=flat,
         scratch_shapes=[
             pltpu.VMEM((2, wide, 2 * rows), F32),
@@ -213,7 +217,7 @@
 
 
 def meta_items(payload, block, rows):
-    meta = payload[2 * rows :, :].astype(F32)
+    meta = payload[payload.shape[0] - META :, :].astype(F32)
     meta = meta[block * META // 2 : (block + 1) * META // 2, :]
     return [meta[:, i * rows : (i + 1) * rows] for i in range(8)]
 
@@ -228,44 +232,39 @@
     return jnp.where(hits > 0, rank, F32(-1.0))
 
 
-def pick_matrices(payload, block, rows, capacity, wanted):
-    item = meta_items(payload, block, rows)
-    named = [(item[0] == e, item[1] == e) for e in wanted]
-    ranks = slot_rows(
-        jnp.concatenate([jnp.where(a | b, F32(1.0), F32(0.0)) for a, b in named], axis=0)
-    )
-    slot = lax.broadcasted_iota(jnp.int32, (capacity, rows), 0).astype(F32)
-    result = []
-    for i, (a, b) in enumerate(named):
-        gate = jnp.where(a, item[2] + item[3] + item[4], F32(0.0))
-        gate = gate + jnp.where(b, item[5] + item[6] + item[7], F32(0.0))
-        result.append((slot == ranks[i * META // 2 : i * META // 2 + 1, :], gate[:1, :]))
-    return result
-
-
 def experts_kernel(order, rows, capacity, me, *refs):
-    payloads = refs[:-8]
-    w_gate, w_up, w_down, out_mine, out_sib, x, hidden, tail = refs[-8:]
+    payloads = refs[:-9]
+    w_gate, w_up, w_down, out_mine, out_sib, scatter, x, hidden, tail = refs[-9:]
     width, model, step = w_gate.shape[1], w_down.shape[1], 256
-    expert = me[0].astype(F32)
+    expert, other = me[0].astype(F32), me[1].astype(F32)
     groups = len(order) // 2
-    hits = []
-    for array, block in order:
-        item = meta_items(payloads[array], block, rows)
-        hits.append(jnp.where((item[0] == expert) | (item[1] == expert), F32(1.0), F32(0.0)))
-    ranks = slot_rows(jnp.concatenate(hits, axis=0))
+    items = [meta_items(payloads[holder], block, rows) for _, _, holder, block in order]
+
+    def hits(item, wanted):
+        return jnp.where((item[0] == wanted) | (item[1] == wanted), F32(1.0), F32(0.0))
+
+    named = [hits(item, expert) for item in items] + [hits(item, other) for item in items[::2]]
+    ranks = slot_rows(jnp.concatenate(named, axis=0))
+    ranks = [ranks[i * META // 2 : i * META // 2 + 1, :] for i in range(len(named))]
     slot = lax.broadcasted_iota(jnp.int32, (2 * capacity, rows), 0).astype(F32)
     for g in range(groups):
-        first = ranks[g * META : g * META + 1, :]
-        second = ranks[g * META + META // 2 : g * META + META // 2 + 1, :]
+        first, second = ranks[2 * g : 2 * g + 2]
         second = jnp.where(second >= 0, second + capacity, F32(-1.0))
         hot = jnp.concatenate([slot == first, slot == second], axis=1)
         hot = jnp.where(hot, F32(1.0), F32(0.0)).astype(BF16)
-        tokens = []
-        for array, block in order[2 * g : 2 * g + 2]:
-            tokens.append(payloads[array][block * rows : (block + 1) * rows, :])
+        tokens = [payloads[a][at : at + rows, :] for a, at, _, _ in order[2 * g : 2 * g + 2]]
         picked = jnp.dot(hot, jnp.concatenate(tokens, axis=0), preferred_element_type=F32)
         x[2 * g * capacity : (2 * g + 2) * capacity, :] = picked.astype(BF16)
+    for g in range(groups):
+        item = items[2 * g]
+        for i, (wanted, rank) in enumerate(((expert, ranks[2 * g]), (other, ranks[2 * groups + g]))):
+            gate = jnp.where(item[0] == wanted, item[2] + item[3] + item[4], F32(0.0))
+            gate = gate + jnp.where(item[1] == wanted, item[5] + item[6] + item[7], F32(0.0))
+            full = jnp.where(slot[:capacity] == rank, gate[:1, :], F32(0.0))
+            high = full.astype(BF16)
+            at = (4 * g + 2 * i) * capacity
+            scatter[at : at + capacity, :] = high
+            scatter[at + capacity : at + 2 * capacity, :] = (full - high.astype(F32)).astype(BF16)
     for at in range(0, width, step):
         wide = min(step, width - at)
         cols = slice(at, at + wide)
@@ -292,11 +291,12 @@
     slots = len(order) * capacity
     left = width % 256
     outs = [jax.ShapeDtypeStruct((slots // 2, model), BF16)] * 2
+    outs.append(jax.ShapeDtypeStruct((2 * slots, rows), BF16))
     args = [me, *payloads, *weights]
     return pl.pallas_call(
         functools.partial(experts_kernel, order, rows, capacity),
         in_specs=[SMEM] + [VMEM] * (len(args) - 1),
-        out_specs=[VMEM] * 2,
+        out_specs=[VMEM] * 3,
         out_shape=outs,
         scratch_shapes=[
             pltpu.VMEM((slots, model), BF16),
@@ -309,41 +309,30 @@
     )(*args)
 
 
-def spread(payload, block, rows, capacity, experts_two, outs_two):
-    weights, values = [], []
-    picks = pick_matrices(payload, block, rows, capacity, experts_two)
-    for (hot, gate), out in zip(picks, outs_two):
-        full = jnp.where(hot, gate, F32(0.0))
-        high = full.astype(BF16)
-        weights += [high, (full - high.astype(F32)).astype(BF16)]
-        values += [out, out]
-    return lax.dot_general(
-        jnp.concatenate(weights, axis=0),
-        jnp.concatenate(values, axis=0),
-        (((0,), (0,)), ((), ())),
-        preferred_element_type=F32,
-    )
-
-
-def combine_kernel(rows, capacity, me, payload, outs_me, outs_sib, *refs):
+def combine_kernel(rows, capacity, parts, *refs):
+    scatters, outs_me, outs_sib = refs[:parts], refs[parts : 2 * parts], refs[2 * parts : 3 * parts]
+    refs = refs[3 * parts :]
     result = refs[-1]
-    both = (me[0].astype(F32), me[1].astype(F32))
     for block in range(2):
-        span = slice(block * capacity, (block + 1) * capacity)
-        total = spread(payload, block, rows, capacity, both, (outs_me[span, :], outs_sib[span, :]))
+        part, at = (block, 0) if parts == 2 else (0, block)
+        gates = scatters[part][4 * at * capacity : 4 * (at + 1) * capacity, :]
+        span = slice(at * capacity, (at + 1) * capacity)
+        mine, theirs = outs_me[part][span, :], outs_sib[part][span, :]
+        values = jnp.concatenate([mine, mine, theirs, theirs], axis=0)
+        total = lax.dot_general(gates, values, TN, preferred_element_type=F32)
         at = slice(block * rows, (block + 1) * rows)
         if len(refs) == 2:
             total = total + refs[0][at, :].astype(F32)
         result[at, :] = total.astype(result.dtype)
 
 
-def combine(me, payload, outs_me, outs_sib, rows, capacity, start=None, dtype=BF16):
-    model = payload.shape[1]
-    args = [me, payload, outs_me, outs_sib] + ([] if start is None else [start])
+def combine(scatters, outs_me, outs_sib, rows, capacity, start=None, dtype=BF16):
+    model = outs_me[0].shape[1]
+    args = [*scatters, *outs_me, *outs_sib] + ([] if start is None else [start])
     out = jax.ShapeDtypeStruct((2 * rows, model), dtype)
     return pl.pallas_call(
-        functools.partial(combine_kernel, rows, capacity),
-        in_specs=[SMEM] + [VMEM] * (len(args) - 1),
+        functools.partial(combine_kernel, rows, capacity, len(outs_me)),
+        in_specs=[VMEM] * len(args),
         out_specs=VMEM,
         out_shape=out,
         compiler_params=pltpu.CompilerParams(vmem_limit_bytes=12 * MIB),
@@ -424,35 +413,53 @@
     return lax.optimization_barrier((first, *later))[1:]
 
 
-def routed_gather(me, payload, resid, weights, rows, capacity):
+def routed_gather(me, payloads, whole, resid, weights, rows, capacity):
     sizes = dict(rows=rows, capacity=capacity)
 
     def evaluate(mine, theirs):
-        order = [(0, 0), (1, 0), (0, 1), (1, 1)]
-        kept, sent = experts(me, (mine, theirs), order, weights, **sizes)
-        return kept, swap(sent, 1)
-
-    sib = swap(payload, 1)
-    first = swap_by_core(payload, (2, 4))
-    out_own = evaluate(payload, sib)
-    total = combine(me, payload, *out_own, start=resid, dtype=F32, **sizes)
-    (first,) = after(total, first)
-    diag = swap_by_core(first, (4, 2))
-    out_first = evaluate(first, swap(first, 1))
-    (diag,) = after(out_first[0], diag)
-    second = swap_by_core(*after(diag, payload), (4, 2))
-    (diag,) = after(out_first[0], diag)
-    out_diag = evaluate(diag, swap(diag, 1))
-    sum_diag = combine(me, diag, *out_diag, **sizes)
+        count = len(mine)
+        order = []
+        for block in range(2):
+            array, at = (block, 0) if count == 2 else (0, block * rows)
+            order += [(array, at, 0, block), (count + array, at, count, block)]
+        kept, sent, scatter = experts(me, (*mine, *theirs), order, weights, **sizes)
+        return (scatter,), (kept,), (swap(sent, 1),)
+
+    def siblings(arrays):
+        return [swap(a, 1) for a in arrays]
+
+    first = [swap_by_core(p, (2, 4)) for p in payloads]
+    sib = siblings(payloads)
+    order = [(0, 0, 0, 0), (1, 0, 1, 0)]
+    own0, sent0, scatter0 = experts(me, (payloads[0], sib[0]), order, weights, **sizes)
+    (first[0],) = after(own0, first[0])
+    diag0 = swap_by_core(first[0], (4, 2))
+    later = after(first[0], payloads[1], sib[1])
+    order = [(0, 0, 2, 1), (1, 0, 3, 1)]
+    own1, sent1, scatter1 = experts(me, (*later, payloads[0], sib[0]), order, weights, **sizes)
+    (first[1],) = after(own1, first[1])
+    diag1 = swap_by_core(first[1], (4, 2))
+    far = siblings(first)
+    first[0], _ = lax.optimization_barrier((first[0], diag0))
+    out_first = evaluate(first, far)
+    (diag1,) = after(out_first[1][0], diag1)
+    second = swap_by_core(*after(diag1, whole), (4, 2))
+    diag = [diag0, diag1]
+    out_diag = evaluate(diag, siblings(diag))
+    sum_diag = combine(*out_diag, **sizes)
     carry = swap_by_core(sum_diag, (4, 2))
     (second,) = after(sum_diag, second)
-    out_second = evaluate(second, swap(second, 1))
-    sum_first = combine(
-        me, first, *out_first[:1], *after(out_second[0], *out_first[1:]), dtype=F32, **sizes
-    )
-    sum_second = combine(me, second, out_second[0], *after(sum_first, out_second[1]), **sizes)
+    out_second = evaluate([second], siblings([second]))
+    scatter, mine, theirs = out_first
+    theirs = after(out_second[1][0], *theirs)
+    sum_first = combine(scatter, mine, theirs, dtype=F32, **sizes)
+    scatter, mine, theirs = out_second
+    sum_second = combine(scatter, mine, after(sum_first, *theirs), **sizes)
     back_second = swap_by_core(sum_second, (4, 2))
-    back_first = swap_by_core(add(sum_first, *after(sum_second, carry), BF16), (2, 4))
+    sum_first = add(sum_first, *after(sum_second, carry), BF16)
+    back_first = swap_by_core(sum_first, (2, 4))
+    own = (scatter0, scatter1), (own0, own1), siblings((sent0, sent1))
+    total = combine(*own, start=resid, dtype=F32, **sizes)
     return add(add(total, back_second, F32), back_first, BF16)
 
 
@@ -495,14 +502,14 @@
         meta = jnp.stack(items).reshape(len(items), 2, rows).swapaxes(0, 1)
         meta = meta.reshape(2, len(items) * rows).astype(BF16)
     acc, tops, sums = interior(queries, key_vectors, values)
-    resid, payload = edge(
+    resid, *payloads, whole = edge(
         live, queries, before, behind, acc, tops, sums, inputs, out_weight,
         norm_gain[None, :], meta,
     )
     if fast:
         weights = (w_gate[0], w_up[0], w_down[0])
-        return routed_gather(me, payload, resid, weights, rows, capacity)
-    return routed_all_to_all(payload, resid, routes, route_gates, w_gate[0], w_up[0], w_down[0])
+        return routed_gather(me, payloads, whole, resid, weights, rows, capacity)
+    return routed_all_to_all(whole, resid, routes, route_gates, w_gate[0], w_up[0], w_down[0])
 
 
 def solution(mesh):

time: 75.1 us -> 72.7 us (0.968)
  waiting for transfers between devices: 26.2 us -> 23.4 us
  starting transfers between devices: 18.1 us -> 20.9 us
  Pallas kernels: 28.5 us -> 26.1 us
    pallas_call x5, Pallas kernels: 7.61 us -> 4.16 us  [the longest x1 2.82 us: edge(): pl.pallas_call(edge_kernel, in_specs=specs, out_specs=[VMEM] * 4, out_sha...]
    ppermute x8 -> x12, waiting for transfers between devices: 6.98 us -> 4.64 us  [swap(): return lax.ppermute(array, 'tile', [(i, i ^ bit) for i in range(8)])]
    ppermute x8 -> x12, starting transfers between devices: 11 us -> 12.9 us  [swap(): return lax.ppermute(array, 'tile', [(i, i ^ bit) for i in range(8)])]
    pallas_call x4 -> x5, Pallas kernels: 14.1 us -> 15.1 us  [experts(): pl.pallas_call(functools.partial(experts_kernel, order, rows, capacity),...]
    ppermute x6 -> x8, starting transfers between devices: 3.39 us -> 4.31 us  [swap_by_core(): return lax.ppermute(array, 'tile', [(i, i ^ bits[i % 2]) for i in range(8)])]
    ppermute x6 -> x8, waiting for transfers between devices: 19.2 us -> 18.7 us  [swap_by_core(): return lax.ppermute(array, 'tile', [(i, i ^ bits[i % 2]) for i in range(8)])]
  transfers between devices with their start and end apart: 16 -> 22, of which waited for: 12 -> 13; matrix products, arithmetic and copies ran while one was open for 2% -> 2% of each run, Pallas kernels for 32% -> 29%
where the time goes in v6:
time: 72.7 us; the launch traced here: 72.4 us
  Pallas kernels  26.1 us (36%)
  waiting for transfers between devices  23.4 us (32%)
  starting transfers between devices  20.9 us (29%)
  other arithmetic  1 us (1%)
  local copies, waits for them, and re-layouts  0.82 us (1%)
    ppermute x8, waiting for transfers between devices, swap_by_core(): return lax.ppermute(array, 'tile', [(i, i ^ bits[i % 2]) for i in range(8)])  18.7 us
    pallas_call x5, Pallas kernels, experts(): pl.pallas_call(functools.partial(experts_kernel, order, rows, capacity),...  15.1 us
    ppermute x12, starting transfers between devices, swap(): return lax.ppermute(array, 'tile', [(i, i ^ bit) for i in range(8)])  12.9 us
    ppermute x12, waiting for transfers between devices, swap(): return lax.ppermute(array, 'tile', [(i, i ^ bit) for i in range(8)])  4.64 us
    pallas_call x1, Pallas kernels, interior(): pl.pallas_call(interior_kernel, in_specs=[VMEM] * 3, out_specs=[VMEM] * 3...  4.51 us
    ppermute x8, starting transfers between devices, swap_by_core(): return lax.ppermute(array, 'tile', [(i, i ^ bits[i % 2]) for i in range(8)])  4.31 us
    pallas_call x1, Pallas kernels, edge(): pl.pallas_call(edge_kernel, in_specs=specs, out_specs=[VMEM] * 4, out_sha...  2.82 us
    ppermute x1, starting transfers between devices, local(): before = lax.ppermute(last, 'tile', up)  2.39 us
  transfers between devices with their start and end apart: 22, of which 13 were waited for; matrix products, arithmetic and copies ran while one was open for 2% of the time, Pallas kernels for 29%

profile of v6, /device:TPU:0, one launch (start us, length us, event | category | flops | bytes accessed | tf_op | source)
XLA Modules:
  0.0 72.4 jit_solution(9049152445466675472)
XLA Ops:
  0.2 1.2 %pack.1 = (bf16[256,1024]{1,0:T(8,128)(2,1)S(1)}, bf16[256,1024]{1,0:T(8,128)(2,1)S(1)}) custom-call(bf16[256,1024]{1,0:T(8,128)(2,1)} %k.1, bf16[256,1024]{1,0:T(8,128)(2,1)} %v.3), custom_call_target="tpu_custom_call" | custom-call | bytes 2097152 | tf_op jit(solution)/shard_map/pack/pallas_call | solution.py:81
  1.4 2.4 %collective-permute-start = (bf16[256,1024]{1,0:T(8,128)(2,1)S(1)}, bf16[256,1024]{1,0:T(8,128)(2,1)S(1)}, u32[]{:S(2)}, u32[]{:S(2)}) collective-permute-start(bf16[256,1024]{1,0:T(8,128)(2,1)S(1)} %get-tuple-element.46), channel_id=1, source_target_pairs={{0,4},{4,8},{8,12},{12,16},{16,20},{20,24},{24,28},{1,5},{5,9},{9,... | collective-permute-start | bytes 1572872 | tf_op jit(solution)/shard_map/ppermute | solution.py:491
  3.8 1.3 %collective-permute-start.1 = (bf16[256,1024]{1,0:T(8,128)(2,1)S(1)}, bf16[256,1024]{1,0:T(8,128)(2,1)S(1)}, u32[]{:S(2)}, u32[]{:S(2)}) collective-permute-start(bf16[256,1024]{1,0:T(8,128)(2,1)S(1)} %get-tuple-element.47), channel_id=1, source_target_pairs={{4,0},{8,4},{12,8},{16,12},{20,16},{24,20},{28,24},{5,1},{9,5},{13... | collective-permute-start | bytes 1572872 | tf_op jit(solution)/shard_map/ppermute | solution.py:492
  6.8 4.5 %interior.1 = (f32[1024,256]{1,0:T(8,128)S(1)}, f32[16,256]{1,0:T(8,128)S(1)}, f32[16,256]{1,0:T(8,128)S(1)}) custom-call(bf16[256,1024]{1,0:T(8,128)(2,1)} %q.3, bf16[256,1024]{1,0:T(8,128)(2,1)} %k.1, bf16[256,1024]{1,0:T(8,128)(2,1)} %v.3), custom_call_target="tpu_custom_call" | custom-call | flops 8053063680 | bytes 2654208 | tf_op jit(solution)/shard_map/interior/pallas_call | solution.py:117
  11.4 2.8 %edge.1 = (bf16[256,1024]{1,0:T(8,128)(2,1)S(1)}, bf16[144,1024]{1,0:T(8,128)(2,1)S(1)}, bf16[128,1024]{1,0:T(8,128)(2,1)S(1)}, bf16[272,1024]{1,0:T(8,128)(2,1)S(1)}) custom-call(s32[2]{0:T(128)S(1)} %add_convert_fusion.live, bf16[256,1024]{1,0:T(8,128)(2,1)S(1)} %copy-done.4, bf16[256,1024]{1,0:T(8,128)(2,1)S(1)} %collective-permute-done.before, ...), custom_call_target="tpu_custom_call" | custom-call | flops 20132659200 | bytes 6922248 | tf_op jit(solution)/shard_map/edge/pallas_call | solution.py:202
  14.2 8.5 %collective-permute-start.2 = (bf16[144,1024]{1,0:T(8,128)(2,1)S(1)}, bf16[144,1024]{1,0:T(8,128)(2,1)S(1)}, u32[]{:S(2)}, u32[]{:S(2)}) collective-permute-start(bf16[144,1024]{1,0:T(8,128)(2,1)S(1)} %get-tuple-element.51.refs_0_.refs_2_), channel_id=1, source_target_pairs={{0,4},{4,0},{8,12},{12,8},{16,20},{20,16},{24,28},{28,24},{1,5},{5... | collective-permute-start | bytes 884744 | tf_op jit(solution)/shard_map/ppermute | solution.py:405
  22.7 1.5 %collective-permute-start.3 = (bf16[144,1024]{1,0:T(8,128)(2,1)S(1)}, bf16[144,1024]{1,0:T(8,128)(2,1)S(1)}, u32[]{:S(2)}, u32[]{:S(2)}) collective-permute-start(bf16[144,1024]{1,0:T(8,128)(2,1)S(1)} %get-tuple-element.51.refs_0_.refs_2_), channel_id=1, source_target_pairs={{0,8},{4,20},{8,0},{12,28},{16,24},{20,4},{24,16},{28,12},{1,9},{5... | collective-permute-start | bytes 884744 | tf_op jit(solution)/shard_map/ppermute | solution.py:409
  24.7 2.2 %experts_128.2 = (bf16[64,1024]{1,0:T(8,128)(2,1)S(1)}, bf16[64,1024]{1,0:T(8,128)(2,1)S(1)}, bf16[256,128]{1,0:T(8,128)(2,1)S(1)}) custom-call(s32[2]{0:T(128)S(1)} %pad_add_fusion.me, bf16[144,1024]{1,0:T(8,128)(2,1)S(1)} %get-tuple-element.51.refs_0_.refs_2_, bf16[144,1024]{1,0:T(8,128)(2,1)S(1)} %collective-permute-done.2.refs_1_.refs_3_, ...), custom_call_target="tpu_custom_call" | custom-call | flops 1107296256 | bytes 9568264 | tf_op jit(solution)/shard_map/experts_128/pallas_call | solution.py:296
  27.0 2.4 %collective-permute-done.3.refs_0_ = bf16[144,1024]{1,0:T(8,128)(2,1)S(1)} collective-permute-done((bf16[144,1024]{1,0:T(8,128)(2,1)S(1)}, bf16[144,1024]{1,0:T(8,128)(2,1)S(1)}, u32[]{:S(2)}, u32[]{:S(2)}) %collective-permute-start.3) | collective-permute-done | bytes 294944 | tf_op jit(solution)/shard_map/ppermute | solution.py:409
  29.4 2.3 %experts_128.3 = (bf16[64,1024]{1,0:T(8,128)(2,1)S(1)}, bf16[64,1024]{1,0:T(8,128)(2,1)S(1)}, bf16[256,128]{1,0:T(8,128)(2,1)S(1)}) custom-call(s32[2]{0:T(128)S(1)} %pad_add_fusion.me, bf16[128,1024]{1,0:T(8,128)(2,1)S(1)} %get-tuple-element.56.refs_0_, bf16[128,1024]{1,0:T(8,128)(2,1)S(1)} %collective-permute-done.4.refs_1_, ...), custom_call_target="tpu_custom_call" | custom-call | flops 1107296256 | bytes 10092552 | tf_op jit(solution)/shard_map/experts_128/pallas_call | solution.py:296
  32.2 1.2 %collective-permute-start.10 = (bf16[128,1024]{1,0:T(8,128)(2,1)S(1)}, bf16[128,1024]{1,0:T(8,128)(2,1)S(1)}, u32[]{:S(2)}, u32[]{:S(2)}) collective-permute-start(bf16[128,1024]{1,0:T(8,128)(2,1)S(1)} %collective-permute-done.8.refs_1_), channel_id=1, source_target_pairs={{0,4},{4,0},{8,12},{12,8},{16,20},{20,16},{24,28},{28,24},{1,5},{5... | collective-permute-start | bytes 786440 | tf_op jit(solution)/shard_map/ppermute | solution.py:405
  33.8 2.3 %collective-permute-done.7.refs_0_ = bf16[144,1024]{1,0:T(8,128)(2,1)S(1)} collective-permute-done((bf16[144,1024]{1,0:T(8,128)(2,1)S(1)}, bf16[144,1024]{1,0:T(8,128)(2,1)S(1)}, u32[]{:S(2)}, u32[]{:S(2)}) %collective-permute-start.7) | collective-permute-done | bytes 294944 | tf_op jit(solution)/shard_map/ppermute | solution.py:409
  36.1 3.5 %experts_256.3 = (bf16[128,1024]{1,0:T(8,128)(2,1)S(1)}, bf16[128,1024]{1,0:T(8,128)(2,1)S(1)}, bf16[512,128]{1,0:T(8,128)(2,1)S(1)}) custom-call(s32[2]{0:T(128)S(1)} %pad_add_fusion.me, bf16[144,1024]{1,0:T(8,128)(2,1)S(1)} %collective-permute-done.3.refs_0_, bf16[128,1024]{1,0:T(8,128)(2,1)S(1)} %collective-permute-done.8.refs_1_, ...), custom_call_target="tpu_custom_call" | custom-call | flops 2214592512 | bytes 10420232 | tf_op jit(solution)/shard_map/experts_256/pallas_call | solution.py:296
  40.2 1.1 %collective-permute-done.13.refs_3_ = bf16[128,1024]{1,0:T(8,128)(2,1)S(1)} collective-permute-done((bf16[128,1024]{1,0:T(8,128)(2,1)S(1)}, bf16[128,1024]{1,0:T(8,128)(2,1)S(1)}, u32[]{:S(2)}, u32[]{:S(2)}) %collective-permute-start.13) | collective-permute-done | bytes 262176 | tf_op jit(solution)/shard_map/ppermute | solution.py:405
  41.4 3.7 %experts_256.4 = (bf16[128,1024]{1,0:T(8,128)(2,1)S(1)}, bf16[128,1024]{1,0:T(8,128)(2,1)S(1)}, bf16[512,128]{1,0:T(8,128)(2,1)S(1)}) custom-call(s32[2]{0:T(128)S(1)} %pad_add_fusion.me, bf16[144,1024]{1,0:T(8,128)(2,1)S(1)} %collective-permute-done.7.refs_0_, bf16[128,1024]{1,0:T(8,128)(2,1)S(1)} %collective-permute-done.11.refs_1_, ...), custom_call_target="tpu_custom_call" | custom-call | flops 2214592512 | bytes 10420232 | tf_op jit(solution)/shard_map/experts_256/pallas_call | solution.py:296
  45.5 1.2 %collective-permute-done.14.refs_2_ = bf16[128,1024]{1,0:T(8,128)(2,1)S(1)} collective-permute-done((bf16[128,1024]{1,0:T(8,128)(2,1)S(1)}, bf16[128,1024]{1,0:T(8,128)(2,1)S(1)}, u32[]{:S(2)}, u32[]{:S(2)}) %collective-permute-start.14) | collective-permute-done | bytes 262176 | tf_op jit(solution)/shard_map/ppermute | solution.py:405
  47.0 2.7 %collective-permute-done.15.refs_0_ = bf16[272,1024]{1,0:T(8,128)(2,1)S(1)} collective-permute-done((bf16[272,1024]{1,0:T(8,128)(2,1)S(1)}, bf16[272,1024]{1,0:T(8,128)(2,1)S(1)}, u32[]{:S(2)}, u32[]{:S(2)}) %collective-permute-start.15) | collective-permute-done | bytes 557088 | tf_op jit(solution)/shard_map/ppermute | solution.py:409
  49.8 1.7 %collective-permute-start.17 = (bf16[128,1024]{1,0:T(8,128)(2,1)S(1)}, bf16[128,1024]{1,0:T(8,128)(2,1)S(1)}, u32[]{:S(2)}, u32[]{:S(2)}) collective-permute-start(bf16[128,1024]{1,0:T(8,128)(2,1)S(1)} %get-tuple-element.76), channel_id=1, source_target_pairs={{0,4},{4,0},{8,12},{12,8},{16,20},{20,16},{24,28},{28,24},{1,5},{5... | collective-permute-start | bytes 786440 | tf_op jit(solution)/shard_map/ppermute | solution.py:405
  51.7 3.5 %experts_256.5 = (bf16[128,1024]{1,0:T(8,128)(2,1)S(1)}, bf16[128,1024]{1,0:T(8,128)(2,1)S(1)}, bf16[512,128]{1,0:T(8,128)(2,1)S(1)}) custom-call(s32[2]{0:T(128)S(1)} %pad_add_fusion.me, bf16[272,1024]{1,0:T(8,128)(2,1)S(1)} %collective-permute-done.15.refs_0_, bf16[272,1024]{1,0:T(8,128)(2,1)S(1)} %collective-permute-done.16.refs_1_, ...), custom_call_target="tpu_custom_call" | custom-call | flops 2214592512 | bytes 10420232 | tf_op jit(solution)/shard_map/experts_256/pallas_call | solution.py:296
  55.7 1.1 %collective-permute-done.18.refs_2_ = bf16[128,1024]{1,0:T(8,128)(2,1)S(1)} collective-permute-done((bf16[128,1024]{1,0:T(8,128)(2,1)S(1)}, bf16[128,1024]{1,0:T(8,128)(2,1)S(1)}, u32[]{:S(2)}, u32[]{:S(2)}) %collective-permute-start.18) | collective-permute-done | bytes 262176 | tf_op jit(solution)/shard_map/ppermute | solution.py:405
  57.4 1.5 %collective-permute-done.20.b = bf16[256,1024]{1,0:T(8,128)(2,1)S(1)} collective-permute-done((bf16[256,1024]{1,0:T(8,128)(2,1)S(1)}, bf16[256,1024]{1,0:T(8,128)(2,1)S(1)}, u32[]{:S(2)}, u32[]{:S(2)}) %collective-permute-start.20) | collective-permute-done | bytes 524320 | tf_op jit(solution)/shard_map/ppermute | solution.py:409
  59.0 1.6 %collective-permute-start.21 = (bf16[256,1024]{1,0:T(8,128)(2,1)S(1)}, bf16[256,1024]{1,0:T(8,128)(2,1)S(1)}, u32[]{:S(2)}, u32[]{:S(2)}) collective-permute-start(bf16[256,1024]{1,0:T(8,128)(2,1)S(1)} %add.10), channel_id=1, source_target_pairs={{0,8},{4,20},{8,0},{12,28},{16,24},{20,4},{24,16},{28,12},{1,9},{5... | collective-permute-start | bytes 1572872 | tf_op jit(solution)/shard_map/ppermute | solution.py:409
  62.4 9.0 %collective-permute-done.19.b = bf16[256,1024]{1,0:T(8,128)(2,1)S(1)} collective-permute-done((bf16[256,1024]{1,0:T(8,128)(2,1)S(1)}, bf16[256,1024]{1,0:T(8,128)(2,1)S(1)}, u32[]{:S(2)}, u32[]{:S(2)}) %collective-permute-start.19) | collective-permute-done | bytes 524320 | tf_op jit(solution)/shard_map/ppermute | solution.py:409
  71.6 0.9 %add.11 = bf16[256,1024]{1,0:T(8,128)(2,1)} custom-call(f32[256,1024]{1,0:T(8,128)S(1)} %add.9.a, bf16[256,1024]{1,0:T(8,128)(2,1)S(1)} %collective-permute-done.21.b), custom_call_target="tpu_custom_call" | custom-call | flops 262144 | bytes 2097152 | tf_op jit(solution)/shard_map/add/pallas_call | solution.py:350
  (61 shorter events, 8.1 us)
Async XLA Ops:
  1.4 9.9 %collective-permute-start = (bf16[256,1024]{1,0:T(8,128)(2,1)S(1)}, bf16[256,1024]{1,0:T(8,128)(2,1)S(1)}, u32[]{:S(2)}, u32[]{:S(2)}) collective-permute-start(bf16[256,1024]{1,0:T(8,128)(2,1)S(1)} %get-tuple-element.46), channel_id=1, source_target_pairs={{0,4},{4,8},{8,12},{12,16},{16,20},{20,24},{24,28},{1,5},{5,9},{9,... | collective-permute-start | bytes 1572872 | tf_op jit(solution)/shard_map/ppermute | solution.py:491
  3.8 7.5 %collective-permute-start.1 = (bf16[256,1024]{1,0:T(8,128)(2,1)S(1)}, bf16[256,1024]{1,0:T(8,128)(2,1)S(1)}, u32[]{:S(2)}, u32[]{:S(2)}) collective-permute-start(bf16[256,1024]{1,0:T(8,128)(2,1)S(1)} %get-tuple-element.47), channel_id=1, source_target_pairs={{4,0},{8,4},{12,8},{16,12},{20,16},{24,20},{28,24},{5,1},{9,5},{13... | collective-permute-start | bytes 1572872 | tf_op jit(solution)/shard_map/ppermute | solution.py:492
  11.3 13.4 %copy-start = (bf16[1,1024,1408]{2,1,0:T(8,128)(2,1)S(1)}, bf16[1,1024,1408]{2,1,0:T(8,128)(2,1)}, u32[]{:S(2)}) copy-start(bf16[1,1024,1408]{2,1,0:T(8,128)(2,1)} %param.19) | copy-start | bytes 8650756
  11.3 13.4 %copy-start.1 = (bf16[1,1024,1408]{2,1,0:T(8,128)(2,1)S(1)}, bf16[1,1024,1408]{2,1,0:T(8,128)(2,1)}, u32[]{:S(2)}) copy-start(bf16[1,1024,1408]{2,1,0:T(8,128)(2,1)} %param.20) | copy-start | bytes 8650756
  14.2 10.5 %collective-permute-start.2 = (bf16[144,1024]{1,0:T(8,128)(2,1)S(1)}, bf16[144,1024]{1,0:T(8,128)(2,1)S(1)}, u32[]{:S(2)}, u32[]{:S(2)}) collective-permute-start(bf16[144,1024]{1,0:T(8,128)(2,1)S(1)} %get-tuple-element.51.refs_0_.refs_2_), channel_id=1, source_target_pairs={{0,4},{4,0},{8,12},{12,8},{16,20},{20,16},{24,28},{28,24},{1,5},{5... | collective-permute-start | bytes 884744 | tf_op jit(solution)/shard_map/ppermute | solution.py:405
  22.7 6.7 %collective-permute-start.3 = (bf16[144,1024]{1,0:T(8,128)(2,1)S(1)}, bf16[144,1024]{1,0:T(8,128)(2,1)S(1)}, u32[]{:S(2)}, u32[]{:S(2)}) collective-permute-start(bf16[144,1024]{1,0:T(8,128)(2,1)S(1)} %get-tuple-element.51.refs_0_.refs_2_), channel_id=1, source_target_pairs={{0,8},{4,20},{8,0},{12,28},{16,24},{20,4},{24,16},{28,12},{1,9},{5... | collective-permute-start | bytes 884744 | tf_op jit(solution)/shard_map/ppermute | solution.py:409
  24.2 5.2 %collective-permute-start.4 = (bf16[128,1024]{1,0:T(8,128)(2,1)S(1)}, bf16[128,1024]{1,0:T(8,128)(2,1)S(1)}, u32[]{:S(2)}, u32[]{:S(2)}) collective-permute-start(bf16[128,1024]{1,0:T(8,128)(2,1)S(1)} %get-tuple-element.56.refs_0_), channel_id=1, source_target_pairs={{0,4},{4,0},{8,12},{12,8},{16,20},{20,16},{24,28},{28,24},{1,5},{5... | collective-permute-start | bytes 786440 | tf_op jit(solution)/shard_map/ppermute | solution.py:405
  24.2 8.0 %collective-permute-start.8 = (bf16[128,1024]{1,0:T(8,128)(2,1)S(1)}, bf16[128,1024]{1,0:T(8,128)(2,1)S(1)}, u32[]{:S(2)}, u32[]{:S(2)}) collective-permute-start(bf16[128,1024]{1,0:T(8,128)(2,1)S(1)} %get-tuple-element.56.refs_0_), channel_id=1, source_target_pairs={{0,8},{4,20},{8,0},{12,28},{16,24},{20,4},{24,16},{28,12},{1,9},{5... | collective-permute-start | bytes 786440 | tf_op jit(solution)/shard_map/ppermute | solution.py:409
  29.4 6.7 %collective-permute-start.9 = (bf16[144,1024]{1,0:T(8,128)(2,1)S(1)}, bf16[144,1024]{1,0:T(8,128)(2,1)S(1)}, u32[]{:S(2)}, u32[]{:S(2)}) collective-permute-start(bf16[144,1024]{1,0:T(8,128)(2,1)S(1)} %collective-permute-done.3.refs_0_), channel_id=1, source_target_pairs={{0,4},{4,0},{8,12},{12,8},{16,20},{20,16},{24,28},{28,24},{1,5},{5... | collective-permute-start | bytes 884744 | tf_op jit(solution)/shard_map/ppermute | solution.py:405
  29.4 6.7 %collective-permute-start.7 = (bf16[144,1024]{1,0:T(8,128)(2,1)S(1)}, bf16[144,1024]{1,0:T(8,128)(2,1)S(1)}, u32[]{:S(2)}, u32[]{:S(2)}) collective-permute-start(bf16[144,1024]{1,0:T(8,128)(2,1)S(1)} %collective-permute-done.3.refs_0_), channel_id=1, source_target_pairs={{0,16},{4,12},{8,24},{12,4},{16,0},{20,28},{24,8},{28,20},{1,17},{... | collective-permute-start | bytes 884744 | tf_op jit(solution)/shard_map/ppermute | solution.py:409
  32.2 3.9 %collective-permute-start.10 = (bf16[128,1024]{1,0:T(8,128)(2,1)S(1)}, bf16[128,1024]{1,0:T(8,128)(2,1)S(1)}, u32[]{:S(2)}, u32[]{:S(2)}) collective-permute-start(bf16[128,1024]{1,0:T(8,128)(2,1)S(1)} %collective-permute-done.8.refs_1_), channel_id=1, source_target_pairs={{0,4},{4,0},{8,12},{12,8},{16,20},{20,16},{24,28},{28,24},{1,5},{5... | collective-permute-start | bytes 786440 | tf_op jit(solution)/shard_map/ppermute | solution.py:405
  33.4 6.4 %collective-permute-start.11 = (bf16[128,1024]{1,0:T(8,128)(2,1)S(1)}, bf16[128,1024]{1,0:T(8,128)(2,1)S(1)}, u32[]{:S(2)}, u32[]{:S(2)}) collective-permute-start(bf16[128,1024]{1,0:T(8,128)(2,1)S(1)} %collective-permute-done.8.refs_1_), channel_id=1, source_target_pairs={{0,16},{4,12},{8,24},{12,4},{16,0},{20,28},{24,8},{28,20},{1,17},{... | collective-permute-start | bytes 786440 | tf_op jit(solution)/shard_map/ppermute | solution.py:409
  36.1 5.2 %collective-permute-start.12 = (bf16[144,1024]{1,0:T(8,128)(2,1)S(1)}, bf16[144,1024]{1,0:T(8,128)(2,1)S(1)}, u32[]{:S(2)}, u32[]{:S(2)}) collective-permute-start(bf16[144,1024]{1,0:T(8,128)(2,1)S(1)} %collective-permute-done.7.refs_0_), channel_id=1, source_target_pairs={{0,4},{4,0},{8,12},{12,8},{16,20},{20,16},{24,28},{28,24},{1,5},{5... | collective-permute-start | bytes 884744 | tf_op jit(solution)/shard_map/ppermute | solution.py:405
  39.8 1.5 %collective-permute-start.13 = (bf16[128,1024]{1,0:T(8,128)(2,1)S(1)}, bf16[128,1024]{1,0:T(8,128)(2,1)S(1)}, u32[]{:S(2)}, u32[]{:S(2)}) collective-permute-start(bf16[128,1024]{1,0:T(8,128)(2,1)S(1)} %collective-permute-done.11.refs_1_), channel_id=1, source_target_pairs={{0,4},{4,0},{8,12},{12,8},{16,20},{20,16},{24,28},{28,24},{1,5},{5... | collective-permute-start | bytes 786440 | tf_op jit(solution)/shard_map/ppermute | solution.py:405
  40.2 9.5 %collective-permute-start.15 = (bf16[272,1024]{1,0:T(8,128)(2,1)S(1)}, bf16[272,1024]{1,0:T(8,128)(2,1)S(1)}, u32[]{:S(2)}, u32[]{:S(2)}) collective-permute-start(bf16[272,1024]{1,0:T(8,128)(2,1)S(1)} %get-tuple-element.71), channel_id=1, source_target_pairs={{0,16},{4,12},{8,24},{12,4},{16,0},{20,28},{24,8},{28,20},{1,17},{... | collective-permute-start | bytes 1671176 | tf_op jit(solution)/shard_map/ppermute | solution.py:409
  45.0 1.6 %collective-permute-start.14 = (bf16[128,1024]{1,0:T(8,128)(2,1)S(1)}, bf16[128,1024]{1,0:T(8,128)(2,1)S(1)}, u32[]{:S(2)}, u32[]{:S(2)}) collective-permute-start(bf16[128,1024]{1,0:T(8,128)(2,1)S(1)} %get-tuple-element.69), channel_id=1, source_target_pairs={{0,4},{4,0},{8,12},{12,8},{16,20},{20,16},{24,28},{28,24},{1,5},{5... | collective-permute-start | bytes 786440 | tf_op jit(solution)/shard_map/ppermute | solution.py:405
  49.7 2.0 %collective-permute-start.16 = (bf16[272,1024]{1,0:T(8,128)(2,1)S(1)}, bf16[272,1024]{1,0:T(8,128)(2,1)S(1)}, u32[]{:S(2)}, u32[]{:S(2)}) collective-permute-start(bf16[272,1024]{1,0:T(8,128)(2,1)S(1)} %collective-permute-done.15.refs_0_), channel_id=1, source_target_pairs={{0,4},{4,0},{8,12},{12,8},{16,20},{20,16},{24,28},{28,24},{1,5},{5... | collective-permute-start | bytes 1671176 | tf_op jit(solution)/shard_map/ppermute | solution.py:405
  49.7 9.2 %collective-permute-start.20 = (bf16[256,1024]{1,0:T(8,128)(2,1)S(1)}, bf16[256,1024]{1,0:T(8,128)(2,1)S(1)}, u32[]{:S(2)}, u32[]{:S(2)}) collective-permute-start(bf16[256,1024]{1,0:T(8,128)(2,1)S(1)} %combine.5), channel_id=1, source_target_pairs={{0,16},{4,12},{8,24},{12,4},{16,0},{20,28},{24,8},{28,20},{1,17},{... | collective-permute-start | bytes 1572872 | tf_op jit(solution)/shard_map/ppermute | solution.py:409
  49.8 5.6 %collective-permute-start.17 = (bf16[128,1024]{1,0:T(8,128)(2,1)S(1)}, bf16[128,1024]{1,0:T(8,128)(2,1)S(1)}, u32[]{:S(2)}, u32[]{:S(2)}) collective-permute-start(bf16[128,1024]{1,0:T(8,128)(2,1)S(1)} %get-tuple-element.76), channel_id=1, source_target_pairs={{0,4},{4,0},{8,12},{12,8},{16,20},{20,16},{24,28},{28,24},{1,5},{5... | collective-permute-start | bytes 786440 | tf_op jit(solution)/shard_map/ppermute | solution.py:405
  55.2 1.6 %collective-permute-start.18 = (bf16[128,1024]{1,0:T(8,128)(2,1)S(1)}, bf16[128,1024]{1,0:T(8,128)(2,1)S(1)}, u32[]{:S(2)}, u32[]{:S(2)}) collective-permute-start(bf16[128,1024]{1,0:T(8,128)(2,1)S(1)} %get-tuple-element.78), channel_id=1, source_target_pairs={{0,4},{4,0},{8,12},{12,8},{16,20},{20,16},{24,28},{28,24},{1,5},{5... | collective-permute-start | bytes 786440 | tf_op jit(solution)/shard_map/ppermute | solution.py:405
  57.1 14.3 %collective-permute-start.19 = (bf16[256,1024]{1,0:T(8,128)(2,1)S(1)}, bf16[256,1024]{1,0:T(8,128)(2,1)S(1)}, u32[]{:S(2)}, u32[]{:S(2)}) collective-permute-start(bf16[256,1024]{1,0:T(8,128)(2,1)S(1)} %combine.7), channel_id=1, source_target_pairs={{0,16},{4,12},{8,24},{12,4},{16,0},{20,28},{24,8},{28,20},{1,17},{... | collective-permute-start | bytes 1572872 | tf_op jit(solution)/shard_map/ppermute | solution.py:409
  59.0 12.5 %collective-permute-start.21 = (bf16[256,1024]{1,0:T(8,128)(2,1)S(1)}, bf16[256,1024]{1,0:T(8,128)(2,1)S(1)}, u32[]{:S(2)}, u32[]{:S(2)}) collective-permute-start(bf16[256,1024]{1,0:T(8,128)(2,1)S(1)} %add.10), channel_id=1, source_target_pairs={{0,8},{4,20},{8,0},{12,28},{16,24},{20,4},{24,16},{28,12},{1,9},{5... | collective-permute-start | bytes 1572872 | tf_op jit(solution)/shard_map/ppermute | solution.py:409
  60.6 1.3 %collective-permute-start.6 = (bf16[64,1024]{1,0:T(8,128)(2,1)S(1)}, bf16[64,1024]{1,0:T(8,128)(2,1)S(1)}, u32[]{:S(2)}, u32[]{:S(2)}) collective-permute-start(bf16[64,1024]{1,0:T(8,128)(2,1)S(1)} %get-tuple-element.61), channel_id=1, source_target_pairs={{0,4},{4,0},{8,12},{12,8},{16,20},{20,16},{24,28},{28,24},{1,5},{5... | collective-permute-start | bytes 393224 | tf_op jit(solution)/shard_map/ppermute | solution.py:405
  60.6 1.5 %collective-permute-start.5 = (bf16[64,1024]{1,0:T(8,128)(2,1)S(1)}, bf16[64,1024]{1,0:T(8,128)(2,1)S(1)}, u32[]{:S(2)}, u32[]{:S(2)}) collective-permute-start(bf16[64,1024]{1,0:T(8,128)(2,1)S(1)} %get-tuple-element.60), channel_id=1, source_target_pairs={{0,4},{4,0},{8,12},{12,8},{16,20},{20,16},{24,28},{28,24},{1,5},{5... | collective-permute-start | bytes 393224 | tf_op jit(solution)/shard_map/ppermute | solution.py:405
  (5 other events, 31.7 us)

commit v7 on v6

--- a/solution.py
+++ b/solution.py
@@ -442,14 +442,16 @@
     far = siblings(first)
     first[0], _ = lax.optimization_barrier((first[0], diag0))
     out_first = evaluate(first, far)
+    second1 = swap_by_core(*after(diag0, payloads[1]), (4, 2))
     (diag1,) = after(out_first[1][0], diag1)
-    second = swap_by_core(*after(diag1, whole), (4, 2))
+    second0 = swap_by_core(*after(diag1, payloads[0]), (4, 2))
     diag = [diag0, diag1]
-    out_diag = evaluate(diag, siblings(diag))
-    sum_diag = combine(*out_diag, **sizes)
+    out_diag = evaluate(after(second1, *diag), siblings(diag))
+    scatter, mine, theirs = out_diag
+    sum_diag = combine(scatter, mine, after(second0, *theirs), **sizes)
     carry = swap_by_core(sum_diag, (4, 2))
-    (second,) = after(sum_diag, second)
-    out_second = evaluate([second], siblings([second]))
+    second = after(sum_diag, second0, second1)
+    out_second = evaluate(second, siblings(second))
     scatter, mine, theirs = out_first
     theirs = after(out_second[1][0], *theirs)
     sum_first = combine(scatter, mine, theirs, dtype=F32, **sizes)

time: 72.7 us -> 71.7 us (0.986)
  waiting for transfers between devices: 23.4 us -> 18.8 us
  starting transfers between devices: 20.9 us -> 23.7 us
    ppermute x8 -> x9, starting transfers between devices: 4.31 us -> 9 us  [swap_by_core(): return lax.ppermute(array, 'tile', [(i, i ^ bits[i % 2]) for i in range(8)])]
    ppermute x8 -> x9, waiting for transfers between devices: 18.7 us -> 16 us  [swap_by_core(): return lax.ppermute(array, 'tile', [(i, i ^ bits[i % 2]) for i in range(8)])]
    ppermute x12 -> x13, starting transfers between devices: 12.9 us -> 11 us  [swap(): return lax.ppermute(array, 'tile', [(i, i ^ bit) for i in range(8)])]
    ppermute x12 -> x13, waiting for transfers between devices: 4.64 us -> 2.83 us  [swap(): return lax.ppermute(array, 'tile', [(i, i ^ bit) for i in range(8)])]
    pallas_call x1, Pallas kernels: 2.82 us -> 3.59 us  [edge(): pl.pallas_call(edge_kernel, in_specs=specs, out_specs=[VMEM] * 4, out_sha...]
  transfers between devices with their start and end apart: 22 -> 24, of which waited for: 13 -> 12; matrix products, arithmetic and copies ran while one was open for 2% -> 2% of each run, Pallas kernels for 29% -> 29%
where the time goes in v7:
time: 71.7 us; the launch traced here: 71.4 us
  Pallas kernels  26.8 us (37%)
  starting transfers between devices  23.7 us (33%)
  waiting for transfers between devices  18.8 us (26%)
  other arithmetic  1 us (1%)
  local copies, waits for them, and re-layouts  0.82 us (1%)
    ppermute x9, waiting for transfers between devices, swap_by_core(): return lax.ppermute(array, 'tile', [(i, i ^ bits[i % 2]) for i in range(8)])  16 us
    pallas_call x5, Pallas kernels, experts(): pl.pallas_call(functools.partial(experts_kernel, order, rows, capacity),...  15.1 us
    ppermute x13, starting transfers between devices, swap(): return lax.ppermute(array, 'tile', [(i, i ^ bit) for i in range(8)])  11 us
    ppermute x9, starting transfers between devices, swap_by_core(): return lax.ppermute(array, 'tile', [(i, i ^ bits[i % 2]) for i in range(8)])  9 us
    pallas_call x1, Pallas kernels, interior(): pl.pallas_call(interior_kernel, in_specs=[VMEM] * 3, out_specs=[VMEM] * 3...  4.5 us
    pallas_call x1, Pallas kernels, edge(): pl.pallas_call(edge_kernel, in_specs=specs, out_specs=[VMEM] * 4, out_sha...  3.59 us
    ppermute x13, waiting for transfers between devices, swap(): return lax.ppermute(array, 'tile', [(i, i ^ bit) for i in range(8)])  2.83 us
    ppermute x1, starting transfers between devices, local(): before = lax.ppermute(last, 'tile', up)  2.39 us
  transfers between devices with their start and end apart: 24, of which 12 were waited for; matrix products, arithmetic and copies ran while one was open for 2% of the time, Pallas kernels for 29%

profile of v7, /device:TPU:0, one launch (start us, length us, event | category | flops | bytes accessed | tf_op | source)
XLA Modules:
  0.0 71.4 jit_solution(5310192506541435243)
XLA Ops:
  0.2 1.2 %pack.1 = (bf16[256,1024]{1,0:T(8,128)(2,1)S(1)}, bf16[256,1024]{1,0:T(8,128)(2,1)S(1)}) custom-call(bf16[256,1024]{1,0:T(8,128)(2,1)} %k.1, bf16[256,1024]{1,0:T(8,128)(2,1)} %v.3), custom_call_target="tpu_custom_call" | custom-call | bytes 2097152 | tf_op jit(solution)/shard_map/pack/pallas_call | solution.py:81
  1.4 2.4 %collective-permute-start = (bf16[256,1024]{1,0:T(8,128)(2,1)S(1)}, bf16[256,1024]{1,0:T(8,128)(2,1)S(1)}, u32[]{:S(2)}, u32[]{:S(2)}) collective-permute-start(bf16[256,1024]{1,0:T(8,128)(2,1)S(1)} %get-tuple-element.50), channel_id=1, source_target_pairs={{0,4},{4,8},{8,12},{12,16},{16,20},{20,24},{24,28},{1,5},{5,9},{9,... | collective-permute-start | bytes 1572872 | tf_op jit(solution)/shard_map/ppermute | solution.py:493
  3.8 1.3 %collective-permute-start.1 = (bf16[256,1024]{1,0:T(8,128)(2,1)S(1)}, bf16[256,1024]{1,0:T(8,128)(2,1)S(1)}, u32[]{:S(2)}, u32[]{:S(2)}) collective-permute-start(bf16[256,1024]{1,0:T(8,128)(2,1)S(1)} %get-tuple-element.51), channel_id=1, source_target_pairs={{4,0},{8,4},{12,8},{16,12},{20,16},{24,20},{28,24},{5,1},{9,5},{13... | collective-permute-start | bytes 1572872 | tf_op jit(solution)/shard_map/ppermute | solution.py:494
  6.8 4.5 %interior.1 = (f32[1024,256]{1,0:T(8,128)S(1)}, f32[16,256]{1,0:T(8,128)S(1)}, f32[16,256]{1,0:T(8,128)S(1)}) custom-call(bf16[256,1024]{1,0:T(8,128)(2,1)} %q.3, bf16[256,1024]{1,0:T(8,128)(2,1)} %k.1, bf16[256,1024]{1,0:T(8,128)(2,1)} %v.3), custom_call_target="tpu_custom_call" | custom-call | flops 8053063680 | bytes 2654208 | tf_op jit(solution)/shard_map/interior/pallas_call | solution.py:117
  11.4 3.6 %edge.1 = (bf16[256,1024]{1,0:T(8,128)(2,1)S(1)}, bf16[144,1024]{1,0:T(8,128)(2,1)S(1)}, bf16[128,1024]{1,0:T(8,128)(2,1)S(1)}, bf16[272,1024]{1,0:T(8,128)(2,1)}) custom-call(s32[2]{0:T(128)S(1)} %add_convert_fusion.live, bf16[256,1024]{1,0:T(8,128)(2,1)S(1)} %copy-done.4, bf16[256,1024]{1,0:T(8,128)(2,1)S(1)} %collective-permute-done.before, ...), custom_call_target="tpu_custom_call" | custom-call | flops 20132659200 | bytes 6922248 | tf_op jit(solution)/shard_map/edge/pallas_call | solution.py:202
  15.0 8.4 %collective-permute-start.2 = (bf16[144,1024]{1,0:T(8,128)(2,1)S(1)}, bf16[144,1024]{1,0:T(8,128)(2,1)S(1)}, u32[]{:S(2)}, u32[]{:S(2)}) collective-permute-start(bf16[144,1024]{1,0:T(8,128)(2,1)S(1)} %get-tuple-element.76.refs_0_.refs_2_), channel_id=1, source_target_pairs={{0,4},{4,0},{8,12},{12,8},{16,20},{20,16},{24,28},{28,24},{1,5},{5... | collective-permute-start | bytes 884744 | tf_op jit(solution)/shard_map/ppermute | solution.py:405
  23.4 1.5 %collective-permute-start.3 = (bf16[144,1024]{1,0:T(8,128)(2,1)S(1)}, bf16[144,1024]{1,0:T(8,128)(2,1)S(1)}, u32[]{:S(2)}, u32[]{:S(2)}) collective-permute-start(bf16[144,1024]{1,0:T(8,128)(2,1)S(1)} %get-tuple-element.76.refs_0_.refs_2_), channel_id=1, source_target_pairs={{0,8},{4,20},{8,0},{12,28},{16,24},{20,4},{24,16},{28,12},{1,9},{5... | collective-permute-start | bytes 884744 | tf_op jit(solution)/shard_map/ppermute | solution.py:409
  25.4 2.3 %experts_128.2 = (bf16[64,1024]{1,0:T(8,128)(2,1)S(1)}, bf16[64,1024]{1,0:T(8,128)(2,1)S(1)}, bf16[256,128]{1,0:T(8,128)(2,1)S(1)}) custom-call(s32[2]{0:T(128)S(1)} %pad_add_fusion.me, bf16[144,1024]{1,0:T(8,128)(2,1)S(1)} %get-tuple-element.76.refs_0_.refs_2_, bf16[144,1024]{1,0:T(8,128)(2,1)S(1)} %collective-permute-done.2.refs_1_.refs_3_, ...), custom_call_target="tpu_custom_call" | custom-call | flops 1107296256 | bytes 9568264 | tf_op jit(solution)/shard_map/experts_128/pallas_call | solution.py:296
  27.7 2.4 %collective-permute-done.3.refs_0_ = bf16[144,1024]{1,0:T(8,128)(2,1)S(1)} collective-permute-done((bf16[144,1024]{1,0:T(8,128)(2,1)S(1)}, bf16[144,1024]{1,0:T(8,128)(2,1)S(1)}, u32[]{:S(2)}, u32[]{:S(2)}) %collective-permute-start.3) | collective-permute-done | bytes 294944 | tf_op jit(solution)/shard_map/ppermute | solution.py:409
  30.5 2.3 %experts_128.3 = (bf16[64,1024]{1,0:T(8,128)(2,1)S(1)}, bf16[64,1024]{1,0:T(8,128)(2,1)S(1)}, bf16[256,128]{1,0:T(8,128)(2,1)S(1)}) custom-call(s32[2]{0:T(128)S(1)} %pad_add_fusion.me, bf16[128,1024]{1,0:T(8,128)(2,1)S(1)} %get-tuple-element.67.refs_0_, bf16[128,1024]{1,0:T(8,128)(2,1)S(1)} %collective-permute-done.4.refs_1_, ...), custom_call_target="tpu_custom_call" | custom-call | flops 1107296256 | bytes 10092552 | tf_op jit(solution)/shard_map/experts_128/pallas_call | solution.py:296
  32.7 1.2 %collective-permute-done.9.refs_1_ = bf16[128,1024]{1,0:T(8,128)(2,1)S(1)} collective-permute-done((bf16[128,1024]{1,0:T(8,128)(2,1)S(1)}, bf16[128,1024]{1,0:T(8,128)(2,1)S(1)}, u32[]{:S(2)}, u32[]{:S(2)}) %collective-permute-start.9) | collective-permute-done | bytes 262176 | tf_op jit(solution)/shard_map/ppermute | solution.py:409
  33.9 1.1 %collective-permute-start.12 = (bf16[128,1024]{1,0:T(8,128)(2,1)S(1)}, bf16[128,1024]{1,0:T(8,128)(2,1)S(1)}, u32[]{:S(2)}, u32[]{:S(2)}) collective-permute-start(bf16[128,1024]{1,0:T(8,128)(2,1)S(1)} %collective-permute-done.9.refs_1_), channel_id=1, source_target_pairs={{0,16},{4,12},{8,24},{12,4},{16,0},{20,28},{24,8},{28,20},{1,17},{... | collective-permute-start | bytes 786440 | tf_op jit(solution)/shard_map/ppermute | solution.py:409
  35.0 1.9 %collective-permute-done.7.refs_0_ = bf16[144,1024]{1,0:T(8,128)(2,1)S(1)} collective-permute-done((bf16[144,1024]{1,0:T(8,128)(2,1)S(1)}, bf16[144,1024]{1,0:T(8,128)(2,1)S(1)}, u32[]{:S(2)}, u32[]{:S(2)}) %collective-permute-start.7) | collective-permute-done | bytes 294944 | tf_op jit(solution)/shard_map/ppermute | solution.py:409
  37.4 3.5 %experts_256.3 = (bf16[128,1024]{1,0:T(8,128)(2,1)S(1)}, bf16[128,1024]{1,0:T(8,128)(2,1)S(1)}, bf16[512,128]{1,0:T(8,128)(2,1)S(1)}) custom-call(s32[2]{0:T(128)S(1)} %pad_add_fusion.me, bf16[144,1024]{1,0:T(8,128)(2,1)S(1)} %collective-permute-done.3.refs_0_, bf16[128,1024]{1,0:T(8,128)(2,1)S(1)} %collective-permute-done.9.refs_1_, ...), custom_call_target="tpu_custom_call" | custom-call | flops 2214592512 | bytes 10420232 | tf_op jit(solution)/shard_map/experts_256/pallas_call | solution.py:296
  41.0 2.0 %collective-permute-start.15 = (bf16[144,1024]{1,0:T(8,128)(2,1)S(1)}, bf16[144,1024]{1,0:T(8,128)(2,1)S(1)}, u32[]{:S(2)}, u32[]{:S(2)}) collective-permute-start(bf16[144,1024]{1,0:T(8,128)(2,1)S(1)} %get-tuple-element.76.refs_0_.refs_2_), channel_id=1, source_target_pairs={{0,16},{4,12},{8,24},{12,4},{16,0},{20,28},{24,8},{28,20},{1,17},{... | collective-permute-start | bytes 884744 | tf_op jit(solution)/shard_map/ppermute | solution.py:409
  43.2 3.7 %experts_256.4 = (bf16[128,1024]{1,0:T(8,128)(2,1)S(1)}, bf16[128,1024]{1,0:T(8,128)(2,1)S(1)}, bf16[512,128]{1,0:T(8,128)(2,1)S(1)}) custom-call(s32[2]{0:T(128)S(1)} %pad_add_fusion.me, bf16[144,1024]{1,0:T(8,128)(2,1)S(1)} %collective-permute-done.7.refs_0_, bf16[128,1024]{1,0:T(8,128)(2,1)S(1)} %collective-permute-done.12.refs_1_, ...), custom_call_target="tpu_custom_call" | custom-call | flops 2214592512 | bytes 10420232 | tf_op jit(solution)/shard_map/experts_256/pallas_call | solution.py:296
  49.4 1.2 %collective-permute-start.22 = (bf16[256,1024]{1,0:T(8,128)(2,1)S(1)}, bf16[256,1024]{1,0:T(8,128)(2,1)S(1)}, u32[]{:S(2)}, u32[]{:S(2)}) collective-permute-start(bf16[256,1024]{1,0:T(8,128)(2,1)S(1)} %combine.5), channel_id=1, source_target_pairs={{0,16},{4,12},{8,24},{12,4},{16,0},{20,28},{24,8},{28,20},{1,17},{... | collective-permute-start | bytes 1572872 | tf_op jit(solution)/shard_map/ppermute | solution.py:409
  50.8 3.5 %experts_256.5 = (bf16[128,1024]{1,0:T(8,128)(2,1)S(1)}, bf16[128,1024]{1,0:T(8,128)(2,1)S(1)}, bf16[512,128]{1,0:T(8,128)(2,1)S(1)}) custom-call(s32[2]{0:T(128)S(1)} %pad_add_fusion.me, bf16[144,1024]{1,0:T(8,128)(2,1)S(1)} %collective-permute-done.15.refs_0_, bf16[128,1024]{1,0:T(8,128)(2,1)S(1)} %collective-permute-done.8.refs_1_, ...), custom_call_target="tpu_custom_call" | custom-call | flops 2214592512 | bytes 10420232 | tf_op jit(solution)/shard_map/experts_256/pallas_call | solution.py:296
  54.9 1.0 %collective-permute-done.20.refs_2_ = bf16[128,1024]{1,0:T(8,128)(2,1)S(1)} collective-permute-done((bf16[128,1024]{1,0:T(8,128)(2,1)S(1)}, bf16[128,1024]{1,0:T(8,128)(2,1)S(1)}, u32[]{:S(2)}, u32[]{:S(2)}) %collective-permute-start.20) | collective-permute-done | bytes 262176 | tf_op jit(solution)/shard_map/ppermute | solution.py:405
  56.3 1.2 %collective-permute-start.21 = (bf16[256,1024]{1,0:T(8,128)(2,1)S(1)}, bf16[256,1024]{1,0:T(8,128)(2,1)S(1)}, u32[]{:S(2)}, u32[]{:S(2)}) collective-permute-start(bf16[256,1024]{1,0:T(8,128)(2,1)S(1)} %combine.7), channel_id=1, source_target_pairs={{0,16},{4,12},{8,24},{12,4},{16,0},{20,28},{24,8},{28,20},{1,17},{... | collective-permute-start | bytes 1572872 | tf_op jit(solution)/shard_map/ppermute | solution.py:409
  57.5 1.1 %collective-permute-done.22.b = bf16[256,1024]{1,0:T(8,128)(2,1)S(1)} collective-permute-done((bf16[256,1024]{1,0:T(8,128)(2,1)S(1)}, bf16[256,1024]{1,0:T(8,128)(2,1)S(1)}, u32[]{:S(2)}, u32[]{:S(2)}) %collective-permute-start.22) | collective-permute-done | bytes 524320 | tf_op jit(solution)/shard_map/ppermute | solution.py:409
  58.7 1.6 %collective-permute-start.23 = (bf16[256,1024]{1,0:T(8,128)(2,1)S(1)}, bf16[256,1024]{1,0:T(8,128)(2,1)S(1)}, u32[]{:S(2)}, u32[]{:S(2)}) collective-permute-start(bf16[256,1024]{1,0:T(8,128)(2,1)S(1)} %add.10), channel_id=1, source_target_pairs={{0,8},{4,20},{8,0},{12,28},{16,24},{20,4},{24,16},{28,12},{1,9},{5... | collective-permute-start | bytes 1572872 | tf_op jit(solution)/shard_map/ppermute | solution.py:409
  62.1 8.3 %collective-permute-done.21.b = bf16[256,1024]{1,0:T(8,128)(2,1)S(1)} collective-permute-done((bf16[256,1024]{1,0:T(8,128)(2,1)S(1)}, bf16[256,1024]{1,0:T(8,128)(2,1)S(1)}, u32[]{:S(2)}, u32[]{:S(2)}) %collective-permute-start.21) | collective-permute-done | bytes 524320 | tf_op jit(solution)/shard_map/ppermute | solution.py:409
  70.5 0.9 %add.11 = bf16[256,1024]{1,0:T(8,128)(2,1)} custom-call(f32[256,1024]{1,0:T(8,128)S(1)} %add.9.a, bf16[256,1024]{1,0:T(8,128)(2,1)S(1)} %collective-permute-done.23.b), custom_call_target="tpu_custom_call" | custom-call | flops 262144 | bytes 2097152 | tf_op jit(solution)/shard_map/add/pallas_call | solution.py:350
  (65 shorter events, 9.5 us)
Async XLA Ops:
  1.4 9.9 %collective-permute-start = (bf16[256,1024]{1,0:T(8,128)(2,1)S(1)}, bf16[256,1024]{1,0:T(8,128)(2,1)S(1)}, u32[]{:S(2)}, u32[]{:S(2)}) collective-permute-start(bf16[256,1024]{1,0:T(8,128)(2,1)S(1)} %get-tuple-element.50), channel_id=1, source_target_pairs={{0,4},{4,8},{8,12},{12,16},{16,20},{20,24},{24,28},{1,5},{5,9},{9,... | collective-permute-start | bytes 1572872 | tf_op jit(solution)/shard_map/ppermute | solution.py:493
  3.8 7.5 %collective-permute-start.1 = (bf16[256,1024]{1,0:T(8,128)(2,1)S(1)}, bf16[256,1024]{1,0:T(8,128)(2,1)S(1)}, u32[]{:S(2)}, u32[]{:S(2)}) collective-permute-start(bf16[256,1024]{1,0:T(8,128)(2,1)S(1)} %get-tuple-element.51), channel_id=1, source_target_pairs={{4,0},{8,4},{12,8},{16,12},{20,16},{24,20},{28,24},{5,1},{9,5},{13... | collective-permute-start | bytes 1572872 | tf_op jit(solution)/shard_map/ppermute | solution.py:494
  15.0 10.4 %collective-permute-start.2 = (bf16[144,1024]{1,0:T(8,128)(2,1)S(1)}, bf16[144,1024]{1,0:T(8,128)(2,1)S(1)}, u32[]{:S(2)}, u32[]{:S(2)}) collective-permute-start(bf16[144,1024]{1,0:T(8,128)(2,1)S(1)} %get-tuple-element.76.refs_0_.refs_2_), channel_id=1, source_target_pairs={{0,4},{4,0},{8,12},{12,8},{16,20},{20,16},{24,28},{28,24},{1,5},{5... | collective-permute-start | bytes 884744 | tf_op jit(solution)/shard_map/ppermute | solution.py:405
  23.4 6.7 %collective-permute-start.3 = (bf16[144,1024]{1,0:T(8,128)(2,1)S(1)}, bf16[144,1024]{1,0:T(8,128)(2,1)S(1)}, u32[]{:S(2)}, u32[]{:S(2)}) collective-permute-start(bf16[144,1024]{1,0:T(8,128)(2,1)S(1)} %get-tuple-element.76.refs_0_.refs_2_), channel_id=1, source_target_pairs={{0,8},{4,20},{8,0},{12,28},{16,24},{20,4},{24,16},{28,12},{1,9},{5... | collective-permute-start | bytes 884744 | tf_op jit(solution)/shard_map/ppermute | solution.py:409
  24.9 5.6 %collective-permute-start.4 = (bf16[128,1024]{1,0:T(8,128)(2,1)S(1)}, bf16[128,1024]{1,0:T(8,128)(2,1)S(1)}, u32[]{:S(2)}, u32[]{:S(2)}) collective-permute-start(bf16[128,1024]{1,0:T(8,128)(2,1)S(1)} %get-tuple-element.67.refs_0_), channel_id=1, source_target_pairs={{0,4},{4,0},{8,12},{12,8},{16,20},{20,16},{24,28},{28,24},{1,5},{5... | collective-permute-start | bytes 786440 | tf_op jit(solution)/shard_map/ppermute | solution.py:405
  24.9 9.0 %collective-permute-start.9 = (bf16[128,1024]{1,0:T(8,128)(2,1)S(1)}, bf16[128,1024]{1,0:T(8,128)(2,1)S(1)}, u32[]{:S(2)}, u32[]{:S(2)}) collective-permute-start(bf16[128,1024]{1,0:T(8,128)(2,1)S(1)} %get-tuple-element.67.refs_0_), channel_id=1, source_target_pairs={{0,8},{4,20},{8,0},{12,28},{16,24},{20,4},{24,16},{28,12},{1,9},{5... | collective-permute-start | bytes 786440 | tf_op jit(solution)/shard_map/ppermute | solution.py:409
  30.1 6.7 %collective-permute-start.7 = (bf16[144,1024]{1,0:T(8,128)(2,1)S(1)}, bf16[144,1024]{1,0:T(8,128)(2,1)S(1)}, u32[]{:S(2)}, u32[]{:S(2)}) collective-permute-start(bf16[144,1024]{1,0:T(8,128)(2,1)S(1)} %collective-permute-done.3.refs_0_), channel_id=1, source_target_pairs={{0,16},{4,12},{8,24},{12,4},{16,0},{20,28},{24,8},{28,20},{1,17},{... | collective-permute-start | bytes 884744 | tf_op jit(solution)/shard_map/ppermute | solution.py:409
  30.1 7.3 %collective-permute-start.10 = (bf16[144,1024]{1,0:T(8,128)(2,1)S(1)}, bf16[144,1024]{1,0:T(8,128)(2,1)S(1)}, u32[]{:S(2)}, u32[]{:S(2)}) collective-permute-start(bf16[144,1024]{1,0:T(8,128)(2,1)S(1)} %collective-permute-done.3.refs_0_), channel_id=1, source_target_pairs={{0,4},{4,0},{8,12},{12,8},{16,20},{20,16},{24,28},{28,24},{1,5},{5... | collective-permute-start | bytes 884744 | tf_op jit(solution)/shard_map/ppermute | solution.py:405
  33.9 3.5 %collective-permute-start.11 = (bf16[128,1024]{1,0:T(8,128)(2,1)S(1)}, bf16[128,1024]{1,0:T(8,128)(2,1)S(1)}, u32[]{:S(2)}, u32[]{:S(2)}) collective-permute-start(bf16[128,1024]{1,0:T(8,128)(2,1)S(1)} %collective-permute-done.9.refs_1_), channel_id=1, source_target_pairs={{0,4},{4,0},{8,12},{12,8},{16,20},{20,16},{24,28},{28,24},{1,5},{5... | collective-permute-start | bytes 786440 | tf_op jit(solution)/shard_map/ppermute | solution.py:405
  33.9 7.0 %collective-permute-start.12 = (bf16[128,1024]{1,0:T(8,128)(2,1)S(1)}, bf16[128,1024]{1,0:T(8,128)(2,1)S(1)}, u32[]{:S(2)}, u32[]{:S(2)}) collective-permute-start(bf16[128,1024]{1,0:T(8,128)(2,1)S(1)} %collective-permute-done.9.refs_1_), channel_id=1, source_target_pairs={{0,16},{4,12},{8,24},{12,4},{16,0},{20,28},{24,8},{28,20},{1,17},{... | collective-permute-start | bytes 786440 | tf_op jit(solution)/shard_map/ppermute | solution.py:409
  36.8 6.4 %collective-permute-start.8 = (bf16[128,1024]{1,0:T(8,128)(2,1)S(1)}, bf16[128,1024]{1,0:T(8,128)(2,1)S(1)}, u32[]{:S(2)}, u32[]{:S(2)}) collective-permute-start(bf16[128,1024]{1,0:T(8,128)(2,1)S(1)} %get-tuple-element.67.refs_0_), channel_id=1, source_target_pairs={{0,16},{4,12},{8,24},{12,4},{16,0},{20,28},{24,8},{28,20},{1,17},{... | collective-permute-start | bytes 786440 | tf_op jit(solution)/shard_map/ppermute | solution.py:409
  36.8 6.4 %collective-permute-start.13 = (bf16[144,1024]{1,0:T(8,128)(2,1)S(1)}, bf16[144,1024]{1,0:T(8,128)(2,1)S(1)}, u32[]{:S(2)}, u32[]{:S(2)}) collective-permute-start(bf16[144,1024]{1,0:T(8,128)(2,1)S(1)} %collective-permute-done.7.refs_0_), channel_id=1, source_target_pairs={{0,4},{4,0},{8,12},{12,8},{16,20},{20,16},{24,28},{28,24},{1,5},{5... | collective-permute-start | bytes 884744 | tf_op jit(solution)/shard_map/ppermute | solution.py:405
  40.9 2.3 %collective-permute-start.14 = (bf16[128,1024]{1,0:T(8,128)(2,1)S(1)}, bf16[128,1024]{1,0:T(8,128)(2,1)S(1)}, u32[]{:S(2)}, u32[]{:S(2)}) collective-permute-start(bf16[128,1024]{1,0:T(8,128)(2,1)S(1)} %collective-permute-done.12.refs_1_), channel_id=1, source_target_pairs={{0,4},{4,0},{8,12},{12,8},{16,20},{20,16},{24,28},{28,24},{1,5},{5... | collective-permute-start | bytes 786440 | tf_op jit(solution)/shard_map/ppermute | solution.py:405
  41.0 6.8 %collective-permute-start.15 = (bf16[144,1024]{1,0:T(8,128)(2,1)S(1)}, bf16[144,1024]{1,0:T(8,128)(2,1)S(1)}, u32[]{:S(2)}, u32[]{:S(2)}) collective-permute-start(bf16[144,1024]{1,0:T(8,128)(2,1)S(1)} %get-tuple-element.76.refs_0_.refs_2_), channel_id=1, source_target_pairs={{0,16},{4,12},{8,24},{12,4},{16,0},{20,28},{24,8},{28,20},{1,17},{... | collective-permute-start | bytes 884744 | tf_op jit(solution)/shard_map/ppermute | solution.py:409
  46.9 1.6 %collective-permute-start.16 = (bf16[128,1024]{1,0:T(8,128)(2,1)S(1)}, bf16[128,1024]{1,0:T(8,128)(2,1)S(1)}, u32[]{:S(2)}, u32[]{:S(2)}) collective-permute-start(bf16[128,1024]{1,0:T(8,128)(2,1)S(1)} %get-tuple-element.77), channel_id=1, source_target_pairs={{0,4},{4,0},{8,12},{12,8},{16,20},{20,16},{24,28},{28,24},{1,5},{5... | collective-permute-start | bytes 786440 | tf_op jit(solution)/shard_map/ppermute | solution.py:405
  48.8 2.0 %collective-permute-start.17 = (bf16[144,1024]{1,0:T(8,128)(2,1)S(1)}, bf16[144,1024]{1,0:T(8,128)(2,1)S(1)}, u32[]{:S(2)}, u32[]{:S(2)}) collective-permute-start(bf16[144,1024]{1,0:T(8,128)(2,1)S(1)} %collective-permute-done.15.refs_0_), channel_id=1, source_target_pairs={{0,4},{4,0},{8,12},{12,8},{16,20},{20,16},{24,28},{28,24},{1,5},{5... | collective-permute-start | bytes 884744 | tf_op jit(solution)/shard_map/ppermute | solution.py:405
  49.0 1.8 %collective-permute-start.18 = (bf16[128,1024]{1,0:T(8,128)(2,1)S(1)}, bf16[128,1024]{1,0:T(8,128)(2,1)S(1)}, u32[]{:S(2)}, u32[]{:S(2)}) collective-permute-start(bf16[128,1024]{1,0:T(8,128)(2,1)S(1)} %collective-permute-done.8.refs_1_), channel_id=1, source_target_pairs={{0,4},{4,0},{8,12},{12,8},{16,20},{20,16},{24,28},{28,24},{1,5},{5... | collective-permute-start | bytes 786440 | tf_op jit(solution)/shard_map/ppermute | solution.py:405
  49.4 9.2 %collective-permute-start.22 = (bf16[256,1024]{1,0:T(8,128)(2,1)S(1)}, bf16[256,1024]{1,0:T(8,128)(2,1)S(1)}, u32[]{:S(2)}, u32[]{:S(2)}) collective-permute-start(bf16[256,1024]{1,0:T(8,128)(2,1)S(1)} %combine.5), channel_id=1, source_target_pairs={{0,16},{4,12},{8,24},{12,4},{16,0},{20,28},{24,8},{28,20},{1,17},{... | collective-permute-start | bytes 1572872 | tf_op jit(solution)/shard_map/ppermute | solution.py:409
  50.6 4.1 %collective-permute-start.19 = (bf16[128,1024]{1,0:T(8,128)(2,1)S(1)}, bf16[128,1024]{1,0:T(8,128)(2,1)S(1)}, u32[]{:S(2)}, u32[]{:S(2)}) collective-permute-start(bf16[128,1024]{1,0:T(8,128)(2,1)S(1)} %get-tuple-element.84), channel_id=1, source_target_pairs={{0,4},{4,0},{8,12},{12,8},{16,20},{20,16},{24,28},{28,24},{1,5},{5... | collective-permute-start | bytes 786440 | tf_op jit(solution)/shard_map/ppermute | solution.py:405
  54.3 1.6 %collective-permute-start.20 = (bf16[128,1024]{1,0:T(8,128)(2,1)S(1)}, bf16[128,1024]{1,0:T(8,128)(2,1)S(1)}, u32[]{:S(2)}, u32[]{:S(2)}) collective-permute-start(bf16[128,1024]{1,0:T(8,128)(2,1)S(1)} %get-tuple-element.86), channel_id=1, source_target_pairs={{0,4},{4,0},{8,12},{12,8},{16,20},{20,16},{24,28},{28,24},{1,5},{5... | collective-permute-start | bytes 786440 | tf_op jit(solution)/shard_map/ppermute | solution.py:405
  56.3 14.2 %collective-permute-start.21 = (bf16[256,1024]{1,0:T(8,128)(2,1)S(1)}, bf16[256,1024]{1,0:T(8,128)(2,1)S(1)}, u32[]{:S(2)}, u32[]{:S(2)}) collective-permute-start(bf16[256,1024]{1,0:T(8,128)(2,1)S(1)} %combine.7), channel_id=1, source_target_pairs={{0,16},{4,12},{8,24},{12,4},{16,0},{20,28},{24,8},{28,20},{1,17},{... | collective-permute-start | bytes 1572872 | tf_op jit(solution)/shard_map/ppermute | solution.py:409
  58.7 11.9 %collective-permute-start.23 = (bf16[256,1024]{1,0:T(8,128)(2,1)S(1)}, bf16[256,1024]{1,0:T(8,128)(2,1)S(1)}, u32[]{:S(2)}, u32[]{:S(2)}) collective-permute-start(bf16[256,1024]{1,0:T(8,128)(2,1)S(1)} %add.10), channel_id=1, source_target_pairs={{0,8},{4,20},{8,0},{12,28},{16,24},{20,4},{24,16},{28,12},{1,9},{5... | collective-permute-start | bytes 1572872 | tf_op jit(solution)/shard_map/ppermute | solution.py:409
  60.2 1.3 %collective-permute-start.6 = (bf16[64,1024]{1,0:T(8,128)(2,1)S(1)}, bf16[64,1024]{1,0:T(8,128)(2,1)S(1)}, u32[]{:S(2)}, u32[]{:S(2)}) collective-permute-start(bf16[64,1024]{1,0:T(8,128)(2,1)S(1)} %get-tuple-element.65), channel_id=1, source_target_pairs={{0,4},{4,0},{8,12},{12,8},{16,20},{20,16},{24,28},{28,24},{1,5},{5... | collective-permute-start | bytes 393224 | tf_op jit(solution)/shard_map/ppermute | solution.py:405
  60.2 1.5 %collective-permute-start.5 = (bf16[64,1024]{1,0:T(8,128)(2,1)S(1)}, bf16[64,1024]{1,0:T(8,128)(2,1)S(1)}, u32[]{:S(2)}, u32[]{:S(2)}) collective-permute-start(bf16[64,1024]{1,0:T(8,128)(2,1)S(1)} %get-tuple-element.64), channel_id=1, source_target_pairs={{0,4},{4,0},{8,12},{12,8},{16,20},{20,16},{24,28},{28,24},{1,5},{5... | collective-permute-start | bytes 393224 | tf_op jit(solution)/shard_map/ppermute | solution.py:405
  (7 other events, 60.5 us)

commit v8 on v7

--- a/solution.py
+++ b/solution.py
@@ -126,28 +126,24 @@
     )(*args)
 
 
-def edge_kernel(live, q, before, behind, tops, sums, gain, acc, x, w, *rest):
-    meta = rest[0] if len(rest) == 7 else None
-    resid, payload0, payload1, whole = rest[-6:-2]
-    bias, att = rest[-2:]
+def edge_kernel(half, live, q, halo, tops, sums, gain, acc, x, w, *rest):
+    meta = rest[0] if len(rest) == 5 else None
+    resid, payload, bias, att = rest[-4:]
     step = 2 * HD
-    pairs = HEADS // 2
+    pairs = range(HEADS // 2)
     rows = q.shape[0] // 2
-    wide = before.shape[0] // 2
-    halos = (before, behind)
-    for half in range(2):
-        first = -wide if half == 0 else 2 * rows
-        bias[half] = window_bias(wide, first, rows, half * rows, live[half])
-    cells = [(pair, half) for pair in range(pairs) for half in range(2)]
+    wide = halo.shape[0] // 2
+    span = slice(half * rows, (half + 1) * rows)
+    first = -wide if half == 0 else 2 * rows
+    bias[...] = window_bias(wide, first, rows, half * rows, live[half])
     scores = []
-    for pair, half in cells:
+    for pair in pairs:
         cols = slice(pair * step, (pair + 1) * step)
-        queries = two_heads(q[half * rows : (half + 1) * rows, cols])
-        s = lax.dot_general(halos[half][:wide, cols], queries, NT, preferred_element_type=F32)
-        scores.append(s + bias[half])
+        queries = two_heads(q[span, cols])
+        s = lax.dot_general(halo[:wide, cols], queries, NT, preferred_element_type=F32)
+        scores.append(s + bias[...])
     weights = []
-    for (pair, half), s in zip(cells, scores):
-        span = slice(half * rows, (half + 1) * rows)
+    for pair, s in zip(pairs, scores):
         both = [slice(2 * pair + side, 2 * pair + side + 1) for side in range(2)]
         old = jnp.concatenate([tops[b, span] for b in both], axis=1)
         top = jnp.maximum(old, jnp.max(s, axis=0, keepdims=True))
@@ -156,63 +152,53 @@
         total = jnp.concatenate([sums[b, span] for b in both], axis=1) * shrink
         total = total + jnp.sum(p, axis=0, keepdims=True)
         weights.append((p.astype(BF16), shrink, 1.0 / total))
-    for (pair, half), (p, shrink, inverse) in zip(cells, weights):
-        span = slice(half * rows, (half + 1) * rows)
+    for pair, (p, shrink, inverse) in zip(pairs, weights):
         cols = slice(pair * step, (pair + 1) * step)
-        o = lax.dot_general(halos[half][wide:, cols], p, TN, preferred_element_type=F32)
+        o = lax.dot_general(halo[wide:, cols], p, TN, preferred_element_type=F32)
         for side in range(2):
             at = slice(side * rows, (side + 1) * rows)
             base = pair * step + side * HD
             value = acc[base : base + HD, span] * shrink[:, at]
             value = value + o[side * HD : (side + 1) * HD, at]
-            att[base : base + HD, span] = (value * inverse[:, at]).astype(BF16)
-    for half in range(2):
-        span = slice(half * rows, (half + 1) * rows)
-        res = x[span, :].astype(F32)
-        res = res + lax.dot_general(att[:, span], w[...], TN, preferred_element_type=F32)
-        res = res.astype(BF16)
-        resid[span, :] = res
-        res = res.astype(F32)
-        square = jnp.mean(res * res, axis=1, keepdims=True)
-        normed = (res * lax.rsqrt(square + 1e-06) * gain[...]).astype(BF16)
-        (payload0, payload1)[half][:rows, :] = normed
-        whole[span, :] = normed
+            att[base : base + HD, :] = (value * inverse[:, at]).astype(BF16)
+    res = x[span, :].astype(F32)
+    res = res + lax.dot_general(att[...], w[...], TN, preferred_element_type=F32)
+    res = res.astype(BF16)
+    resid[...] = res
+    res = res.astype(F32)
+    square = jnp.mean(res * res, axis=1, keepdims=True)
+    payload[:rows, :] = (res * lax.rsqrt(square + 1e-06) * gain[...]).astype(BF16)
     if meta is not None:
         copies = [
-            jnp.broadcast_to(meta[half : half + 1, :], (META // 2, meta.shape[1]))
-            for half in range(2)
+            jnp.broadcast_to(meta[i : i + 1, :], (META // 2, meta.shape[1])) for i in range(2)
         ]
-        payload0[rows:, :] = jnp.concatenate(copies, axis=0)
-        whole[2 * rows :, :] = jnp.concatenate(copies, axis=0)
-
-
-def edge(live, q, before, behind, acc, tops, sums, x, w, gain, meta):
+        payload[rows:, :] = jnp.concatenate(copies, axis=0)
+
+
+def edge(half, live, q, halo, acc, tops, sums, x, w, gain, meta):
     rows, model = q.shape[0] // 2, q.shape[1]
-    wide = before.shape[0] // 2
-    args = [live, q, before, behind, tops, sums, gain, acc, x, w]
+    wide = halo.shape[0] // 2
+    args = [live, q, halo, tops, sums, gain, acc, x, w]
     args += [] if meta is None else [meta]
-    specs = [SMEM] + [VMEM] * 9 + ([] if meta is None else [VMEM])
     extra = 0 if meta is None else META
     flat = [
-        jax.ShapeDtypeStruct((2 * rows, model), BF16),
+        jax.ShapeDtypeStruct((rows, model), BF16),
         jax.ShapeDtypeStruct((rows + extra, model), BF16),
-        jax.ShapeDtypeStruct((rows, model), BF16),
-        jax.ShapeDtypeStruct((2 * rows + extra, model), BF16),
     ]
     return pl.pallas_call(
-        edge_kernel,
-        in_specs=specs,
-        out_specs=[VMEM] * 4,
+        functools.partial(edge_kernel, half),
+        in_specs=[SMEM] + [VMEM] * (len(args) - 1),
+        out_specs=[VMEM] * 2,
         out_shape=flat,
         scratch_shapes=[
-            pltpu.VMEM((2, wide, 2 * rows), F32),
-            pltpu.VMEM((model, 2 * rows), BF16),
+            pltpu.VMEM((wide, 2 * rows), F32),
+            pltpu.VMEM((model, rows), BF16),
         ],
         compiler_params=pltpu.CompilerParams(vmem_limit_bytes=12 * MIB),
         cost_estimate=cost(
-            LONG * (8 * rows * wide * model + 4 * rows * model * model), 2 * HEADS * rows * wide, args, flat
+            4 * rows * wide * model + 2 * rows * model * model, HEADS * rows * wide, args, flat
         ),
-        name="edge",
+        name=f"edge_half{half}",
     )(*args)
 
 
@@ -321,14 +307,14 @@
         values = jnp.concatenate([mine, mine, theirs, theirs], axis=0)
         total = lax.dot_general(gates, values, TN, preferred_element_type=F32)
         at = slice(block * rows, (block + 1) * rows)
-        if len(refs) == 2:
-            total = total + refs[0][at, :].astype(F32)
+        if len(refs) == 3:
+            total = total + refs[block][...].astype(F32)
         result[at, :] = total.astype(result.dtype)
 
 
-def combine(scatters, outs_me, outs_sib, rows, capacity, start=None, dtype=BF16):
+def combine(scatters, outs_me, outs_sib, rows, capacity, start=(), dtype=BF16):
     model = outs_me[0].shape[1]
-    args = [*scatters, *outs_me, *outs_sib] + ([] if start is None else [start])
+    args = [*scatters, *outs_me, *outs_sib, *start]
     out = jax.ShapeDtypeStruct((2 * rows, model), dtype)
     return pl.pallas_call(
         functools.partial(combine_kernel, rows, capacity, len(outs_me)),
@@ -413,7 +399,7 @@
     return lax.optimization_barrier((first, *later))[1:]
 
 
-def routed_gather(me, payloads, whole, resid, weights, rows, capacity):
+def routed_gather(me, payloads, resids, weights, rows, capacity):
     sizes = dict(rows=rows, capacity=capacity)
 
     def evaluate(mine, theirs):
@@ -461,7 +447,7 @@
     sum_first = add(sum_first, *after(sum_second, carry), BF16)
     back_first = swap_by_core(sum_first, (2, 4))
     own = (scatter0, scatter1), (own0, own1), siblings((sent0, sent1))
-    total = combine(*own, start=resid, dtype=F32, **sizes)
+    total = combine(*own, start=resids, dtype=F32, **sizes)
     return add(add(total, back_second, F32), back_first, BF16)
 
 
@@ -504,14 +490,19 @@
         meta = jnp.stack(items).reshape(len(items), 2, rows).swapaxes(0, 1)
         meta = meta.reshape(2, len(items) * rows).astype(BF16)
     acc, tops, sums = interior(queries, key_vectors, values)
-    resid, *payloads, whole = edge(
-        live, queries, before, behind, acc, tops, sums, inputs, out_weight,
-        norm_gain[None, :], meta,
-    )
+    halves = [
+        edge(
+            half, live, queries, halo, acc, tops, sums, inputs, out_weight, norm_gain[None, :],
+            meta if half == 0 else None,
+        )
+        for half, halo in enumerate((before, behind))
+    ]
+    resids, payloads = zip(*halves)
     if fast:
         weights = (w_gate[0], w_up[0], w_down[0])
-        return routed_gather(me, payloads, whole, resid, weights, rows, capacity)
-    return routed_all_to_all(whole, resid, routes, route_gates, w_gate[0], w_up[0], w_down[0])
+        return routed_gather(me, payloads, resids, weights, rows, capacity)
+    payload, resid = jnp.concatenate(payloads, axis=0), jnp.concatenate(resids, axis=0)
+    return routed_all_to_all(payload, resid, routes, route_gates, w_gate[0], w_up[0], w_down[0])
 
 
 def solution(mesh):

time: 71.7 us -> 68.1 us (0.950)
  starting transfers between devices: 23.7 us -> 21 us
  waiting for transfers between devices: 18.8 us -> 17.9 us
    ppermute x13, starting transfers between devices: 11 us -> 7.76 us  [swap(): return lax.ppermute(array, 'tile', [(i, i ^ bit) for i in range(8)])]
    ppermute x9, waiting for transfers between devices: 16 us -> 15.2 us  [swap_by_core(): return lax.ppermute(array, 'tile', [(i, i ^ bits[i % 2]) for i in range(8)])]
    pallas_call x1 -> x2, Pallas kernels: 3.59 us -> 3.63 us  [edge(): pl.pallas_call(functools.partial(edge_kernel, half), in_specs=[SMEM] + [V...]
  transfers between devices with their start and end apart: 24 -> 24, of which waited for: 12 -> 10; matrix products, arithmetic and copies ran while one was open for 2% -> 2% of each run, Pallas kernels for 29% -> 36%
where the time goes in v8:
time: 68.1 us; the launch traced here: 67.8 us
  Pallas kernels  26.9 us (40%)
  starting transfers between devices  21 us (31%)
  waiting for transfers between devices  17.9 us (26%)
  other arithmetic  1 us (1%)
  local copies, waits for them, and re-layouts  0.82 us (1%)
    ppermute x9, waiting for transfers between devices, swap_by_core(): return lax.ppermute(array, 'tile', [(i, i ^ bits[i % 2]) for i in range(8)])  15.2 us
    pallas_call x5, Pallas kernels, experts(): pl.pallas_call(functools.partial(experts_kernel, order, rows, capacity),...  15.1 us
    ppermute x9, starting transfers between devices, swap_by_core(): return lax.ppermute(array, 'tile', [(i, i ^ bits[i % 2]) for i in range(8)])  9.57 us
    ppermute x13, starting transfers between devices, swap(): return lax.ppermute(array, 'tile', [(i, i ^ bit) for i in range(8)])  7.76 us
    pallas_call x1, Pallas kernels, interior(): pl.pallas_call(interior_kernel, in_specs=[VMEM] * 3, out_specs=[VMEM] * 3...  4.5 us
    pallas_call x2, Pallas kernels, edge(): pl.pallas_call(functools.partial(edge_kernel, half), in_specs=[SMEM] + [V...  3.63 us
    ppermute x13, waiting for transfers between devices, swap(): return lax.ppermute(array, 'tile', [(i, i ^ bit) for i in range(8)])  2.69 us
    ppermute x1, starting transfers between devices, local(): before = lax.ppermute(last, 'tile', up)  2.39 us
  transfers between devices with their start and end apart: 24, of which 10 were waited for; matrix products, arithmetic and copies ran while one was open for 2% of the time, Pallas kernels for 36%

profile of v8, /device:TPU:0, one launch (start us, length us, event | category | flops | bytes accessed | tf_op | source)
XLA Modules:
  0.0 67.8 jit_solution(11152845637642415629)
XLA Ops:
  0.2 1.2 %pack.1 = (bf16[256,1024]{1,0:T(8,128)(2,1)S(1)}, bf16[256,1024]{1,0:T(8,128)(2,1)S(1)}) custom-call(bf16[256,1024]{1,0:T(8,128)(2,1)} %k.1, bf16[256,1024]{1,0:T(8,128)(2,1)} %v.3), custom_call_target="tpu_custom_call" | custom-call | bytes 2097152 | tf_op jit(solution)/shard_map/pack/pallas_call | solution.py:81
  1.4 2.4 %collective-permute-start = (bf16[256,1024]{1,0:T(8,128)(2,1)S(1)}, bf16[256,1024]{1,0:T(8,128)(2,1)S(1)}, u32[]{:S(2)}, u32[]{:S(2)}) collective-permute-start(bf16[256,1024]{1,0:T(8,128)(2,1)S(1)} %get-tuple-element.51), channel_id=1, source_target_pairs={{0,4},{4,8},{8,12},{12,16},{16,20},{20,24},{24,28},{1,5},{5,9},{9,... | collective-permute-start | bytes 1572872 | tf_op jit(solution)/shard_map/ppermute | solution.py:479
  3.8 1.3 %collective-permute-start.3 = (bf16[256,1024]{1,0:T(8,128)(2,1)S(1)}, bf16[256,1024]{1,0:T(8,128)(2,1)S(1)}, u32[]{:S(2)}, u32[]{:S(2)}) collective-permute-start(bf16[256,1024]{1,0:T(8,128)(2,1)S(1)} %get-tuple-element.59), channel_id=1, source_target_pairs={{4,0},{8,4},{12,8},{16,12},{20,16},{24,20},{28,24},{5,1},{9,5},{13... | collective-permute-start | bytes 1572872 | tf_op jit(solution)/shard_map/ppermute | solution.py:480
  6.7 4.5 %interior.1 = (f32[1024,256]{1,0:T(8,128)S(1)}, f32[16,256]{1,0:T(8,128)S(1)}, f32[16,256]{1,0:T(8,128)S(1)}) custom-call(bf16[256,1024]{1,0:T(8,128)(2,1)} %q.5, bf16[256,1024]{1,0:T(8,128)(2,1)} %k.1, bf16[256,1024]{1,0:T(8,128)(2,1)} %v.3), custom_call_target="tpu_custom_call" | custom-call | flops 8053063680 | bytes 2654208 | tf_op jit(solution)/shard_map/interior/pallas_call | solution.py:117
  11.4 1.8 %edge_half0.1 = (bf16[128,1024]{1,0:T(8,128)(2,1)S(1)}, bf16[144,1024]{1,0:T(8,128)(2,1)S(1)}) custom-call(s32[2]{0:T(128)S(1)} %add_convert_fusion.live, bf16[256,1024]{1,0:T(8,128)(2,1)S(1)} %copy-done.4, bf16[256,1024]{1,0:T(8,128)(2,1)S(1)} %collective-permute-done.halo, f32[16,256]{1,0:T(8,128)S(1)} %get-tuple-element.52.tops, ...), custom_call_target="tpu_custom_call" | custom-call | flops 335544320 | bytes 5316616 | tf_op jit(solution)/shard_map/edge_half0/pallas_call | solution.py:188
  13.2 3.3 %collective-permute-start.1 = (bf16[144,1024]{1,0:T(8,128)(2,1)S(1)}, bf16[144,1024]{1,0:T(8,128)(2,1)S(1)}, u32[]{:S(2)}, u32[]{:S(2)}) collective-permute-start(bf16[144,1024]{1,0:T(8,128)(2,1)S(1)} %get-tuple-element.78.refs_0_.refs_2_), channel_id=1, source_target_pairs={{0,4},{4,0},{8,12},{12,8},{16,20},{20,16},{24,28},{28,24},{1,5},{5... | collective-permute-start | bytes 884744 | tf_op jit(solution)/shard_map/ppermute | solution.py:391
  16.5 2.2 %collective-permute-start.2 = (bf16[144,1024]{1,0:T(8,128)(2,1)S(1)}, bf16[144,1024]{1,0:T(8,128)(2,1)S(1)}, u32[]{:S(2)}, u32[]{:S(2)}) collective-permute-start(bf16[144,1024]{1,0:T(8,128)(2,1)S(1)} %get-tuple-element.78.refs_0_.refs_2_), channel_id=1, source_target_pairs={{0,8},{4,20},{8,0},{12,28},{16,24},{20,4},{24,16},{28,12},{1,9},{5... | collective-permute-start | bytes 884744 | tf_op jit(solution)/shard_map/ppermute | solution.py:395
  18.7 1.8 %edge_half1.1 = (bf16[128,1024]{1,0:T(8,128)(2,1)S(1)}, bf16[128,1024]{1,0:T(8,128)(2,1)S(1)}) custom-call(s32[2]{0:T(128)S(1)} %add_convert_fusion.live, bf16[256,1024]{1,0:T(8,128)(2,1)S(1)} %copy-done.4, bf16[256,1024]{1,0:T(8,128)(2,1)S(1)} %collective-permute-done.3.halo, f32[16,256]{1,0:T(8,128)S(1)} %get-tuple-element.52.tops, ...), custom_call_target="tpu_custom_call" | custom-call | flops 335544320 | bytes 5279752 | tf_op jit(solution)/shard_map/edge_half1/pallas_call | solution.py:188
  20.5 2.1 %collective-permute-start.4 = (bf16[128,1024]{1,0:T(8,128)(2,1)S(1)}, bf16[128,1024]{1,0:T(8,128)(2,1)S(1)}, u32[]{:S(2)}, u32[]{:S(2)}) collective-permute-start(bf16[128,1024]{1,0:T(8,128)(2,1)S(1)} %get-tuple-element.69.refs_0_), channel_id=1, source_target_pairs={{0,4},{4,0},{8,12},{12,8},{16,20},{20,16},{24,28},{28,24},{1,5},{5... | collective-permute-start | bytes 786440 | tf_op jit(solution)/shard_map/ppermute | solution.py:391
  23.1 2.2 %experts_128.2 = (bf16[64,1024]{1,0:T(8,128)(2,1)S(1)}, bf16[64,1024]{1,0:T(8,128)(2,1)S(1)}, bf16[256,128]{1,0:T(8,128)(2,1)S(1)}) custom-call(s32[2]{0:T(128)S(1)} %pad_add_fusion.me, bf16[144,1024]{1,0:T(8,128)(2,1)S(1)} %get-tuple-element.78.refs_0_.refs_2_, bf16[144,1024]{1,0:T(8,128)(2,1)S(1)} %collective-permute-done.1.refs_1_.refs_3_, ...), custom_call_target="tpu_custom_call" | custom-call | flops 1107296256 | bytes 9568264 | tf_op jit(solution)/shard_map/experts_128/pallas_call | solution.py:282
  25.4 1.9 %collective-permute-start.7 = (bf16[144,1024]{1,0:T(8,128)(2,1)S(1)}, bf16[144,1024]{1,0:T(8,128)(2,1)S(1)}, u32[]{:S(2)}, u32[]{:S(2)}) collective-permute-start(bf16[144,1024]{1,0:T(8,128)(2,1)S(1)} %collective-permute-done.2.refs_0_), channel_id=1, source_target_pairs={{0,16},{4,12},{8,24},{12,4},{16,0},{20,28},{24,8},{28,20},{1,17},{... | collective-permute-start | bytes 884744 | tf_op jit(solution)/shard_map/ppermute | solution.py:395
  27.3 2.3 %experts_128.3 = (bf16[64,1024]{1,0:T(8,128)(2,1)S(1)}, bf16[64,1024]{1,0:T(8,128)(2,1)S(1)}, bf16[256,128]{1,0:T(8,128)(2,1)S(1)}) custom-call(s32[2]{0:T(128)S(1)} %pad_add_fusion.me, bf16[128,1024]{1,0:T(8,128)(2,1)S(1)} %get-tuple-element.69.refs_0_, bf16[128,1024]{1,0:T(8,128)(2,1)S(1)} %collective-permute-done.4.refs_1_, ...), custom_call_target="tpu_custom_call" | custom-call | flops 1107296256 | bytes 10092552 | tf_op jit(solution)/shard_map/experts_128/pallas_call | solution.py:282
  30.7 1.5 %collective-permute-done.7.refs_0_ = bf16[144,1024]{1,0:T(8,128)(2,1)S(1)} collective-permute-done((bf16[144,1024]{1,0:T(8,128)(2,1)S(1)}, bf16[144,1024]{1,0:T(8,128)(2,1)S(1)}, u32[]{:S(2)}, u32[]{:S(2)}) %collective-permute-start.7) | collective-permute-done | bytes 294944 | tf_op jit(solution)/shard_map/ppermute | solution.py:395
  32.2 1.9 %collective-permute-start.8 = (bf16[128,1024]{1,0:T(8,128)(2,1)S(1)}, bf16[128,1024]{1,0:T(8,128)(2,1)S(1)}, u32[]{:S(2)}, u32[]{:S(2)}) collective-permute-start(bf16[128,1024]{1,0:T(8,128)(2,1)S(1)} %get-tuple-element.69.refs_0_), channel_id=1, source_target_pairs={{0,16},{4,12},{8,24},{12,4},{16,0},{20,28},{24,8},{28,20},{1,17},{... | collective-permute-start | bytes 786440 | tf_op jit(solution)/shard_map/ppermute | solution.py:395
  34.0 3.5 %experts_256.3 = (bf16[128,1024]{1,0:T(8,128)(2,1)S(1)}, bf16[128,1024]{1,0:T(8,128)(2,1)S(1)}, bf16[512,128]{1,0:T(8,128)(2,1)S(1)}) custom-call(s32[2]{0:T(128)S(1)} %pad_add_fusion.me, bf16[144,1024]{1,0:T(8,128)(2,1)S(1)} %collective-permute-done.2.refs_0_, bf16[128,1024]{1,0:T(8,128)(2,1)S(1)} %collective-permute-done.9.refs_1_, ...), custom_call_target="tpu_custom_call" | custom-call | flops 2214592512 | bytes 10420232 | tf_op jit(solution)/shard_map/experts_256/pallas_call | solution.py:282
  38.3 1.1 %collective-permute-done.8.refs_1_ = bf16[128,1024]{1,0:T(8,128)(2,1)S(1)} collective-permute-done((bf16[128,1024]{1,0:T(8,128)(2,1)S(1)}, bf16[128,1024]{1,0:T(8,128)(2,1)S(1)}, u32[]{:S(2)}, u32[]{:S(2)}) %collective-permute-start.8) | collective-permute-done | bytes 262176 | tf_op jit(solution)/shard_map/ppermute | solution.py:395
  39.3 3.7 %experts_256.4 = (bf16[128,1024]{1,0:T(8,128)(2,1)S(1)}, bf16[128,1024]{1,0:T(8,128)(2,1)S(1)}, bf16[512,128]{1,0:T(8,128)(2,1)S(1)}) custom-call(s32[2]{0:T(128)S(1)} %pad_add_fusion.me, bf16[144,1024]{1,0:T(8,128)(2,1)S(1)} %collective-permute-done.7.refs_0_, bf16[128,1024]{1,0:T(8,128)(2,1)S(1)} %collective-permute-done.12.refs_1_, ...), custom_call_target="tpu_custom_call" | custom-call | flops 2214592512 | bytes 10420232 | tf_op jit(solution)/shard_map/experts_256/pallas_call | solution.py:282
  43.4 1.4 %collective-permute-done.15.refs_0_ = bf16[144,1024]{1,0:T(8,128)(2,1)S(1)} collective-permute-done((bf16[144,1024]{1,0:T(8,128)(2,1)S(1)}, bf16[144,1024]{1,0:T(8,128)(2,1)S(1)}, u32[]{:S(2)}, u32[]{:S(2)}) %collective-permute-start.15) | collective-permute-done | bytes 294944 | tf_op jit(solution)/shard_map/ppermute | solution.py:395
  47.2 3.5 %experts_256.5 = (bf16[128,1024]{1,0:T(8,128)(2,1)S(1)}, bf16[128,1024]{1,0:T(8,128)(2,1)S(1)}, bf16[512,128]{1,0:T(8,128)(2,1)S(1)}) custom-call(s32[2]{0:T(128)S(1)} %pad_add_fusion.me, bf16[144,1024]{1,0:T(8,128)(2,1)S(1)} %collective-permute-done.15.refs_0_, bf16[128,1024]{1,0:T(8,128)(2,1)S(1)} %collective-permute-done.8.refs_1_, ...), custom_call_target="tpu_custom_call" | custom-call | flops 2214592512 | bytes 10420232 | tf_op jit(solution)/shard_map/experts_256/pallas_call | solution.py:282
  51.2 1.1 %collective-permute-done.20.refs_2_ = bf16[128,1024]{1,0:T(8,128)(2,1)S(1)} collective-permute-done((bf16[128,1024]{1,0:T(8,128)(2,1)S(1)}, bf16[128,1024]{1,0:T(8,128)(2,1)S(1)}, u32[]{:S(2)}, u32[]{:S(2)}) %collective-permute-start.20) | collective-permute-done | bytes 262176 | tf_op jit(solution)/shard_map/ppermute | solution.py:391
  52.6 0.9 %collective-permute-start.21 = (bf16[256,1024]{1,0:T(8,128)(2,1)S(1)}, bf16[256,1024]{1,0:T(8,128)(2,1)S(1)}, u32[]{:S(2)}, u32[]{:S(2)}) collective-permute-start(bf16[256,1024]{1,0:T(8,128)(2,1)S(1)} %combine.7), channel_id=1, source_target_pairs={{0,16},{4,12},{8,24},{12,4},{16,0},{20,28},{24,8},{28,20},{1,17},{... | collective-permute-start | bytes 1572872 | tf_op jit(solution)/shard_map/ppermute | solution.py:395
  53.5 1.4 %collective-permute-done.22.b = bf16[256,1024]{1,0:T(8,128)(2,1)S(1)} collective-permute-done((bf16[256,1024]{1,0:T(8,128)(2,1)S(1)}, bf16[256,1024]{1,0:T(8,128)(2,1)S(1)}, u32[]{:S(2)}, u32[]{:S(2)}) %collective-permute-start.22) | collective-permute-done | bytes 524320 | tf_op jit(solution)/shard_map/ppermute | solution.py:395
  57.5 9.3 %collective-permute-done.21.b = bf16[256,1024]{1,0:T(8,128)(2,1)S(1)} collective-permute-done((bf16[256,1024]{1,0:T(8,128)(2,1)S(1)}, bf16[256,1024]{1,0:T(8,128)(2,1)S(1)}, u32[]{:S(2)}, u32[]{:S(2)}) %collective-permute-start.21) | collective-permute-done | bytes 524320 | tf_op jit(solution)/shard_map/ppermute | solution.py:395
  66.9 0.9 %add.11 = bf16[256,1024]{1,0:T(8,128)(2,1)} custom-call(f32[256,1024]{1,0:T(8,128)S(1)} %add.9.a, bf16[256,1024]{1,0:T(8,128)(2,1)S(1)} %collective-permute-done.23.b), custom_call_target="tpu_custom_call" | custom-call | flops 262144 | bytes 2097152 | tf_op jit(solution)/shard_map/add/pallas_call | solution.py:336
  (66 shorter events, 10.4 us)
Async XLA Ops:
  1.4 9.9 %collective-permute-start = (bf16[256,1024]{1,0:T(8,128)(2,1)S(1)}, bf16[256,1024]{1,0:T(8,128)(2,1)S(1)}, u32[]{:S(2)}, u32[]{:S(2)}) collective-permute-start(bf16[256,1024]{1,0:T(8,128)(2,1)S(1)} %get-tuple-element.51), channel_id=1, source_target_pairs={{0,4},{4,8},{8,12},{12,16},{16,20},{20,24},{24,28},{1,5},{5,9},{9,... | collective-permute-start | bytes 1572872 | tf_op jit(solution)/shard_map/ppermute | solution.py:479
  3.8 14.9 %collective-permute-start.3 = (bf16[256,1024]{1,0:T(8,128)(2,1)S(1)}, bf16[256,1024]{1,0:T(8,128)(2,1)S(1)}, u32[]{:S(2)}, u32[]{:S(2)}) collective-permute-start(bf16[256,1024]{1,0:T(8,128)(2,1)S(1)} %get-tuple-element.59), channel_id=1, source_target_pairs={{4,0},{8,4},{12,8},{16,12},{20,16},{24,20},{28,24},{5,1},{9,5},{13... | collective-permute-start | bytes 1572872 | tf_op jit(solution)/shard_map/ppermute | solution.py:480
  13.2 9.9 %collective-permute-start.1 = (bf16[144,1024]{1,0:T(8,128)(2,1)S(1)}, bf16[144,1024]{1,0:T(8,128)(2,1)S(1)}, u32[]{:S(2)}, u32[]{:S(2)}) collective-permute-start(bf16[144,1024]{1,0:T(8,128)(2,1)S(1)} %get-tuple-element.78.refs_0_.refs_2_), channel_id=1, source_target_pairs={{0,4},{4,0},{8,12},{12,8},{16,20},{20,16},{24,28},{28,24},{1,5},{5... | collective-permute-start | bytes 884744 | tf_op jit(solution)/shard_map/ppermute | solution.py:391
  16.5 8.9 %collective-permute-start.2 = (bf16[144,1024]{1,0:T(8,128)(2,1)S(1)}, bf16[144,1024]{1,0:T(8,128)(2,1)S(1)}, u32[]{:S(2)}, u32[]{:S(2)}) collective-permute-start(bf16[144,1024]{1,0:T(8,128)(2,1)S(1)} %get-tuple-element.78.refs_0_.refs_2_), channel_id=1, source_target_pairs={{0,8},{4,20},{8,0},{12,28},{16,24},{20,4},{24,16},{28,12},{1,9},{5... | collective-permute-start | bytes 884744 | tf_op jit(solution)/shard_map/ppermute | solution.py:395
  20.5 6.8 %collective-permute-start.4 = (bf16[128,1024]{1,0:T(8,128)(2,1)S(1)}, bf16[128,1024]{1,0:T(8,128)(2,1)S(1)}, u32[]{:S(2)}, u32[]{:S(2)}) collective-permute-start(bf16[128,1024]{1,0:T(8,128)(2,1)S(1)} %get-tuple-element.69.refs_0_), channel_id=1, source_target_pairs={{0,4},{4,0},{8,12},{12,8},{16,20},{20,16},{24,28},{28,24},{1,5},{5... | collective-permute-start | bytes 786440 | tf_op jit(solution)/shard_map/ppermute | solution.py:391
  22.6 7.4 %collective-permute-start.9 = (bf16[128,1024]{1,0:T(8,128)(2,1)S(1)}, bf16[128,1024]{1,0:T(8,128)(2,1)S(1)}, u32[]{:S(2)}, u32[]{:S(2)}) collective-permute-start(bf16[128,1024]{1,0:T(8,128)(2,1)S(1)} %get-tuple-element.69.refs_0_), channel_id=1, source_target_pairs={{0,8},{4,20},{8,0},{12,28},{16,24},{20,4},{24,16},{28,12},{1,9},{5... | collective-permute-start | bytes 786440 | tf_op jit(solution)/shard_map/ppermute | solution.py:395
  25.4 6.8 %collective-permute-start.7 = (bf16[144,1024]{1,0:T(8,128)(2,1)S(1)}, bf16[144,1024]{1,0:T(8,128)(2,1)S(1)}, u32[]{:S(2)}, u32[]{:S(2)}) collective-permute-start(bf16[144,1024]{1,0:T(8,128)(2,1)S(1)} %collective-permute-done.2.refs_0_), channel_id=1, source_target_pairs={{0,16},{4,12},{8,24},{12,4},{16,0},{20,28},{24,8},{28,20},{1,17},{... | collective-permute-start | bytes 884744 | tf_op jit(solution)/shard_map/ppermute | solution.py:395
  27.3 6.7 %collective-permute-start.10 = (bf16[144,1024]{1,0:T(8,128)(2,1)S(1)}, bf16[144,1024]{1,0:T(8,128)(2,1)S(1)}, u32[]{:S(2)}, u32[]{:S(2)}) collective-permute-start(bf16[144,1024]{1,0:T(8,128)(2,1)S(1)} %collective-permute-done.2.refs_0_), channel_id=1, source_target_pairs={{0,4},{4,0},{8,12},{12,8},{16,20},{20,16},{24,28},{28,24},{1,5},{5... | collective-permute-start | bytes 884744 | tf_op jit(solution)/shard_map/ppermute | solution.py:391
  30.0 4.0 %collective-permute-start.11 = (bf16[128,1024]{1,0:T(8,128)(2,1)S(1)}, bf16[128,1024]{1,0:T(8,128)(2,1)S(1)}, u32[]{:S(2)}, u32[]{:S(2)}) collective-permute-start(bf16[128,1024]{1,0:T(8,128)(2,1)S(1)} %collective-permute-done.9.refs_1_), channel_id=1, source_target_pairs={{0,4},{4,0},{8,12},{12,8},{16,20},{20,16},{24,28},{28,24},{1,5},{5... | collective-permute-start | bytes 786440 | tf_op jit(solution)/shard_map/ppermute | solution.py:391
  30.1 7.4 %collective-permute-start.12 = (bf16[128,1024]{1,0:T(8,128)(2,1)S(1)}, bf16[128,1024]{1,0:T(8,128)(2,1)S(1)}, u32[]{:S(2)}, u32[]{:S(2)}) collective-permute-start(bf16[128,1024]{1,0:T(8,128)(2,1)S(1)} %collective-permute-done.9.refs_1_), channel_id=1, source_target_pairs={{0,16},{4,12},{8,24},{12,4},{16,0},{20,28},{24,8},{28,20},{1,17},{... | collective-permute-start | bytes 786440 | tf_op jit(solution)/shard_map/ppermute | solution.py:395
  32.2 7.2 %collective-permute-start.8 = (bf16[128,1024]{1,0:T(8,128)(2,1)S(1)}, bf16[128,1024]{1,0:T(8,128)(2,1)S(1)}, u32[]{:S(2)}, u32[]{:S(2)}) collective-permute-start(bf16[128,1024]{1,0:T(8,128)(2,1)S(1)} %get-tuple-element.69.refs_0_), channel_id=1, source_target_pairs={{0,16},{4,12},{8,24},{12,4},{16,0},{20,28},{24,8},{28,20},{1,17},{... | collective-permute-start | bytes 786440 | tf_op jit(solution)/shard_map/ppermute | solution.py:395
  34.0 5.3 %collective-permute-start.13 = (bf16[144,1024]{1,0:T(8,128)(2,1)S(1)}, bf16[144,1024]{1,0:T(8,128)(2,1)S(1)}, u32[]{:S(2)}, u32[]{:S(2)}) collective-permute-start(bf16[144,1024]{1,0:T(8,128)(2,1)S(1)} %collective-permute-done.7.refs_0_), channel_id=1, source_target_pairs={{0,4},{4,0},{8,12},{12,8},{16,20},{20,16},{24,28},{28,24},{1,5},{5... | collective-permute-start | bytes 884744 | tf_op jit(solution)/shard_map/ppermute | solution.py:391
  37.5 1.8 %collective-permute-start.14 = (bf16[128,1024]{1,0:T(8,128)(2,1)S(1)}, bf16[128,1024]{1,0:T(8,128)(2,1)S(1)}, u32[]{:S(2)}, u32[]{:S(2)}) collective-permute-start(bf16[128,1024]{1,0:T(8,128)(2,1)S(1)} %collective-permute-done.12.refs_1_), channel_id=1, source_target_pairs={{0,4},{4,0},{8,12},{12,8},{16,20},{20,16},{24,28},{28,24},{1,5},{5... | collective-permute-start | bytes 786440 | tf_op jit(solution)/shard_map/ppermute | solution.py:391
  38.1 6.7 %collective-permute-start.15 = (bf16[144,1024]{1,0:T(8,128)(2,1)S(1)}, bf16[144,1024]{1,0:T(8,128)(2,1)S(1)}, u32[]{:S(2)}, u32[]{:S(2)}) collective-permute-start(bf16[144,1024]{1,0:T(8,128)(2,1)S(1)} %get-tuple-element.78.refs_0_.refs_2_), channel_id=1, source_target_pairs={{0,16},{4,12},{8,24},{12,4},{16,0},{20,28},{24,8},{28,20},{1,17},{... | collective-permute-start | bytes 884744 | tf_op jit(solution)/shard_map/ppermute | solution.py:395
  43.0 1.8 %collective-permute-start.16 = (bf16[128,1024]{1,0:T(8,128)(2,1)S(1)}, bf16[128,1024]{1,0:T(8,128)(2,1)S(1)}, u32[]{:S(2)}, u32[]{:S(2)}) collective-permute-start(bf16[128,1024]{1,0:T(8,128)(2,1)S(1)} %get-tuple-element.79), channel_id=1, source_target_pairs={{0,4},{4,0},{8,12},{12,8},{16,20},{20,16},{24,28},{28,24},{1,5},{5... | collective-permute-start | bytes 786440 | tf_op jit(solution)/shard_map/ppermute | solution.py:391
  45.2 2.0 %collective-permute-start.17 = (bf16[144,1024]{1,0:T(8,128)(2,1)S(1)}, bf16[144,1024]{1,0:T(8,128)(2,1)S(1)}, u32[]{:S(2)}, u32[]{:S(2)}) collective-permute-start(bf16[144,1024]{1,0:T(8,128)(2,1)S(1)} %collective-permute-done.15.refs_0_), channel_id=1, source_target_pairs={{0,4},{4,0},{8,12},{12,8},{16,20},{20,16},{24,28},{28,24},{1,5},{5... | collective-permute-start | bytes 884744 | tf_op jit(solution)/shard_map/ppermute | solution.py:391
  45.3 1.9 %collective-permute-start.18 = (bf16[128,1024]{1,0:T(8,128)(2,1)S(1)}, bf16[128,1024]{1,0:T(8,128)(2,1)S(1)}, u32[]{:S(2)}, u32[]{:S(2)}) collective-permute-start(bf16[128,1024]{1,0:T(8,128)(2,1)S(1)} %collective-permute-done.8.refs_1_), channel_id=1, source_target_pairs={{0,4},{4,0},{8,12},{12,8},{16,20},{20,16},{24,28},{28,24},{1,5},{5... | collective-permute-start | bytes 786440 | tf_op jit(solution)/shard_map/ppermute | solution.py:391
  45.7 9.2 %collective-permute-start.22 = (bf16[256,1024]{1,0:T(8,128)(2,1)S(1)}, bf16[256,1024]{1,0:T(8,128)(2,1)S(1)}, u32[]{:S(2)}, u32[]{:S(2)}) collective-permute-start(bf16[256,1024]{1,0:T(8,128)(2,1)S(1)} %combine.5), channel_id=1, source_target_pairs={{0,16},{4,12},{8,24},{12,4},{16,0},{20,28},{24,8},{28,20},{1,17},{... | collective-permute-start | bytes 1572872 | tf_op jit(solution)/shard_map/ppermute | solution.py:395
  46.6 4.3 %collective-permute-start.19 = (bf16[128,1024]{1,0:T(8,128)(2,1)S(1)}, bf16[128,1024]{1,0:T(8,128)(2,1)S(1)}, u32[]{:S(2)}, u32[]{:S(2)}) collective-permute-start(bf16[128,1024]{1,0:T(8,128)(2,1)S(1)} %get-tuple-element.86), channel_id=1, source_target_pairs={{0,4},{4,0},{8,12},{12,8},{16,20},{20,16},{24,28},{28,24},{1,5},{5... | collective-permute-start | bytes 786440 | tf_op jit(solution)/shard_map/ppermute | solution.py:391
  50.7 1.6 %collective-permute-start.20 = (bf16[128,1024]{1,0:T(8,128)(2,1)S(1)}, bf16[128,1024]{1,0:T(8,128)(2,1)S(1)}, u32[]{:S(2)}, u32[]{:S(2)}) collective-permute-start(bf16[128,1024]{1,0:T(8,128)(2,1)S(1)} %get-tuple-element.88), channel_id=1, source_target_pairs={{0,4},{4,0},{8,12},{12,8},{16,20},{20,16},{24,28},{28,24},{1,5},{5... | collective-permute-start | bytes 786440 | tf_op jit(solution)/shard_map/ppermute | solution.py:391
  52.6 14.2 %collective-permute-start.21 = (bf16[256,1024]{1,0:T(8,128)(2,1)S(1)}, bf16[256,1024]{1,0:T(8,128)(2,1)S(1)}, u32[]{:S(2)}, u32[]{:S(2)}) collective-permute-start(bf16[256,1024]{1,0:T(8,128)(2,1)S(1)} %combine.7), channel_id=1, source_target_pairs={{0,16},{4,12},{8,24},{12,4},{16,0},{20,28},{24,8},{28,20},{1,17},{... | collective-permute-start | bytes 1572872 | tf_op jit(solution)/shard_map/ppermute | solution.py:395
  55.0 11.9 %collective-permute-start.23 = (bf16[256,1024]{1,0:T(8,128)(2,1)S(1)}, bf16[256,1024]{1,0:T(8,128)(2,1)S(1)}, u32[]{:S(2)}, u32[]{:S(2)}) collective-permute-start(bf16[256,1024]{1,0:T(8,128)(2,1)S(1)} %add.10), channel_id=1, source_target_pairs={{0,8},{4,20},{8,0},{12,28},{16,24},{20,4},{24,16},{28,12},{1,9},{5... | collective-permute-start | bytes 1572872 | tf_op jit(solution)/shard_map/ppermute | solution.py:395
  55.6 1.3 %collective-permute-start.6 = (bf16[64,1024]{1,0:T(8,128)(2,1)S(1)}, bf16[64,1024]{1,0:T(8,128)(2,1)S(1)}, u32[]{:S(2)}, u32[]{:S(2)}) collective-permute-start(bf16[64,1024]{1,0:T(8,128)(2,1)S(1)} %get-tuple-element.66), channel_id=1, source_target_pairs={{0,4},{4,0},{8,12},{12,8},{16,20},{20,16},{24,28},{28,24},{1,5},{5... | collective-permute-start | bytes 393224 | tf_op jit(solution)/shard_map/ppermute | solution.py:391
  55.6 1.5 %collective-permute-start.5 = (bf16[64,1024]{1,0:T(8,128)(2,1)S(1)}, bf16[64,1024]{1,0:T(8,128)(2,1)S(1)}, u32[]{:S(2)}, u32[]{:S(2)}) collective-permute-start(bf16[64,1024]{1,0:T(8,128)(2,1)S(1)} %get-tuple-element.65), channel_id=1, source_target_pairs={{0,4},{4,0},{8,12},{12,8},{16,20},{20,16},{24,28},{28,24},{1,5},{5... | collective-permute-start | bytes 393224 | tf_op jit(solution)/shard_map/ppermute | solution.py:391
  (7 other events, 51.9 us)

commit v9 on v8

--- a/solution.py
+++ b/solution.py
@@ -61,33 +61,25 @@
     )
 
 
-def pack_kernel(width, k, v, last, first, sems):
-    end = k.shape[0] - width
-    copies = [
-        (k.at[pl.ds(end, width)], last.at[pl.ds(0, width)]),
-        (v.at[pl.ds(end, width)], last.at[pl.ds(width, width)]),
-        (k.at[pl.ds(0, width)], first.at[pl.ds(0, width)]),
-        (v.at[pl.ds(0, width)], first.at[pl.ds(width, width)]),
-    ]
-    copies = [pltpu.make_async_copy(a, b, sems.at[i]) for i, (a, b) in enumerate(copies)]
-    for copy in copies:
-        copy.start()
-    for copy in copies:
-        copy.wait()
-
-
-def pack(k, v, width):
-    flat = [jax.ShapeDtypeStruct((2 * width, k.shape[1]), k.dtype)] * 2
-    return pl.pallas_call(
-        functools.partial(pack_kernel, width),
-        in_specs=[ANY] * 2,
+def pack_kernel(info, k, v, near, other):
+    width = near.shape[0] // 2
+    for piece, target in enumerate((near, other)):
+        source = pl.ds(pl.multiple_of(info[piece] * width, width), width)
+        target[:width, :] = k[source, :]
+        target[width:, :] = v[source, :]
+
+
+def pack(info, k, v):
+    flat = [jax.ShapeDtypeStruct(k.shape, k.dtype)] * 2
+    return pl.pallas_call(
+        pack_kernel,
+        in_specs=[SMEM] + [VMEM] * 2,
         out_specs=[VMEM] * 2,
         out_shape=flat,
-        scratch_shapes=[pltpu.SemaphoreType.DMA((4,))],
         compiler_params=pltpu.CompilerParams(vmem_limit_bytes=12 * MIB),
         cost_estimate=cost(0, 0, flat, flat),
         name="pack",
-    )(*[far(a) for a in (k, v)])
+    )(info, *[far(a) for a in (k, v)])
 
 
 def interior_kernel(q, k, v, acc, tops, sums, bias):
@@ -126,16 +118,17 @@
     )(*args)
 
 
-def edge_kernel(half, live, q, halo, tops, sums, gain, acc, x, w, *rest):
+def edge_kernel(piece, info, q, halo, tops, sums, gain, acc, x, w, *rest):
     meta = rest[0] if len(rest) == 5 else None
     resid, payload, bias, att = rest[-4:]
     step = 2 * HD
     pairs = range(HEADS // 2)
     rows = q.shape[0] // 2
     wide = halo.shape[0] // 2
-    span = slice(half * rows, (half + 1) * rows)
-    first = -wide if half == 0 else 2 * rows
-    bias[...] = window_bias(wide, first, rows, half * rows, live[half])
+    half = info[piece]
+    span = pl.ds(pl.multiple_of(half * rows, rows), rows)
+    first = jnp.where(half == 0, -wide, 2 * rows)
+    bias[...] = window_bias(wide, first, rows, half * rows, info[2 + half])
     scores = []
     for pair in pairs:
         cols = slice(pair * step, (pair + 1) * step)
@@ -175,10 +168,10 @@
         payload[rows:, :] = jnp.concatenate(copies, axis=0)
 
 
-def edge(half, live, q, halo, acc, tops, sums, x, w, gain, meta):
+def edge(piece, info, q, halo, acc, tops, sums, x, w, gain, meta):
     rows, model = q.shape[0] // 2, q.shape[1]
     wide = halo.shape[0] // 2
-    args = [live, q, halo, tops, sums, gain, acc, x, w]
+    args = [info, q, halo, tops, sums, gain, acc, x, w]
     args += [] if meta is None else [meta]
     extra = 0 if meta is None else META
     flat = [
@@ -186,7 +179,7 @@
         jax.ShapeDtypeStruct((rows + extra, model), BF16),
     ]
     return pl.pallas_call(
-        functools.partial(edge_kernel, half),
+        functools.partial(edge_kernel, piece),
         in_specs=[SMEM] + [VMEM] * (len(args) - 1),
         out_specs=[VMEM] * 2,
         out_shape=flat,
@@ -198,7 +191,7 @@
         cost_estimate=cost(
             4 * rows * wide * model + 2 * rows * model * model, HEADS * rows * wide, args, flat
         ),
-        name=f"edge_half{half}",
+        name=f"edge_piece{piece}",
     )(*args)
 
 
@@ -331,6 +324,30 @@
     result[...] = (a[...].astype(F32) + b[...].astype(F32)).astype(result.dtype)
 
 
+def place_kernel(turned, a, b, result):
+    rows = a.shape[0] // 2
+    first, second = [
+        (a[at, :] + b[at, :].astype(F32)).astype(result.dtype)
+        for at in (slice(0, rows), slice(rows, 2 * rows))
+    ]
+    straight = jnp.broadcast_to(turned[...], first.shape) == 0
+    result[:rows, :] = jnp.where(straight, first, second)
+    result[rows:, :] = jnp.where(straight, second, first)
+
+
+def place(turned, a, b):
+    out = jax.ShapeDtypeStruct(b.shape, b.dtype)
+    return pl.pallas_call(
+        place_kernel,
+        in_specs=[VMEM] * 3,
+        out_specs=VMEM,
+        out_shape=out,
+        compiler_params=pltpu.CompilerParams(vmem_limit_bytes=12 * MIB),
+        cost_estimate=cost(out.size, 0, (a, b), [out]),
+        name="place",
+    )(turned, a, b)
+
+
 def add(a, b, dtype):
     out = jax.ShapeDtypeStruct(a.shape, dtype)
     return pl.pallas_call(
@@ -399,7 +416,7 @@
     return lax.optimization_barrier((first, *later))[1:]
 
 
-def routed_gather(me, payloads, resids, weights, rows, capacity):
+def routed_gather(me, turned, payloads, resids, weights, rows, capacity):
     sizes = dict(rows=rows, capacity=capacity)
 
     def evaluate(mine, theirs):
@@ -448,7 +465,7 @@
     back_first = swap_by_core(sum_first, (2, 4))
     own = (scatter0, scatter1), (own0, own1), siblings((sent0, sent1))
     total = combine(*own, start=resids, dtype=F32, **sizes)
-    return add(add(total, back_second, F32), back_first, BF16)
+    return place(turned, add(total, back_second, F32), back_first)
 
 
 def local(
@@ -470,14 +487,15 @@
     width = R_IL * PLANE
     rows = row_count // 2
     capacity = row_count * routes.shape[1] // tiles
-    up = [(i, i + 1) for i in range(tiles - 1)]
-    down = [(j, i) for i, j in up]
-    live = jnp.stack([tile > 0, tile < tiles - 1]).astype(jnp.int32)
+    pairs = [(i, i ^ 1) for i in range(tiles)]
+    others = [(i, i + 1) for i in range(1, tiles - 1, 2)]
+    others += [(j, i) for i, j in others]
+    info = jnp.stack([1 - tile % 2, tile % 2, tile > 0, tile < tiles - 1]).astype(jnp.int32)
     me = jnp.stack([tile, tile ^ 1]).astype(jnp.int32)
-    live, me, key_vectors = lax.optimization_barrier((live, me, key_vectors))
-    last, first = pack(key_vectors, values, width)
-    before = lax.ppermute(last, "tile", up)
-    behind = lax.ppermute(first, "tile", down)
+    turned = jnp.full((1, inputs.shape[1]), 1 - tile % 2, F32)
+    info, me, turned, key_vectors = lax.optimization_barrier((info, me, turned, key_vectors))
+    near, other = pack(info, key_vectors, values)
+    halos = lax.ppermute(near, "tile", pairs), lax.ppermute(other, "tile", others)
     fast = tiles == 8
     meta = None
     if fast:
@@ -488,20 +506,25 @@
             mid = lax.reduce_precision(gate - high, 8, 7)
             items += [high, mid, gate - high - mid]
         meta = jnp.stack(items).reshape(len(items), 2, rows).swapaxes(0, 1)
-        meta = meta.reshape(2, len(items) * rows).astype(BF16)
+        meta = meta.reshape(2, len(items) * rows)
+        other = jnp.concatenate([meta[1:], meta[:1]], axis=0)
+        meta = jnp.where(turned == 0, meta, other).astype(BF16)
     acc, tops, sums = interior(queries, key_vectors, values)
-    halves = [
+    pieces = [
         edge(
-            half, live, queries, halo, acc, tops, sums, inputs, out_weight, norm_gain[None, :],
-            meta if half == 0 else None,
+            piece, info, queries, halo, acc, tops, sums, inputs, out_weight,
+            norm_gain[None, :], meta if piece == 0 else None,
         )
-        for half, halo in enumerate((before, behind))
+        for piece, halo in enumerate(halos)
     ]
-    resids, payloads = zip(*halves)
+    resids, payloads = zip(*pieces)
     if fast:
         weights = (w_gate[0], w_up[0], w_down[0])
-        return routed_gather(me, payloads, resids, weights, rows, capacity)
-    payload, resid = jnp.concatenate(payloads, axis=0), jnp.concatenate(resids, axis=0)
+        return routed_gather(me, turned, payloads, resids, weights, rows, capacity)
+    payload, resid = [
+        jnp.where(info[0] == 0, jnp.concatenate(a, axis=0), jnp.concatenate(a[::-1], axis=0))
+        for a in (payloads, resids)
+    ]
     return routed_all_to_all(payload, resid, routes, route_gates, w_gate[0], w_up[0], w_down[0])
 
 

time: 68.1 us -> 67.2 us (0.987)
  starting transfers between devices: 21 us -> 24.6 us
  waiting for transfers between devices: 17.9 us -> 14.8 us
  local copies, waits for them, and re-layouts: 0.82 us -> 0.09 us
  other arithmetic: 1 us -> 0.28 us
    ppermute x9, starting transfers between devices: 9.57 us -> 13.3 us  [swap_by_core(): return lax.ppermute(array, 'tile', [(i, i ^ bits[i % 2]) for i in range(8)])]
    ppermute x9, waiting for transfers between devices: 15.2 us -> 12.7 us  [swap_by_core(): return lax.ppermute(array, 'tile', [(i, i ^ bits[i % 2]) for i in range(8)])]
    ppermute x13, starting transfers between devices: 7.76 us -> 6.26 us  [swap(): return lax.ppermute(array, 'tile', [(i, i ^ bit) for i in range(8)])]
    ppermute x2, starting transfers between devices: 3.68 us -> 5.03 us  [the longest x1 4.33 us: local(): lax.ppermute(near, 'tile', pairs)]
    pallas_call x3 -> x4, Pallas kernels: 4.85 us -> 6.01 us  [the longest x2 3.8 us: edge(): pl.pallas_call(functools.partial(edge_kernel, piece), in_specs=[SMEM] + [...]
    pallas_call x3 -> x2, Pallas kernels: 1.06 us -> 0.18 us  [add(): pl.pallas_call(add_kernel, in_specs=[VMEM] * 2, out_specs=VMEM, out_shape...]
    slice x1, local copies, waits for them, and re-layouts: 0.76 us -> 0.01 us  [local(): gate = route_gates[:, k]]
    another operation x1, other arithmetic: 0.78 us -> 0.08 us  [local(): jnp.stack([1 - tile % 2, tile % 2, tile > 0, tile < tiles - 1])]
  transfers between devices with their start and end apart: 24 -> 24, of which waited for: 10 -> 9; matrix products, arithmetic and copies ran while one was open for 2% -> 0% of each run, Pallas kernels for 36% -> 36%
where the time goes in v9:
time: 67.2 us; the launch traced here: 67 us
  Pallas kernels  27 us (40%)
  starting transfers between devices  24.6 us (37%)
  waiting for transfers between devices  14.8 us (22%)
    pallas_call x5, Pallas kernels, experts(): pl.pallas_call(functools.partial(experts_kernel, order, rows, capacity),...  15.1 us
    ppermute x9, starting transfers between devices, swap_by_core(): return lax.ppermute(array, 'tile', [(i, i ^ bits[i % 2]) for i in range(8)])  13.3 us
    ppermute x9, waiting for transfers between devices, swap_by_core(): return lax.ppermute(array, 'tile', [(i, i ^ bits[i % 2]) for i in range(8)])  12.7 us
    ppermute x13, starting transfers between devices, swap(): return lax.ppermute(array, 'tile', [(i, i ^ bit) for i in range(8)])  6.26 us
    pallas_call x1, Pallas kernels, interior(): pl.pallas_call(interior_kernel, in_specs=[VMEM] * 3, out_specs=[VMEM] * 3...  4.36 us
    ppermute x1, starting transfers between devices, local(): lax.ppermute(near, 'tile', pairs)  4.33 us
    pallas_call x2, Pallas kernels, edge(): pl.pallas_call(functools.partial(edge_kernel, piece), in_specs=[SMEM] + [...  3.8 us
    ppermute x13, waiting for transfers between devices, swap(): return lax.ppermute(array, 'tile', [(i, i ^ bit) for i in range(8)])  2.08 us
  transfers between devices with their start and end apart: 24, of which 9 were waited for; matrix products, arithmetic and copies ran while one was open for 0% of the time, Pallas kernels for 36%

profile of v9, /device:TPU:0, one launch (start us, length us, event | category | flops | bytes accessed | tf_op | source)
XLA Modules:
  0.0 67.0 jit_solution(16472088695985094179)
XLA Ops:
  0.2 1.3 %pack.1 = (bf16[256,1024]{1,0:T(8,128)(2,1)S(1)}, bf16[256,1024]{1,0:T(8,128)(2,1)S(1)}) custom-call(s32[4]{0:T(128)S(1)} %pad_add_fusion.info, bf16[256,1024]{1,0:T(8,128)(2,1)} %k.1, bf16[256,1024]{1,0:T(8,128)(2,1)} %v.3), custom_call_target="tpu_custom_call" | custom-call | bytes 2097152 | tf_op jit(solution)/shard_map/pack/pallas_call | solution.py:74
  2.2 4.3 %collective-permute-start = (bf16[256,1024]{1,0:T(8,128)(2,1)S(1)}, bf16[256,1024]{1,0:T(8,128)(2,1)S(1)}, u32[]{:S(2)}, u32[]{:S(2)}) collective-permute-start(bf16[256,1024]{1,0:T(8,128)(2,1)S(1)} %get-tuple-element.53), channel_id=1, source_target_pairs={{0,4},{4,0},{8,12},{12,8},{16,20},{20,16},{24,28},{28,24},{1,5},{5... | collective-permute-start | bytes 1572872 | tf_op jit(solution)/shard_map/ppermute | solution.py:498
  6.6 4.4 %interior.1 = (f32[1024,256]{1,0:T(8,128)S(1)}, f32[16,256]{1,0:T(8,128)S(1)}, f32[16,256]{1,0:T(8,128)S(1)}) custom-call(bf16[256,1024]{1,0:T(8,128)(2,1)} %q.5, bf16[256,1024]{1,0:T(8,128)(2,1)} %k.1, bf16[256,1024]{1,0:T(8,128)(2,1)} %v.3), custom_call_target="tpu_custom_call" | custom-call | flops 8053063680 | bytes 2654208 | tf_op jit(solution)/shard_map/interior/pallas_call | solution.py:109
  11.2 1.9 %edge_piece0.1 = (bf16[128,1024]{1,0:T(8,128)(2,1)S(1)}, bf16[144,1024]{1,0:T(8,128)(2,1)S(1)}) custom-call(s32[4]{0:T(128)S(1)} %pad_add_fusion.info, bf16[256,1024]{1,0:T(8,128)(2,1)S(1)} %copy-done.4, bf16[256,1024]{1,0:T(8,128)(2,1)S(1)} %collective-permute-done.halo, f32[16,256]{1,0:T(8,128)S(1)} %get-tuple-element.54.tops, ...), custom_call_target="tpu_custom_call" | custom-call | flops 335544320 | bytes 5316624 | tf_op jit(solution)/shard_map/edge_piece0/pallas_call | solution.py:181
  13.4 1.5 %collective-permute-start.2 = (bf16[144,1024]{1,0:T(8,128)(2,1)S(1)}, bf16[144,1024]{1,0:T(8,128)(2,1)S(1)}, u32[]{:S(2)}, u32[]{:S(2)}) collective-permute-start(bf16[144,1024]{1,0:T(8,128)(2,1)S(1)} %get-tuple-element.80.refs_0_.refs_2_), channel_id=1, source_target_pairs={{0,8},{4,20},{8,0},{12,28},{16,24},{20,4},{24,16},{28,12},{1,9},{5... | collective-permute-start | bytes 884744 | tf_op jit(solution)/shard_map/ppermute | solution.py:412
  14.9 1.9 %edge_piece1.1 = (bf16[128,1024]{1,0:T(8,128)(2,1)S(1)}, bf16[128,1024]{1,0:T(8,128)(2,1)S(1)}) custom-call(s32[4]{0:T(128)S(1)} %pad_add_fusion.info, bf16[256,1024]{1,0:T(8,128)(2,1)S(1)} %copy-done.4, bf16[256,1024]{1,0:T(8,128)(2,1)S(1)} %collective-permute-done.3.halo, f32[16,256]{1,0:T(8,128)S(1)} %get-tuple-element.54.tops, ...), custom_call_target="tpu_custom_call" | custom-call | flops 335544320 | bytes 5279760 | tf_op jit(solution)/shard_map/edge_piece1/pallas_call | solution.py:181
  16.8 3.2 %collective-permute-start.4 = (bf16[128,1024]{1,0:T(8,128)(2,1)S(1)}, bf16[128,1024]{1,0:T(8,128)(2,1)S(1)}, u32[]{:S(2)}, u32[]{:S(2)}) collective-permute-start(bf16[128,1024]{1,0:T(8,128)(2,1)S(1)} %get-tuple-element.71.refs_0_), channel_id=1, source_target_pairs={{0,4},{4,0},{8,12},{12,8},{16,20},{20,16},{24,28},{28,24},{1,5},{5... | collective-permute-start | bytes 786440 | tf_op jit(solution)/shard_map/ppermute | solution.py:408
  20.0 3.2 %collective-permute-start.9 = (bf16[128,1024]{1,0:T(8,128)(2,1)S(1)}, bf16[128,1024]{1,0:T(8,128)(2,1)S(1)}, u32[]{:S(2)}, u32[]{:S(2)}) collective-permute-start(bf16[128,1024]{1,0:T(8,128)(2,1)S(1)} %get-tuple-element.71.refs_0_), channel_id=1, source_target_pairs={{0,8},{4,20},{8,0},{12,28},{16,24},{20,4},{24,16},{28,12},{1,9},{5... | collective-permute-start | bytes 786440 | tf_op jit(solution)/shard_map/ppermute | solution.py:412
  23.2 2.3 %experts_128.2 = (bf16[64,1024]{1,0:T(8,128)(2,1)S(1)}, bf16[64,1024]{1,0:T(8,128)(2,1)S(1)}, bf16[256,128]{1,0:T(8,128)(2,1)S(1)}) custom-call(s32[2]{0:T(128)S(1)} %pad_add_fusion.1.me, bf16[144,1024]{1,0:T(8,128)(2,1)S(1)} %get-tuple-element.80.refs_0_.refs_2_, bf16[144,1024]{1,0:T(8,128)(2,1)S(1)} %collective-permute-done.1.refs_1_.refs_3_, ...), custom_call_target="tpu_custom_call" | custom-call | flops 1107296256 | bytes 9568264 | tf_op jit(solution)/shard_map/experts_128/pallas_call | solution.py:275
  25.4 1.0 %collective-permute-start.7 = (bf16[144,1024]{1,0:T(8,128)(2,1)S(1)}, bf16[144,1024]{1,0:T(8,128)(2,1)S(1)}, u32[]{:S(2)}, u32[]{:S(2)}) collective-permute-start(bf16[144,1024]{1,0:T(8,128)(2,1)S(1)} %collective-permute-done.2.refs_0_), channel_id=1, source_target_pairs={{0,16},{4,12},{8,24},{12,4},{16,0},{20,28},{24,8},{28,20},{1,17},{... | collective-permute-start | bytes 884744 | tf_op jit(solution)/shard_map/ppermute | solution.py:412
  26.4 2.3 %experts_128.3 = (bf16[64,1024]{1,0:T(8,128)(2,1)S(1)}, bf16[64,1024]{1,0:T(8,128)(2,1)S(1)}, bf16[256,128]{1,0:T(8,128)(2,1)S(1)}) custom-call(s32[2]{0:T(128)S(1)} %pad_add_fusion.1.me, bf16[128,1024]{1,0:T(8,128)(2,1)S(1)} %get-tuple-element.71.refs_0_, bf16[128,1024]{1,0:T(8,128)(2,1)S(1)} %collective-permute-done.4.refs_1_, ...), custom_call_target="tpu_custom_call" | custom-call | flops 1107296256 | bytes 10092552 | tf_op jit(solution)/shard_map/experts_128/pallas_call | solution.py:275
  29.3 1.5 %collective-permute-start.12 = (bf16[128,1024]{1,0:T(8,128)(2,1)S(1)}, bf16[128,1024]{1,0:T(8,128)(2,1)S(1)}, u32[]{:S(2)}, u32[]{:S(2)}) collective-permute-start(bf16[128,1024]{1,0:T(8,128)(2,1)S(1)} %collective-permute-done.9.refs_1_), channel_id=1, source_target_pairs={{0,16},{4,12},{8,24},{12,4},{16,0},{20,28},{24,8},{28,20},{1,17},{... | collective-permute-start | bytes 786440 | tf_op jit(solution)/shard_map/ppermute | solution.py:412
  30.8 1.5 %collective-permute-done.7.refs_0_ = bf16[144,1024]{1,0:T(8,128)(2,1)S(1)} collective-permute-done((bf16[144,1024]{1,0:T(8,128)(2,1)S(1)}, bf16[144,1024]{1,0:T(8,128)(2,1)S(1)}, u32[]{:S(2)}, u32[]{:S(2)}) %collective-permute-start.7) | collective-permute-done | bytes 294944 | tf_op jit(solution)/shard_map/ppermute | solution.py:412
  33.2 3.5 %experts_256.3 = (bf16[128,1024]{1,0:T(8,128)(2,1)S(1)}, bf16[128,1024]{1,0:T(8,128)(2,1)S(1)}, bf16[512,128]{1,0:T(8,128)(2,1)S(1)}) custom-call(s32[2]{0:T(128)S(1)} %pad_add_fusion.1.me, bf16[144,1024]{1,0:T(8,128)(2,1)S(1)} %collective-permute-done.2.refs_0_, bf16[128,1024]{1,0:T(8,128)(2,1)S(1)} %collective-permute-done.9.refs_1_, ...), custom_call_target="tpu_custom_call" | custom-call | flops 2214592512 | bytes 10420232 | tf_op jit(solution)/shard_map/experts_256/pallas_call | solution.py:275
  37.2 1.1 %collective-permute-start.15 = (bf16[144,1024]{1,0:T(8,128)(2,1)S(1)}, bf16[144,1024]{1,0:T(8,128)(2,1)S(1)}, u32[]{:S(2)}, u32[]{:S(2)}) collective-permute-start(bf16[144,1024]{1,0:T(8,128)(2,1)S(1)} %get-tuple-element.80.refs_0_.refs_2_), channel_id=1, source_target_pairs={{0,16},{4,12},{8,24},{12,4},{16,0},{20,28},{24,8},{28,20},{1,17},{... | collective-permute-start | bytes 884744 | tf_op jit(solution)/shard_map/ppermute | solution.py:412
  38.6 3.7 %experts_256.4 = (bf16[128,1024]{1,0:T(8,128)(2,1)S(1)}, bf16[128,1024]{1,0:T(8,128)(2,1)S(1)}, bf16[512,128]{1,0:T(8,128)(2,1)S(1)}) custom-call(s32[2]{0:T(128)S(1)} %pad_add_fusion.1.me, bf16[144,1024]{1,0:T(8,128)(2,1)S(1)} %collective-permute-done.7.refs_0_, bf16[128,1024]{1,0:T(8,128)(2,1)S(1)} %collective-permute-done.12.refs_1_, ...), custom_call_target="tpu_custom_call" | custom-call | flops 2214592512 | bytes 10420232 | tf_op jit(solution)/shard_map/experts_256/pallas_call | solution.py:275
  42.5 1.5 %collective-permute-done.15.refs_0_ = bf16[144,1024]{1,0:T(8,128)(2,1)S(1)} collective-permute-done((bf16[144,1024]{1,0:T(8,128)(2,1)S(1)}, bf16[144,1024]{1,0:T(8,128)(2,1)S(1)}, u32[]{:S(2)}, u32[]{:S(2)}) %collective-permute-start.15) | collective-permute-done | bytes 294944 | tf_op jit(solution)/shard_map/ppermute | solution.py:412
  44.9 1.3 %collective-permute-start.22 = (bf16[256,1024]{1,0:T(8,128)(2,1)S(1)}, bf16[256,1024]{1,0:T(8,128)(2,1)S(1)}, u32[]{:S(2)}, u32[]{:S(2)}) collective-permute-start(bf16[256,1024]{1,0:T(8,128)(2,1)S(1)} %combine.5), channel_id=1, source_target_pairs={{0,16},{4,12},{8,24},{12,4},{16,0},{20,28},{24,8},{28,20},{1,17},{... | collective-permute-start | bytes 1572872 | tf_op jit(solution)/shard_map/ppermute | solution.py:412
  46.3 3.5 %experts_256.5 = (bf16[128,1024]{1,0:T(8,128)(2,1)S(1)}, bf16[128,1024]{1,0:T(8,128)(2,1)S(1)}, bf16[512,128]{1,0:T(8,128)(2,1)S(1)}) custom-call(s32[2]{0:T(128)S(1)} %pad_add_fusion.1.me, bf16[144,1024]{1,0:T(8,128)(2,1)S(1)} %collective-permute-done.15.refs_0_, bf16[128,1024]{1,0:T(8,128)(2,1)S(1)} %collective-permute-done.8.refs_1_, ...), custom_call_target="tpu_custom_call" | custom-call | flops 2214592512 | bytes 10420232 | tf_op jit(solution)/shard_map/experts_256/pallas_call | solution.py:275
  51.7 1.3 %collective-permute-start.21 = (bf16[256,1024]{1,0:T(8,128)(2,1)S(1)}, bf16[256,1024]{1,0:T(8,128)(2,1)S(1)}, u32[]{:S(2)}, u32[]{:S(2)}) collective-permute-start(bf16[256,1024]{1,0:T(8,128)(2,1)S(1)} %combine.7), channel_id=1, source_target_pairs={{0,16},{4,12},{8,24},{12,4},{16,0},{20,28},{24,8},{28,20},{1,17},{... | collective-permute-start | bytes 1572872 | tf_op jit(solution)/shard_map/ppermute | solution.py:412
  53.1 1.0 %collective-permute-done.22.b = bf16[256,1024]{1,0:T(8,128)(2,1)S(1)} collective-permute-done((bf16[256,1024]{1,0:T(8,128)(2,1)S(1)}, bf16[256,1024]{1,0:T(8,128)(2,1)S(1)}, u32[]{:S(2)}, u32[]{:S(2)}) %collective-permute-start.22) | collective-permute-done | bytes 524320 | tf_op jit(solution)/shard_map/ppermute | solution.py:412
  54.1 1.5 %collective-permute-start.23 = (bf16[256,1024]{1,0:T(8,128)(2,1)S(1)}, bf16[256,1024]{1,0:T(8,128)(2,1)S(1)}, u32[]{:S(2)}, u32[]{:S(2)}) collective-permute-start(bf16[256,1024]{1,0:T(8,128)(2,1)S(1)} %add.19), channel_id=1, source_target_pairs={{0,8},{4,20},{8,0},{12,28},{16,24},{20,4},{24,16},{28,12},{1,9},{5... | collective-permute-start | bytes 1572872 | tf_op jit(solution)/shard_map/ppermute | solution.py:412
  57.5 8.5 %collective-permute-done.21.b = bf16[256,1024]{1,0:T(8,128)(2,1)S(1)} collective-permute-done((bf16[256,1024]{1,0:T(8,128)(2,1)S(1)}, bf16[256,1024]{1,0:T(8,128)(2,1)S(1)}, u32[]{:S(2)}, u32[]{:S(2)}) %collective-permute-start.21) | collective-permute-done | bytes 524320 | tf_op jit(solution)/shard_map/ppermute | solution.py:412
  66.1 0.9 %place.1 = bf16[256,1024]{1,0:T(8,128)(2,1)} custom-call(f32[1,1024]{1,0:T(1,128)S(1)} %broadcast_in_dim.17.turned, f32[256,1024]{1,0:T(8,128)S(1)} %add.18.a, bf16[256,1024]{1,0:T(8,128)(2,1)S(1)} %collective-permute-done.23.b), custom_call_target="tpu_custom_call" | custom-call | flops 262144 | bytes 2097152 | tf_op jit(solution)/shard_map/place/pallas_call | solution.py:340
  (74 shorter events, 8.9 us)
Async XLA Ops:
  1.4 13.4 %collective-permute-start.3 = (bf16[256,1024]{1,0:T(8,128)(2,1)S(1)}, bf16[256,1024]{1,0:T(8,128)(2,1)S(1)}, u32[]{:S(2)}, u32[]{:S(2)}) collective-permute-start(bf16[256,1024]{1,0:T(8,128)(2,1)S(1)} %get-tuple-element.61), channel_id=1, source_target_pairs={{4,8},{12,16},{20,24},{8,4},{16,12},{24,20},{5,9},{13,17},{21,25},... | collective-permute-start | bytes 1572872 | tf_op jit(solution)/shard_map/ppermute | solution.py:498
  2.2 8.9 %collective-permute-start = (bf16[256,1024]{1,0:T(8,128)(2,1)S(1)}, bf16[256,1024]{1,0:T(8,128)(2,1)S(1)}, u32[]{:S(2)}, u32[]{:S(2)}) collective-permute-start(bf16[256,1024]{1,0:T(8,128)(2,1)S(1)} %get-tuple-element.53), channel_id=1, source_target_pairs={{0,4},{4,0},{8,12},{12,8},{16,20},{20,16},{24,28},{28,24},{1,5},{5... | collective-permute-start | bytes 1572872 | tf_op jit(solution)/shard_map/ppermute | solution.py:498
  13.1 10.0 %collective-permute-start.1 = (bf16[144,1024]{1,0:T(8,128)(2,1)S(1)}, bf16[144,1024]{1,0:T(8,128)(2,1)S(1)}, u32[]{:S(2)}, u32[]{:S(2)}) collective-permute-start(bf16[144,1024]{1,0:T(8,128)(2,1)S(1)} %get-tuple-element.80.refs_0_.refs_2_), channel_id=1, source_target_pairs={{0,4},{4,0},{8,12},{12,8},{16,20},{20,16},{24,28},{28,24},{1,5},{5... | collective-permute-start | bytes 884744 | tf_op jit(solution)/shard_map/ppermute | solution.py:408
  13.4 12.1 %collective-permute-start.2 = (bf16[144,1024]{1,0:T(8,128)(2,1)S(1)}, bf16[144,1024]{1,0:T(8,128)(2,1)S(1)}, u32[]{:S(2)}, u32[]{:S(2)}) collective-permute-start(bf16[144,1024]{1,0:T(8,128)(2,1)S(1)} %get-tuple-element.80.refs_0_.refs_2_), channel_id=1, source_target_pairs={{0,8},{4,20},{8,0},{12,28},{16,24},{20,4},{24,16},{28,12},{1,9},{5... | collective-permute-start | bytes 884744 | tf_op jit(solution)/shard_map/ppermute | solution.py:412
  16.8 9.7 %collective-permute-start.4 = (bf16[128,1024]{1,0:T(8,128)(2,1)S(1)}, bf16[128,1024]{1,0:T(8,128)(2,1)S(1)}, u32[]{:S(2)}, u32[]{:S(2)}) collective-permute-start(bf16[128,1024]{1,0:T(8,128)(2,1)S(1)} %get-tuple-element.71.refs_0_), channel_id=1, source_target_pairs={{0,4},{4,0},{8,12},{12,8},{16,20},{20,16},{24,28},{28,24},{1,5},{5... | collective-permute-start | bytes 786440 | tf_op jit(solution)/shard_map/ppermute | solution.py:408
  20.0 8.7 %collective-permute-start.9 = (bf16[128,1024]{1,0:T(8,128)(2,1)S(1)}, bf16[128,1024]{1,0:T(8,128)(2,1)S(1)}, u32[]{:S(2)}, u32[]{:S(2)}) collective-permute-start(bf16[128,1024]{1,0:T(8,128)(2,1)S(1)} %get-tuple-element.71.refs_0_), channel_id=1, source_target_pairs={{0,8},{4,20},{8,0},{12,28},{16,24},{20,4},{24,16},{28,12},{1,9},{5... | collective-permute-start | bytes 786440 | tf_op jit(solution)/shard_map/ppermute | solution.py:412
  25.4 6.8 %collective-permute-start.7 = (bf16[144,1024]{1,0:T(8,128)(2,1)S(1)}, bf16[144,1024]{1,0:T(8,128)(2,1)S(1)}, u32[]{:S(2)}, u32[]{:S(2)}) collective-permute-start(bf16[144,1024]{1,0:T(8,128)(2,1)S(1)} %collective-permute-done.2.refs_0_), channel_id=1, source_target_pairs={{0,16},{4,12},{8,24},{12,4},{16,0},{20,28},{24,8},{28,20},{1,17},{... | collective-permute-start | bytes 884744 | tf_op jit(solution)/shard_map/ppermute | solution.py:412
  26.4 6.7 %collective-permute-start.10 = (bf16[144,1024]{1,0:T(8,128)(2,1)S(1)}, bf16[144,1024]{1,0:T(8,128)(2,1)S(1)}, u32[]{:S(2)}, u32[]{:S(2)}) collective-permute-start(bf16[144,1024]{1,0:T(8,128)(2,1)S(1)} %collective-permute-done.2.refs_0_), channel_id=1, source_target_pairs={{0,4},{4,0},{8,12},{12,8},{16,20},{20,16},{24,28},{28,24},{1,5},{5... | collective-permute-start | bytes 884744 | tf_op jit(solution)/shard_map/ppermute | solution.py:408
  28.7 4.5 %collective-permute-start.11 = (bf16[128,1024]{1,0:T(8,128)(2,1)S(1)}, bf16[128,1024]{1,0:T(8,128)(2,1)S(1)}, u32[]{:S(2)}, u32[]{:S(2)}) collective-permute-start(bf16[128,1024]{1,0:T(8,128)(2,1)S(1)} %collective-permute-done.9.refs_1_), channel_id=1, source_target_pairs={{0,4},{4,0},{8,12},{12,8},{16,20},{20,16},{24,28},{28,24},{1,5},{5... | collective-permute-start | bytes 786440 | tf_op jit(solution)/shard_map/ppermute | solution.py:408
  29.3 7.4 %collective-permute-start.12 = (bf16[128,1024]{1,0:T(8,128)(2,1)S(1)}, bf16[128,1024]{1,0:T(8,128)(2,1)S(1)}, u32[]{:S(2)}, u32[]{:S(2)}) collective-permute-start(bf16[128,1024]{1,0:T(8,128)(2,1)S(1)} %collective-permute-done.9.refs_1_), channel_id=1, source_target_pairs={{0,16},{4,12},{8,24},{12,4},{16,0},{20,28},{24,8},{28,20},{1,17},{... | collective-permute-start | bytes 786440 | tf_op jit(solution)/shard_map/ppermute | solution.py:412
  32.2 6.4 %collective-permute-start.8 = (bf16[128,1024]{1,0:T(8,128)(2,1)S(1)}, bf16[128,1024]{1,0:T(8,128)(2,1)S(1)}, u32[]{:S(2)}, u32[]{:S(2)}) collective-permute-start(bf16[128,1024]{1,0:T(8,128)(2,1)S(1)} %get-tuple-element.71.refs_0_), channel_id=1, source_target_pairs={{0,16},{4,12},{8,24},{12,4},{16,0},{20,28},{24,8},{28,20},{1,17},{... | collective-permute-start | bytes 786440 | tf_op jit(solution)/shard_map/ppermute | solution.py:412
  33.1 5.5 %collective-permute-start.13 = (bf16[144,1024]{1,0:T(8,128)(2,1)S(1)}, bf16[144,1024]{1,0:T(8,128)(2,1)S(1)}, u32[]{:S(2)}, u32[]{:S(2)}) collective-permute-start(bf16[144,1024]{1,0:T(8,128)(2,1)S(1)} %collective-permute-done.7.refs_0_), channel_id=1, source_target_pairs={{0,4},{4,0},{8,12},{12,8},{16,20},{20,16},{24,28},{28,24},{1,5},{5... | collective-permute-start | bytes 884744 | tf_op jit(solution)/shard_map/ppermute | solution.py:408
  36.7 2.0 %collective-permute-start.14 = (bf16[128,1024]{1,0:T(8,128)(2,1)S(1)}, bf16[128,1024]{1,0:T(8,128)(2,1)S(1)}, u32[]{:S(2)}, u32[]{:S(2)}) collective-permute-start(bf16[128,1024]{1,0:T(8,128)(2,1)S(1)} %collective-permute-done.12.refs_1_), channel_id=1, source_target_pairs={{0,4},{4,0},{8,12},{12,8},{16,20},{20,16},{24,28},{28,24},{1,5},{5... | collective-permute-start | bytes 786440 | tf_op jit(solution)/shard_map/ppermute | solution.py:408
  37.2 6.7 %collective-permute-start.15 = (bf16[144,1024]{1,0:T(8,128)(2,1)S(1)}, bf16[144,1024]{1,0:T(8,128)(2,1)S(1)}, u32[]{:S(2)}, u32[]{:S(2)}) collective-permute-start(bf16[144,1024]{1,0:T(8,128)(2,1)S(1)} %get-tuple-element.80.refs_0_.refs_2_), channel_id=1, source_target_pairs={{0,16},{4,12},{8,24},{12,4},{16,0},{20,28},{24,8},{28,20},{1,17},{... | collective-permute-start | bytes 884744 | tf_op jit(solution)/shard_map/ppermute | solution.py:412
  42.3 1.7 %collective-permute-start.16 = (bf16[128,1024]{1,0:T(8,128)(2,1)S(1)}, bf16[128,1024]{1,0:T(8,128)(2,1)S(1)}, u32[]{:S(2)}, u32[]{:S(2)}) collective-permute-start(bf16[128,1024]{1,0:T(8,128)(2,1)S(1)} %get-tuple-element.81), channel_id=1, source_target_pairs={{0,4},{4,0},{8,12},{12,8},{16,20},{20,16},{24,28},{28,24},{1,5},{5... | collective-permute-start | bytes 786440 | tf_op jit(solution)/shard_map/ppermute | solution.py:408
  44.3 2.0 %collective-permute-start.17 = (bf16[144,1024]{1,0:T(8,128)(2,1)S(1)}, bf16[144,1024]{1,0:T(8,128)(2,1)S(1)}, u32[]{:S(2)}, u32[]{:S(2)}) collective-permute-start(bf16[144,1024]{1,0:T(8,128)(2,1)S(1)} %collective-permute-done.15.refs_0_), channel_id=1, source_target_pairs={{0,4},{4,0},{8,12},{12,8},{16,20},{20,16},{24,28},{28,24},{1,5},{5... | collective-permute-start | bytes 884744 | tf_op jit(solution)/shard_map/ppermute | solution.py:408
  44.4 1.9 %collective-permute-start.18 = (bf16[128,1024]{1,0:T(8,128)(2,1)S(1)}, bf16[128,1024]{1,0:T(8,128)(2,1)S(1)}, u32[]{:S(2)}, u32[]{:S(2)}) collective-permute-start(bf16[128,1024]{1,0:T(8,128)(2,1)S(1)} %collective-permute-done.8.refs_1_), channel_id=1, source_target_pairs={{0,4},{4,0},{8,12},{12,8},{16,20},{20,16},{24,28},{28,24},{1,5},{5... | collective-permute-start | bytes 786440 | tf_op jit(solution)/shard_map/ppermute | solution.py:408
  44.9 9.2 %collective-permute-start.22 = (bf16[256,1024]{1,0:T(8,128)(2,1)S(1)}, bf16[256,1024]{1,0:T(8,128)(2,1)S(1)}, u32[]{:S(2)}, u32[]{:S(2)}) collective-permute-start(bf16[256,1024]{1,0:T(8,128)(2,1)S(1)} %combine.5), channel_id=1, source_target_pairs={{0,16},{4,12},{8,24},{12,4},{16,0},{20,28},{24,8},{28,20},{1,17},{... | collective-permute-start | bytes 1572872 | tf_op jit(solution)/shard_map/ppermute | solution.py:412
  46.1 4.1 %collective-permute-start.19 = (bf16[128,1024]{1,0:T(8,128)(2,1)S(1)}, bf16[128,1024]{1,0:T(8,128)(2,1)S(1)}, u32[]{:S(2)}, u32[]{:S(2)}) collective-permute-start(bf16[128,1024]{1,0:T(8,128)(2,1)S(1)} %get-tuple-element.88), channel_id=1, source_target_pairs={{0,4},{4,0},{8,12},{12,8},{16,20},{20,16},{24,28},{28,24},{1,5},{5... | collective-permute-start | bytes 786440 | tf_op jit(solution)/shard_map/ppermute | solution.py:408
  49.8 1.6 %collective-permute-start.20 = (bf16[128,1024]{1,0:T(8,128)(2,1)S(1)}, bf16[128,1024]{1,0:T(8,128)(2,1)S(1)}, u32[]{:S(2)}, u32[]{:S(2)}) collective-permute-start(bf16[128,1024]{1,0:T(8,128)(2,1)S(1)} %get-tuple-element.90), channel_id=1, source_target_pairs={{0,4},{4,0},{8,12},{12,8},{16,20},{20,16},{24,28},{28,24},{1,5},{5... | collective-permute-start | bytes 786440 | tf_op jit(solution)/shard_map/ppermute | solution.py:408
  51.7 14.2 %collective-permute-start.21 = (bf16[256,1024]{1,0:T(8,128)(2,1)S(1)}, bf16[256,1024]{1,0:T(8,128)(2,1)S(1)}, u32[]{:S(2)}, u32[]{:S(2)}) collective-permute-start(bf16[256,1024]{1,0:T(8,128)(2,1)S(1)} %combine.7), channel_id=1, source_target_pairs={{0,16},{4,12},{8,24},{12,4},{16,0},{20,28},{24,8},{28,20},{1,17},{... | collective-permute-start | bytes 1572872 | tf_op jit(solution)/shard_map/ppermute | solution.py:412
  54.1 11.9 %collective-permute-start.23 = (bf16[256,1024]{1,0:T(8,128)(2,1)S(1)}, bf16[256,1024]{1,0:T(8,128)(2,1)S(1)}, u32[]{:S(2)}, u32[]{:S(2)}) collective-permute-start(bf16[256,1024]{1,0:T(8,128)(2,1)S(1)} %add.19), channel_id=1, source_target_pairs={{0,8},{4,20},{8,0},{12,28},{16,24},{20,4},{24,16},{28,12},{1,9},{5... | collective-permute-start | bytes 1572872 | tf_op jit(solution)/shard_map/ppermute | solution.py:412
  55.6 1.3 %collective-permute-start.6 = (bf16[64,1024]{1,0:T(8,128)(2,1)S(1)}, bf16[64,1024]{1,0:T(8,128)(2,1)S(1)}, u32[]{:S(2)}, u32[]{:S(2)}) collective-permute-start(bf16[64,1024]{1,0:T(8,128)(2,1)S(1)} %get-tuple-element.68), channel_id=1, source_target_pairs={{0,4},{4,0},{8,12},{12,8},{16,20},{20,16},{24,28},{28,24},{1,5},{5... | collective-permute-start | bytes 393224 | tf_op jit(solution)/shard_map/ppermute | solution.py:408
  55.6 1.5 %collective-permute-start.5 = (bf16[64,1024]{1,0:T(8,128)(2,1)S(1)}, bf16[64,1024]{1,0:T(8,128)(2,1)S(1)}, u32[]{:S(2)}, u32[]{:S(2)}) collective-permute-start(bf16[64,1024]{1,0:T(8,128)(2,1)S(1)} %get-tuple-element.67), channel_id=1, source_target_pairs={{0,4},{4,0},{8,12},{12,8},{16,20},{20,16},{24,28},{28,24},{1,5},{5... | collective-permute-start | bytes 393224 | tf_op jit(solution)/shard_map/ppermute | solution.py:408
  (9 other events, 87.5 us)
